TPU v7x, 512 devices: a whole 4x8x8 slice. The times are simulated.
512 devices in a mesh: dom: 64 (over x, z, core), rep: 8 (over y).
Axes of the slice: x: 4, y: 8, z: 8, core: 2. Of those that a mesh axis runs over, the one named last changes fastest.
Arguments:
- node_feats: bfloat16 [196608, 256], P(('dom', 'rep')), may hold values from -6 to 6
- node_ids: int32 [196608], replicated, may hold values from 0 to 4194303
- tile_row: int32 [64, 8, 64], replicated, may hold values from -1 to 1535, as said below
- tile_col: int32 [64, 8, 64], replicated, may hold values from -1 to 1535, as said below
- tile_count: int32 [64, 8, 64], replicated, may hold values from 1 to 128, as said below
- self_weight: bfloat16 [256, 512], replicated, may hold values from -0.375 to 0.375
- neigh_weight: bfloat16 [256, 512], replicated, may hold values from -3 to 3
- out_grad: bfloat16 [196608, 512], P(('dom', 'rep')), may hold values from -6 to 6
Outputs:
- hidden_out: bfloat16 [196608, 512], P(('dom', 'rep'))
- feat_grad: bfloat16 [196608, 256], P(('dom', 'rep'))
- self_grad: float32 [256, 512], replicated
- neigh_grad: float32 [256, 512], replicated
Inputs may be any that keep to these rules, and one draw needn't show every extreme that they name: `tile_row`: entry [d, r, s] is -1 where the slot holds no tile, else a block row of dom group d: d * 24 plus 0 to 23. In every draw some pair (d, r) has all 64 of its slots filled. `tile_col`: -1 exactly where tile_row is -1; else one of the blocks of device (s, r): s * 24 + r * 3 plus 0 to 2. `tile_count`: read only where a tile is present.
All inputs are finite; a program needn't handle non-finite values.
Results may differ from a plain program's by a relative error of at most 0.01.
Values may be sent and summed in bfloat16 or wider, within the bound.
No kernel may reach another device: no remote copies, remote signals or barrier semaphores. Data moves between devices by JAX's collectives and lax.ppermute only.
A program may use at most 64 MiB of HBM per device.

v0:
```python
import math

import jax
import jax.numpy as jnp
from jax import lax
from jax.sharding import Mesh
from jax.sharding import PartitionSpec as P

TILE = 128
DOM = ("dom_0", "dom_1", "dom_2")
DOM_REP = ("dom_0", "dom_1", "dom_2", "rep")


def split_up(x, dim, length):
    shape = x.shape
    pieces = x.reshape(*shape[:dim], length, shape[dim] // length, *shape[dim + 1 :])
    return jnp.moveaxis(pieces, dim, 0)


def sum_at_owner(x, axis, dim):
    pieces = split_up(x, dim, lax.axis_size(axis))
    arrived = lax.all_to_all(pieces, axis, split_axis=0, concat_axis=0, tiled=True)
    return arrived.astype(jnp.float32).sum(axis=0)


def sum_at_owner_2(x, axis, dim):
    length = lax.axis_size(axis)
    pieces = lax.all_to_all(split_up(x, dim, length), axis, 0, 0, tiled=True)
    return jnp.sum(pieces, axis=0)


def summed_rows(x, axes, dim):
    far, near = axes
    own = sum_at_owner_2(split_up(x, dim, lax.axis_size(far)), near, dim + 1)
    return jnp.sum(lax.all_to_all(own, far, 0, 0, tiled=True), axis=0)


def rows_for(lines, length):
    spare = -len(lines) % length
    return jnp.pad(lines, [(0, spare)] + [(0, 0)] * (lines.ndim - 1))


def copy_for_each(x, axis):
    length = lax.axis_size(axis)
    return lax.all_to_all(jnp.broadcast_to(x[None], (length, *x.shape)), axis, 0, 0, tiled=True)


def joined_along(pieces, dim):
    shape = list(pieces.shape[1:])
    shape[dim] *= pieces.shape[0]
    return jnp.moveaxis(pieces, 0, dim).reshape(shape)


def gather_axes(x, axes, dim):
    far, near = axes
    pieces = copy_for_each(copy_for_each(x, far), near)
    return joined_along(pieces.swapaxes(0, 1).reshape(-1, *x.shape), dim)


def total_of(x, axes):
    own = summed_rows(rows_for(x, lax.axis_size(axes[0]) * lax.axis_size(axes[1])), axes, 0)
    whole = gather_axes(own, axes, 0)
    return whole[: len(x)].reshape(x.shape)


def packed_total(arrays, axis):
    ends = [0]
    for a in arrays:
        ends.append(ends[-1] + a.size)
    subtotal = total_of(jnp.concatenate([a.ravel() for a in arrays]), axis)
    return tuple((subtotal[b:e].reshape(a.shape) for a, b, e in zip(arrays, ends, ends[1:])))


def gather_directly(x, axis, dim):
    return joined_along(copy_for_each(x, axis), dim)


def edge_masks(row_ids, col_ids, limits, tile_size):
    left_ids = (row_ids % 4093)[:, :, None]
    right_ids = (col_ids % 4091)[:, None, :]
    hashed = (left_ids * right_ids + left_ids + 3 * right_ids) % 4099 % tile_size
    return (hashed < limits[:, None, None]).astype(jnp.bfloat16)


def shards(
    node_feats, node_ids, tile_row, tile_col, tile_count, self_weight, neigh_weight, out_grad
):
    dom_total = lax.axis_size(DOM)
    rep_total = lax.axis_size("rep")
    dom_here = lax.axis_index(DOM)
    rep_here = lax.axis_index("rep")
    rows_here, width_in = node_feats.shape
    blocks_here = rows_here // TILE
    group_blocks = blocks_here * rep_total
    id_blocks = node_ids.reshape(-1, TILE)
    group_first = dom_here * group_blocks
    own_first = group_first + rep_here * blocks_here
    inbound_rows = tile_row[dom_here, rep_here]
    inbound_present = inbound_rows >= 0
    inbound_block = jnp.where(inbound_present, inbound_rows, 0)
    inbound_cols = jnp.where(inbound_present, tile_col[dom_here, rep_here], 0)
    inbound_limits = jnp.where(inbound_present, tile_count[dom_here, rep_here], 0)
    inbound_masks = edge_masks(
        id_blocks[inbound_block], id_blocks[inbound_cols], inbound_limits, TILE
    )
    inbound_offset = jnp.where(inbound_present, inbound_block - group_first, 0)
    row_select = (
        (jnp.arange(group_blocks)[:, None] == inbound_offset[None, :]) & inbound_present[None, :]
    ).astype(jnp.float32)
    outbound_cols = tile_col[:, rep_here, dom_here]
    outbound_present = outbound_cols >= 0
    outbound_offset = jnp.where(outbound_present, outbound_cols - own_first, 0)
    own_select = (
        (outbound_offset[:, None] == jnp.arange(blocks_here)[None, :]) & outbound_present[:, None]
    ).astype(jnp.float32)
    feat_blocks = node_feats.reshape(blocks_here, TILE, width_in)
    outgoing = jnp.where(
        outbound_present[:, None, None], feat_blocks[outbound_offset], jnp.zeros((), jnp.bfloat16)
    )
    products = jnp.einsum(
        "sij,sjf->sif",
        inbound_masks,
        lax.all_to_all(outgoing, DOM, split_axis=0, concat_axis=0, tiled=True),
        preferred_element_type=jnp.float32,
    )
    partial_value = jnp.einsum("bs,sif->bif", row_select, products)
    summed = sum_at_owner(
        partial_value.reshape(group_blocks * TILE, width_in).astype(jnp.bfloat16), "rep", 0
    )
    group_rows = tile_row[dom_here].reshape(-1)
    group_limits = tile_count[dom_here].reshape(-1)
    owned_rows = group_rows[:, None] == own_first + jnp.arange(blocks_here)[None, :]
    degree = jnp.sum(jnp.where(owned_rows, group_limits[:, None], 0), axis=0).astype(jnp.float32)
    divisor = jnp.repeat(jnp.maximum(degree, 1.0), TILE)[:, None]
    mean_feats = (summed / divisor).astype(jnp.bfloat16)
    preact = jnp.dot(node_feats, self_weight, preferred_element_type=jnp.float32) + jnp.dot(
        mean_feats, neigh_weight, preferred_element_type=jnp.float32
    )
    hidden_out = jax.nn.silu(preact).astype(jnp.bfloat16)
    logistic = jax.nn.sigmoid(preact)
    pre_grad = (out_grad.astype(jnp.float32) * logistic * (1.0 + preact * (1.0 - logistic))).astype(
        jnp.bfloat16
    )
    over_rows = (((0,), (0,)), ((), ()))
    over_cols = (((1,), (1,)), ((), ()))
    self_term = lax.dot_general(node_feats, pre_grad, over_rows, preferred_element_type=jnp.float32)
    neigh_term = lax.dot_general(
        mean_feats, pre_grad, over_rows, preferred_element_type=jnp.float32
    )
    self_sum, neigh_sum = packed_total(
        (self_term, neigh_term), (("dom_0", "dom_1"), ("dom_2", "rep"))
    )
    grad_scale = 1.0 / math.sqrt(rows_here * dom_total * rep_total)
    mean_grad = lax.dot_general(
        pre_grad, neigh_weight, over_cols, preferred_element_type=jnp.float32
    )
    spread = (mean_grad / divisor).astype(jnp.bfloat16)
    group_spread = gather_directly(spread, "rep", 0).reshape(group_blocks, TILE, width_in)
    picked_rows = group_spread[inbound_offset]
    outbound_rows = tile_row[:, rep_here, dom_here]
    outbound_masks = edge_masks(
        id_blocks[jnp.where(outbound_present, outbound_rows, 0)],
        id_blocks[jnp.where(outbound_present, outbound_cols, 0)],
        jnp.where(outbound_present, tile_count[:, rep_here, dom_here], 0),
        TILE,
    )
    products = jnp.einsum(
        "dij,dif->djf",
        outbound_masks,
        lax.all_to_all(picked_rows, DOM, split_axis=0, concat_axis=0, tiled=True),
        preferred_element_type=jnp.float32,
    )
    transposed = jnp.einsum("db,djf->bjf", own_select, products)
    self_back = lax.dot_general(
        pre_grad, self_weight, over_cols, preferred_element_type=jnp.float32
    )
    feat_grad = (self_back + transposed.reshape(rows_here, width_in)).astype(jnp.bfloat16)
    return (hidden_out, feat_grad, self_sum * grad_scale, neigh_sum * grad_scale)


def solution(mesh):
    torus = Mesh(
        mesh.devices.reshape(4, 8, 2, mesh.shape["rep"]), ("dom_0", "dom_1", "dom_2", "rep")
    )
    in_specs = (P(DOM_REP, None), P(), P(), P(), P(), P(), P(), P(DOM_REP, None))
    out_specs = (P(DOM_REP, None), P(DOM_REP, None), P(), P())
    return jax.shard_map(
        shards, mesh=torus, in_specs=in_specs, out_specs=out_specs, check_vma=False
    )
```

profile of v0, /device:TPU:1, one launch (start us, length us, event | category | flops | bytes accessed | tf_op | source)
XLA Modules:
  0.0 439.1 jit_solution(2671826600485298556)
XLA Ops:
  0.7 2.3 compare_reduce_fusion
  3.0 6.0 %subtract_reduce_fusion = (s32[64]{0:T(128)S(1)}, s32[64]{0:T(128)S(1)}, s32[64]{0:T(128)S(1)}, s32[64]{0:T(128)S(1)}) fusion(s32[]{:T(128)S(6)} %add.217, s32[64,8,64]{2,1,0:T(8,128)} %param.11, s32[]{:T(128)S(6)} %select_n.239, s32[]{:T(128)S(6)} %select_n.238, s32[64,8,64]{2,1,0:T(8,128)} %param.12, s32[64,8,64]{2,1,0:T(8,128)} %param.10), kind=kLoop, calls=%fused_computation.78 | loop fusion | flops 192 | bytes 1804 | tf_op jit(solution)/shard_map/sub | solution.py:112
  9.1 3.7 gather_fusion.2
  12.8 4.5 %broadcast_select_fusion = bf16[64,128,256]{2,1,0:T(8,128)(2,1)} fusion(bf16[64,128,256]{2,1,0:T(8,128)(2,1)} %gather_fusion.2, pred[64]{0:T(512)(128)(4,1)S(1)} %compare_reduce_fusion), kind=kLoop, calls=%fused_computation.28 | loop fusion | flops 2097152 | bytes 8388672 | tf_op jit(solution)/shard_map/jit(_where)/select_n | solution.py:117
  17.3 15.0 %all-to-all-start = ((bf16[64,128,256]{2,1,0:T(8,128)(2,1)}), bf16[64,128,256]{2,1,0:T(8,128)(2,1)}, u32[]{:S(2)}, u32[]{:S(2)}) async-start(bf16[64,128,256]{2,1,0:T(8,128)(2,1)} %broadcast_select_fusion), calls=%async_computation | async-start | bytes 8388608 | tf_op jit(solution)/shard_map/all_to_all | solution.py:123
  32.3 0.7 fusion.67
  35.7 92.5 %all-to-all-done = bf16[64,128,256]{2,1,0:T(8,128)(2,1)} async-done(((bf16[64,128,256]{2,1,0:T(8,128)(2,1)}), bf16[64,128,256]{2,1,0:T(8,128)(2,1)}, u32[]{:S(2)}, u32[]{:S(2)}) %all-to-all-start) | async-done | bytes 4194336 | tf_op jit(solution)/shard_map/all_to_all | solution.py:123
  128.2 8.4 %fusion.16 = bf16[64,128,256]{2,1,0:T(8,128)(2,1)S(1)} fusion(bf16[64,128,256]{2,1,0:T(8,128)(2,1)} %all-to-all-done, s32[64]{0:T(128)S(1)} %get-tuple-element.21, s32[64,128]{1,0:T(8,128)S(1)} %get-tuple-element.16, s32[64,128]{1,0:T(8,128)S(1)} %get-tuple-element.15, s32[64,128]{1,0:T(8,128)S(1)} %add_select_fusion.7), kind=kOutput, calls=%fused_computation.32 | convolution fusion | flops 558891008 | bytes 8487168 | tf_op jit(solution)/shard_map/sij,sjf->sif/dot_general | solution.py:120
  136.6 2.4 fusion.40
  139.0 1.5 copy.32
  140.6 6.8 %all-to-all-start.1 = ((bf16[8,384,256]{2,1,0:T(8,128)(2,1)}), bf16[8,384,256]{2,1,0:T(8,128)(2,1)S(1)}, u32[]{:S(2)}, u32[]{:S(2)}) async-start(bf16[8,384,256]{2,1,0:T(8,128)(2,1)} %bitcast.10), calls=%async_computation.1 | async-start | bytes 3145728 | tf_op jit(solution)/shard_map/all_to_all | solution.py:22
  147.4 0.7 constant_dynamic-slice_fusion
  148.5 1.2 fusion.77
  149.7 36.0 %all-to-all-done.1 = bf16[8,384,256]{2,1,0:T(8,128)(2,1)S(1)} async-done(((bf16[8,384,256]{2,1,0:T(8,128)(2,1)}), bf16[8,384,256]{2,1,0:T(8,128)(2,1)S(1)}, u32[]{:S(2)}, u32[]{:S(2)}) %all-to-all-start.1) | async-done | bytes 1572896 | tf_op jit(solution)/shard_map/all_to_all | solution.py:22
  185.9 2.6 multiply_convert_fusion
  189.9 31.2 %all_to_all.45 = f32[16,32,512]{2,1,0:T(8,128)S(1)} all-to-all(f32[16,32,512]{2,1,0:T(8,128)S(1)} %maximum_bitcast_fusion), channel_id=1, replica_groups=mesh['dom_0'=4,'dom_1'=8,'dom_2'=2,'rep'=8] {'dom_2','rep'}, dimensions={0} | all-to-all | bytes 2097152 | tf_op jit(solution)/shard_map/all_to_all | solution.py:28
  221.2 13.8 %all_to_all.46 = f32[32,1,512]{2,1,0:T(1,128)S(1)} all-to-all(f32[32,1,512]{2,1,0:T(1,128)S(1)} %all_to_all.33), channel_id=1, replica_groups=mesh['dom_0'=4,'dom_1'=8,'dom_2'=2,'rep'=8] {'dom_0','dom_1'}, dimensions={0} | all-to-all | bytes 131072 | tf_op jit(solution)/shard_map/all_to_all | solution.py:35
  235.8 3.9 all-to-all-start.6
  240.0 8.6 %all-to-all-done.6 = f32[32,1,512]{2,1,0:T(1,128)S(1)} async-done(((f32[32,1,512]{2,1,0:T(1,128)}), f32[32,1,512]{2,1,0:T(1,128)S(1)}, u32[]{:S(2)}, u32[]{:S(2)}) %all-to-all-start.6) | async-done | bytes 65568 | tf_op jit(solution)/shard_map/all_to_all | solution.py:45
  248.6 1.3 broadcast_in_dim.87
  249.8 4.6 %all-to-all-start.2 = ((bf16[8,384,256]{2,1,0:T(8,128)(2,1)}), bf16[8,384,256]{2,1,0:T(8,128)(2,1)S(1)}, u32[]{:S(2)}, u32[]{:S(2)}) async-start(bf16[8,384,256]{2,1,0:T(8,128)(2,1)} %broadcast_in_dim.87), calls=%async_computation.2 | async-start | bytes 3145728 | tf_op jit(solution)/shard_map/all_to_all | solution.py:45
  254.4 38.2 %all-to-all-done.2 = bf16[8,384,256]{2,1,0:T(8,128)(2,1)S(1)} async-done(((bf16[8,384,256]{2,1,0:T(8,128)(2,1)}), bf16[8,384,256]{2,1,0:T(8,128)(2,1)S(1)}, u32[]{:S(2)}, u32[]{:S(2)}) %all-to-all-start.2) | async-done | bytes 1572896 | tf_op jit(solution)/shard_map/all_to_all | solution.py:45
  292.6 1.1 broadcast_in_dim.90
  293.7 6.2 %all-to-all-start.7 = ((f32[16,32,512]{2,1,0:T(8,128)}), f32[16,32,512]{2,1,0:T(8,128)S(1)}, u32[]{:S(2)}, u32[]{:S(2)}) async-start(f32[16,32,512]{2,1,0:T(8,128)} %broadcast_in_dim.90), calls=%async_computation.7 | async-start | bytes 2097152 | tf_op jit(solution)/shard_map/all_to_all | solution.py:45
  299.9 2.8 gather_fusion.5
  302.7 23.9 %all-to-all-done.7 = f32[16,32,512]{2,1,0:T(8,128)S(1)} async-done(((f32[16,32,512]{2,1,0:T(8,128)}), f32[16,32,512]{2,1,0:T(8,128)S(1)}, u32[]{:S(2)}, u32[]{:S(2)}) %all-to-all-start.7) | async-done | bytes 1048608 | tf_op jit(solution)/shard_map/all_to_all | solution.py:45
  326.5 5.2 %all-to-all-start.3 = ((bf16[64,128,256]{2,1,0:T(8,128)(2,1)}), bf16[64,128,256]{2,1,0:T(8,128)(2,1)}, u32[]{:S(2)}, u32[]{:S(2)}) async-start(bf16[64,128,256]{2,1,0:T(8,128)(2,1)} %gather_fusion.5), calls=%async_computation.3 | async-start | bytes 8388608 | tf_op jit(solution)/shard_map/all_to_all | solution.py:170
  333.7 1.1 slice_multiply_fusion
  334.8 92.7 %all-to-all-done.3 = bf16[64,128,256]{2,1,0:T(8,128)(2,1)} async-done(((bf16[64,128,256]{2,1,0:T(8,128)(2,1)}), bf16[64,128,256]{2,1,0:T(8,128)(2,1)}, u32[]{:S(2)}, u32[]{:S(2)}) %all-to-all-start.3) | async-done | bytes 4194336 | tf_op jit(solution)/shard_map/all_to_all | solution.py:170
  427.5 8.2 %fusion.14 = bf16[64,128,256]{2,1,0:T(8,128)(2,1)S(1)} fusion(bf16[64,128,256]{2,1,0:T(8,128)(2,1)} %all-to-all-done.3, s32[64]{0:T(128)S(1)} %get-tuple-element.6, s32[64,128]{1,0:T(8,128)S(1)} %get-tuple-element.14, s32[64,128]{1,0:T(8,128)S(1)} %get-tuple-element.13, s32[64,128]{1,0:T(8,128)S(1)} %add_select_fusion.5), kind=kOutput, calls=%fused_computation.31 | convolution fusion | flops 558891008 | bytes 8487168 | tf_op jit(solution)/shard_map/dij,dif->djf/dot_general | solution.py:167
  435.7 2.3 fusion
  438.1 1.0 fusion.43
  (54 shorter events, 7.9 us)
Async XLA Ops:
  0.6 33.1 %copy-start = (s32[196608]{0:T(1024)S(1)}, s32[196608]{0:T(1024)}, u32[]{:S(2)}) copy-start(s32[196608]{0:T(1024)} %param.9) | copy-start | bytes 2359300
  17.3 110.9 %all-to-all-start = ((bf16[64,128,256]{2,1,0:T(8,128)(2,1)}), bf16[64,128,256]{2,1,0:T(8,128)(2,1)}, u32[]{:S(2)}, u32[]{:S(2)}) async-start(bf16[64,128,256]{2,1,0:T(8,128)(2,1)} %broadcast_select_fusion), calls=%async_computation | async-start | bytes 8388608 | tf_op jit(solution)/shard_map/all_to_all | solution.py:123
  139.0 9.5 %copy-start.1 = (bf16[384,256]{1,0:T(8,128)(2,1)S(1)}, bf16[384,256]{1,0:T(8,128)(2,1)}, u32[]{:S(2)}) copy-start(bf16[384,256]{1,0:T(8,128)(2,1)} %param.8) | copy-start | bytes 589828
  139.0 9.5 %copy-start.4 = (bf16[256,512]{1,0:T(8,128)(2,1)S(1)}, bf16[256,512]{1,0:T(8,128)(2,1)}, u32[]{:S(2)}) copy-start(bf16[256,512]{1,0:T(8,128)(2,1)} %param.13) | copy-start | bytes 786436
  139.0 46.8 %copy-start.6 = (bf16[384,512]{1,0:T(8,128)(2,1)S(1)}, bf16[384,512]{1,0:T(8,128)(2,1)}, u32[]{:S(2)}) copy-start(bf16[384,512]{1,0:T(8,128)(2,1)} %param.15) | copy-start | bytes 1179652
  140.6 45.1 %all-to-all-start.1 = ((bf16[8,384,256]{2,1,0:T(8,128)(2,1)}), bf16[8,384,256]{2,1,0:T(8,128)(2,1)S(1)}, u32[]{:S(2)}, u32[]{:S(2)}) async-start(bf16[8,384,256]{2,1,0:T(8,128)(2,1)} %bitcast.10), calls=%async_computation.1 | async-start | bytes 3145728 | tf_op jit(solution)/shard_map/all_to_all | solution.py:22
  188.4 51.2 %copy-start.2 = (bf16[384,512]{1,0:T(8,128)(2,1)}, bf16[384,512]{1,0:T(8,128)(2,1)S(1)}, u32[]{:S(2)}) copy-start(bf16[384,512]{1,0:T(8,128)(2,1)S(1)} %get-tuple-element.11) | copy-start | bytes 1179652
  189.2 50.5 %copy-start.7 = (bf16[256,512]{1,0:T(8,128)(2,1)S(1)}, bf16[256,512]{1,0:T(8,128)(2,1)}, u32[]{:S(2)}) copy-start(bf16[256,512]{1,0:T(8,128)(2,1)} %param.14) | copy-start | bytes 786436
  235.8 12.8 %all-to-all-start.6 = ((f32[32,1,512]{2,1,0:T(1,128)}), f32[32,1,512]{2,1,0:T(1,128)S(1)}, u32[]{:S(2)}, u32[]{:S(2)}) async-start(f32[32,1,512]{2,1,0:T(1,128)} %broadcast_in_dim.88), calls=%async_computation.6 | async-start | bytes 131072 | tf_op jit(solution)/shard_map/all_to_all | solution.py:45
  249.8 42.7 %all-to-all-start.2 = ((bf16[8,384,256]{2,1,0:T(8,128)(2,1)}), bf16[8,384,256]{2,1,0:T(8,128)(2,1)S(1)}, u32[]{:S(2)}, u32[]{:S(2)}) async-start(bf16[8,384,256]{2,1,0:T(8,128)(2,1)} %broadcast_in_dim.87), calls=%async_computation.2 | async-start | bytes 3145728 | tf_op jit(solution)/shard_map/all_to_all | solution.py:45
  293.7 32.9 %all-to-all-start.7 = ((f32[16,32,512]{2,1,0:T(8,128)}), f32[16,32,512]{2,1,0:T(8,128)S(1)}, u32[]{:S(2)}, u32[]{:S(2)}) async-start(f32[16,32,512]{2,1,0:T(8,128)} %broadcast_in_dim.90), calls=%async_computation.7 | async-start | bytes 2097152 | tf_op jit(solution)/shard_map/all_to_all | solution.py:45
  326.5 100.9 %all-to-all-start.3 = ((bf16[64,128,256]{2,1,0:T(8,128)(2,1)}), bf16[64,128,256]{2,1,0:T(8,128)(2,1)}, u32[]{:S(2)}, u32[]{:S(2)}) async-start(bf16[64,128,256]{2,1,0:T(8,128)(2,1)} %gather_fusion.5), calls=%async_computation.3 | async-start | bytes 8388608 | tf_op jit(solution)/shard_map/all_to_all | solution.py:170
  435.6 2.5 copy-start.3
  435.6 2.5 copy-start.5
where the time goes:
time: 440 us; the launch traced here: 439 us
  waiting for transfers between devices  292 us (66%)
  blocking collectives  45 us (10%)
  starting transfers between devices  41.7 us (9%)
  matrix products  27.1 us (6%)
  other arithmetic  16.9 us (4%)
  local copies, waits for them, and re-layouts  15.7 us (4%)
    all_to_all x1, waiting for transfers between devices, shards(): lax.all_to_all(picked_rows, DOM, split_axis=0, concat_axis=0, tiled=True)  92.7 us
    all_to_all x1, waiting for transfers between devices, shards(): lax.all_to_all(outgoing, DOM, split_axis=0, concat_axis=0, tiled=True)  92.5 us
    all_to_all x3, waiting for transfers between devices, copy_for_each(): lax.all_to_all(jnp.broadcast_to(x[None], (length, *x.shape)), axis, 0, 0,...  70.6 us
    all_to_all x1, waiting for transfers between devices, sum_at_owner(): lax.all_to_all(pieces, axis, split_axis=0, concat_axis=0, tiled=True)  36 us
    all_to_all x1, blocking collectives, sum_at_owner_2(): pieces = lax.all_to_all(split_up(x, dim, length), axis, 0, 0, tiled=True)  31.2 us
    all_to_all x1, starting transfers between devices, shards(): lax.all_to_all(outgoing, DOM, split_axis=0, concat_axis=0, tiled=True)  15 us
    all_to_all x3, starting transfers between devices, copy_for_each(): lax.all_to_all(jnp.broadcast_to(x[None], (length, *x.shape)), axis, 0, 0,...  14.7 us
    all_to_all x1, blocking collectives, summed_rows(): return jnp.sum(lax.all_to_all(own, far, 0, 0, tiled=True), axis=0)  13.8 us
  transfers between devices with their start and end apart: 6, of which 6 were waited for; matrix products, arithmetic and copies ran while one was open for 3% of the time, Pallas kernels for 0%

commit v1 on v0

v1 whole, which is shorter than its diff:
```python
import math

import jax
import jax.numpy as jnp
from jax import lax
from jax.experimental import pallas as pl
from jax.experimental.pallas import tpu as pltpu
from jax.sharding import Mesh
from jax.sharding import PartitionSpec as P

TILE = 128
DOM = ("x", "z", "core")
ALL = ("x", "z", "core", "rep")
STEP = 8


def edge_masks(row_ids, col_ids, limits, swapped):
    u = row_ids % 4093
    v = col_ids % 4091
    if swapped:
        u, v = u[:, None, :], v[:, :, None]
    else:
        u, v = u[:, :, None], v[:, None, :]
    hashed = (u * v + u + 3 * v) % 4099 % TILE
    return (hashed < limits[:, None, None]).astype(jnp.bfloat16)


def pair_swap(x, axis, bit):
    n = lax.axis_size(axis)
    return lax.ppermute(x, axis, [(i, i ^ bit) for i in range(n)])


def forward_kernel(offset_ref, mask_ref, feat_ref, out_ref, total_ref):
    step = pl.program_id(0)

    @pl.when(step == 0)
    def _():
        total_ref[...] = jnp.zeros_like(total_ref)

    for t in range(STEP):
        at = offset_ref[step * STEP + t]
        total_ref[at] += jnp.dot(mask_ref[t], feat_ref[t], preferred_element_type=jnp.float32)

    @pl.when(step == pl.num_programs(0) - 1)
    def _():
        out_ref[...] = total_ref[...].astype(out_ref.dtype)


def tile_sums(offsets, masks, feats, blocks):
    slots, tile, width = feats.shape
    return pl.pallas_call(
        forward_kernel,
        grid_spec=pltpu.PrefetchScalarGridSpec(
            num_scalar_prefetch=1,
            grid=(slots // STEP,),
            in_specs=[
                pl.BlockSpec((STEP, tile, tile), lambda i, o: (i, 0, 0)),
                pl.BlockSpec((STEP, tile, width), lambda i, o: (i, 0, 0)),
            ],
            out_specs=pl.BlockSpec((blocks, tile, width), lambda i, o: (0, 0, 0)),
            scratch_shapes=[pltpu.VMEM((blocks, tile, width), jnp.float32)],
        ),
        out_shape=jax.ShapeDtypeStruct((blocks, tile, width), jnp.bfloat16),
        cost_estimate=pl.CostEstimate(
            flops=2 * slots * tile * tile * width,
            bytes_accessed=slots * tile * (tile + width) * 2,
            transcendentals=0,
        ),
        name="tile_sums",
    )(offsets, masks, feats)


def backward_kernel(offset_ref, mask_ref, feat_ref, base_ref, out_ref, total_ref):
    step = pl.program_id(0)

    @pl.when(step == 0)
    def _():
        total_ref[...] = base_ref[...]

    for t in range(STEP):
        at = offset_ref[step * STEP + t]
        total_ref[at] += jnp.dot(mask_ref[t], feat_ref[t], preferred_element_type=jnp.float32)

    @pl.when(step == pl.num_programs(0) - 1)
    def _():
        out_ref[...] = total_ref[...].astype(out_ref.dtype)


def tile_sums_onto(offsets, masks, feats, base):
    slots, tile, width = feats.shape
    blocks = base.shape[0]
    whole = pl.BlockSpec((blocks, tile, width), lambda i, o: (0, 0, 0))
    return pl.pallas_call(
        backward_kernel,
        grid_spec=pltpu.PrefetchScalarGridSpec(
            num_scalar_prefetch=1,
            grid=(slots // STEP,),
            in_specs=[
                pl.BlockSpec((STEP, tile, tile), lambda i, o: (i, 0, 0)),
                pl.BlockSpec((STEP, tile, width), lambda i, o: (i, 0, 0)),
                whole,
            ],
            out_specs=whole,
            scratch_shapes=[pltpu.VMEM((blocks, tile, width), jnp.float32)],
        ),
        out_shape=jax.ShapeDtypeStruct((blocks, tile, width), jnp.bfloat16),
        cost_estimate=pl.CostEstimate(
            flops=2 * slots * tile * tile * width,
            bytes_accessed=slots * tile * (tile + width) * 2,
            transcendentals=0,
        ),
        name="tile_sums_onto",
    )(offsets, masks, feats, base)


def pick_kernel(offset_ref, block_ref, out_ref):
    step = pl.program_id(0)
    for t in range(STEP):
        out_ref[t] = block_ref[offset_ref[step * STEP + t]]


def picked(offsets, blocks):
    slots = offsets.shape[0]
    n, tile, width = blocks.shape
    return pl.pallas_call(
        pick_kernel,
        grid_spec=pltpu.PrefetchScalarGridSpec(
            num_scalar_prefetch=1,
            grid=(slots // STEP,),
            in_specs=[pl.BlockSpec((n, tile, width), lambda i, o: (0, 0, 0))],
            out_specs=pl.BlockSpec((STEP, tile, width), lambda i, o: (i, 0, 0)),
        ),
        out_shape=jax.ShapeDtypeStruct((slots, tile, width), blocks.dtype),
        cost_estimate=pl.CostEstimate(
            flops=0, bytes_accessed=(n + slots) * tile * width * 2, transcendentals=0
        ),
        name="picked",
    )(offsets, blocks)


def shards(
    node_feats, node_ids, tile_row, tile_col, tile_count, self_weight, neigh_weight, out_grad
):
    dom_total = lax.axis_size(DOM)
    rep_total = lax.axis_size("rep")
    dom_here = lax.axis_index(DOM)
    rep_here = lax.axis_index("rep")
    core = lax.axis_index("core")
    rows_here, width_in = node_feats.shape
    width_out = self_weight.shape[1]
    blocks_here = rows_here // TILE
    group_blocks = blocks_here * rep_total
    id_blocks = node_ids.reshape(-1, TILE)
    group_first = dom_here * group_blocks
    own_first = group_first + rep_here * blocks_here

    def sent_tiles(table):
        return lax.dynamic_slice(table, (0, rep_here, dom_here), (dom_total, 1, 1)).reshape(-1)

    def held_tiles(table):
        return lax.dynamic_slice(table, (dom_here, rep_here, 0), (1, 1, dom_total)).reshape(-1)

    sent_cols = sent_tiles(tile_col)
    sent_there = sent_cols >= 0
    sent_offset = jnp.where(sent_there, sent_cols - own_first, 0)
    feat_blocks = node_feats.reshape(blocks_here, 1, TILE, width_in)
    choice = sent_offset[:, None, None]
    outgoing = jnp.broadcast_to(feat_blocks[0], (dom_total, TILE, width_in))
    for b in range(1, blocks_here):
        outgoing = jnp.where(choice == b, feat_blocks[b], outgoing)
    arrived = lax.all_to_all(outgoing, DOM, split_axis=0, concat_axis=0, tiled=True)

    held_rows = held_tiles(tile_row)
    held_there = held_rows >= 0
    held_block = jnp.where(held_there, held_rows, 0)
    held_cols = jnp.where(held_there, held_tiles(tile_col), 0)
    held_limits = jnp.where(held_there, held_tiles(tile_count), 0)
    held_offset = jnp.where(held_there, held_block - group_first, 0)
    held_masks = edge_masks(id_blocks[held_block], id_blocks[held_cols], held_limits, False)

    sent_rows = jnp.where(sent_there, sent_tiles(tile_row), 0)
    sent_limits = jnp.where(sent_there, sent_tiles(tile_count), 0)
    sent_masks = edge_masks(
        id_blocks[sent_rows], id_blocks[jnp.where(sent_there, sent_cols, 0)], sent_limits, True
    )

    partial_sums = tile_sums(held_offset, held_masks, arrived, group_blocks)
    pieces = lax.all_to_all(
        partial_sums.reshape(rep_total, rows_here, width_in), "rep", 0, 0, tiled=True
    )
    summed = pieces.astype(jnp.float32).sum(axis=0)

    group_rows = lax.dynamic_slice_in_dim(tile_row, dom_here, 1, 0).reshape(-1)
    group_limits = lax.dynamic_slice_in_dim(tile_count, dom_here, 1, 0).reshape(-1)
    owned_rows = group_rows[:, None] == own_first + jnp.arange(blocks_here)[None, :]
    degree = jnp.sum(jnp.where(owned_rows, group_limits[:, None], 0), axis=0).astype(jnp.float32)
    divisor = jnp.repeat(jnp.maximum(degree, 1.0), TILE)[:, None]
    mean_feats = (summed / divisor).astype(jnp.bfloat16)
    preact = jnp.dot(node_feats, self_weight, preferred_element_type=jnp.float32) + jnp.dot(
        mean_feats, neigh_weight, preferred_element_type=jnp.float32
    )
    hidden_out = jax.nn.silu(preact).astype(jnp.bfloat16)
    logistic = jax.nn.sigmoid(preact)
    pre_grad = (out_grad.astype(jnp.float32) * logistic * (1.0 + preact * (1.0 - logistic))).astype(
        jnp.bfloat16
    )
    over_rows = (((0,), (0,)), ((), ()))
    over_cols = (((1,), (1,)), ((), ()))
    mean_grad = lax.dot_general(
        pre_grad, neigh_weight, over_cols, preferred_element_type=jnp.float32
    )
    spread = (mean_grad / divisor).astype(jnp.bfloat16)
    self_term = lax.dot_general(node_feats, pre_grad, over_rows, preferred_element_type=jnp.float32)
    neigh_term = lax.dot_general(
        mean_feats, pre_grad, over_rows, preferred_element_type=jnp.float32
    )
    first = core == 0
    kept = jnp.where(first, self_term, neigh_term) + lax.ppermute(
        jnp.where(first, neigh_term, self_term), "core", [(0, 1), (1, 0)]
    )
    grad_rows = width_in * width_out // rep_total // width_in
    kept = kept.reshape(rep_total, -1, width_out).astype(jnp.bfloat16)
    kept = jnp.concatenate([kept[:, :, :width_in], kept[:, :, width_in:]], axis=1)
    both = jnp.concatenate(
        [jnp.broadcast_to(spread[None], (rep_total, rows_here, width_in)), kept], axis=1
    )
    both = lax.all_to_all(both, "rep", 0, 0, tiled=True)
    group_spread = both[:, :rows_here].reshape(group_blocks, TILE, width_in)
    share = both[:, rows_here:].astype(jnp.float32).sum(axis=0)

    returning = picked(held_offset, group_spread)
    returning, share = lax.optimization_barrier((returning, share))
    returned = lax.all_to_all(returning, DOM, split_axis=0, concat_axis=0, tiled=True)

    for axis in ("x", "z"):
        bit = 1
        while bit < lax.axis_size(axis):
            share = share + pair_swap(share, axis, bit)
            bit *= 2
    share = share[None] * (1.0 / math.sqrt(rows_here * dom_total * rep_total))
    bit = 1
    while bit < rep_total:
        other = pair_swap(share, "rep", bit)
        low = (rep_here & bit) == 0
        share = jnp.where(
            low, jnp.concatenate([share, other]), jnp.concatenate([other, share])
        )
        bit *= 2
    half = grad_rows // 2
    share = jnp.concatenate([share[:, :half], share[:, half:]], axis=2).reshape(width_in, width_out)
    other = lax.ppermute(share, "core", [(0, 1), (1, 0)])
    self_grad = jnp.where(first, share, other)
    neigh_grad = jnp.where(first, other, share)

    self_back = lax.dot_general(
        pre_grad, self_weight, over_cols, preferred_element_type=jnp.float32
    )
    feat_grad = tile_sums_onto(
        sent_offset, sent_masks, returned, self_back.reshape(blocks_here, TILE, width_in)
    ).reshape(rows_here, width_in)
    return (hidden_out, feat_grad, self_grad, neigh_grad)


def solution(mesh):
    torus = Mesh(mesh.devices.reshape(4, 8, 2, mesh.shape["rep"]), ALL)
    in_specs = (P(ALL, None), P(), P(), P(), P(), P(), P(), P(ALL, None))
    out_specs = (P(ALL, None), P(ALL, None), P(), P())
    return jax.shard_map(
        shards, mesh=torus, in_specs=in_specs, out_specs=out_specs, check_vma=False
    )
```

time: 440 us -> 413 us (0.939)
  waiting for transfers between devices: 292 us -> 238 us
  Pallas kernels: 0 us -> 21.9 us
  matrix products: 27.1 us -> 5.98 us
  starting transfers between devices: 41.7 us -> 61.1 us
  other arithmetic: 16.9 us -> 26.9 us
  local copies, waits for them, and re-layouts: 15.7 us -> 7.95 us
    all_to_all x5 -> x2, waiting for transfers between devices: 199 us -> 36 us  [the longest x1 36 us: shards(): lax.all_to_all(partial_sums.reshape(rep_total, rows_here, width_in), 'rep...]
    ppermute x0 -> x10, waiting for transfers between devices: none -> 118 us  [the longest x8 117 us: pair_swap(): return lax.ppermute(x, axis, [(i, i ^ bit) for i in range(n)])]
    ppermute x0 -> x10, starting transfers between devices: none -> 32.6 us  [the longest x8 23.9 us: pair_swap(): return lax.ppermute(x, axis, [(i, i ^ bit) for i in range(n)])]
    pallas_call x0 -> x3, Pallas kernels: none -> 21.9 us  [the longest x1 8.53 us: tile_sums(): pl.pallas_call(forward_kernel, grid_spec=pltpu.PrefetchScalarGridSpec(num...]
    dot_general x4 -> x0, matrix products: 21.3 us -> none  [the longest x1 8.45 us: shards(): jnp.einsum('sij,sjf->sif', inbound_masks, lax.all_to_all(outgoing, DOM, s...]
    all_to_all x5 -> x2, starting transfers between devices: 26.7 us -> 13.5 us  [the longest x1 6.82 us: shards(): lax.all_to_all(partial_sums.reshape(rep_total, rows_here, width_in), 'rep...]
    convert_element_type x0 -> x3, other arithmetic: none -> 12.9 us  [the longest x2 12.7 us: edge_masks(): return (hashed < limits[:, None, None]).astype(jnp.bfloat16)]
    all_to_all x1, waiting for transfers between devices: 92.5 us -> 84.4 us  [shards(): lax.all_to_all(outgoing, DOM, split_axis=0, concat_axis=0, tiled=True)]
  transfers between devices with their start and end apart: 6 -> 13, of which waited for: 6 -> 11; matrix products, arithmetic and copies ran while one was open for 3% -> 6% of each run, Pallas kernels for 0% -> 0%
where the time goes in v1:
time: 413 us; the launch traced here: 411 us
  waiting for transfers between devices  238 us (58%)
  starting transfers between devices  61.1 us (15%)
  blocking collectives  48.1 us (12%)
  other arithmetic  26.9 us (7%)
  Pallas kernels  21.9 us (5%)
  local copies, waits for them, and re-layouts  7.95 us (2%)
  matrix products  5.98 us (1%)
    ppermute x8, waiting for transfers between devices, pair_swap(): return lax.ppermute(x, axis, [(i, i ^ bit) for i in range(n)])  117 us
    all_to_all x1, waiting for transfers between devices, shards(): lax.all_to_all(outgoing, DOM, split_axis=0, concat_axis=0, tiled=True)  84.4 us
    all_to_all x1, blocking collectives, shards(): both = lax.all_to_all(both, 'rep', 0, 0, tiled=True)  48.1 us
    all_to_all x1, waiting for transfers between devices, shards(): lax.all_to_all(partial_sums.reshape(rep_total, rows_here, width_in), 'rep...  36 us
    ppermute x8, starting transfers between devices, pair_swap(): return lax.ppermute(x, axis, [(i, i ^ bit) for i in range(n)])  23.9 us
    all_to_all x1, starting transfers between devices, shards(): lax.all_to_all(outgoing, DOM, split_axis=0, concat_axis=0, tiled=True)  15 us
    convert_element_type x2, other arithmetic, edge_masks(): return (hashed < limits[:, None, None]).astype(jnp.bfloat16)  12.7 us
    pallas_call x1, Pallas kernels, tile_sums(): pl.pallas_call(forward_kernel, grid_spec=pltpu.PrefetchScalarGridSpec(num...  8.53 us
  transfers between devices with their start and end apart: 13, of which 11 were waited for; matrix products, arithmetic and copies ran while one was open for 6% of the time, Pallas kernels for 0%

profile of v1, /device:TPU:1, one launch (start us, length us, event | category | flops | bytes accessed | tf_op | source)
XLA Modules:
  0.0 411.4 jit_solution(4645061242632012726)
XLA Ops:
  0.7 5.2 %fusion.14 = (s32[64]{0:T(128)S(1)}, s32[64]{0:T(128)S(1)}, s32[64]{0:T(128)}, s32[64,1,1]{2,1,0:T(1,128)S(1)}) fusion(s32[64,8,64]{2,1,0:T(8,128)} %param.11, s32[]{:T(128)S(6)} %select_n.235, s32[]{:T(128)S(6)} %select_n.234, s32[64,8,64]{2,1,0:T(8,128)} %param.12, s32[]{:T(128)S(6)} %add.206), kind=kLoop, calls=%fused_computation.78 | loop fusion | flops 256 | bytes 1548 | tf_op jit(solution)/shard_map/dynamic_slice | solution.py:158
  5.9 2.4 compare_reduce_fusion.1
  9.2 2.5 select_select_fusion
  11.7 15.0 %all-to-all-start = ((bf16[64,128,256]{2,1,0:T(8,128)(2,1)}), bf16[64,128,256]{2,1,0:T(8,128)(2,1)}, u32[]{:S(2)}, u32[]{:S(2)}) async-start(bf16[64,128,256]{2,1,0:T(8,128)(2,1)} %select_select_fusion), calls=%async_computation | async-start | bytes 8388608 | tf_op jit(solution)/shard_map/all_to_all | solution.py:171
  26.7 2.3 dynamic-slice_reduce_fusion
  32.2 6.0 %fusion.11.mask_ref = bf16[64,128,128]{2,1,0:T(8,128)(2,1)} fusion(s32[64]{0:T(128)S(1)} %get-tuple-element.26, s32[64,128]{1,0:T(8,128)S(1)} %get-tuple-element.34, s32[64,128]{1,0:T(8,128)S(1)} %get-tuple-element.33, s32[64,128]{1,0:T(8,128)S(1)} %add_select_fusion.7), kind=kLoop, calls=%fused_computation.26 | loop fusion | flops 23068672 | bytes 2195712 | tf_op jit(solution)/shard_map/convert_element_type | solution.py:25
  38.2 84.4 %all-to-all-done.feat_ref = bf16[64,128,256]{2,1,0:T(8,128)(2,1)} async-done(((bf16[64,128,256]{2,1,0:T(8,128)(2,1)}), bf16[64,128,256]{2,1,0:T(8,128)(2,1)}, u32[]{:S(2)}, u32[]{:S(2)}) %all-to-all-start) | async-done | bytes 4194336 | tf_op jit(solution)/shard_map/all_to_all | solution.py:171
  122.6 8.5 %tile_sums.1 = bf16[24,128,256]{2,1,0:T(8,128)(2,1)} custom-call(s32[64]{0:T(128)} %get-tuple-element.27.offset_ref, bf16[64,128,128]{2,1,0:T(8,128)(2,1)} %fusion.11.mask_ref, bf16[64,128,256]{2,1,0:T(8,128)(2,1)} %all-to-all-done.feat_ref), custom_call_target="tpu_custom_call" | custom-call | flops 536870912 | bytes 6291456 | tf_op jit(solution)/shard_map/tile_sums/pallas_call | solution.py:51
  131.1 6.8 %all-to-all-start.1 = ((bf16[8,384,256]{2,1,0:T(8,128)(2,1)}), bf16[8,384,256]{2,1,0:T(8,128)(2,1)S(1)}, u32[]{:S(2)}, u32[]{:S(2)}) async-start(bf16[8,384,256]{2,1,0:T(8,128)(2,1)} %bitcast.65), calls=%async_computation.1 | async-start | bytes 3145728 | tf_op jit(solution)/shard_map/all_to_all | solution.py:188
  140.2 36.0 %all-to-all-done.1 = bf16[8,384,256]{2,1,0:T(8,128)(2,1)S(1)} async-done(((bf16[8,384,256]{2,1,0:T(8,128)(2,1)}), bf16[8,384,256]{2,1,0:T(8,128)(2,1)S(1)}, u32[]{:S(2)}, u32[]{:S(2)}) %all-to-all-start.1) | async-done | bytes 1572896 | tf_op jit(solution)/shard_map/all_to_all | solution.py:188
  176.4 2.7 multiply_convert_fusion
  179.9 4.6 %collective-permute-start = (f32[256,512]{1,0:T(8,128)S(1)}, f32[256,512]{1,0:T(8,128)S(1)}, u32[]{:S(2)}, u32[]{:S(2)}) collective-permute-start(f32[256,512]{1,0:T(8,128)S(1)} %get-tuple-element.37), channel_id=1, source_target_pairs={{0,8},{8,0},{1,9},{9,1},{2,10},{10,2},{3,11},{11,3},{4,12},{12,4},... | collective-permute-start | bytes 1572872 | tf_op jit(solution)/shard_map/ppermute | solution.py:218
  186.5 48.1 %all_to_all.20 = bf16[8,448,256]{2,1,0:T(8,128)(2,1)S(1)} all-to-all(bf16[8,448,256]{2,1,0:T(8,128)(2,1)S(1)} %pad_maximum_fusion), channel_id=1, replica_groups=mesh['x'=4,'z'=8,'core'=2,'rep'=8] {'rep'}, dimensions={0} | all-to-all | bytes 3670016 | tf_op jit(solution)/shard_map/all_to_all | solution.py:227
  235.8 5.7 %picked.1 = bf16[64,128,256]{2,1,0:T(8,128)(2,1)} custom-call(s32[64]{0:T(128)} %get-tuple-element.27.offset_ref, bf16[24,128,256]{2,1,0:T(8,128)(2,1)} %bitcast.64), custom_call_target="tpu_custom_call" | custom-call | bytes 5767168 | tf_op jit(solution)/shard_map/picked/pallas_call | solution.py:125
  241.5 6.7 %all-to-all-start.3 = ((bf16[64,128,256]{2,1,0:T(8,128)(2,1)}), bf16[64,128,256]{2,1,0:T(8,128)(2,1)}, u32[]{:S(2)}, u32[]{:S(2)}) async-start(bf16[64,128,256]{2,1,0:T(8,128)(2,1)} %picked.1), calls=%async_computation.3 | async-start | bytes 8388608 | tf_op jit(solution)/shard_map/all_to_all | solution.py:233
  248.2 3.3 collective-permute-start.1
  251.5 9.2 %collective-permute-done.1 = f32[64,256]{1,0:T(8,128)S(1)} collective-permute-done((f32[64,256]{1,0:T(8,128)S(1)}, f32[64,256]{1,0:T(8,128)S(1)}, u32[]{:S(2)}, u32[]{:S(2)}) %collective-permute-start.1) | collective-permute-done | bytes 65568 | tf_op jit(solution)/shard_map/ppermute | solution.py:30
  260.7 4.5 %collective-permute-start.2 = (f32[64,256]{1,0:T(8,128)S(1)}, f32[64,256]{1,0:T(8,128)S(1)}, u32[]{:S(2)}, u32[]{:S(2)}) collective-permute-start(f32[64,256]{1,0:T(8,128)S(1)} %add.222), channel_id=1, source_target_pairs={{0,256},{128,384},{256,0},{384,128},{1,257},{129,385},{257,1},{385... | collective-permute-start | bytes 196616 | tf_op jit(solution)/shard_map/ppermute | solution.py:30
  265.2 2.6 collective-permute-done.2
  267.8 3.6 collective-permute-start.3
  271.5 69.9 %collective-permute-done.3 = f32[64,256]{1,0:T(8,128)S(1)} collective-permute-done((f32[64,256]{1,0:T(8,128)S(1)}, f32[64,256]{1,0:T(8,128)S(1)}, u32[]{:S(2)}, u32[]{:S(2)}) %collective-permute-start.3) | collective-permute-done | bytes 65568 | tf_op jit(solution)/shard_map/ppermute | solution.py:30
  341.4 2.2 collective-permute-start.4
  343.6 6.0 %collective-permute-done.4 = f32[64,256]{1,0:T(8,128)S(1)} collective-permute-done((f32[64,256]{1,0:T(8,128)S(1)}, f32[64,256]{1,0:T(8,128)S(1)}, u32[]{:S(2)}, u32[]{:S(2)}) %collective-permute-start.4) | collective-permute-done | bytes 65568 | tf_op jit(solution)/shard_map/ppermute | solution.py:30
  349.6 4.2 %collective-permute-start.5 = (f32[64,256]{1,0:T(8,128)S(1)}, f32[64,256]{1,0:T(8,128)S(1)}, u32[]{:S(2)}, u32[]{:S(2)}) collective-permute-start(f32[64,256]{1,0:T(8,128)S(1)} %add.225), channel_id=1, source_target_pairs={{0,64},{16,80},{32,96},{48,112},{64,0},{80,16},{96,32},{112,48},{1... | collective-permute-start | bytes 196616 | tf_op jit(solution)/shard_map/ppermute | solution.py:30
  353.8 6.1 %collective-permute-done.5 = f32[64,256]{1,0:T(8,128)S(1)} collective-permute-done((f32[64,256]{1,0:T(8,128)S(1)}, f32[64,256]{1,0:T(8,128)S(1)}, u32[]{:S(2)}, u32[]{:S(2)}) %collective-permute-start.5) | collective-permute-done | bytes 65568 | tf_op jit(solution)/shard_map/ppermute | solution.py:30
  360.0 2.2 collective-permute-start.6
  362.8 2.2 collective-permute-done.6
  367.0 8.2 %collective-permute-done.7 = f32[2,64,256]{2,1,0:T(8,128)S(1)} collective-permute-done((f32[2,64,256]{2,1,0:T(8,128)S(1)}, f32[2,64,256]{2,1,0:T(8,128)S(1)}, u32[]{:S(2)}, u32[]{:S(2)}) %collective-permute-start.7) | collective-permute-done | bytes 131104 | tf_op jit(solution)/shard_map/ppermute | solution.py:30
  377.8 12.6 %collective-permute-done.8 = f32[4,64,256]{2,1,0:T(8,128)S(1)} collective-permute-done((f32[4,64,256]{2,1,0:T(8,128)S(1)}, f32[4,64,256]{2,1,0:T(8,128)S(1)}, u32[]{:S(2)}, u32[]{:S(2)}) %collective-permute-start.8) | collective-permute-done | bytes 262176 | tf_op jit(solution)/shard_map/ppermute | solution.py:30
  390.6 4.1 %collective-permute-start.9 = (f32[256,512]{1,0:T(8,128)S(1)}, f32[256,512]{1,0:T(8,128)S(1)}, u32[]{:S(2)}, u32[]{:S(2)}) collective-permute-start(f32[256,512]{1,0:T(8,128)S(1)} %bitcast.66), channel_id=1, source_target_pairs={{0,8},{8,0},{1,9},{9,1},{2,10},{10,2},{3,11},{11,3},{4,12},{12,4},... | collective-permute-start | bytes 1572872 | tf_op jit(solution)/shard_map/ppermute | solution.py:251
  394.7 6.8 %fusion.10.mask_ref = bf16[64,128,128]{2,1,0:T(8,128)(2,1)} fusion(s32[64]{0:T(128)S(1)} %get-tuple-element.9, s32[64,128]{1,0:T(8,128)S(1)} %get-tuple-element.32, s32[64,128]{1,0:T(8,128)S(1)} %get-tuple-element.31, s32[64,128]{1,0:T(8,128)S(1)} %add_select_fusion.5), kind=kLoop, calls=%fused_computation.25 | loop fusion | flops 23068672 | bytes 2195712 | tf_op jit(solution)/shard_map/convert_element_type | solution.py:25
  403.7 7.7 %tile_sums_onto.1 = bf16[3,128,256]{2,1,0:T(8,128)(2,1)} custom-call(s32[64]{0:T(128)} %get-tuple-element.22.offset_ref, bf16[64,128,128]{2,1,0:T(8,128)(2,1)} %fusion.10.mask_ref, bf16[64,128,256]{2,1,0:T(8,128)(2,1)} %all-to-all-done.3.feat_ref, f32[3,128,256]{2,1,0:T(8,128)} %bitcast.67), custom_call_target="tpu_custom_call" | custom-call | flops 536870912 | bytes 6291456 | tf_op jit(solution)/shard_map/tile_sums_onto/pallas_call | solution.py:93
  (58 shorter events, 18.1 us)
Async XLA Ops:
  0.6 29.1 %copy-start = (s32[196608]{0:T(1024)S(1)}, s32[196608]{0:T(1024)}, u32[]{:S(2)}) copy-start(s32[196608]{0:T(1024)} %param.9) | copy-start | bytes 2359300
  11.7 110.9 %all-to-all-start = ((bf16[64,128,256]{2,1,0:T(8,128)(2,1)}), bf16[64,128,256]{2,1,0:T(8,128)(2,1)}, u32[]{:S(2)}, u32[]{:S(2)}) async-start(bf16[64,128,256]{2,1,0:T(8,128)(2,1)} %select_select_fusion), calls=%async_computation | async-start | bytes 8388608 | tf_op jit(solution)/shard_map/all_to_all | solution.py:171
  122.6 16.5 %copy-start.1 = (bf16[384,256]{1,0:T(8,128)(2,1)S(1)}, bf16[384,256]{1,0:T(8,128)(2,1)}, u32[]{:S(2)}) copy-start(bf16[384,256]{1,0:T(8,128)(2,1)} %param.8) | copy-start | bytes 589828
  122.6 16.5 %copy-start.2 = (bf16[256,512]{1,0:T(8,128)(2,1)S(1)}, bf16[256,512]{1,0:T(8,128)(2,1)}, u32[]{:S(2)}) copy-start(bf16[256,512]{1,0:T(8,128)(2,1)} %param.13) | copy-start | bytes 786436
  131.1 45.1 %all-to-all-start.1 = ((bf16[8,384,256]{2,1,0:T(8,128)(2,1)}), bf16[8,384,256]{2,1,0:T(8,128)(2,1)S(1)}, u32[]{:S(2)}, u32[]{:S(2)}) async-start(bf16[8,384,256]{2,1,0:T(8,128)(2,1)} %bitcast.65), calls=%async_computation.1 | async-start | bytes 3145728 | tf_op jit(solution)/shard_map/all_to_all | solution.py:188
  176.4 8.1 %copy-start.3 = (bf16[256,512]{1,0:T(8,128)(2,1)S(1)}, bf16[256,512]{1,0:T(8,128)(2,1)}, u32[]{:S(2)}) copy-start(bf16[256,512]{1,0:T(8,128)(2,1)} %param.14) | copy-start | bytes 786436
  179.9 6.1 %collective-permute-start = (f32[256,512]{1,0:T(8,128)S(1)}, f32[256,512]{1,0:T(8,128)S(1)}, u32[]{:S(2)}, u32[]{:S(2)}) collective-permute-start(f32[256,512]{1,0:T(8,128)S(1)} %get-tuple-element.37), channel_id=1, source_target_pairs={{0,8},{8,0},{1,9},{9,1},{2,10},{10,2},{3,11},{11,3},{4,12},{12,4},... | collective-permute-start | bytes 1572872 | tf_op jit(solution)/shard_map/ppermute | solution.py:218
  241.5 162.2 %all-to-all-start.3 = ((bf16[64,128,256]{2,1,0:T(8,128)(2,1)}), bf16[64,128,256]{2,1,0:T(8,128)(2,1)}, u32[]{:S(2)}, u32[]{:S(2)}) async-start(bf16[64,128,256]{2,1,0:T(8,128)(2,1)} %picked.1), calls=%async_computation.3 | async-start | bytes 8388608 | tf_op jit(solution)/shard_map/all_to_all | solution.py:233
  248.2 12.5 %collective-permute-start.1 = (f32[64,256]{1,0:T(8,128)S(1)}, f32[64,256]{1,0:T(8,128)S(1)}, u32[]{:S(2)}, u32[]{:S(2)}) collective-permute-start(f32[64,256]{1,0:T(8,128)S(1)} %convert_reduce_fusion.1), channel_id=1, source_target_pairs={{0,128},{128,0},{256,384},{384,256},{1,129},{129,1},{257,385},{385... | collective-permute-start | bytes 196616 | tf_op jit(solution)/shard_map/ppermute | solution.py:30
  260.7 7.1 %collective-permute-start.2 = (f32[64,256]{1,0:T(8,128)S(1)}, f32[64,256]{1,0:T(8,128)S(1)}, u32[]{:S(2)}, u32[]{:S(2)}) collective-permute-start(f32[64,256]{1,0:T(8,128)S(1)} %add.222), channel_id=1, source_target_pairs={{0,256},{128,384},{256,0},{384,128},{1,257},{129,385},{257,1},{385... | collective-permute-start | bytes 196616 | tf_op jit(solution)/shard_map/ppermute | solution.py:30
  267.8 73.6 %collective-permute-start.3 = (f32[64,256]{1,0:T(8,128)S(1)}, f32[64,256]{1,0:T(8,128)S(1)}, u32[]{:S(2)}, u32[]{:S(2)}) collective-permute-start(f32[64,256]{1,0:T(8,128)S(1)} %add.223), channel_id=1, source_target_pairs={{0,16},{16,0},{32,48},{48,32},{64,80},{80,64},{96,112},{112,96},{1... | collective-permute-start | bytes 196616 | tf_op jit(solution)/shard_map/ppermute | solution.py:30
  341.4 8.2 %collective-permute-start.4 = (f32[64,256]{1,0:T(8,128)S(1)}, f32[64,256]{1,0:T(8,128)S(1)}, u32[]{:S(2)}, u32[]{:S(2)}) collective-permute-start(f32[64,256]{1,0:T(8,128)S(1)} %add.224), channel_id=1, source_target_pairs={{0,32},{16,48},{32,0},{48,16},{64,96},{80,112},{96,64},{112,80},{1... | collective-permute-start | bytes 196616 | tf_op jit(solution)/shard_map/ppermute | solution.py:30
  349.6 10.4 %collective-permute-start.5 = (f32[64,256]{1,0:T(8,128)S(1)}, f32[64,256]{1,0:T(8,128)S(1)}, u32[]{:S(2)}, u32[]{:S(2)}) collective-permute-start(f32[64,256]{1,0:T(8,128)S(1)} %add.225), channel_id=1, source_target_pairs={{0,64},{16,80},{32,96},{48,112},{64,0},{80,16},{96,32},{112,48},{1... | collective-permute-start | bytes 196616 | tf_op jit(solution)/shard_map/ppermute | solution.py:30
  360.0 5.0 %collective-permute-start.6 = (f32[1,64,256]{2,1,0:T(8,128)S(1)}, f32[1,64,256]{2,1,0:T(8,128)S(1)}, u32[]{:S(2)}, u32[]{:S(2)}) collective-permute-start(f32[1,64,256]{2,1,0:T(8,128)S(1)} %multiply_bitcast_fusion), channel_id=1, source_target_pairs={{0,1},{1,0},{2,3},{3,2},{4,5},{5,4},{6,7},{7,6},{8,9},{9,8},{10,11... | collective-permute-start | bytes 196616 | tf_op jit(solution)/shard_map/ppermute | solution.py:30
  365.0 10.2 %collective-permute-start.7 = (f32[2,64,256]{2,1,0:T(8,128)S(1)}, f32[2,64,256]{2,1,0:T(8,128)S(1)}, u32[]{:S(2)}, u32[]{:S(2)}) collective-permute-start(f32[2,64,256]{2,1,0:T(8,128)S(1)} %maximum_select_fusion.2), channel_id=1, source_target_pairs={{0,2},{1,3},{2,0},{3,1},{4,6},{5,7},{6,4},{7,5},{8,10},{9,11},{10,... | collective-permute-start | bytes 393224 | tf_op jit(solution)/shard_map/ppermute | solution.py:30
  375.2 15.2 %collective-permute-start.8 = (f32[4,64,256]{2,1,0:T(8,128)S(1)}, f32[4,64,256]{2,1,0:T(8,128)S(1)}, u32[]{:S(2)}, u32[]{:S(2)}) collective-permute-start(f32[4,64,256]{2,1,0:T(8,128)S(1)} %maximum_select_fusion.1), channel_id=1, source_target_pairs={{0,4},{1,5},{2,6},{3,7},{4,0},{5,1},{6,2},{7,3},{8,12},{9,13},{10,... | collective-permute-start | bytes 786440 | tf_op jit(solution)/shard_map/ppermute | solution.py:30
  390.6 12.0 %collective-permute-start.9 = (f32[256,512]{1,0:T(8,128)S(1)}, f32[256,512]{1,0:T(8,128)S(1)}, u32[]{:S(2)}, u32[]{:S(2)}) collective-permute-start(f32[256,512]{1,0:T(8,128)S(1)} %bitcast.66), channel_id=1, source_target_pairs={{0,8},{8,0},{1,9},{9,1},{2,10},{10,2},{3,11},{11,3},{4,12},{12,4},... | collective-permute-start | bytes 1572872 | tf_op jit(solution)/shard_map/ppermute | solution.py:251

commit v2 on v1

v2 whole, which is shorter than its diff:
```python
import math

import jax
import jax.numpy as jnp
from jax import lax
from jax.experimental import pallas as pl
from jax.experimental.pallas import tpu as pltpu
from jax.sharding import Mesh
from jax.sharding import PartitionSpec as P

TILE = 128
DOM = ("x", "z", "core")
ALL = ("x", "z", "core", "rep")
STEP = 8


def edge_masks(row_ids, col_ids, limits, swapped):
    u = row_ids % 4093
    v = col_ids % 4091
    if swapped:
        u, v = u[:, None, :], v[:, :, None]
    else:
        u, v = u[:, :, None], v[:, None, :]
    hashed = (u * v + u + 3 * v) % 4099 % TILE
    return (hashed < limits[:, None, None]).astype(jnp.bfloat16)


def pair_swap(x, axis, bit):
    n = lax.axis_size(axis)
    return lax.ppermute(x, axis, [(i, i ^ bit) for i in range(n)])


def forward_kernel(offset_ref, mask_ref, feat_ref, out_ref, total_ref):
    step = pl.program_id(0)

    @pl.when(step == 0)
    def _():
        total_ref[...] = jnp.zeros_like(total_ref)

    products = [
        jnp.dot(mask_ref[t], feat_ref[t], preferred_element_type=jnp.float32) for t in range(STEP)
    ]
    for t in range(STEP):
        total_ref[offset_ref[step * STEP + t]] += products[t]

    @pl.when(step == pl.num_programs(0) - 1)
    def _():
        out_ref[...] = total_ref[...].astype(out_ref.dtype)


def tile_sums(offsets, masks, feats, blocks):
    slots, tile, width = feats.shape
    return pl.pallas_call(
        forward_kernel,
        grid_spec=pltpu.PrefetchScalarGridSpec(
            num_scalar_prefetch=1,
            grid=(slots // STEP,),
            in_specs=[
                pl.BlockSpec((STEP, tile, tile), lambda i, o: (i, 0, 0)),
                pl.BlockSpec((STEP, tile, width), lambda i, o: (i, 0, 0)),
            ],
            out_specs=pl.BlockSpec((blocks, tile, width), lambda i, o: (0, 0, 0)),
            scratch_shapes=[pltpu.VMEM((blocks, tile, width), jnp.float32)],
        ),
        out_shape=jax.ShapeDtypeStruct((blocks, tile, width), jnp.bfloat16),
        cost_estimate=pl.CostEstimate(
            flops=2 * slots * tile * tile * width,
            bytes_accessed=slots * tile * (tile + width) * 2,
            transcendentals=0,
        ),
        name="tile_sums",
    )(offsets, masks, feats)


def products_kernel(offset_ref, mask_ref, block_ref, out_ref):
    step = pl.program_id(0)
    for t in range(STEP):
        out_ref[t] = jnp.dot(
            mask_ref[t],
            block_ref[offset_ref[step * STEP + t]],
            preferred_element_type=jnp.float32,
        ).astype(out_ref.dtype)


def tile_products(offsets, masks, blocks):
    slots, tile, _ = masks.shape
    n, _, width = blocks.shape
    return pl.pallas_call(
        products_kernel,
        grid_spec=pltpu.PrefetchScalarGridSpec(
            num_scalar_prefetch=1,
            grid=(slots // STEP,),
            in_specs=[
                pl.BlockSpec((STEP, tile, tile), lambda i, o: (i, 0, 0)),
                pl.BlockSpec((n, tile, width), lambda i, o: (0, 0, 0)),
            ],
            out_specs=pl.BlockSpec((STEP, tile, width), lambda i, o: (i, 0, 0)),
        ),
        out_shape=jax.ShapeDtypeStruct((slots, tile, width), jnp.bfloat16),
        cost_estimate=pl.CostEstimate(
            flops=2 * slots * tile * tile * width,
            bytes_accessed=slots * tile * (tile + width) * 2,
            transcendentals=0,
        ),
        name="tile_products",
    )(offsets, masks, blocks)


def gathered_kernel(offset_ref, part_ref, out_ref, total_ref):
    step = pl.program_id(0)

    @pl.when(step == 0)
    def _():
        total_ref[...] = jnp.zeros_like(total_ref)

    for t in range(STEP):
        total_ref[offset_ref[step * STEP + t]] += part_ref[t].astype(jnp.float32)

    @pl.when(step == pl.num_programs(0) - 1)
    def _():
        out_ref[...] = total_ref[...].astype(out_ref.dtype)


def summed_into(offsets, parts, blocks):
    slots, tile, width = parts.shape
    return pl.pallas_call(
        gathered_kernel,
        grid_spec=pltpu.PrefetchScalarGridSpec(
            num_scalar_prefetch=1,
            grid=(slots // STEP,),
            in_specs=[pl.BlockSpec((STEP, tile, width), lambda i, o: (i, 0, 0))],
            out_specs=pl.BlockSpec((blocks, tile, width), lambda i, o: (0, 0, 0)),
            scratch_shapes=[pltpu.VMEM((blocks, tile, width), jnp.float32)],
        ),
        out_shape=jax.ShapeDtypeStruct((blocks, tile, width), jnp.bfloat16),
        cost_estimate=pl.CostEstimate(
            flops=slots * tile * width, bytes_accessed=slots * tile * width * 2, transcendentals=0
        ),
        name="summed_into",
    )(offsets, parts)


def pick_kernel(offset_ref, block_ref, out_ref, sems):
    slots = out_ref.shape[0]
    copies = [
        pltpu.make_async_copy(block_ref.at[offset_ref[t]], out_ref.at[t], sems.at[t])
        for t in range(slots)
    ]
    for copy in copies:
        copy.start()
    for copy in copies:
        copy.wait()


def picked(offsets, blocks):
    slots = offsets.shape[0]
    n, tile, width = blocks.shape
    return pl.pallas_call(
        pick_kernel,
        in_specs=[
            pl.BlockSpec(memory_space=pltpu.SMEM),
            pl.BlockSpec(memory_space=pltpu.VMEM),
        ],
        out_specs=pl.BlockSpec(memory_space=pl.ANY),
        scratch_shapes=[pltpu.SemaphoreType.DMA((slots,))],
        out_shape=jax.ShapeDtypeStruct((slots, tile, width), blocks.dtype),
        cost_estimate=pl.CostEstimate(
            flops=0, bytes_accessed=(n + slots) * tile * width * 2, transcendentals=0
        ),
        name="picked",
    )(offsets, blocks)


def halved(x, axis, bit):
    half = x.shape[0] // 2
    low = (lax.axis_index(axis) & bit) == 0
    other = pair_swap(jnp.where(low, x[half:], x[:half]), axis, bit)
    return jnp.where(low, x[:half], x[half:]) + other


def doubled(x, axis, bit):
    low = (lax.axis_index(axis) & bit) == 0
    other = pair_swap(x, axis, bit)
    return jnp.where(low, jnp.concatenate([x, other]), jnp.concatenate([other, x]))


def shards(
    node_feats, node_ids, tile_row, tile_col, tile_count, self_weight, neigh_weight, out_grad
):
    dom_total = lax.axis_size(DOM)
    rep_total = lax.axis_size("rep")
    x_total, z_total, core_total = (lax.axis_size(a) for a in DOM)
    dom_here = lax.axis_index(DOM)
    rep_here = lax.axis_index("rep")
    x_here, z_here, core = (lax.axis_index(a) for a in DOM)
    rows_here, width_in = node_feats.shape
    blocks_here = rows_here // TILE
    group_blocks = blocks_here * rep_total
    id_blocks = node_ids.reshape(-1, TILE)
    group_first = dom_here * group_blocks
    bits_of = {
        a: [1 << i for i in range(lax.axis_size(a).bit_length() - 1)] for a in ("x", "z", "rep")
    }

    column = lax.all_to_all(
        jnp.broadcast_to(node_feats[None], (z_total, rows_here, width_in)), "z", 0, 0, tiled=True
    ).reshape(z_total * blocks_here, TILE, width_in)

    def passed_tiles(table):
        table = table.reshape(x_total, z_total, core_total, rep_total, dom_total)
        table = lax.dynamic_slice(
            table, (0, z_here, 0, rep_here, 0), (x_total, 1, core_total, 1, dom_total)
        ).reshape(x_total * core_total, x_total, z_total, core_total)
        table = lax.dynamic_slice_in_dim(table, x_here, 1, 1)
        return lax.dynamic_slice_in_dim(table, core, 1, 3).reshape(-1)

    passed_cols = passed_tiles(tile_col)
    place = jnp.tile(jnp.arange(z_total), x_total * core_total)
    passed_first = ((x_here * z_total + place) * core_total + core) * group_blocks
    passed_first = passed_first + rep_here * blocks_here
    passed_offset = place * blocks_here + jnp.where(
        passed_cols >= 0, passed_cols - passed_first, 0
    )

    def held_tiles(table):
        row = lax.dynamic_slice(table, (dom_here, rep_here, 0), (1, 1, dom_total))
        return row.reshape(x_total, z_total, core_total).swapaxes(1, 2).reshape(-1)

    held_rows = held_tiles(tile_row)
    held_there = held_rows >= 0
    held_block = jnp.where(held_there, held_rows, 0)
    held_cols = jnp.where(held_there, held_tiles(tile_col), 0)
    held_limits = jnp.where(held_there, held_tiles(tile_count), 0)
    held_offset = jnp.where(held_there, held_block - group_first, 0)
    row_ids, col_ids = id_blocks[held_block], id_blocks[held_cols]
    masks = edge_masks(row_ids, col_ids, held_limits, False)
    masks_swapped = edge_masks(row_ids, col_ids, held_limits, True)

    arrived = lax.all_to_all(
        picked(passed_offset, column), ("x", "core"), 0, 0, tiled=True
    )
    partial_sums = tile_sums(held_offset, masks, arrived, group_blocks)
    pieces = lax.all_to_all(
        partial_sums.reshape(rep_total, rows_here, width_in), "rep", 0, 0, tiled=True
    )
    summed = pieces.astype(jnp.float32).sum(axis=0)

    own_first = group_first + rep_here * blocks_here
    group_rows = lax.dynamic_slice_in_dim(tile_row, dom_here, 1, 0).reshape(-1)
    group_limits = lax.dynamic_slice_in_dim(tile_count, dom_here, 1, 0).reshape(-1)
    owned_rows = group_rows[:, None] == own_first + jnp.arange(blocks_here)[None, :]
    degree = jnp.sum(jnp.where(owned_rows, group_limits[:, None], 0), axis=0).astype(jnp.float32)
    divisor = jnp.repeat(jnp.maximum(degree, 1.0), TILE)[:, None]
    mean_feats = (summed / divisor).astype(jnp.bfloat16)
    preact = jnp.dot(node_feats, self_weight, preferred_element_type=jnp.float32) + jnp.dot(
        mean_feats, neigh_weight, preferred_element_type=jnp.float32
    )
    hidden_out = jax.nn.silu(preact).astype(jnp.bfloat16)
    logistic = jax.nn.sigmoid(preact)
    pre_grad = (out_grad.astype(jnp.float32) * logistic * (1.0 + preact * (1.0 - logistic))).astype(
        jnp.bfloat16
    )
    over_rows = (((0,), (0,)), ((), ()))
    over_cols = (((1,), (1,)), ((), ()))
    mean_grad = lax.dot_general(
        pre_grad, neigh_weight, over_cols, preferred_element_type=jnp.float32
    )
    spread = (mean_grad / divisor).astype(jnp.bfloat16)
    group_spread = lax.all_to_all(
        jnp.broadcast_to(spread[None], (rep_total, rows_here, width_in)), "rep", 0, 0, tiled=True
    ).reshape(group_blocks, TILE, width_in)

    self_term = lax.dot_general(node_feats, pre_grad, over_rows, preferred_element_type=jnp.float32)
    neigh_term = lax.dot_general(
        mean_feats, pre_grad, over_rows, preferred_element_type=jnp.float32
    )
    first = core == 0
    share = jnp.where(first, self_term, neigh_term) + lax.ppermute(
        jnp.where(first, neigh_term, self_term), "core", [(0, 1), (1, 0)]
    )
    for axis in ("x", "z"):
        for bit in bits_of[axis]:
            share = halved(share, axis, bit)

    returning = tile_products(held_offset, masks_swapped, group_spread)
    returning, share = lax.optimization_barrier((returning, share))
    returned = lax.all_to_all(returning, ("x", "core"), 0, 0, tiled=True)
    for bit in bits_of["rep"]:
        share = share + pair_swap(share, "rep", bit)
    share = share * (1.0 / math.sqrt(rows_here * dom_total * rep_total))
    for bit in reversed(bits_of["z"]):
        share = doubled(share, "z", bit)
    column_sums = summed_into(passed_offset, returned, z_total * blocks_here)
    column_sums, share = lax.optimization_barrier((column_sums, share))
    parts = lax.all_to_all(
        column_sums.reshape(z_total, rows_here, width_in), "z", 0, 0, tiled=True
    )
    for bit in reversed(bits_of["x"]):
        share = doubled(share, "x", bit)
    other = lax.ppermute(share, "core", [(0, 1), (1, 0)])
    self_grad = jnp.where(first, share, other)
    neigh_grad = jnp.where(first, other, share)

    self_back = lax.dot_general(
        pre_grad, self_weight, over_cols, preferred_element_type=jnp.float32
    )
    transposed = parts.astype(jnp.float32).sum(axis=0)
    feat_grad = (self_back + transposed).astype(jnp.bfloat16)
    return (hidden_out, feat_grad, self_grad, neigh_grad)


def solution(mesh):
    torus = Mesh(mesh.devices.reshape(4, 8, 2, mesh.shape["rep"]), ALL)
    in_specs = (P(ALL, None), P(), P(), P(), P(), P(), P(), P(ALL, None))
    out_specs = (P(ALL, None), P(ALL, None), P(), P())
    return jax.shard_map(
        shards, mesh=torus, in_specs=in_specs, out_specs=out_specs, check_vma=False
    )
```

time: 413 us -> 341 us (0.83)
  blocking collectives: 48.1 us -> 0 us
  waiting for transfers between devices: 238 us -> 191 us
  starting transfers between devices: 61.1 us -> 83.7 us
  other arithmetic: 26.9 us -> 15.4 us
  Pallas kernels: 21.9 us -> 27.9 us
  local copies, waits for them, and re-layouts: 7.95 us -> 12.7 us
    ppermute x8 -> x13, waiting for transfers between devices: 117 us -> 56.1 us  [pair_swap(): return lax.ppermute(x, axis, [(i, i ^ bit) for i in range(n)])]
    all_to_all x1 -> x0, blocking collectives: 48.1 us -> none  [shards(): both = lax.all_to_all(both, 'rep', 0, 0, tiled=True)]
    all_to_all x2 -> x5, starting transfers between devices: 21.7 us -> 34.1 us  [the longest x1 10.9 us: shards(): lax.all_to_all(jnp.broadcast_to(node_feats[None], (z_total, rows_here, wi...]
    ppermute x8 -> x13, starting transfers between devices: 23.9 us -> 35.7 us  [pair_swap(): return lax.ppermute(x, axis, [(i, i ^ bit) for i in range(n)])]
    all_to_all x2 -> x5, waiting for transfers between devices: 84.4 us -> 95.3 us  [the longest x1 36.2 us: shards(): lax.all_to_all(jnp.broadcast_to(node_feats[None], (z_total, rows_here, wi...]
    pallas_call x2 -> x3, Pallas kernels: 13.4 us -> 19.4 us  [the longest x1 8.3 us: tile_products(): pl.pallas_call(products_kernel, grid_spec=pltpu.PrefetchScalarGridSpec(nu...]
    dynamic_slice x1 -> x0, other arithmetic: 5.25 us -> none  [sent_tiles(): lax.dynamic_slice(table, (0, rep_here, dom_here), (dom_total, 1, 1))]
    convert_element_type x2 -> x1, other arithmetic: 12.7 us -> 11 us  [edge_masks(): return (hashed < limits[:, None, None]).astype(jnp.bfloat16)]
  transfers between devices with their start and end apart: 13 -> 21, of which waited for: 11 -> 19; matrix products, arithmetic and copies ran while one was open for 6% -> 7% of each run, Pallas kernels for 0% -> 0%
where the time goes in v2:
time: 341 us; the launch traced here: 339 us
  waiting for transfers between devices  191 us (56%)
  starting transfers between devices  83.7 us (25%)
  Pallas kernels  27.9 us (8%)
  other arithmetic  15.4 us (5%)
  local copies, waits for them, and re-layouts  12.7 us (4%)
  matrix products  6.76 us (2%)
    ppermute x13, waiting for transfers between devices, pair_swap(): return lax.ppermute(x, axis, [(i, i ^ bit) for i in range(n)])  56.1 us
    all_to_all x1, waiting for transfers between devices, shards(): lax.all_to_all(partial_sums.reshape(rep_total, rows_here, width_in), 'rep...  38.1 us
    all_to_all x1, waiting for transfers between devices, shards(): lax.all_to_all(jnp.broadcast_to(node_feats[None], (z_total, rows_here, wi...  36.2 us
    ppermute x13, starting transfers between devices, pair_swap(): return lax.ppermute(x, axis, [(i, i ^ bit) for i in range(n)])  35.7 us
    all_to_all x1, waiting for transfers between devices, shards(): lax.all_to_all(picked(passed_offset, column), ('x', 'core'), 0, 0, tiled=...  33.7 us
    all_to_all x1, waiting for transfers between devices, shards(): lax.all_to_all(column_sums.reshape(z_total, rows_here, width_in), 'z', 0,...  15.4 us
    convert_element_type x1, other arithmetic, edge_masks(): return (hashed < limits[:, None, None]).astype(jnp.bfloat16)  11 us
    all_to_all x1, starting transfers between devices, shards(): lax.all_to_all(jnp.broadcast_to(node_feats[None], (z_total, rows_here, wi...  10.9 us
  transfers between devices with their start and end apart: 21, of which 19 were waited for; matrix products, arithmetic and copies ran while one was open for 7% of the time, Pallas kernels for 0%

profile of v2, /device:TPU:1, one launch (start us, length us, event | category | flops | bytes accessed | tf_op | source)
XLA Modules:
  0.0 338.8 jit_solution(11738900290500008294)
XLA Ops:
  2.9 10.9 %all-to-all-start = ((bf16[8,384,256]{2,1,0:T(8,128)(2,1)}), bf16[8,384,256]{2,1,0:T(8,128)(2,1)S(1)}, u32[]{:S(2)}, u32[]{:S(2)}) async-start(bf16[8,384,256]{2,1,0:T(8,128)(2,1)} %broadcast_in_dim.26), calls=%async_computation | async-start | bytes 3145728 | tf_op jit(solution)/shard_map/all_to_all | solution.py:205
  15.8 36.2 %all-to-all-done = bf16[8,384,256]{2,1,0:T(8,128)(2,1)S(1)} async-done(((bf16[8,384,256]{2,1,0:T(8,128)(2,1)}), bf16[8,384,256]{2,1,0:T(8,128)(2,1)S(1)}, u32[]{:S(2)}, u32[]{:S(2)}) %all-to-all-start) | async-done | bytes 1572896 | tf_op jit(solution)/shard_map/all_to_all | solution.py:205
  53.2 4.0 %picked.1 = bf16[64,128,256]{2,1,0:T(8,128)(2,1)} custom-call(s32[64]{0:T(128)} %fusion.18.offset_ref, bf16[24,128,256]{2,1,0:T(8,128)(2,1)} %bitcast.32), custom_call_target="tpu_custom_call" | custom-call | bytes 5767168 | tf_op jit(solution)/shard_map/picked/pallas_call | solution.py:158
  57.3 7.1 %all-to-all-start.1 = ((bf16[64,128,256]{2,1,0:T(8,128)(2,1)}), bf16[64,128,256]{2,1,0:T(8,128)(2,1)}, u32[]{:S(2)}, u32[]{:S(2)}) async-start(bf16[64,128,256]{2,1,0:T(8,128)(2,1)} %picked.1), calls=%async_computation.1 | async-start | bytes 8388608 | tf_op jit(solution)/shard_map/all_to_all | solution.py:239
  68.6 11.0 %fusion.10 = (bf16[64,128,128]{2,1,0:T(8,128)(2,1)}, bf16[64,128,128]{2,1,0:T(8,128)(2,1)}) fusion(s32[64,128]{1,0:T(8,128)S(1)} %get-tuple-element.19, s32[64,128]{1,0:T(8,128)S(1)} %get-tuple-element.18, s32[64,128]{1,0:T(8,128)S(1)} %add_select_fusion.5, s32[64]{0:T(128)S(1)} %get-tuple-element.22), kind=kLoop, calls=%fused_computation.22 | loop fusion | flops 46137344 | bytes 4292864 | tf_op jit(solution)/shard_map/convert_element_type | solution.py:25
  79.5 33.7 %all-to-all-done.1.feat_ref = bf16[64,128,256]{2,1,0:T(8,128)(2,1)} async-done(((bf16[64,128,256]{2,1,0:T(8,128)(2,1)}), bf16[64,128,256]{2,1,0:T(8,128)(2,1)}, u32[]{:S(2)}, u32[]{:S(2)}) %all-to-all-start.1) | async-done | bytes 4194336 | tf_op jit(solution)/shard_map/all_to_all | solution.py:239
  113.3 8.5 %tile_sums.1 = bf16[24,128,256]{2,1,0:T(8,128)(2,1)} custom-call(s32[64]{0:T(128)} %get-tuple-element.23.offset_ref, bf16[64,128,128]{2,1,0:T(8,128)(2,1)} %get-tuple-element.17.mask_ref, bf16[64,128,256]{2,1,0:T(8,128)(2,1)} %all-to-all-done.1.feat_ref), custom_call_target="tpu_custom_call" | custom-call | flops 536870912 | bytes 6291456 | tf_op jit(solution)/shard_map/tile_sums/pallas_call | solution.py:53
  121.8 7.0 %all-to-all-start.2 = ((bf16[8,384,256]{2,1,0:T(8,128)(2,1)}), bf16[8,384,256]{2,1,0:T(8,128)(2,1)S(1)}, u32[]{:S(2)}, u32[]{:S(2)}) async-start(bf16[8,384,256]{2,1,0:T(8,128)(2,1)} %bitcast.35), calls=%async_computation.2 | async-start | bytes 3145728 | tf_op jit(solution)/shard_map/all_to_all | solution.py:243
  131.1 38.1 %all-to-all-done.2 = bf16[8,384,256]{2,1,0:T(8,128)(2,1)S(1)} async-done(((bf16[8,384,256]{2,1,0:T(8,128)(2,1)}), bf16[8,384,256]{2,1,0:T(8,128)(2,1)S(1)}, u32[]{:S(2)}, u32[]{:S(2)}) %all-to-all-start.2) | async-done | bytes 1572896 | tf_op jit(solution)/shard_map/all_to_all | solution.py:243
  169.5 2.6 multiply_convert_fusion
  177.8 3.6 %all-to-all-start.3 = ((bf16[8,384,256]{2,1,0:T(8,128)(2,1)}), bf16[8,384,256]{2,1,0:T(8,128)(2,1)S(1)}, u32[]{:S(2)}, u32[]{:S(2)}) async-start(bf16[8,384,256]{2,1,0:T(8,128)(2,1)} %broadcast_in_dim.49), calls=%async_computation.3 | async-start | bytes 3145728 | tf_op jit(solution)/shard_map/all_to_all | solution.py:269
  185.8 7.7 %collective-permute-done.1 = f32[128,512]{1,0:T(8,128)S(1)} collective-permute-done((f32[128,512]{1,0:T(8,128)S(1)}, f32[128,512]{1,0:T(8,128)S(1)}, u32[]{:S(2)}, u32[]{:S(2)}) %collective-permute-start.1) | collective-permute-done | bytes 262176 | tf_op jit(solution)/shard_map/ppermute | solution.py:30
  193.6 2.8 collective-permute-start.2
  196.4 4.9 %collective-permute-done.2 = f32[64,512]{1,0:T(8,128)S(1)} collective-permute-done((f32[64,512]{1,0:T(8,128)S(1)}, f32[64,512]{1,0:T(8,128)S(1)}, u32[]{:S(2)}, u32[]{:S(2)}) %collective-permute-start.2) | collective-permute-done | bytes 131104 | tf_op jit(solution)/shard_map/ppermute | solution.py:30
  203.6 3.1 collective-permute-done.3
  208.9 3.7 %collective-permute-done.4 = f32[16,512]{1,0:T(8,128)S(1)} collective-permute-done((f32[16,512]{1,0:T(8,128)S(1)}, f32[16,512]{1,0:T(8,128)S(1)}, u32[]{:S(2)}, u32[]{:S(2)}) %collective-permute-start.4) | collective-permute-done | bytes 32800 | tf_op jit(solution)/shard_map/ppermute | solution.py:30
  214.5 6.8 %collective-permute-done.5 = f32[8,512]{1,0:T(8,128)S(1)} collective-permute-done((f32[8,512]{1,0:T(8,128)S(1)}, f32[8,512]{1,0:T(8,128)S(1)}, u32[]{:S(2)}, u32[]{:S(2)}) %collective-permute-start.5) | collective-permute-done | bytes 16416 | tf_op jit(solution)/shard_map/ppermute | solution.py:30
  222.5 8.3 %tile_products.1 = bf16[64,128,256]{2,1,0:T(8,128)(2,1)} custom-call(s32[64]{0:T(128)} %get-tuple-element.23.offset_ref, bf16[64,128,128]{2,1,0:T(8,128)(2,1)} %get-tuple-element.16.mask_ref, bf16[24,128,256]{2,1,0:T(8,128)(2,1)} %bitcast.34), custom_call_target="tpu_custom_call" | custom-call | flops 536870912 | bytes 6291456 | tf_op jit(solution)/shard_map/tile_products/pallas_call | solution.py:88
  230.8 8.9 %all-to-all-start.4 = ((bf16[64,128,256]{2,1,0:T(8,128)(2,1)}), bf16[64,128,256]{2,1,0:T(8,128)(2,1)}, u32[]{:S(2)}, u32[]{:S(2)}) async-start(bf16[64,128,256]{2,1,0:T(8,128)(2,1)} %tile_products.1), calls=%async_computation.4 | async-start | bytes 8388608 | tf_op jit(solution)/shard_map/all_to_all | solution.py:287
  239.7 3.0 collective-permute-start.6
  244.5 3.9 %collective-permute-start.7 = (f32[8,512]{1,0:T(8,128)S(1)}, f32[8,512]{1,0:T(8,128)S(1)}, u32[]{:S(2)}, u32[]{:S(2)}) collective-permute-start(f32[8,512]{1,0:T(8,128)S(1)} %add.252), channel_id=1, source_target_pairs={{0,2},{1,3},{2,0},{3,1},{4,6},{5,7},{6,4},{7,5},{8,10},{9,11},{10,... | collective-permute-start | bytes 49160 | tf_op jit(solution)/shard_map/ppermute | solution.py:30
  250.3 7.1 %collective-permute-start.8 = (f32[8,512]{1,0:T(8,128)S(1)}, f32[8,512]{1,0:T(8,128)S(1)}, u32[]{:S(2)}, u32[]{:S(2)}) collective-permute-start(f32[8,512]{1,0:T(8,128)S(1)} %add.253), channel_id=1, source_target_pairs={{0,4},{1,5},{2,6},{3,7},{4,0},{5,1},{6,2},{7,3},{8,12},{9,13},{10,... | collective-permute-start | bytes 49160 | tf_op jit(solution)/shard_map/ppermute | solution.py:30
  260.7 6.4 %collective-permute-done.9 = f32[8,512]{1,0:T(8,128)S(1)} collective-permute-done((f32[8,512]{1,0:T(8,128)S(1)}, f32[8,512]{1,0:T(8,128)S(1)}, u32[]{:S(2)}, u32[]{:S(2)}) %collective-permute-start.9) | collective-permute-done | bytes 16416 | tf_op jit(solution)/shard_map/ppermute | solution.py:30
  269.1 4.2 %collective-permute-done.10 = f32[16,512]{1,0:T(8,128)S(1)} collective-permute-done((f32[16,512]{1,0:T(8,128)S(1)}, f32[16,512]{1,0:T(8,128)S(1)}, u32[]{:S(2)}, u32[]{:S(2)}) %collective-permute-start.10) | collective-permute-done | bytes 32800 | tf_op jit(solution)/shard_map/ppermute | solution.py:30
  275.2 3.5 %collective-permute-done.11 = f32[32,512]{1,0:T(8,128)S(1)} collective-permute-done((f32[32,512]{1,0:T(8,128)S(1)}, f32[32,512]{1,0:T(8,128)S(1)}, u32[]{:S(2)}, u32[]{:S(2)}) %collective-permute-start.11) | collective-permute-done | bytes 65568 | tf_op jit(solution)/shard_map/ppermute | solution.py:30
  278.7 9.9 %all-to-all-done.4.part_ref = bf16[64,128,256]{2,1,0:T(8,128)(2,1)} async-done(((bf16[64,128,256]{2,1,0:T(8,128)(2,1)}), bf16[64,128,256]{2,1,0:T(8,128)(2,1)}, u32[]{:S(2)}, u32[]{:S(2)}) %all-to-all-start.4) | async-done | bytes 4194336 | tf_op jit(solution)/shard_map/all_to_all | solution.py:287
  288.6 7.1 %summed_into.1 = bf16[24,128,256]{2,1,0:T(8,128)(2,1)} custom-call(s32[64]{0:T(128)} %fusion.18.offset_ref, bf16[64,128,256]{2,1,0:T(8,128)(2,1)} %all-to-all-done.4.part_ref), custom_call_target="tpu_custom_call" | custom-call | flops 2097152 | bytes 4194304 | tf_op jit(solution)/shard_map/summed_into/pallas_call | solution.py:126
  295.7 3.7 %all-to-all-start.5 = ((bf16[8,384,256]{2,1,0:T(8,128)(2,1)}), bf16[8,384,256]{2,1,0:T(8,128)(2,1)S(1)}, u32[]{:S(2)}, u32[]{:S(2)}) async-start(bf16[8,384,256]{2,1,0:T(8,128)(2,1)} %bitcast.33), calls=%async_computation.5 | async-start | bytes 3145728 | tf_op jit(solution)/shard_map/all_to_all | solution.py:295
  301.6 5.3 %collective-permute-done.12 = f32[64,512]{1,0:T(8,128)S(1)} collective-permute-done((f32[64,512]{1,0:T(8,128)S(1)}, f32[64,512]{1,0:T(8,128)S(1)}, u32[]{:S(2)}, u32[]{:S(2)}) %collective-permute-start.12) | collective-permute-done | bytes 131104 | tf_op jit(solution)/shard_map/ppermute | solution.py:30
  309.2 5.7 %collective-permute-done.13 = f32[128,512]{1,0:T(8,128)S(1)} collective-permute-done((f32[128,512]{1,0:T(8,128)S(1)}, f32[128,512]{1,0:T(8,128)S(1)}, u32[]{:S(2)}, u32[]{:S(2)}) %collective-permute-start.13) | collective-permute-done | bytes 262176 | tf_op jit(solution)/shard_map/ppermute | solution.py:30
  314.9 4.6 %collective-permute-start.14 = (f32[256,512]{1,0:T(8,128)S(1)}, f32[256,512]{1,0:T(8,128)S(1)}, u32[]{:S(2)}, u32[]{:S(2)}) collective-permute-start(f32[256,512]{1,0:T(8,128)S(1)} %maximum_select_fusion), channel_id=1, source_target_pairs={{0,8},{8,0},{1,9},{9,1},{2,10},{10,2},{3,11},{11,3},{4,12},{12,4},... | collective-permute-start | bytes 1572872 | tf_op jit(solution)/shard_map/ppermute | solution.py:300
  322.1 15.4 %all-to-all-done.5 = bf16[8,384,256]{2,1,0:T(8,128)(2,1)S(1)} async-done(((bf16[8,384,256]{2,1,0:T(8,128)(2,1)}), bf16[8,384,256]{2,1,0:T(8,128)(2,1)S(1)}, u32[]{:S(2)}, u32[]{:S(2)}) %all-to-all-start.5) | async-done | bytes 1572896 | tf_op jit(solution)/shard_map/all_to_all | solution.py:295
  (103 shorter events, 49.0 us)
Async XLA Ops:
  0.6 66.2 %copy-start = (s32[196608]{0:T(1024)S(1)}, s32[196608]{0:T(1024)}, u32[]{:S(2)}) copy-start(s32[196608]{0:T(1024)} %param.9) | copy-start | bytes 2359300
  2.9 49.1 %all-to-all-start = ((bf16[8,384,256]{2,1,0:T(8,128)(2,1)}), bf16[8,384,256]{2,1,0:T(8,128)(2,1)S(1)}, u32[]{:S(2)}, u32[]{:S(2)}) async-start(bf16[8,384,256]{2,1,0:T(8,128)(2,1)} %broadcast_in_dim.26), calls=%async_computation | async-start | bytes 3145728 | tf_op jit(solution)/shard_map/all_to_all | solution.py:205
  52.1 1.2 copy-start.1
  57.3 56.0 %all-to-all-start.1 = ((bf16[64,128,256]{2,1,0:T(8,128)(2,1)}), bf16[64,128,256]{2,1,0:T(8,128)(2,1)}, u32[]{:S(2)}, u32[]{:S(2)}) async-start(bf16[64,128,256]{2,1,0:T(8,128)(2,1)} %picked.1), calls=%async_computation.1 | async-start | bytes 8388608 | tf_op jit(solution)/shard_map/all_to_all | solution.py:239
  113.3 16.6 %copy-start.5 = (bf16[384,256]{1,0:T(8,128)(2,1)S(1)}, bf16[384,256]{1,0:T(8,128)(2,1)}, u32[]{:S(2)}) copy-start(bf16[384,256]{1,0:T(8,128)(2,1)} %param.8) | copy-start | bytes 589828
  113.3 16.6 %copy-start.6 = (bf16[256,512]{1,0:T(8,128)(2,1)S(1)}, bf16[256,512]{1,0:T(8,128)(2,1)}, u32[]{:S(2)}) copy-start(bf16[256,512]{1,0:T(8,128)(2,1)} %param.13) | copy-start | bytes 786436
  121.8 47.6 %copy-start.9 = (bf16[384,512]{1,0:T(8,128)(2,1)S(1)}, bf16[384,512]{1,0:T(8,128)(2,1)}, u32[]{:S(2)}) copy-start(bf16[384,512]{1,0:T(8,128)(2,1)} %param.15) | copy-start | bytes 1179652
  121.8 47.4 %all-to-all-start.2 = ((bf16[8,384,256]{2,1,0:T(8,128)(2,1)}), bf16[8,384,256]{2,1,0:T(8,128)(2,1)S(1)}, u32[]{:S(2)}, u32[]{:S(2)}) async-start(bf16[8,384,256]{2,1,0:T(8,128)(2,1)} %bitcast.35), calls=%async_computation.2 | async-start | bytes 3145728 | tf_op jit(solution)/shard_map/all_to_all | solution.py:243
  169.5 6.8 %copy-start.10 = (bf16[256,512]{1,0:T(8,128)(2,1)S(1)}, bf16[256,512]{1,0:T(8,128)(2,1)}, u32[]{:S(2)}) copy-start(bf16[256,512]{1,0:T(8,128)(2,1)} %param.14) | copy-start | bytes 786436
  172.1 5.7 %copy-start.3 = (bf16[384,512]{1,0:T(8,128)(2,1)}, bf16[384,512]{1,0:T(8,128)(2,1)S(1)}, u32[]{:S(2)}) copy-start(bf16[384,512]{1,0:T(8,128)(2,1)S(1)} %get-tuple-element.14) | copy-start | bytes 1179652
  173.8 7.6 %collective-permute-start = (f32[256,512]{1,0:T(8,128)}, f32[256,512]{1,0:T(8,128)S(1)}, u32[]{:S(2)}, u32[]{:S(2)}) collective-permute-start(f32[256,512]{1,0:T(8,128)} %get-tuple-element.24), channel_id=1, source_target_pairs={{0,8},{8,0},{1,9},{9,1},{2,10},{10,2},{3,11},{11,3},{4,12},{12,4},... | collective-permute-start | bytes 1572872 | tf_op jit(solution)/shard_map/ppermute | solution.py:278
  177.8 43.5 %all-to-all-start.3 = ((bf16[8,384,256]{2,1,0:T(8,128)(2,1)}), bf16[8,384,256]{2,1,0:T(8,128)(2,1)S(1)}, u32[]{:S(2)}, u32[]{:S(2)}) async-start(bf16[8,384,256]{2,1,0:T(8,128)(2,1)} %broadcast_in_dim.49), calls=%async_computation.3 | async-start | bytes 3145728 | tf_op jit(solution)/shard_map/all_to_all | solution.py:269
  181.4 0.8 copy-start.8
  183.6 9.9 %collective-permute-start.1 = (f32[128,512]{1,0:T(8,128)S(1)}, f32[128,512]{1,0:T(8,128)S(1)}, u32[]{:S(2)}, u32[]{:S(2)}) collective-permute-start(f32[128,512]{1,0:T(8,128)S(1)} %slice_select_fusion), channel_id=1, source_target_pairs={{0,128},{128,0},{256,384},{384,256},{1,129},{129,1},{257,385},{385... | collective-permute-start | bytes 786440 | tf_op jit(solution)/shard_map/ppermute | solution.py:30
  193.6 7.7 %collective-permute-start.2 = (f32[64,512]{1,0:T(8,128)S(1)}, f32[64,512]{1,0:T(8,128)S(1)}, u32[]{:S(2)}, u32[]{:S(2)}) collective-permute-start(f32[64,512]{1,0:T(8,128)S(1)} %slice_select_fusion.1), channel_id=1, source_target_pairs={{0,256},{128,384},{256,0},{384,128},{1,257},{129,385},{257,1},{385... | collective-permute-start | bytes 393224 | tf_op jit(solution)/shard_map/ppermute | solution.py:30
  201.3 5.3 %collective-permute-start.3 = (f32[32,512]{1,0:T(8,128)S(1)}, f32[32,512]{1,0:T(8,128)S(1)}, u32[]{:S(2)}, u32[]{:S(2)}) collective-permute-start(f32[32,512]{1,0:T(8,128)S(1)} %slice_select_fusion.2), channel_id=1, source_target_pairs={{0,16},{16,0},{32,48},{48,32},{64,80},{80,64},{96,112},{112,96},{1... | collective-permute-start | bytes 196616 | tf_op jit(solution)/shard_map/ppermute | solution.py:30
  206.7 5.9 %collective-permute-start.4 = (f32[16,512]{1,0:T(8,128)S(1)}, f32[16,512]{1,0:T(8,128)S(1)}, u32[]{:S(2)}, u32[]{:S(2)}) collective-permute-start(f32[16,512]{1,0:T(8,128)S(1)} %slice_select_fusion.3), channel_id=1, source_target_pairs={{0,32},{16,48},{32,0},{48,16},{64,96},{80,112},{96,64},{112,80},{1... | collective-permute-start | bytes 98312 | tf_op jit(solution)/shard_map/ppermute | solution.py:30
  212.6 8.7 %collective-permute-start.5 = (f32[8,512]{1,0:T(8,128)S(1)}, f32[8,512]{1,0:T(8,128)S(1)}, u32[]{:S(2)}, u32[]{:S(2)}) collective-permute-start(f32[8,512]{1,0:T(8,128)S(1)} %slice_select_fusion.4), channel_id=1, source_target_pairs={{0,64},{16,80},{32,96},{48,112},{64,0},{80,16},{96,32},{112,48},{1... | collective-permute-start | bytes 49160 | tf_op jit(solution)/shard_map/ppermute | solution.py:30
  221.3 1.2 copy-start.2
  230.8 57.8 %all-to-all-start.4 = ((bf16[64,128,256]{2,1,0:T(8,128)(2,1)}), bf16[64,128,256]{2,1,0:T(8,128)(2,1)}, u32[]{:S(2)}, u32[]{:S(2)}) async-start(bf16[64,128,256]{2,1,0:T(8,128)(2,1)} %tile_products.1), calls=%async_computation.4 | async-start | bytes 8388608 | tf_op jit(solution)/shard_map/all_to_all | solution.py:287
  239.7 4.9 %collective-permute-start.6 = (f32[8,512]{1,0:T(8,128)S(1)}, f32[8,512]{1,0:T(8,128)S(1)}, u32[]{:S(2)}, u32[]{:S(2)}) collective-permute-start(f32[8,512]{1,0:T(8,128)S(1)} %select_add_fusion.5), channel_id=1, source_target_pairs={{0,1},{1,0},{2,3},{3,2},{4,5},{5,4},{6,7},{7,6},{8,9},{9,8},{10,11... | collective-permute-start | bytes 49160 | tf_op jit(solution)/shard_map/ppermute | solution.py:30
  244.5 5.8 %collective-permute-start.7 = (f32[8,512]{1,0:T(8,128)S(1)}, f32[8,512]{1,0:T(8,128)S(1)}, u32[]{:S(2)}, u32[]{:S(2)}) collective-permute-start(f32[8,512]{1,0:T(8,128)S(1)} %add.252), channel_id=1, source_target_pairs={{0,2},{1,3},{2,0},{3,1},{4,6},{5,7},{6,4},{7,5},{8,10},{9,11},{10,... | collective-permute-start | bytes 49160 | tf_op jit(solution)/shard_map/ppermute | solution.py:30
  250.3 8.5 %collective-permute-start.8 = (f32[8,512]{1,0:T(8,128)S(1)}, f32[8,512]{1,0:T(8,128)S(1)}, u32[]{:S(2)}, u32[]{:S(2)}) collective-permute-start(f32[8,512]{1,0:T(8,128)S(1)} %add.253), channel_id=1, source_target_pairs={{0,4},{1,5},{2,6},{3,7},{4,0},{5,1},{6,2},{7,3},{8,12},{9,13},{10,... | collective-permute-start | bytes 49160 | tf_op jit(solution)/shard_map/ppermute | solution.py:30
  258.8 8.4 %collective-permute-start.9 = (f32[8,512]{1,0:T(8,128)S(1)}, f32[8,512]{1,0:T(8,128)S(1)}, u32[]{:S(2)}, u32[]{:S(2)}) collective-permute-start(f32[8,512]{1,0:T(8,128)S(1)} %add_multiply_fusion), channel_id=1, source_target_pairs={{0,64},{16,80},{32,96},{48,112},{64,0},{80,16},{96,32},{112,48},{1... | collective-permute-start | bytes 49160 | tf_op jit(solution)/shard_map/ppermute | solution.py:30
  267.2 6.1 %collective-permute-start.10 = (f32[16,512]{1,0:T(8,128)S(1)}, f32[16,512]{1,0:T(8,128)S(1)}, u32[]{:S(2)}, u32[]{:S(2)}) collective-permute-start(f32[16,512]{1,0:T(8,128)S(1)} %maximum_select_fusion.4), channel_id=1, source_target_pairs={{0,32},{16,48},{32,0},{48,16},{64,96},{80,112},{96,64},{112,80},{1... | collective-permute-start | bytes 98312 | tf_op jit(solution)/shard_map/ppermute | solution.py:30
  273.3 5.4 %collective-permute-start.11 = (f32[32,512]{1,0:T(8,128)S(1)}, f32[32,512]{1,0:T(8,128)S(1)}, u32[]{:S(2)}, u32[]{:S(2)}) collective-permute-start(f32[32,512]{1,0:T(8,128)S(1)} %maximum_select_fusion.3), channel_id=1, source_target_pairs={{0,16},{16,0},{32,48},{48,32},{64,80},{80,64},{96,112},{112,96},{1... | collective-permute-start | bytes 196616 | tf_op jit(solution)/shard_map/ppermute | solution.py:30
  295.7 42.1 %copy-start.4 = (bf16[384,512]{1,0:T(8,128)(2,1)S(1)}, bf16[384,512]{1,0:T(8,128)(2,1)}, u32[]{:S(2)}) copy-start(bf16[384,512]{1,0:T(8,128)(2,1)} %copy-done.3) | copy-start | bytes 1179652
  295.7 42.1 %copy-start.7 = (bf16[256,512]{1,0:T(8,128)(2,1)S(1)}, bf16[256,512]{1,0:T(8,128)(2,1)}, u32[]{:S(2)}) copy-start(bf16[256,512]{1,0:T(8,128)(2,1)} %param.13) | copy-start | bytes 786436
  295.7 41.9 %all-to-all-start.5 = ((bf16[8,384,256]{2,1,0:T(8,128)(2,1)}), bf16[8,384,256]{2,1,0:T(8,128)(2,1)S(1)}, u32[]{:S(2)}, u32[]{:S(2)}) async-start(bf16[8,384,256]{2,1,0:T(8,128)(2,1)} %bitcast.33), calls=%async_computation.5 | async-start | bytes 3145728 | tf_op jit(solution)/shard_map/all_to_all | solution.py:295
  299.4 7.5 %collective-permute-start.12 = (f32[64,512]{1,0:T(8,128)S(1)}, f32[64,512]{1,0:T(8,128)S(1)}, u32[]{:S(2)}, u32[]{:S(2)}) collective-permute-start(f32[64,512]{1,0:T(8,128)S(1)} %maximum_select_fusion.2), channel_id=1, source_target_pairs={{0,256},{128,384},{256,0},{384,128},{1,257},{129,385},{257,1},{385... | collective-permute-start | bytes 393224 | tf_op jit(solution)/shard_map/ppermute | solution.py:30
  307.0 7.9 %collective-permute-start.13 = (f32[128,512]{1,0:T(8,128)S(1)}, f32[128,512]{1,0:T(8,128)S(1)}, u32[]{:S(2)}, u32[]{:S(2)}) collective-permute-start(f32[128,512]{1,0:T(8,128)S(1)} %maximum_select_fusion.1), channel_id=1, source_target_pairs={{0,128},{128,0},{256,384},{384,256},{1,129},{129,1},{257,385},{385... | collective-permute-start | bytes 786440 | tf_op jit(solution)/shard_map/ppermute | solution.py:30
  314.9 6.1 %collective-permute-start.14 = (f32[256,512]{1,0:T(8,128)S(1)}, f32[256,512]{1,0:T(8,128)S(1)}, u32[]{:S(2)}, u32[]{:S(2)}) collective-permute-start(f32[256,512]{1,0:T(8,128)S(1)} %maximum_select_fusion), channel_id=1, source_target_pairs={{0,8},{8,0},{1,9},{9,1},{2,10},{10,2},{3,11},{11,3},{4,12},{12,4},... | collective-permute-start | bytes 1572872 | tf_op jit(solution)/shard_map/ppermute | solution.py:300

commit v3 on v2

--- a/solution.py
+++ b/solution.py
@@ -159,7 +159,7 @@
         pick_kernel,
         in_specs=[
             pl.BlockSpec(memory_space=pltpu.SMEM),
-            pl.BlockSpec(memory_space=pltpu.VMEM),
+            pl.BlockSpec(memory_space=pl.ANY),
         ],
         out_specs=pl.BlockSpec(memory_space=pl.ANY),
         scratch_shapes=[pltpu.SemaphoreType.DMA((slots,))],
@@ -169,6 +169,35 @@
         ),
         name="picked",
     )(offsets, blocks)
+
+
+def shifted(x, axis, by):
+    n = lax.axis_size(axis)
+    return lax.ppermute(x, axis, [(i, (i + by) % n) for i in range(n)])
+
+
+DISTANCES = (-3, 0, 3, -4, -1, 2, -2, 1)
+
+
+def place_of(device, here):
+    far = (device - here + 4) % 8 - 4
+    return sum(jnp.where(far == d, i, 0) for i, d in enumerate(DISTANCES))
+
+
+def gather_of_eight(x, axis):
+    near = jnp.stack([shifted(x, axis, 3), x, shifted(x, axis, -3)])
+    return jnp.concatenate([near, shifted(near, axis, 1), shifted(near[:2], axis, -1)])
+
+
+def sum_of_eight(x, axis):
+    above = shifted(x[3:6], axis, -1).astype(jnp.float32)
+    below = shifted(x[6:8], axis, 1).astype(jnp.float32)
+    low = x[0].astype(jnp.float32) + above[0] + below[0]
+    own = x[1].astype(jnp.float32) + above[1] + below[1]
+    high = x[2].astype(jnp.float32) + above[2]
+    low = shifted(low.astype(x.dtype), axis, -3).astype(jnp.float32)
+    high = shifted(high.astype(x.dtype), axis, 3).astype(jnp.float32)
+    return own + low + high
 
 
 def halved(x, axis, bit):
@@ -202,9 +231,15 @@
         a: [1 << i for i in range(lax.axis_size(a).bit_length() - 1)] for a in ("x", "z", "rep")
     }
 
-    column = lax.all_to_all(
-        jnp.broadcast_to(node_feats[None], (z_total, rows_here, width_in)), "z", 0, 0, tiled=True
-    ).reshape(z_total * blocks_here, TILE, width_in)
+    half_in = width_in // 2
+
+    column_1 = lax.all_to_all(
+        jnp.broadcast_to(node_feats[None, :, :half_in], (z_total, rows_here, half_in)),
+        "z",
+        0,
+        0,
+        tiled=True,
+    ).reshape(z_total * blocks_here, TILE, half_in)
 
     def passed_tiles(table):
         table = table.reshape(x_total, z_total, core_total, rep_total, dom_total)
@@ -218,9 +253,9 @@
     place = jnp.tile(jnp.arange(z_total), x_total * core_total)
     passed_first = ((x_here * z_total + place) * core_total + core) * group_blocks
     passed_first = passed_first + rep_here * blocks_here
-    passed_offset = place * blocks_here + jnp.where(
-        passed_cols >= 0, passed_cols - passed_first, 0
-    )
+    passed_block = jnp.where(passed_cols >= 0, passed_cols - passed_first, 0)
+    passed_offset = place * blocks_here + passed_block
+    passed_near = place_of(place, z_here) * blocks_here + passed_block
 
     def held_tiles(table):
         row = lax.dynamic_slice(table, (dom_here, rep_here, 0), (1, 1, dom_total))
@@ -236,14 +271,25 @@
     masks = edge_masks(row_ids, col_ids, held_limits, False)
     masks_swapped = edge_masks(row_ids, col_ids, held_limits, True)
 
-    arrived = lax.all_to_all(
-        picked(passed_offset, column), ("x", "core"), 0, 0, tiled=True
-    )
-    partial_sums = tile_sums(held_offset, masks, arrived, group_blocks)
+    held_owner = held_offset // blocks_here
+    held_near = place_of(held_owner, rep_here) * blocks_here + held_offset % blocks_here
+
+    column_1, masks, masks_swapped = lax.optimization_barrier((column_1, masks, masks_swapped))
+    leaving_1 = picked(passed_offset, column_1)
+    leaving_1, second = lax.optimization_barrier((leaving_1, node_feats[:, half_in:]))
+    arrived_1 = lax.all_to_all(leaving_1, ("x", "core"), 0, 0, tiled=True)
+    column_2 = gather_of_eight(second, "z").reshape(z_total * blocks_here, TILE, half_in)
+    leaving_2 = picked(passed_near, column_2)
+    arrived_1, leaving_2 = lax.optimization_barrier((arrived_1, leaving_2))
+    arrived_2 = lax.all_to_all(leaving_2, ("x", "core"), 0, 0, tiled=True)
+    sums_1 = tile_sums(held_near, masks, arrived_1, group_blocks)
+    summed_1 = sum_of_eight(sums_1.reshape(rep_total, rows_here, half_in), "rep")
+    arrived_2, summed_1 = lax.optimization_barrier((arrived_2, summed_1))
+    sums_2 = tile_sums(held_offset, masks, arrived_2, group_blocks)
     pieces = lax.all_to_all(
-        partial_sums.reshape(rep_total, rows_here, width_in), "rep", 0, 0, tiled=True
-    )
-    summed = pieces.astype(jnp.float32).sum(axis=0)
+        sums_2.reshape(rep_total, rows_here, half_in), "rep", 0, 0, tiled=True
+    )
+    summed = jnp.concatenate([summed_1, pieces.astype(jnp.float32).sum(axis=0)], axis=1)
 
     own_first = group_first + rep_here * blocks_here
     group_rows = lax.dynamic_slice_in_dim(tile_row, dom_here, 1, 0).reshape(-1)

time: 341 us -> 461 us (1.35)
  Pallas kernels: 27.9 us -> 161 us
  waiting for transfers between devices: 191 us -> 126 us
  starting transfers between devices: 83.7 us -> 126 us
  local copies, waits for them, and re-layouts: 12.7 us -> 21.9 us
    pallas_call x1 -> x2, Pallas kernels: 4.01 us -> 132 us  [picked(): pl.pallas_call(pick_kernel, in_specs=[pl.BlockSpec(memory_space=pltpu.SME...]
    all_to_all x3 -> x4, waiting for transfers between devices: 108 us -> 25.6 us  [the longest x1 19.6 us: shards(): lax.all_to_all(sums_2.reshape(rep_total, rows_here, half_in), 'rep', 0, 0...]
    ppermute x0 -> x8, starting transfers between devices: none -> 26.4 us  [shifted(): return lax.ppermute(x, axis, [(i, (i + by) % n) for i in range(n)])]
    ppermute x0 -> x8, waiting for transfers between devices: none -> 25.5 us  [shifted(): return lax.ppermute(x, axis, [(i, (i + by) % n) for i in range(n)])]
    ppermute x13, waiting for transfers between devices: 56.1 us -> 44.8 us  [pair_swap(): return lax.ppermute(x, axis, [(i, i ^ bit) for i in range(n)])]
    ppermute x13, starting transfers between devices: 35.7 us -> 45.8 us  [pair_swap(): return lax.ppermute(x, axis, [(i, i ^ bit) for i in range(n)])]
    pallas_call x1 -> x2, Pallas kernels: 8.54 us -> 14.4 us  [tile_sums(): pl.pallas_call(forward_kernel, grid_spec=pltpu.PrefetchScalarGridSpec(num...]
    unnamed x22 -> x30, local copies, waits for them, and re-layouts: 3.18 us -> 8.24 us
  transfers between devices with their start and end apart: 21 -> 30, of which waited for: 19 -> 24; matrix products, arithmetic and copies ran while one was open for 7% -> 7% of each run, Pallas kernels for 0% -> 16%
where the time goes in v3:
time: 461 us; the launch traced here: 459 us
  Pallas kernels  161 us (35%)
  starting transfers between devices  126 us (27%)
  waiting for transfers between devices  126 us (27%)
  local copies, waits for them, and re-layouts  21.9 us (5%)
  other arithmetic  15.1 us (3%)
  matrix products  7.54 us (2%)
    pallas_call x2, Pallas kernels, picked(): pl.pallas_call(pick_kernel, in_specs=[pl.BlockSpec(memory_space=pltpu.SME...  132 us
    ppermute x13, starting transfers between devices, pair_swap(): return lax.ppermute(x, axis, [(i, i ^ bit) for i in range(n)])  45.8 us
    ppermute x13, waiting for transfers between devices, pair_swap(): return lax.ppermute(x, axis, [(i, i ^ bit) for i in range(n)])  44.8 us
    ppermute x8, starting transfers between devices, shifted(): return lax.ppermute(x, axis, [(i, (i + by) % n) for i in range(n)])  26.4 us
    ppermute x8, waiting for transfers between devices, shifted(): return lax.ppermute(x, axis, [(i, (i + by) % n) for i in range(n)])  25.5 us
    all_to_all x1, waiting for transfers between devices, shards(): lax.all_to_all(sums_2.reshape(rep_total, rows_here, half_in), 'rep', 0, 0...  19.6 us
    all_to_all x1, waiting for transfers between devices, shards(): lax.all_to_all(column_sums.reshape(z_total, rows_here, width_in), 'z', 0,...  18 us
    pallas_call x2, Pallas kernels, tile_sums(): pl.pallas_call(forward_kernel, grid_spec=pltpu.PrefetchScalarGridSpec(num...  14.4 us
  transfers between devices with their start and end apart: 30, of which 24 were waited for; matrix products, arithmetic and copies ran while one was open for 7% of the time, Pallas kernels for 16%

profile of v3, /device:TPU:1, one launch (start us, length us, event | category | flops | bytes accessed | tf_op | source)
XLA Modules:
  0.0 458.6 jit_solution(14289963675574736752)
XLA Ops:
  2.7 10.9 %all-to-all-start = ((bf16[8,384,128]{2,1,0:T(8,128)(2,1)}), bf16[8,384,128]{2,1,0:T(8,128)(2,1)S(1)}, u32[]{:S(2)}, u32[]{:S(2)}) async-start(bf16[8,384,128]{2,1,0:T(8,128)(2,1)} %broadcast_in_dim.84), calls=%async_computation | async-start | bytes 1572864 | tf_op jit(solution)/shard_map/all_to_all | solution.py:236
  20.1 11.0 %fusion.10 = (bf16[64,128,128]{2,1,0:T(8,128)(2,1)}, bf16[64,128,128]{2,1,0:T(8,128)(2,1)}) fusion(s32[64,128]{1,0:T(8,128)S(1)} %get-tuple-element.46, s32[64,128]{1,0:T(8,128)S(1)} %get-tuple-element.45, s32[64,128]{1,0:T(8,128)S(1)} %add_select_fusion.5, s32[64]{0:T(128)S(1)} %get-tuple-element.51), kind=kLoop, calls=%fused_computation.22 | loop fusion | flops 46137344 | bytes 4292864 | tf_op jit(solution)/shard_map/convert_element_type | solution.py:25
  31.1 6.0 %all-to-all-done = bf16[8,384,128]{2,1,0:T(8,128)(2,1)S(1)} async-done(((bf16[8,384,128]{2,1,0:T(8,128)(2,1)}), bf16[8,384,128]{2,1,0:T(8,128)(2,1)S(1)}, u32[]{:S(2)}, u32[]{:S(2)}) %all-to-all-start) | async-done | bytes 786464 | tf_op jit(solution)/shard_map/all_to_all | solution.py:236
  38.0 65.9 %picked.2 = bf16[64,128,128]{2,1,0:T(8,128)(2,1)} custom-call(s32[64]{0:T(128)} %get-tuple-element.54.offset_ref, bf16[24,128,128]{2,1,0:T(8,128)(2,1)} %bitcast.85), custom_call_target="tpu_custom_call" | custom-call | bytes 2883584 | tf_op jit(solution)/shard_map/picked/pallas_call | solution.py:158
  103.9 4.8 %all-to-all-start.1 = ((bf16[64,128,128]{2,1,0:T(8,128)(2,1)}), bf16[64,128,128]{2,1,0:T(8,128)(2,1)S(1)}, u32[]{:S(2)}, u32[]{:S(2)}) async-start(bf16[64,128,128]{2,1,0:T(8,128)(2,1)} %picked.2), calls=%async_computation.1 | async-start | bytes 4194304 | tf_op jit(solution)/shard_map/all_to_all | solution.py:280
  110.6 6.4 %collective-permute-start.1 = (bf16[384,128]{1,0:T(8,128)(2,1)S(1)}, bf16[384,128]{1,0:T(8,128)(2,1)S(1)}, u32[]{:S(2)}, u32[]{:S(2)}) collective-permute-start(bf16[384,128]{1,0:T(8,128)(2,1)S(1)} %get-tuple-element.19), channel_id=1, source_target_pairs={{0,80},{16,96},{32,112},{48,0},{64,16},{80,32},{96,48},{112,64},{1... | collective-permute-start | bytes 294920 | tf_op jit(solution)/shard_map/ppermute | solution.py:176
  127.4 7.0 %collective-permute-done.2 = bf16[3,384,128]{2,1,0:T(8,128)(2,1)S(1)} collective-permute-done((bf16[3,384,128]{2,1,0:T(8,128)(2,1)S(1)}, bf16[3,384,128]{2,1,0:T(8,128)(2,1)S(1)}, u32[]{:S(2)}, u32[]{:S(2)}) %collective-permute-start.2) | collective-permute-done | bytes 294944 | tf_op jit(solution)/shard_map/ppermute | solution.py:176
  135.9 65.9 %picked.3 = bf16[64,128,128]{2,1,0:T(8,128)(2,1)} custom-call(s32[64]{0:T(128)} %get-tuple-element.55.offset_ref, bf16[24,128,128]{2,1,0:T(8,128)(2,1)} %bitcast.11.block_ref), custom_call_target="tpu_custom_call" | custom-call | bytes 2883584 | tf_op jit(solution)/shard_map/picked/pallas_call | solution.py:158
  203.1 6.1 %all-to-all-start.2 = ((bf16[64,128,128]{2,1,0:T(8,128)(2,1)}), bf16[64,128,128]{2,1,0:T(8,128)(2,1)S(1)}, u32[]{:S(2)}, u32[]{:S(2)}) async-start(bf16[64,128,128]{2,1,0:T(8,128)(2,1)} %picked.3), calls=%async_computation.2 | async-start | bytes 4194304 | tf_op jit(solution)/shard_map/all_to_all | solution.py:284
  209.2 7.2 %tile_sums.2 = bf16[24,128,128]{2,1,0:T(8,128)(2,1)} custom-call(s32[64]{0:T(128)} %get-tuple-element.30.offset_ref, bf16[64,128,128]{2,1,0:T(8,128)(2,1)} %get-tuple-element.21.mask_ref, bf16[64,128,128]{2,1,0:T(8,128)(2,1)} %copy-done.2), custom_call_target="tpu_custom_call" | custom-call | flops 268435456 | bytes 4194304 | tf_op jit(solution)/shard_map/tile_sums/pallas_call | solution.py:53
  217.4 5.1 %collective-permute-start.4 = (bf16[3,384,128]{2,1,0:T(8,128)(2,1)S(1)}, bf16[3,384,128]{2,1,0:T(8,128)(2,1)S(1)}, u32[]{:S(2)}, u32[]{:S(2)}) collective-permute-start(bf16[3,384,128]{2,1,0:T(8,128)(2,1)S(1)} %bitcast.91), channel_id=1, source_target_pairs={{0,7},{1,0},{2,1},{3,2},{4,3},{5,4},{6,5},{7,6},{8,15},{9,8},{10,9... | collective-permute-start | bytes 884744 | tf_op jit(solution)/shard_map/ppermute | solution.py:176
  226.4 6.4 %collective-permute-done.5 = bf16[2,384,128]{2,1,0:T(8,128)(2,1)S(1)} collective-permute-done((bf16[2,384,128]{2,1,0:T(8,128)(2,1)S(1)}, bf16[2,384,128]{2,1,0:T(8,128)(2,1)S(1)}, u32[]{:S(2)}, u32[]{:S(2)}) %collective-permute-start.5) | collective-permute-done | bytes 196640 | tf_op jit(solution)/shard_map/ppermute | solution.py:176
  241.5 6.3 %collective-permute-done.7 = bf16[384,128]{1,0:T(8,128)(2,1)S(1)} collective-permute-done((bf16[384,128]{1,0:T(8,128)(2,1)S(1)}, bf16[384,128]{1,0:T(8,128)(2,1)S(1)}, u32[]{:S(2)}, u32[]{:S(2)}) %collective-permute-start.7) | collective-permute-done | bytes 98336 | tf_op jit(solution)/shard_map/ppermute | solution.py:176
  249.2 7.2 %tile_sums.3 = bf16[24,128,128]{2,1,0:T(8,128)(2,1)} custom-call(s32[64]{0:T(128)} %get-tuple-element.31.offset_ref, bf16[64,128,128]{2,1,0:T(8,128)(2,1)} %get-tuple-element.21.mask_ref, bf16[64,128,128]{2,1,0:T(8,128)(2,1)} %copy-done.1), custom_call_target="tpu_custom_call" | custom-call | flops 268435456 | bytes 4194304 | tf_op jit(solution)/shard_map/tile_sums/pallas_call | solution.py:53
  256.4 3.9 all-to-all-start.3
  261.6 19.6 %all-to-all-done.3 = bf16[8,384,128]{2,1,0:T(8,128)(2,1)S(1)} async-done(((bf16[8,384,128]{2,1,0:T(8,128)(2,1)}), bf16[8,384,128]{2,1,0:T(8,128)(2,1)S(1)}, u32[]{:S(2)}, u32[]{:S(2)}) %all-to-all-start.3) | async-done | bytes 786464 | tf_op jit(solution)/shard_map/all_to_all | solution.py:289
  286.4 5.0 %collective-permute-start.8 = (f32[256,512]{1,0:T(8,128)}, f32[256,512]{1,0:T(8,128)S(1)}, u32[]{:S(2)}, u32[]{:S(2)}) collective-permute-start(f32[256,512]{1,0:T(8,128)} %get-tuple-element.52), channel_id=1, source_target_pairs={{0,8},{8,0},{1,9},{9,1},{2,10},{10,2},{3,11},{11,3},{4,12},{12,4},... | collective-permute-start | bytes 1572872 | tf_op jit(solution)/shard_map/ppermute | solution.py:324
  302.5 7.1 %collective-permute-done.9 = f32[128,512]{1,0:T(8,128)S(1)} collective-permute-done((f32[128,512]{1,0:T(8,128)S(1)}, f32[128,512]{1,0:T(8,128)S(1)}, u32[]{:S(2)}, u32[]{:S(2)}) %collective-permute-start.9) | collective-permute-done | bytes 262176 | tf_op jit(solution)/shard_map/ppermute | solution.py:30
  309.7 4.3 collective-permute-start.10
  328.5 5.7 %collective-permute-start.13 = (f32[8,512]{1,0:T(8,128)S(1)}, f32[8,512]{1,0:T(8,128)S(1)}, u32[]{:S(2)}, u32[]{:S(2)}) collective-permute-start(f32[8,512]{1,0:T(8,128)S(1)} %slice_select_fusion.4), channel_id=1, source_target_pairs={{0,64},{16,80},{32,96},{48,112},{64,0},{80,16},{96,32},{112,48},{1... | collective-permute-start | bytes 49160 | tf_op jit(solution)/shard_map/ppermute | solution.py:30
  338.4 8.2 %tile_products.1 = bf16[64,128,256]{2,1,0:T(8,128)(2,1)} custom-call(s32[64]{0:T(128)} %get-tuple-element.31.offset_ref, bf16[64,128,128]{2,1,0:T(8,128)(2,1)} %get-tuple-element.25.mask_ref, bf16[24,128,256]{2,1,0:T(8,128)(2,1)} %bitcast.83), custom_call_target="tpu_custom_call" | custom-call | flops 536870912 | bytes 6291456 | tf_op jit(solution)/shard_map/tile_products/pallas_call | solution.py:88
  346.6 8.8 %all-to-all-start.5 = ((bf16[64,128,256]{2,1,0:T(8,128)(2,1)}), bf16[64,128,256]{2,1,0:T(8,128)(2,1)}, u32[]{:S(2)}, u32[]{:S(2)}) async-start(bf16[64,128,256]{2,1,0:T(8,128)(2,1)} %tile_products.1), calls=%async_computation.5 | async-start | bytes 8388608 | tf_op jit(solution)/shard_map/all_to_all | solution.py:333
  360.3 3.9 collective-permute-start.15
  366.1 7.1 %collective-permute-start.16 = (f32[8,512]{1,0:T(8,128)S(1)}, f32[8,512]{1,0:T(8,128)S(1)}, u32[]{:S(2)}, u32[]{:S(2)}) collective-permute-start(f32[8,512]{1,0:T(8,128)S(1)} %add.371), channel_id=1, source_target_pairs={{0,4},{1,5},{2,6},{3,7},{4,0},{5,1},{6,2},{7,3},{8,12},{9,13},{10,... | collective-permute-start | bytes 49160 | tf_op jit(solution)/shard_map/ppermute | solution.py:30
  374.6 5.5 %collective-permute-start.17 = (f32[8,512]{1,0:T(8,128)S(1)}, f32[8,512]{1,0:T(8,128)S(1)}, u32[]{:S(2)}, u32[]{:S(2)}) collective-permute-start(f32[8,512]{1,0:T(8,128)S(1)} %add_multiply_fusion), channel_id=1, source_target_pairs={{0,64},{16,80},{32,96},{48,112},{64,0},{80,16},{96,32},{112,48},{1... | collective-permute-start | bytes 49160 | tf_op jit(solution)/shard_map/ppermute | solution.py:30
  394.3 10.0 %all-to-all-done.5.part_ref = bf16[64,128,256]{2,1,0:T(8,128)(2,1)} async-done(((bf16[64,128,256]{2,1,0:T(8,128)(2,1)}), bf16[64,128,256]{2,1,0:T(8,128)(2,1)}, u32[]{:S(2)}, u32[]{:S(2)}) %all-to-all-start.5) | async-done | bytes 4194336 | tf_op jit(solution)/shard_map/all_to_all | solution.py:333
  404.3 7.1 %summed_into.1 = bf16[24,128,256]{2,1,0:T(8,128)(2,1)} custom-call(s32[64]{0:T(128)} %get-tuple-element.54.offset_ref, bf16[64,128,256]{2,1,0:T(8,128)(2,1)} %all-to-all-done.5.part_ref), custom_call_target="tpu_custom_call" | custom-call | flops 2097152 | bytes 4194304 | tf_op jit(solution)/shard_map/summed_into/pallas_call | solution.py:126
  411.4 5.5 %all-to-all-start.6 = ((bf16[8,384,256]{2,1,0:T(8,128)(2,1)}), bf16[8,384,256]{2,1,0:T(8,128)(2,1)S(1)}, u32[]{:S(2)}, u32[]{:S(2)}) async-start(bf16[8,384,256]{2,1,0:T(8,128)(2,1)} %bitcast.82), calls=%async_computation.6 | async-start | bytes 3145728 | tf_op jit(solution)/shard_map/all_to_all | solution.py:341
  419.1 5.0 %collective-permute-done.20 = f32[64,512]{1,0:T(8,128)S(1)} collective-permute-done((f32[64,512]{1,0:T(8,128)S(1)}, f32[64,512]{1,0:T(8,128)S(1)}, u32[]{:S(2)}, u32[]{:S(2)}) %collective-permute-start.20) | collective-permute-done | bytes 131104 | tf_op jit(solution)/shard_map/ppermute | solution.py:30
  426.4 5.2 %collective-permute-done.21 = f32[128,512]{1,0:T(8,128)S(1)} collective-permute-done((f32[128,512]{1,0:T(8,128)S(1)}, f32[128,512]{1,0:T(8,128)S(1)}, u32[]{:S(2)}, u32[]{:S(2)}) %collective-permute-start.21) | collective-permute-done | bytes 262176 | tf_op jit(solution)/shard_map/ppermute | solution.py:30
  431.6 5.1 %collective-permute-start.22 = (f32[256,512]{1,0:T(8,128)S(1)}, f32[256,512]{1,0:T(8,128)S(1)}, u32[]{:S(2)}, u32[]{:S(2)}) collective-permute-start(f32[256,512]{1,0:T(8,128)S(1)} %maximum_select_fusion), channel_id=1, source_target_pairs={{0,8},{8,0},{1,9},{9,1},{2,10},{10,2},{3,11},{11,3},{4,12},{12,4},... | collective-permute-start | bytes 1572872 | tf_op jit(solution)/shard_map/ppermute | solution.py:346
  439.3 18.0 %all-to-all-done.6 = bf16[8,384,256]{2,1,0:T(8,128)(2,1)S(1)} async-done(((bf16[8,384,256]{2,1,0:T(8,128)(2,1)}), bf16[8,384,256]{2,1,0:T(8,128)(2,1)S(1)}, u32[]{:S(2)}, u32[]{:S(2)}) %all-to-all-start.6) | async-done | bytes 1572896 | tf_op jit(solution)/shard_map/all_to_all | solution.py:341
  (143 shorter events, 106.3 us)
Async XLA Ops:
  2.7 34.4 %all-to-all-start = ((bf16[8,384,128]{2,1,0:T(8,128)(2,1)}), bf16[8,384,128]{2,1,0:T(8,128)(2,1)S(1)}, u32[]{:S(2)}, u32[]{:S(2)}) async-start(bf16[8,384,128]{2,1,0:T(8,128)(2,1)} %broadcast_in_dim.84), calls=%async_computation | async-start | bytes 1572864 | tf_op jit(solution)/shard_map/all_to_all | solution.py:236
  103.9 97.9 %all-to-all-start.1 = ((bf16[64,128,128]{2,1,0:T(8,128)(2,1)}), bf16[64,128,128]{2,1,0:T(8,128)(2,1)S(1)}, u32[]{:S(2)}, u32[]{:S(2)}) async-start(bf16[64,128,128]{2,1,0:T(8,128)(2,1)} %picked.2), calls=%async_computation.1 | async-start | bytes 4194304 | tf_op jit(solution)/shard_map/all_to_all | solution.py:280
  108.7 11.3 %collective-permute-start = (bf16[384,128]{1,0:T(8,128)(2,1)S(1)}, bf16[384,128]{1,0:T(8,128)(2,1)S(1)}, u32[]{:S(2)}, u32[]{:S(2)}) collective-permute-start(bf16[384,128]{1,0:T(8,128)(2,1)S(1)} %get-tuple-element.19), channel_id=1, source_target_pairs={{0,48},{16,64},{32,80},{48,96},{64,112},{80,0},{96,16},{112,32},{1... | collective-permute-start | bytes 294920 | tf_op jit(solution)/shard_map/ppermute | solution.py:176
  110.6 12.9 %collective-permute-start.1 = (bf16[384,128]{1,0:T(8,128)(2,1)S(1)}, bf16[384,128]{1,0:T(8,128)(2,1)S(1)}, u32[]{:S(2)}, u32[]{:S(2)}) collective-permute-start(bf16[384,128]{1,0:T(8,128)(2,1)S(1)} %get-tuple-element.19), channel_id=1, source_target_pairs={{0,80},{16,96},{32,112},{48,0},{64,16},{80,32},{96,48},{112,64},{1... | collective-permute-start | bytes 294920 | tf_op jit(solution)/shard_map/ppermute | solution.py:176
  120.0 15.2 %collective-permute-start.3 = (bf16[2,384,128]{2,1,0:T(8,128)(2,1)S(1)}, bf16[2,384,128]{2,1,0:T(8,128)(2,1)S(1)}, u32[]{:S(2)}, u32[]{:S(2)}) collective-permute-start(bf16[2,384,128]{2,1,0:T(8,128)(2,1)S(1)} %pad_maximum_fusion.1), channel_id=1, source_target_pairs={{0,112},{16,0},{32,16},{48,32},{64,48},{80,64},{96,80},{112,96},{1... | collective-permute-start | bytes 589832 | tf_op jit(solution)/shard_map/ppermute | solution.py:176
  123.6 10.9 %collective-permute-start.2 = (bf16[3,384,128]{2,1,0:T(8,128)(2,1)S(1)}, bf16[3,384,128]{2,1,0:T(8,128)(2,1)S(1)}, u32[]{:S(2)}, u32[]{:S(2)}) collective-permute-start(bf16[3,384,128]{2,1,0:T(8,128)(2,1)S(1)} %pad_maximum_fusion), channel_id=1, source_target_pairs={{0,16},{16,32},{32,48},{48,64},{64,80},{80,96},{96,112},{112,0},{1... | collective-permute-start | bytes 884744 | tf_op jit(solution)/shard_map/ppermute | solution.py:176
  203.1 44.7 %all-to-all-start.2 = ((bf16[64,128,128]{2,1,0:T(8,128)(2,1)}), bf16[64,128,128]{2,1,0:T(8,128)(2,1)S(1)}, u32[]{:S(2)}, u32[]{:S(2)}) async-start(bf16[64,128,128]{2,1,0:T(8,128)(2,1)} %picked.3), calls=%async_computation.2 | async-start | bytes 4194304 | tf_op jit(solution)/shard_map/all_to_all | solution.py:284
  217.4 15.4 %collective-permute-start.4 = (bf16[3,384,128]{2,1,0:T(8,128)(2,1)S(1)}, bf16[3,384,128]{2,1,0:T(8,128)(2,1)S(1)}, u32[]{:S(2)}, u32[]{:S(2)}) collective-permute-start(bf16[3,384,128]{2,1,0:T(8,128)(2,1)S(1)} %bitcast.91), channel_id=1, source_target_pairs={{0,7},{1,0},{2,1},{3,2},{4,3},{5,4},{6,5},{7,6},{8,15},{9,8},{10,9... | collective-permute-start | bytes 884744 | tf_op jit(solution)/shard_map/ppermute | solution.py:176
  223.5 9.3 %collective-permute-start.5 = (bf16[2,384,128]{2,1,0:T(8,128)(2,1)S(1)}, bf16[2,384,128]{2,1,0:T(8,128)(2,1)S(1)}, u32[]{:S(2)}, u32[]{:S(2)}) collective-permute-start(bf16[2,384,128]{2,1,0:T(8,128)(2,1)S(1)} %bitcast.92), channel_id=1, source_target_pairs={{0,1},{1,2},{2,3},{3,4},{4,5},{5,6},{6,7},{7,0},{8,9},{9,10},{10,1... | collective-permute-start | bytes 589832 | tf_op jit(solution)/shard_map/ppermute | solution.py:176
  233.0 8.5 %collective-permute-start.6 = (bf16[384,128]{1,0:T(8,128)(2,1)S(1)}, bf16[384,128]{1,0:T(8,128)(2,1)S(1)}, u32[]{:S(2)}, u32[]{:S(2)}) collective-permute-start(bf16[384,128]{1,0:T(8,128)(2,1)S(1)} %get-tuple-element.39), channel_id=1, source_target_pairs={{0,5},{1,6},{2,7},{3,0},{4,1},{5,2},{6,3},{7,4},{8,13},{9,14},{10,... | collective-permute-start | bytes 294920 | tf_op jit(solution)/shard_map/ppermute | solution.py:176
  236.5 11.3 %collective-permute-start.7 = (bf16[384,128]{1,0:T(8,128)(2,1)S(1)}, bf16[384,128]{1,0:T(8,128)(2,1)S(1)}, u32[]{:S(2)}, u32[]{:S(2)}) collective-permute-start(bf16[384,128]{1,0:T(8,128)(2,1)S(1)} %get-tuple-element.40), channel_id=1, source_target_pairs={{0,3},{1,4},{2,5},{3,6},{4,7},{5,0},{6,1},{7,2},{8,11},{9,12},{10,... | collective-permute-start | bytes 294920 | tf_op jit(solution)/shard_map/ppermute | solution.py:176
  256.4 24.9 %all-to-all-start.3 = ((bf16[8,384,128]{2,1,0:T(8,128)(2,1)}), bf16[8,384,128]{2,1,0:T(8,128)(2,1)S(1)}, u32[]{:S(2)}, u32[]{:S(2)}) async-start(bf16[8,384,128]{2,1,0:T(8,128)(2,1)} %bitcast.84), calls=%async_computation.3 | async-start | bytes 1572864 | tf_op jit(solution)/shard_map/all_to_all | solution.py:289
  286.4 11.2 %collective-permute-start.8 = (f32[256,512]{1,0:T(8,128)}, f32[256,512]{1,0:T(8,128)S(1)}, u32[]{:S(2)}, u32[]{:S(2)}) collective-permute-start(f32[256,512]{1,0:T(8,128)} %get-tuple-element.52), channel_id=1, source_target_pairs={{0,8},{8,0},{1,9},{9,1},{2,10},{10,2},{3,11},{11,3},{4,12},{12,4},... | collective-permute-start | bytes 1572872 | tf_op jit(solution)/shard_map/ppermute | solution.py:324
  294.0 43.2 %all-to-all-start.4 = ((bf16[8,384,256]{2,1,0:T(8,128)(2,1)}), bf16[8,384,256]{2,1,0:T(8,128)(2,1)S(1)}, u32[]{:S(2)}, u32[]{:S(2)}) async-start(bf16[8,384,256]{2,1,0:T(8,128)(2,1)} %broadcast_in_dim.92), calls=%async_computation.4 | async-start | bytes 3145728 | tf_op jit(solution)/shard_map/all_to_all | solution.py:315
  299.8 9.9 %collective-permute-start.9 = (f32[128,512]{1,0:T(8,128)S(1)}, f32[128,512]{1,0:T(8,128)S(1)}, u32[]{:S(2)}, u32[]{:S(2)}) collective-permute-start(f32[128,512]{1,0:T(8,128)S(1)} %slice_select_fusion), channel_id=1, source_target_pairs={{0,128},{128,0},{256,384},{384,256},{1,129},{129,1},{257,385},{385... | collective-permute-start | bytes 786440 | tf_op jit(solution)/shard_map/ppermute | solution.py:30
  309.7 7.7 %collective-permute-start.10 = (f32[64,512]{1,0:T(8,128)S(1)}, f32[64,512]{1,0:T(8,128)S(1)}, u32[]{:S(2)}, u32[]{:S(2)}) collective-permute-start(f32[64,512]{1,0:T(8,128)S(1)} %slice_select_fusion.1), channel_id=1, source_target_pairs={{0,256},{128,384},{256,0},{384,128},{1,257},{129,385},{257,1},{385... | collective-permute-start | bytes 393224 | tf_op jit(solution)/shard_map/ppermute | solution.py:30
  317.5 5.3 %collective-permute-start.11 = (f32[32,512]{1,0:T(8,128)S(1)}, f32[32,512]{1,0:T(8,128)S(1)}, u32[]{:S(2)}, u32[]{:S(2)}) collective-permute-start(f32[32,512]{1,0:T(8,128)S(1)} %slice_select_fusion.2), channel_id=1, source_target_pairs={{0,16},{16,0},{32,48},{48,32},{64,80},{80,64},{96,112},{112,96},{1... | collective-permute-start | bytes 196616 | tf_op jit(solution)/shard_map/ppermute | solution.py:30
  322.8 5.6 %collective-permute-start.12 = (f32[16,512]{1,0:T(8,128)S(1)}, f32[16,512]{1,0:T(8,128)S(1)}, u32[]{:S(2)}, u32[]{:S(2)}) collective-permute-start(f32[16,512]{1,0:T(8,128)S(1)} %slice_select_fusion.3), channel_id=1, source_target_pairs={{0,32},{16,48},{32,0},{48,16},{64,96},{80,112},{96,64},{112,80},{1... | collective-permute-start | bytes 98312 | tf_op jit(solution)/shard_map/ppermute | solution.py:30
  328.5 8.7 %collective-permute-start.13 = (f32[8,512]{1,0:T(8,128)S(1)}, f32[8,512]{1,0:T(8,128)S(1)}, u32[]{:S(2)}, u32[]{:S(2)}) collective-permute-start(f32[8,512]{1,0:T(8,128)S(1)} %slice_select_fusion.4), channel_id=1, source_target_pairs={{0,64},{16,80},{32,96},{48,112},{64,0},{80,16},{96,32},{112,48},{1... | collective-permute-start | bytes 49160 | tf_op jit(solution)/shard_map/ppermute | solution.py:30
  346.6 57.7 %all-to-all-start.5 = ((bf16[64,128,256]{2,1,0:T(8,128)(2,1)}), bf16[64,128,256]{2,1,0:T(8,128)(2,1)}, u32[]{:S(2)}, u32[]{:S(2)}) async-start(bf16[64,128,256]{2,1,0:T(8,128)(2,1)} %tile_products.1), calls=%async_computation.5 | async-start | bytes 8388608 | tf_op jit(solution)/shard_map/all_to_all | solution.py:333
  355.4 4.9 %collective-permute-start.14 = (f32[8,512]{1,0:T(8,128)S(1)}, f32[8,512]{1,0:T(8,128)S(1)}, u32[]{:S(2)}, u32[]{:S(2)}) collective-permute-start(f32[8,512]{1,0:T(8,128)S(1)} %select_add_fusion.5), channel_id=1, source_target_pairs={{0,1},{1,0},{2,3},{3,2},{4,5},{5,4},{6,7},{7,6},{8,9},{9,8},{10,11... | collective-permute-start | bytes 49160 | tf_op jit(solution)/shard_map/ppermute | solution.py:30
  360.3 5.8 %collective-permute-start.15 = (f32[8,512]{1,0:T(8,128)S(1)}, f32[8,512]{1,0:T(8,128)S(1)}, u32[]{:S(2)}, u32[]{:S(2)}) collective-permute-start(f32[8,512]{1,0:T(8,128)S(1)} %add.370), channel_id=1, source_target_pairs={{0,2},{1,3},{2,0},{3,1},{4,6},{5,7},{6,4},{7,5},{8,10},{9,11},{10,... | collective-permute-start | bytes 49160 | tf_op jit(solution)/shard_map/ppermute | solution.py:30
  366.1 8.5 %collective-permute-start.16 = (f32[8,512]{1,0:T(8,128)S(1)}, f32[8,512]{1,0:T(8,128)S(1)}, u32[]{:S(2)}, u32[]{:S(2)}) collective-permute-start(f32[8,512]{1,0:T(8,128)S(1)} %add.371), channel_id=1, source_target_pairs={{0,4},{1,5},{2,6},{3,7},{4,0},{5,1},{6,2},{7,3},{8,12},{9,13},{10,... | collective-permute-start | bytes 49160 | tf_op jit(solution)/shard_map/ppermute | solution.py:30
  374.6 8.4 %collective-permute-start.17 = (f32[8,512]{1,0:T(8,128)S(1)}, f32[8,512]{1,0:T(8,128)S(1)}, u32[]{:S(2)}, u32[]{:S(2)}) collective-permute-start(f32[8,512]{1,0:T(8,128)S(1)} %add_multiply_fusion), channel_id=1, source_target_pairs={{0,64},{16,80},{32,96},{48,112},{64,0},{80,16},{96,32},{112,48},{1... | collective-permute-start | bytes 49160 | tf_op jit(solution)/shard_map/ppermute | solution.py:30
  382.9 5.9 %collective-permute-start.18 = (f32[16,512]{1,0:T(8,128)S(1)}, f32[16,512]{1,0:T(8,128)S(1)}, u32[]{:S(2)}, u32[]{:S(2)}) collective-permute-start(f32[16,512]{1,0:T(8,128)S(1)} %maximum_select_fusion.4), channel_id=1, source_target_pairs={{0,32},{16,48},{32,0},{48,16},{64,96},{80,112},{96,64},{112,80},{1... | collective-permute-start | bytes 98312 | tf_op jit(solution)/shard_map/ppermute | solution.py:30
  388.9 5.4 %collective-permute-start.19 = (f32[32,512]{1,0:T(8,128)S(1)}, f32[32,512]{1,0:T(8,128)S(1)}, u32[]{:S(2)}, u32[]{:S(2)}) collective-permute-start(f32[32,512]{1,0:T(8,128)S(1)} %maximum_select_fusion.3), channel_id=1, source_target_pairs={{0,16},{16,0},{32,48},{48,32},{64,80},{80,64},{96,112},{112,96},{1... | collective-permute-start | bytes 196616 | tf_op jit(solution)/shard_map/ppermute | solution.py:30
  411.4 46.2 %copy-start.8 = (bf16[384,512]{1,0:T(8,128)(2,1)S(1)}, bf16[384,512]{1,0:T(8,128)(2,1)}, u32[]{:S(2)}) copy-start(bf16[384,512]{1,0:T(8,128)(2,1)} %copy-done.7) | copy-start | bytes 1179652
  411.4 46.2 %copy-start.10 = (bf16[256,512]{1,0:T(8,128)(2,1)S(1)}, bf16[256,512]{1,0:T(8,128)(2,1)}, u32[]{:S(2)}) copy-start(bf16[256,512]{1,0:T(8,128)(2,1)} %param.13) | copy-start | bytes 786436
  411.4 46.0 %all-to-all-start.6 = ((bf16[8,384,256]{2,1,0:T(8,128)(2,1)}), bf16[8,384,256]{2,1,0:T(8,128)(2,1)S(1)}, u32[]{:S(2)}, u32[]{:S(2)}) async-start(bf16[8,384,256]{2,1,0:T(8,128)(2,1)} %bitcast.82), calls=%async_computation.6 | async-start | bytes 3145728 | tf_op jit(solution)/shard_map/all_to_all | solution.py:341
  416.9 7.2 %collective-permute-start.20 = (f32[64,512]{1,0:T(8,128)S(1)}, f32[64,512]{1,0:T(8,128)S(1)}, u32[]{:S(2)}, u32[]{:S(2)}) collective-permute-start(f32[64,512]{1,0:T(8,128)S(1)} %maximum_select_fusion.2), channel_id=1, source_target_pairs={{0,256},{128,384},{256,0},{384,128},{1,257},{129,385},{257,1},{385... | collective-permute-start | bytes 393224 | tf_op jit(solution)/shard_map/ppermute | solution.py:30
  424.2 7.4 %collective-permute-start.21 = (f32[128,512]{1,0:T(8,128)S(1)}, f32[128,512]{1,0:T(8,128)S(1)}, u32[]{:S(2)}, u32[]{:S(2)}) collective-permute-start(f32[128,512]{1,0:T(8,128)S(1)} %maximum_select_fusion.1), channel_id=1, source_target_pairs={{0,128},{128,0},{256,384},{384,256},{1,129},{129,1},{257,385},{385... | collective-permute-start | bytes 786440 | tf_op jit(solution)/shard_map/ppermute | solution.py:30
  431.6 6.6 %collective-permute-start.22 = (f32[256,512]{1,0:T(8,128)S(1)}, f32[256,512]{1,0:T(8,128)S(1)}, u32[]{:S(2)}, u32[]{:S(2)}) collective-permute-start(f32[256,512]{1,0:T(8,128)S(1)} %maximum_select_fusion), channel_id=1, source_target_pairs={{0,8},{8,0},{1,9},{9,1},{2,10},{10,2},{3,11},{11,3},{4,12},{12,4},... | collective-permute-start | bytes 1572872 | tf_op jit(solution)/shard_map/ppermute | solution.py:346
  (11 other events, 145.8 us)

commit v4 on v3

--- a/solution.py
+++ b/solution.py
@@ -11,7 +11,8 @@
 TILE = 128
 DOM = ("x", "z", "core")
 ALL = ("x", "z", "core", "rep")
-STEP = 8
+STEP = 32
+LIMIT = pltpu.CompilerParams(vmem_limit_bytes=40 << 20)
 
 
 def edge_masks(row_ids, col_ids, limits, swapped):
@@ -68,6 +69,7 @@
             bytes_accessed=slots * tile * (tile + width) * 2,
             transcendentals=0,
         ),
+        compiler_params=LIMIT,
         name="tile_sums",
     )(offsets, masks, feats)
 
@@ -102,6 +104,7 @@
             bytes_accessed=slots * tile * (tile + width) * 2,
             transcendentals=0,
         ),
+        compiler_params=LIMIT,
         name="tile_products",
     )(offsets, masks, blocks)
 
@@ -136,15 +139,30 @@
         cost_estimate=pl.CostEstimate(
             flops=slots * tile * width, bytes_accessed=slots * tile * width * 2, transcendentals=0
         ),
+        compiler_params=LIMIT,
         name="summed_into",
     )(offsets, parts)
 
 
-def pick_kernel(offset_ref, block_ref, out_ref, sems):
-    slots = out_ref.shape[0]
+def pick_kernel(offset_ref, *refs):
+    *piece_refs, out_ref, held_ref, in_sems, out_sems = refs
+    first = 0
+    copies = []
+    for piece in piece_refs:
+        count = piece.shape[0]
+        copies.append(
+            pltpu.make_async_copy(
+                piece, held_ref.at[pl.ds(first, count)], in_sems.at[len(copies)]
+            )
+        )
+        first += count
+    for copy in copies:
+        copy.start()
+    for copy in copies:
+        copy.wait()
     copies = [
-        pltpu.make_async_copy(block_ref.at[offset_ref[t]], out_ref.at[t], sems.at[t])
-        for t in range(slots)
+        pltpu.make_async_copy(held_ref.at[offset_ref[t]], out_ref.at[t], out_sems.at[t])
+        for t in range(out_ref.shape[0])
     ]
     for copy in copies:
         copy.start()
@@ -152,23 +170,27 @@
         copy.wait()
 
 
-def picked(offsets, blocks):
+def picked(offsets, *pieces):
     slots = offsets.shape[0]
-    n, tile, width = blocks.shape
+    n = sum(len(piece) for piece in pieces)
+    _, tile, width = pieces[0].shape
+    dtype = pieces[0].dtype
     return pl.pallas_call(
         pick_kernel,
-        in_specs=[
-            pl.BlockSpec(memory_space=pltpu.SMEM),
-            pl.BlockSpec(memory_space=pl.ANY),
+        in_specs=[pl.BlockSpec(memory_space=pltpu.SMEM)]
+        + [pl.BlockSpec(memory_space=pl.ANY)] * len(pieces),
+        out_specs=pl.BlockSpec(memory_space=pl.ANY),
+        scratch_shapes=[
+            pltpu.VMEM((n, tile, width), dtype),
+            pltpu.SemaphoreType.DMA((len(pieces),)),
+            pltpu.SemaphoreType.DMA((slots,)),
         ],
-        out_specs=pl.BlockSpec(memory_space=pl.ANY),
-        scratch_shapes=[pltpu.SemaphoreType.DMA((slots,))],
-        out_shape=jax.ShapeDtypeStruct((slots, tile, width), blocks.dtype),
+        out_shape=jax.ShapeDtypeStruct((slots, tile, width), dtype),
         cost_estimate=pl.CostEstimate(
             flops=0, bytes_accessed=(n + slots) * tile * width * 2, transcendentals=0
         ),
         name="picked",
-    )(offsets, blocks)
+    )(offsets, *pieces)
 
 
 def shifted(x, axis, by):
@@ -186,7 +208,7 @@
 
 def gather_of_eight(x, axis):
     near = jnp.stack([shifted(x, axis, 3), x, shifted(x, axis, -3)])
-    return jnp.concatenate([near, shifted(near, axis, 1), shifted(near[:2], axis, -1)])
+    return near, shifted(near, axis, 1), shifted(near[:2], axis, -1)
 
 
 def sum_of_eight(x, axis):
@@ -195,8 +217,12 @@
     low = x[0].astype(jnp.float32) + above[0] + below[0]
     own = x[1].astype(jnp.float32) + above[1] + below[1]
     high = x[2].astype(jnp.float32) + above[2]
-    low = shifted(low.astype(x.dtype), axis, -3).astype(jnp.float32)
-    high = shifted(high.astype(x.dtype), axis, 3).astype(jnp.float32)
+    return own, low.astype(x.dtype), high.astype(x.dtype)
+
+
+def sum_of_eight_ended(own, low, high, axis):
+    low = shifted(low, axis, -3).astype(jnp.float32)
+    high = shifted(high, axis, 3).astype(jnp.float32)
     return own + low + high
 
 
@@ -278,13 +304,14 @@
     leaving_1 = picked(passed_offset, column_1)
     leaving_1, second = lax.optimization_barrier((leaving_1, node_feats[:, half_in:]))
     arrived_1 = lax.all_to_all(leaving_1, ("x", "core"), 0, 0, tiled=True)
-    column_2 = gather_of_eight(second, "z").reshape(z_total * blocks_here, TILE, half_in)
-    leaving_2 = picked(passed_near, column_2)
+    column_2 = [x.reshape(-1, TILE, half_in) for x in gather_of_eight(second, "z")]
+    leaving_2 = picked(passed_near, *column_2)
     arrived_1, leaving_2 = lax.optimization_barrier((arrived_1, leaving_2))
     arrived_2 = lax.all_to_all(leaving_2, ("x", "core"), 0, 0, tiled=True)
     sums_1 = tile_sums(held_near, masks, arrived_1, group_blocks)
-    summed_1 = sum_of_eight(sums_1.reshape(rep_total, rows_here, half_in), "rep")
-    arrived_2, summed_1 = lax.optimization_barrier((arrived_2, summed_1))
+    begun_1 = sum_of_eight(sums_1.reshape(rep_total, rows_here, half_in), "rep")
+    arrived_2, begun_1 = lax.optimization_barrier((arrived_2, begun_1))
+    summed_1 = sum_of_eight_ended(*begun_1, "rep")
     sums_2 = tile_sums(held_offset, masks, arrived_2, group_blocks)
     pieces = lax.all_to_all(
         sums_2.reshape(rep_total, rows_here, half_in), "rep", 0, 0, tiled=True

time: 461 us -> 323 us (0.70)
  Pallas kernels: 161 us -> 21.4 us
  starting transfers between devices: 126 us -> 144 us
  waiting for transfers between devices: 126 us -> 115 us
  local copies, waits for them, and re-layouts: 21.9 us -> 16 us
    pallas_call x2, Pallas kernels: 132 us -> 7.52 us  [picked(): pl.pallas_call(pick_kernel, in_specs=[pl.BlockSpec(memory_space=pltpu.SME...]
    all_to_all x1, waiting for transfers between devices: 19.6 us -> 0.05 us  [shards(): lax.all_to_all(sums_2.reshape(rep_total, rows_here, half_in), 'rep', 0, 0...]
    pallas_call x2, Pallas kernels: 14.4 us -> 5.93 us  [tile_sums(): pl.pallas_call(forward_kernel, grid_spec=pltpu.PrefetchScalarGridSpec(num...]
    all_to_all x1, waiting for transfers between devices: 0.01 us -> 8.02 us  [shards(): arrived_2 = lax.all_to_all(leaving_2, ('x', 'core'), 0, 0, tiled=True)]
    ppermute x13, starting transfers between devices: 45.8 us -> 53.5 us  [pair_swap(): return lax.ppermute(x, axis, [(i, i ^ bit) for i in range(n)])]
    ppermute x8, waiting for transfers between devices: 25.5 us -> 33 us  [shifted(): return lax.ppermute(x, axis, [(i, (i + by) % n) for i in range(n)])]
    ppermute x13, waiting for transfers between devices: 44.8 us -> 38.1 us  [pair_swap(): return lax.ppermute(x, axis, [(i, i ^ bit) for i in range(n)])]
    pallas_call x1, Pallas kernels: 8.23 us -> 3.39 us  [tile_products(): pl.pallas_call(products_kernel, grid_spec=pltpu.PrefetchScalarGridSpec(nu...]
  transfers between devices with their start and end apart: 30 -> 30, of which waited for: 24 -> 26; matrix products, arithmetic and copies ran while one was open for 7% -> 8% of each run, Pallas kernels for 16% -> 2%
where the time goes in v4:
time: 323 us; the launch traced here: 321 us
  starting transfers between devices  144 us (45%)
  waiting for transfers between devices  115 us (36%)
  Pallas kernels  21.4 us (7%)
  other arithmetic  18.3 us (6%)
  local copies, waits for them, and re-layouts  16 us (5%)
  matrix products  5.59 us (2%)
    ppermute x13, starting transfers between devices, pair_swap(): return lax.ppermute(x, axis, [(i, i ^ bit) for i in range(n)])  53.5 us
    ppermute x13, waiting for transfers between devices, pair_swap(): return lax.ppermute(x, axis, [(i, i ^ bit) for i in range(n)])  38.1 us
    ppermute x8, waiting for transfers between devices, shifted(): return lax.ppermute(x, axis, [(i, (i + by) % n) for i in range(n)])  33 us
    ppermute x8, starting transfers between devices, shifted(): return lax.ppermute(x, axis, [(i, (i + by) % n) for i in range(n)])  30.1 us
    all_to_all x1, waiting for transfers between devices, shards(): lax.all_to_all(column_sums.reshape(z_total, rows_here, width_in), 'z', 0,...  18 us
    all_to_all x1, starting transfers between devices, shards(): lax.all_to_all(jnp.broadcast_to(node_feats[None, :, :half_in], (z_total,...  10.9 us
    convert_element_type x1, other arithmetic, edge_masks(): return (hashed < limits[:, None, None]).astype(jnp.bfloat16)  10.8 us
    all_to_all x1, waiting for transfers between devices, shards(): returned = lax.all_to_all(returning, ('x', 'core'), 0, 0, tiled=True)  9.46 us
  transfers between devices with their start and end apart: 30, of which 26 were waited for; matrix products, arithmetic and copies ran while one was open for 8% of the time, Pallas kernels for 2%

profile of v4, /device:TPU:1, one launch (start us, length us, event | category | flops | bytes accessed | tf_op | source)
XLA Modules:
  0.0 321.1 jit_solution(2981566234182912334)
XLA Ops:
  2.7 10.9 %all-to-all-start = ((bf16[8,384,128]{2,1,0:T(8,128)(2,1)}), bf16[8,384,128]{2,1,0:T(8,128)(2,1)}, u32[]{:S(2)}, u32[]{:S(2)}) async-start(bf16[8,384,128]{2,1,0:T(8,128)(2,1)} %broadcast_in_dim.84), calls=%async_computation | async-start | bytes 1572864 | tf_op jit(solution)/shard_map/all_to_all | solution.py:262
  20.0 10.8 %fusion.10 = (bf16[64,128,128]{2,1,0:T(8,128)(2,1)}, bf16[64,128,128]{2,1,0:T(8,128)(2,1)S(1)}) fusion(s32[64,128]{1,0:T(8,128)S(1)} %get-tuple-element.51, s32[64,128]{1,0:T(8,128)S(1)} %get-tuple-element.50, s32[64,128]{1,0:T(8,128)S(1)} %add_select_fusion.5, s32[64]{0:T(128)S(1)} %get-tuple-element.56), kind=kLoop, calls=%fused_computation.22 | loop fusion | flops 46137344 | bytes 4292864 | tf_op jit(solution)/shard_map/convert_element_type | solution.py:26
  30.9 6.3 %all-to-all-done = bf16[8,384,128]{2,1,0:T(8,128)(2,1)} async-done(((bf16[8,384,128]{2,1,0:T(8,128)(2,1)}), bf16[8,384,128]{2,1,0:T(8,128)(2,1)}, u32[]{:S(2)}, u32[]{:S(2)}) %all-to-all-start) | async-done | bytes 786464 | tf_op jit(solution)/shard_map/all_to_all | solution.py:262
  41.0 4.8 %all-to-all-start.1 = ((bf16[64,128,128]{2,1,0:T(8,128)(2,1)}), bf16[64,128,128]{2,1,0:T(8,128)(2,1)}, u32[]{:S(2)}, u32[]{:S(2)}) async-start(bf16[64,128,128]{2,1,0:T(8,128)(2,1)} %picked.2), calls=%async_computation.1 | async-start | bytes 4194304 | tf_op jit(solution)/shard_map/all_to_all | solution.py:306
  47.7 6.4 %collective-permute-start.1 = (bf16[384,128]{1,0:T(8,128)(2,1)S(1)}, bf16[384,128]{1,0:T(8,128)(2,1)S(1)}, u32[]{:S(2)}, u32[]{:S(2)}) collective-permute-start(bf16[384,128]{1,0:T(8,128)(2,1)S(1)} %get-tuple-element.21), channel_id=1, source_target_pairs={{0,80},{16,96},{32,112},{48,0},{64,16},{80,32},{96,48},{112,64},{1... | collective-permute-start | bytes 294920 | tf_op jit(solution)/shard_map/ppermute | solution.py:198
  62.6 4.6 %collective-permute-start.3 = (bf16[2,384,128]{2,1,0:T(8,128)(2,1)S(1)}, bf16[2,384,128]{2,1,0:T(8,128)(2,1)S(1)}, u32[]{:S(2)}, u32[]{:S(2)}) collective-permute-start(bf16[2,384,128]{2,1,0:T(8,128)(2,1)S(1)} %pad_maximum_fusion.1), channel_id=1, source_target_pairs={{0,112},{16,0},{32,16},{48,32},{64,48},{80,64},{96,80},{112,96},{1... | collective-permute-start | bytes 589832 | tf_op jit(solution)/shard_map/ppermute | solution.py:198
  67.2 4.2 %collective-permute-done.3 = bf16[2,384,128]{2,1,0:T(8,128)(2,1)S(1)} collective-permute-done((bf16[2,384,128]{2,1,0:T(8,128)(2,1)S(1)}, bf16[2,384,128]{2,1,0:T(8,128)(2,1)S(1)}, u32[]{:S(2)}, u32[]{:S(2)}) %collective-permute-start.3) | collective-permute-done | bytes 196640 | tf_op jit(solution)/shard_map/ppermute | solution.py:198
  76.3 5.9 %all-to-all-start.2 = ((bf16[64,128,128]{2,1,0:T(8,128)(2,1)}), bf16[64,128,128]{2,1,0:T(8,128)(2,1)}, u32[]{:S(2)}, u32[]{:S(2)}) async-start(bf16[64,128,128]{2,1,0:T(8,128)(2,1)} %picked.3), calls=%async_computation.2 | async-start | bytes 4194304 | tf_op jit(solution)/shard_map/all_to_all | solution.py:310
  85.1 5.1 %collective-permute-start.4 = (bf16[3,384,128]{2,1,0:T(8,128)(2,1)S(1)}, bf16[3,384,128]{2,1,0:T(8,128)(2,1)S(1)}, u32[]{:S(2)}, u32[]{:S(2)}) collective-permute-start(bf16[3,384,128]{2,1,0:T(8,128)(2,1)S(1)} %bitcast.84), channel_id=1, source_target_pairs={{0,7},{1,0},{2,1},{3,2},{4,3},{5,4},{6,5},{7,6},{8,15},{9,8},{10,9... | collective-permute-start | bytes 884744 | tf_op jit(solution)/shard_map/ppermute | solution.py:198
  92.2 7.5 %collective-permute-done.5 = bf16[2,384,128]{2,1,0:T(8,128)(2,1)S(1)} collective-permute-done((bf16[2,384,128]{2,1,0:T(8,128)(2,1)S(1)}, bf16[2,384,128]{2,1,0:T(8,128)(2,1)S(1)}, u32[]{:S(2)}, u32[]{:S(2)}) %collective-permute-start.5) | collective-permute-done | bytes 196640 | tf_op jit(solution)/shard_map/ppermute | solution.py:198
  100.6 8.0 %all-to-all-done.2.feat_ref = bf16[64,128,128]{2,1,0:T(8,128)(2,1)} async-done(((bf16[64,128,128]{2,1,0:T(8,128)(2,1)}), bf16[64,128,128]{2,1,0:T(8,128)(2,1)}, u32[]{:S(2)}, u32[]{:S(2)}) %all-to-all-start.2) | async-done | bytes 2097184 | tf_op jit(solution)/shard_map/all_to_all | solution.py:310
  112.4 7.0 %all-to-all-start.3 = ((bf16[8,384,128]{2,1,0:T(8,128)(2,1)}), bf16[8,384,128]{2,1,0:T(8,128)(2,1)S(1)}, u32[]{:S(2)}, u32[]{:S(2)}) async-start(bf16[8,384,128]{2,1,0:T(8,128)(2,1)} %bitcast.77), calls=%async_computation.3 | async-start | bytes 1572864 | tf_op jit(solution)/shard_map/all_to_all | solution.py:316
  120.7 6.4 %collective-permute-start.6 = (bf16[384,128]{1,0:T(8,128)(2,1)}, bf16[384,128]{1,0:T(8,128)(2,1)S(1)}, u32[]{:S(2)}, u32[]{:S(2)}) collective-permute-start(bf16[384,128]{1,0:T(8,128)(2,1)} %get-tuple-element.26), channel_id=1, source_target_pairs={{0,5},{1,6},{2,7},{3,0},{4,1},{5,2},{6,3},{7,4},{8,13},{9,14},{10,... | collective-permute-start | bytes 294920 | tf_op jit(solution)/shard_map/ppermute | solution.py:198
  129.1 12.6 %collective-permute-done.6 = bf16[384,128]{1,0:T(8,128)(2,1)S(1)} collective-permute-done((bf16[384,128]{1,0:T(8,128)(2,1)}, bf16[384,128]{1,0:T(8,128)(2,1)S(1)}, u32[]{:S(2)}, u32[]{:S(2)}) %collective-permute-start.6) | collective-permute-done | bytes 98336 | tf_op jit(solution)/shard_map/ppermute | solution.py:198
  148.6 6.9 %collective-permute-start.8 = (f32[256,512]{1,0:T(8,128)}, f32[256,512]{1,0:T(8,128)S(1)}, u32[]{:S(2)}, u32[]{:S(2)}) collective-permute-start(f32[256,512]{1,0:T(8,128)} %get-tuple-element.57), channel_id=1, source_target_pairs={{0,8},{8,0},{1,9},{9,1},{2,10},{10,2},{3,11},{11,3},{4,12},{12,4},... | collective-permute-start | bytes 1572872 | tf_op jit(solution)/shard_map/ppermute | solution.py:351
  157.1 4.4 %all-to-all-start.4 = ((bf16[8,384,256]{2,1,0:T(8,128)(2,1)}), bf16[8,384,256]{2,1,0:T(8,128)(2,1)}, u32[]{:S(2)}, u32[]{:S(2)}) async-start(bf16[8,384,256]{2,1,0:T(8,128)(2,1)} %broadcast_in_dim.92), calls=%async_computation.4 | async-start | bytes 3145728 | tf_op jit(solution)/shard_map/all_to_all | solution.py:342
  166.7 7.9 %collective-permute-done.9 = f32[128,512]{1,0:T(8,128)} collective-permute-done((f32[128,512]{1,0:T(8,128)}, f32[128,512]{1,0:T(8,128)}, u32[]{:S(2)}, u32[]{:S(2)}) %collective-permute-start.9) | collective-permute-done | bytes 262176 | tf_op jit(solution)/shard_map/ppermute | solution.py:31
  179.1 5.0 %collective-permute-done.10 = f32[64,512]{1,0:T(8,128)S(1)} collective-permute-done((f32[64,512]{1,0:T(8,128)S(1)}, f32[64,512]{1,0:T(8,128)S(1)}, u32[]{:S(2)}, u32[]{:S(2)}) %collective-permute-start.10) | collective-permute-done | bytes 131104 | tf_op jit(solution)/shard_map/ppermute | solution.py:31
  190.5 4.4 %collective-permute-start.12 = (f32[16,512]{1,0:T(8,128)S(1)}, f32[16,512]{1,0:T(8,128)S(1)}, u32[]{:S(2)}, u32[]{:S(2)}) collective-permute-start(f32[16,512]{1,0:T(8,128)S(1)} %slice_select_fusion.3), channel_id=1, source_target_pairs={{0,32},{16,48},{32,0},{48,16},{64,96},{80,112},{96,64},{112,80},{1... | collective-permute-start | bytes 98312 | tf_op jit(solution)/shard_map/ppermute | solution.py:31
  196.7 7.2 %collective-permute-start.13 = (f32[8,512]{1,0:T(8,128)S(1)}, f32[8,512]{1,0:T(8,128)S(1)}, u32[]{:S(2)}, u32[]{:S(2)}) collective-permute-start(f32[8,512]{1,0:T(8,128)S(1)} %slice_select_fusion.4), channel_id=1, source_target_pairs={{0,64},{16,80},{32,96},{48,112},{64,0},{80,16},{96,32},{112,48},{1... | collective-permute-start | bytes 49160 | tf_op jit(solution)/shard_map/ppermute | solution.py:31
  210.5 8.6 %all-to-all-start.5 = ((bf16[64,128,256]{2,1,0:T(8,128)(2,1)}), bf16[64,128,256]{2,1,0:T(8,128)(2,1)}, u32[]{:S(2)}, u32[]{:S(2)}) async-start(bf16[64,128,256]{2,1,0:T(8,128)(2,1)} %copy-done.1), calls=%async_computation.5 | async-start | bytes 8388608 | tf_op jit(solution)/shard_map/all_to_all | solution.py:360
  224.0 4.0 %collective-permute-start.15 = (f32[8,512]{1,0:T(8,128)S(1)}, f32[8,512]{1,0:T(8,128)S(1)}, u32[]{:S(2)}, u32[]{:S(2)}) collective-permute-start(f32[8,512]{1,0:T(8,128)S(1)} %add.370), channel_id=1, source_target_pairs={{0,2},{1,3},{2,0},{3,1},{4,6},{5,7},{6,4},{7,5},{8,10},{9,11},{10,... | collective-permute-start | bytes 49160 | tf_op jit(solution)/shard_map/ppermute | solution.py:31
  229.8 7.2 %collective-permute-start.16 = (f32[8,512]{1,0:T(8,128)S(1)}, f32[8,512]{1,0:T(8,128)S(1)}, u32[]{:S(2)}, u32[]{:S(2)}) collective-permute-start(f32[8,512]{1,0:T(8,128)S(1)} %add.371), channel_id=1, source_target_pairs={{0,4},{1,5},{2,6},{3,7},{4,0},{5,1},{6,2},{7,3},{8,12},{9,13},{10,... | collective-permute-start | bytes 49160 | tf_op jit(solution)/shard_map/ppermute | solution.py:31
  238.2 7.4 %collective-permute-start.17 = (f32[8,512]{1,0:T(8,128)S(1)}, f32[8,512]{1,0:T(8,128)S(1)}, u32[]{:S(2)}, u32[]{:S(2)}) collective-permute-start(f32[8,512]{1,0:T(8,128)S(1)} %add_multiply_fusion), channel_id=1, source_target_pairs={{0,64},{16,80},{32,96},{48,112},{64,0},{80,16},{96,32},{112,48},{1... | collective-permute-start | bytes 49160 | tf_op jit(solution)/shard_map/ppermute | solution.py:31
  246.7 4.5 %collective-permute-start.18 = (f32[16,512]{1,0:T(8,128)S(1)}, f32[16,512]{1,0:T(8,128)S(1)}, u32[]{:S(2)}, u32[]{:S(2)}) collective-permute-start(f32[16,512]{1,0:T(8,128)S(1)} %maximum_select_fusion.4), channel_id=1, source_target_pairs={{0,32},{16,48},{32,0},{48,16},{64,96},{80,112},{96,64},{112,80},{1... | collective-permute-start | bytes 98312 | tf_op jit(solution)/shard_map/ppermute | solution.py:31
  258.6 9.5 %all-to-all-done.5.part_ref = bf16[64,128,256]{2,1,0:T(8,128)(2,1)} async-done(((bf16[64,128,256]{2,1,0:T(8,128)(2,1)}), bf16[64,128,256]{2,1,0:T(8,128)(2,1)}, u32[]{:S(2)}, u32[]{:S(2)}) %all-to-all-start.5) | async-done | bytes 4194336 | tf_op jit(solution)/shard_map/all_to_all | solution.py:360
  268.1 4.6 %summed_into.1 = bf16[24,128,256]{2,1,0:T(8,128)(2,1)} custom-call(s32[64]{0:T(128)S(1)} %copy-done.4, bf16[64,128,256]{2,1,0:T(8,128)(2,1)} %all-to-all-done.5.part_ref), custom_call_target="tpu_custom_call" | custom-call | flops 2097152 | bytes 4194304 | tf_op jit(solution)/shard_map/summed_into/pallas_call | solution.py:129
  272.6 6.8 %all-to-all-start.6 = ((bf16[8,384,256]{2,1,0:T(8,128)(2,1)}), bf16[8,384,256]{2,1,0:T(8,128)(2,1)S(1)}, u32[]{:S(2)}, u32[]{:S(2)}) async-start(bf16[8,384,256]{2,1,0:T(8,128)(2,1)} %bitcast.28), calls=%async_computation.6 | async-start | bytes 3145728 | tf_op jit(solution)/shard_map/all_to_all | solution.py:368
  281.6 5.0 %collective-permute-done.20 = f32[64,512]{1,0:T(8,128)S(1)} collective-permute-done((f32[64,512]{1,0:T(8,128)S(1)}, f32[64,512]{1,0:T(8,128)S(1)}, u32[]{:S(2)}, u32[]{:S(2)}) %collective-permute-start.20) | collective-permute-done | bytes 131104 | tf_op jit(solution)/shard_map/ppermute | solution.py:31
  288.9 5.2 %collective-permute-done.21 = f32[128,512]{1,0:T(8,128)S(1)} collective-permute-done((f32[128,512]{1,0:T(8,128)S(1)}, f32[128,512]{1,0:T(8,128)S(1)}, u32[]{:S(2)}, u32[]{:S(2)}) %collective-permute-start.21) | collective-permute-done | bytes 262176 | tf_op jit(solution)/shard_map/ppermute | solution.py:31
  294.1 5.1 %collective-permute-start.22 = (f32[256,512]{1,0:T(8,128)S(1)}, f32[256,512]{1,0:T(8,128)S(1)}, u32[]{:S(2)}, u32[]{:S(2)}) collective-permute-start(f32[256,512]{1,0:T(8,128)S(1)} %maximum_select_fusion), channel_id=1, source_target_pairs={{0,8},{8,0},{1,9},{9,1},{2,10},{10,2},{3,11},{11,3},{4,12},{12,4},... | collective-permute-start | bytes 1572872 | tf_op jit(solution)/shard_map/ppermute | solution.py:373
  301.9 18.0 %all-to-all-done.6 = bf16[8,384,256]{2,1,0:T(8,128)(2,1)S(1)} async-done(((bf16[8,384,256]{2,1,0:T(8,128)(2,1)}), bf16[8,384,256]{2,1,0:T(8,128)(2,1)S(1)}, u32[]{:S(2)}, u32[]{:S(2)}) %all-to-all-start.6) | async-done | bytes 1572896 | tf_op jit(solution)/shard_map/all_to_all | solution.py:368
  (146 shorter events, 97.7 us)
Async XLA Ops:
  2.7 34.5 %all-to-all-start = ((bf16[8,384,128]{2,1,0:T(8,128)(2,1)}), bf16[8,384,128]{2,1,0:T(8,128)(2,1)}, u32[]{:S(2)}, u32[]{:S(2)}) async-start(bf16[8,384,128]{2,1,0:T(8,128)(2,1)} %broadcast_in_dim.84), calls=%async_computation | async-start | bytes 1572864 | tf_op jit(solution)/shard_map/all_to_all | solution.py:262
  41.0 35.3 %all-to-all-start.1 = ((bf16[64,128,128]{2,1,0:T(8,128)(2,1)}), bf16[64,128,128]{2,1,0:T(8,128)(2,1)}, u32[]{:S(2)}, u32[]{:S(2)}) async-start(bf16[64,128,128]{2,1,0:T(8,128)(2,1)} %picked.2), calls=%async_computation.1 | async-start | bytes 4194304 | tf_op jit(solution)/shard_map/all_to_all | solution.py:306
  45.8 11.2 %collective-permute-start = (bf16[384,128]{1,0:T(8,128)(2,1)S(1)}, bf16[384,128]{1,0:T(8,128)(2,1)S(1)}, u32[]{:S(2)}, u32[]{:S(2)}) collective-permute-start(bf16[384,128]{1,0:T(8,128)(2,1)S(1)} %get-tuple-element.21), channel_id=1, source_target_pairs={{0,48},{16,64},{32,80},{48,96},{64,112},{80,0},{96,16},{112,32},{1... | collective-permute-start | bytes 294920 | tf_op jit(solution)/shard_map/ppermute | solution.py:198
  47.7 12.9 %collective-permute-start.1 = (bf16[384,128]{1,0:T(8,128)(2,1)S(1)}, bf16[384,128]{1,0:T(8,128)(2,1)S(1)}, u32[]{:S(2)}, u32[]{:S(2)}) collective-permute-start(bf16[384,128]{1,0:T(8,128)(2,1)S(1)} %get-tuple-element.21), channel_id=1, source_target_pairs={{0,80},{16,96},{32,112},{48,0},{64,16},{80,32},{96,48},{112,64},{1... | collective-permute-start | bytes 294920 | tf_op jit(solution)/shard_map/ppermute | solution.py:198
  60.7 11.1 %collective-permute-start.2 = (bf16[3,384,128]{2,1,0:T(8,128)(2,1)S(1)}, bf16[3,384,128]{2,1,0:T(8,128)(2,1)S(1)}, u32[]{:S(2)}, u32[]{:S(2)}) collective-permute-start(bf16[3,384,128]{2,1,0:T(8,128)(2,1)S(1)} %pad_maximum_fusion), channel_id=1, source_target_pairs={{0,16},{16,32},{32,48},{48,64},{64,80},{80,96},{96,112},{112,0},{1... | collective-permute-start | bytes 884744 | tf_op jit(solution)/shard_map/ppermute | solution.py:198
  62.6 8.8 %collective-permute-start.3 = (bf16[2,384,128]{2,1,0:T(8,128)(2,1)S(1)}, bf16[2,384,128]{2,1,0:T(8,128)(2,1)S(1)}, u32[]{:S(2)}, u32[]{:S(2)}) collective-permute-start(bf16[2,384,128]{2,1,0:T(8,128)(2,1)S(1)} %pad_maximum_fusion.1), channel_id=1, source_target_pairs={{0,112},{16,0},{32,16},{48,32},{64,48},{80,64},{96,80},{112,96},{1... | collective-permute-start | bytes 589832 | tf_op jit(solution)/shard_map/ppermute | solution.py:198
  76.3 32.3 %all-to-all-start.2 = ((bf16[64,128,128]{2,1,0:T(8,128)(2,1)}), bf16[64,128,128]{2,1,0:T(8,128)(2,1)}, u32[]{:S(2)}, u32[]{:S(2)}) async-start(bf16[64,128,128]{2,1,0:T(8,128)(2,1)} %picked.3), calls=%async_computation.2 | async-start | bytes 4194304 | tf_op jit(solution)/shard_map/all_to_all | solution.py:310
  85.1 14.6 %collective-permute-start.4 = (bf16[3,384,128]{2,1,0:T(8,128)(2,1)S(1)}, bf16[3,384,128]{2,1,0:T(8,128)(2,1)S(1)}, u32[]{:S(2)}, u32[]{:S(2)}) collective-permute-start(bf16[3,384,128]{2,1,0:T(8,128)(2,1)S(1)} %bitcast.84), channel_id=1, source_target_pairs={{0,7},{1,0},{2,1},{3,2},{4,3},{5,4},{6,5},{7,6},{8,15},{9,8},{10,9... | collective-permute-start | bytes 884744 | tf_op jit(solution)/shard_map/ppermute | solution.py:198
  90.3 9.4 %collective-permute-start.5 = (bf16[2,384,128]{2,1,0:T(8,128)(2,1)S(1)}, bf16[2,384,128]{2,1,0:T(8,128)(2,1)S(1)}, u32[]{:S(2)}, u32[]{:S(2)}) collective-permute-start(bf16[2,384,128]{2,1,0:T(8,128)(2,1)S(1)} %bitcast.86), channel_id=1, source_target_pairs={{0,1},{1,2},{2,3},{3,4},{4,5},{5,6},{6,7},{7,0},{8,9},{9,10},{10,1... | collective-permute-start | bytes 589832 | tf_op jit(solution)/shard_map/ppermute | solution.py:198
  112.4 31.2 %all-to-all-start.3 = ((bf16[8,384,128]{2,1,0:T(8,128)(2,1)}), bf16[8,384,128]{2,1,0:T(8,128)(2,1)S(1)}, u32[]{:S(2)}, u32[]{:S(2)}) async-start(bf16[8,384,128]{2,1,0:T(8,128)(2,1)} %bitcast.77), calls=%async_computation.3 | async-start | bytes 1572864 | tf_op jit(solution)/shard_map/all_to_all | solution.py:316
  120.7 21.0 %collective-permute-start.6 = (bf16[384,128]{1,0:T(8,128)(2,1)}, bf16[384,128]{1,0:T(8,128)(2,1)S(1)}, u32[]{:S(2)}, u32[]{:S(2)}) collective-permute-start(bf16[384,128]{1,0:T(8,128)(2,1)} %get-tuple-element.26), channel_id=1, source_target_pairs={{0,5},{1,6},{2,7},{3,0},{4,1},{5,2},{6,3},{7,4},{8,13},{9,14},{10,... | collective-permute-start | bytes 294920 | tf_op jit(solution)/shard_map/ppermute | solution.py:198
  127.1 16.4 %collective-permute-start.7 = (bf16[384,128]{1,0:T(8,128)(2,1)}, bf16[384,128]{1,0:T(8,128)(2,1)S(1)}, u32[]{:S(2)}, u32[]{:S(2)}) collective-permute-start(bf16[384,128]{1,0:T(8,128)(2,1)} %get-tuple-element.27), channel_id=1, source_target_pairs={{0,3},{1,4},{2,5},{3,6},{4,7},{5,0},{6,1},{7,2},{8,11},{9,12},{10,... | collective-permute-start | bytes 294920 | tf_op jit(solution)/shard_map/ppermute | solution.py:198
  148.6 13.0 %collective-permute-start.8 = (f32[256,512]{1,0:T(8,128)}, f32[256,512]{1,0:T(8,128)S(1)}, u32[]{:S(2)}, u32[]{:S(2)}) collective-permute-start(f32[256,512]{1,0:T(8,128)} %get-tuple-element.57), channel_id=1, source_target_pairs={{0,8},{8,0},{1,9},{9,1},{2,10},{10,2},{3,11},{11,3},{4,12},{12,4},... | collective-permute-start | bytes 1572872 | tf_op jit(solution)/shard_map/ppermute | solution.py:351
  157.1 47.9 %copy-start.2 = (bf16[64,128,128]{2,1,0:T(8,128)(2,1)S(1)}, bf16[64,128,128]{2,1,0:T(8,128)(2,1)}, u32[]{:S(2)}) copy-start(bf16[64,128,128]{2,1,0:T(8,128)(2,1)} %get-tuple-element.29.mask_ref) | copy-start | bytes 6291460
  157.1 47.9 %all-to-all-start.4 = ((bf16[8,384,256]{2,1,0:T(8,128)(2,1)}), bf16[8,384,256]{2,1,0:T(8,128)(2,1)}, u32[]{:S(2)}, u32[]{:S(2)}) async-start(bf16[8,384,256]{2,1,0:T(8,128)(2,1)} %broadcast_in_dim.92), calls=%async_computation.4 | async-start | bytes 3145728 | tf_op jit(solution)/shard_map/all_to_all | solution.py:342
  164.5 10.1 %collective-permute-start.9 = (f32[128,512]{1,0:T(8,128)}, f32[128,512]{1,0:T(8,128)}, u32[]{:S(2)}, u32[]{:S(2)}) collective-permute-start(f32[128,512]{1,0:T(8,128)} %slice_select_fusion), channel_id=1, source_target_pairs={{0,128},{128,0},{256,384},{384,256},{1,129},{129,1},{257,385},{385... | collective-permute-start | bytes 786440 | tf_op jit(solution)/shard_map/ppermute | solution.py:31
  176.3 7.7 %collective-permute-start.10 = (f32[64,512]{1,0:T(8,128)S(1)}, f32[64,512]{1,0:T(8,128)S(1)}, u32[]{:S(2)}, u32[]{:S(2)}) collective-permute-start(f32[64,512]{1,0:T(8,128)S(1)} %slice_select_fusion.1), channel_id=1, source_target_pairs={{0,256},{128,384},{256,0},{384,128},{1,257},{129,385},{257,1},{385... | collective-permute-start | bytes 393224 | tf_op jit(solution)/shard_map/ppermute | solution.py:31
  185.1 5.4 %collective-permute-start.11 = (f32[32,512]{1,0:T(8,128)S(1)}, f32[32,512]{1,0:T(8,128)S(1)}, u32[]{:S(2)}, u32[]{:S(2)}) collective-permute-start(f32[32,512]{1,0:T(8,128)S(1)} %slice_select_fusion.2), channel_id=1, source_target_pairs={{0,16},{16,0},{32,48},{48,32},{64,80},{80,64},{96,112},{112,96},{1... | collective-permute-start | bytes 196616 | tf_op jit(solution)/shard_map/ppermute | solution.py:31
  190.5 6.1 %collective-permute-start.12 = (f32[16,512]{1,0:T(8,128)S(1)}, f32[16,512]{1,0:T(8,128)S(1)}, u32[]{:S(2)}, u32[]{:S(2)}) collective-permute-start(f32[16,512]{1,0:T(8,128)S(1)} %slice_select_fusion.3), channel_id=1, source_target_pairs={{0,32},{16,48},{32,0},{48,16},{64,96},{80,112},{96,64},{112,80},{1... | collective-permute-start | bytes 98312 | tf_op jit(solution)/shard_map/ppermute | solution.py:31
  196.7 8.4 %collective-permute-start.13 = (f32[8,512]{1,0:T(8,128)S(1)}, f32[8,512]{1,0:T(8,128)S(1)}, u32[]{:S(2)}, u32[]{:S(2)}) collective-permute-start(f32[8,512]{1,0:T(8,128)S(1)} %slice_select_fusion.4), channel_id=1, source_target_pairs={{0,64},{16,80},{32,96},{48,112},{64,0},{80,16},{96,32},{112,48},{1... | collective-permute-start | bytes 49160 | tf_op jit(solution)/shard_map/ppermute | solution.py:31
  210.5 57.5 %copy-start.4 = (s32[64]{0:T(128)S(1)}, s32[64]{0:T(128)}, u32[]{:S(2)}) copy-start(s32[64]{0:T(128)} %get-tuple-element.59.offset_ref) | copy-start | bytes 772
  210.5 57.5 %all-to-all-start.5 = ((bf16[64,128,256]{2,1,0:T(8,128)(2,1)}), bf16[64,128,256]{2,1,0:T(8,128)(2,1)}, u32[]{:S(2)}, u32[]{:S(2)}) async-start(bf16[64,128,256]{2,1,0:T(8,128)(2,1)} %copy-done.1), calls=%async_computation.5 | async-start | bytes 8388608 | tf_op jit(solution)/shard_map/all_to_all | solution.py:360
  219.1 4.9 %collective-permute-start.14 = (f32[8,512]{1,0:T(8,128)S(1)}, f32[8,512]{1,0:T(8,128)S(1)}, u32[]{:S(2)}, u32[]{:S(2)}) collective-permute-start(f32[8,512]{1,0:T(8,128)S(1)} %select_add_fusion.5), channel_id=1, source_target_pairs={{0,1},{1,0},{2,3},{3,2},{4,5},{5,4},{6,7},{7,6},{8,9},{9,8},{10,11... | collective-permute-start | bytes 49160 | tf_op jit(solution)/shard_map/ppermute | solution.py:31
  224.0 5.8 %collective-permute-start.15 = (f32[8,512]{1,0:T(8,128)S(1)}, f32[8,512]{1,0:T(8,128)S(1)}, u32[]{:S(2)}, u32[]{:S(2)}) collective-permute-start(f32[8,512]{1,0:T(8,128)S(1)} %add.370), channel_id=1, source_target_pairs={{0,2},{1,3},{2,0},{3,1},{4,6},{5,7},{6,4},{7,5},{8,10},{9,11},{10,... | collective-permute-start | bytes 49160 | tf_op jit(solution)/shard_map/ppermute | solution.py:31
  229.8 8.4 %collective-permute-start.16 = (f32[8,512]{1,0:T(8,128)S(1)}, f32[8,512]{1,0:T(8,128)S(1)}, u32[]{:S(2)}, u32[]{:S(2)}) collective-permute-start(f32[8,512]{1,0:T(8,128)S(1)} %add.371), channel_id=1, source_target_pairs={{0,4},{1,5},{2,6},{3,7},{4,0},{5,1},{6,2},{7,3},{8,12},{9,13},{10,... | collective-permute-start | bytes 49160 | tf_op jit(solution)/shard_map/ppermute | solution.py:31
  238.2 8.5 %collective-permute-start.17 = (f32[8,512]{1,0:T(8,128)S(1)}, f32[8,512]{1,0:T(8,128)S(1)}, u32[]{:S(2)}, u32[]{:S(2)}) collective-permute-start(f32[8,512]{1,0:T(8,128)S(1)} %add_multiply_fusion), channel_id=1, source_target_pairs={{0,64},{16,80},{32,96},{48,112},{64,0},{80,16},{96,32},{112,48},{1... | collective-permute-start | bytes 49160 | tf_op jit(solution)/shard_map/ppermute | solution.py:31
  246.7 6.1 %collective-permute-start.18 = (f32[16,512]{1,0:T(8,128)S(1)}, f32[16,512]{1,0:T(8,128)S(1)}, u32[]{:S(2)}, u32[]{:S(2)}) collective-permute-start(f32[16,512]{1,0:T(8,128)S(1)} %maximum_select_fusion.4), channel_id=1, source_target_pairs={{0,32},{16,48},{32,0},{48,16},{64,96},{80,112},{96,64},{112,80},{1... | collective-permute-start | bytes 98312 | tf_op jit(solution)/shard_map/ppermute | solution.py:31
  252.9 5.7 %collective-permute-start.19 = (f32[32,512]{1,0:T(8,128)S(1)}, f32[32,512]{1,0:T(8,128)S(1)}, u32[]{:S(2)}, u32[]{:S(2)}) collective-permute-start(f32[32,512]{1,0:T(8,128)S(1)} %maximum_select_fusion.3), channel_id=1, source_target_pairs={{0,16},{16,0},{32,48},{48,32},{64,80},{80,64},{96,112},{112,96},{1... | collective-permute-start | bytes 196616 | tf_op jit(solution)/shard_map/ppermute | solution.py:31
  272.6 47.3 %all-to-all-start.6 = ((bf16[8,384,256]{2,1,0:T(8,128)(2,1)}), bf16[8,384,256]{2,1,0:T(8,128)(2,1)S(1)}, u32[]{:S(2)}, u32[]{:S(2)}) async-start(bf16[8,384,256]{2,1,0:T(8,128)(2,1)} %bitcast.28), calls=%async_computation.6 | async-start | bytes 3145728 | tf_op jit(solution)/shard_map/all_to_all | solution.py:368
  279.5 7.2 %collective-permute-start.20 = (f32[64,512]{1,0:T(8,128)S(1)}, f32[64,512]{1,0:T(8,128)S(1)}, u32[]{:S(2)}, u32[]{:S(2)}) collective-permute-start(f32[64,512]{1,0:T(8,128)S(1)} %maximum_select_fusion.2), channel_id=1, source_target_pairs={{0,256},{128,384},{256,0},{384,128},{1,257},{129,385},{257,1},{385... | collective-permute-start | bytes 393224 | tf_op jit(solution)/shard_map/ppermute | solution.py:31
  286.7 7.4 %collective-permute-start.21 = (f32[128,512]{1,0:T(8,128)S(1)}, f32[128,512]{1,0:T(8,128)S(1)}, u32[]{:S(2)}, u32[]{:S(2)}) collective-permute-start(f32[128,512]{1,0:T(8,128)S(1)} %maximum_select_fusion.1), channel_id=1, source_target_pairs={{0,128},{128,0},{256,384},{384,256},{1,129},{129,1},{257,385},{385... | collective-permute-start | bytes 786440 | tf_op jit(solution)/shard_map/ppermute | solution.py:31
  294.1 6.6 %collective-permute-start.22 = (f32[256,512]{1,0:T(8,128)S(1)}, f32[256,512]{1,0:T(8,128)S(1)}, u32[]{:S(2)}, u32[]{:S(2)}) collective-permute-start(f32[256,512]{1,0:T(8,128)S(1)} %maximum_select_fusion), channel_id=1, source_target_pairs={{0,8},{8,0},{1,9},{9,1},{2,10},{10,2},{3,11},{11,3},{4,12},{12,4},... | collective-permute-start | bytes 1572872 | tf_op jit(solution)/shard_map/ppermute | solution.py:373
  (15 other events, 211.3 us)

commit v5 on v4

--- a/solution.py
+++ b/solution.py
@@ -253,10 +253,6 @@
     group_blocks = blocks_here * rep_total
     id_blocks = node_ids.reshape(-1, TILE)
     group_first = dom_here * group_blocks
-    bits_of = {
-        a: [1 << i for i in range(lax.axis_size(a).bit_length() - 1)] for a in ("x", "z", "rep")
-    }
-
     half_in = width_in // 2
 
     column_1 = lax.all_to_all(
@@ -313,6 +309,7 @@
     arrived_2, begun_1 = lax.optimization_barrier((arrived_2, begun_1))
     summed_1 = sum_of_eight_ended(*begun_1, "rep")
     sums_2 = tile_sums(held_offset, masks, arrived_2, group_blocks)
+    sums_2, summed_1 = lax.optimization_barrier((sums_2, summed_1))
     pieces = lax.all_to_all(
         sums_2.reshape(rep_total, rows_here, half_in), "rep", 0, 0, tiled=True
     )
@@ -339,36 +336,36 @@
         pre_grad, neigh_weight, over_cols, preferred_element_type=jnp.float32
     )
     spread = (mean_grad / divisor).astype(jnp.bfloat16)
-    group_spread = lax.all_to_all(
-        jnp.broadcast_to(spread[None], (rep_total, rows_here, width_in)), "rep", 0, 0, tiled=True
-    ).reshape(group_blocks, TILE, width_in)
-
-    self_term = lax.dot_general(node_feats, pre_grad, over_rows, preferred_element_type=jnp.float32)
+    spread = jnp.broadcast_to(spread[None], (rep_total, rows_here, width_in))
+    spread, mean_feats, summing = lax.optimization_barrier((spread, mean_feats, pre_grad))
+    group_spread = lax.all_to_all(spread, "rep", 0, 0, tiled=True)
+    group_spread = group_spread.reshape(group_blocks, TILE, width_in)
+
+    self_term = lax.dot_general(node_feats, summing, over_rows, preferred_element_type=jnp.float32)
     neigh_term = lax.dot_general(
-        mean_feats, pre_grad, over_rows, preferred_element_type=jnp.float32
+        mean_feats, summing, over_rows, preferred_element_type=jnp.float32
     )
     first = core == 0
     share = jnp.where(first, self_term, neigh_term) + lax.ppermute(
         jnp.where(first, neigh_term, self_term), "core", [(0, 1), (1, 0)]
     )
-    for axis in ("x", "z"):
-        for bit in bits_of[axis]:
-            share = halved(share, axis, bit)
+    for axis, bit in (("x", 1), ("x", 2), ("z", 1), ("z", 2)):
+        share = halved(share, axis, bit)
 
     returning = tile_products(held_offset, masks_swapped, group_spread)
     returning, share = lax.optimization_barrier((returning, share))
     returned = lax.all_to_all(returning, ("x", "core"), 0, 0, tiled=True)
-    for bit in bits_of["rep"]:
-        share = share + pair_swap(share, "rep", bit)
+    for axis, bit in (("z", 4), ("rep", 1), ("rep", 2), ("rep", 4)):
+        share = share + pair_swap(share, axis, bit)
     share = share * (1.0 / math.sqrt(rows_here * dom_total * rep_total))
-    for bit in reversed(bits_of["z"]):
+    for bit in (2, 1):
         share = doubled(share, "z", bit)
     column_sums = summed_into(passed_offset, returned, z_total * blocks_here)
     column_sums, share = lax.optimization_barrier((column_sums, share))
     parts = lax.all_to_all(
         column_sums.reshape(z_total, rows_here, width_in), "z", 0, 0, tiled=True
     )
-    for bit in reversed(bits_of["x"]):
+    for bit in (2, 1):
         share = doubled(share, "x", bit)
     other = lax.ppermute(share, "core", [(0, 1), (1, 0)])
     self_grad = jnp.where(first, share, other)

time: 323 us -> 323 us (level)
  waiting for transfers between devices: 115 us -> 142 us
  starting transfers between devices: 144 us -> 120 us
    all_to_all x1, waiting for transfers between devices: 0.05 us -> 20.2 us  [shards(): lax.all_to_all(sums_2.reshape(rep_total, rows_here, half_in), 'rep', 0, 0...]
    ppermute x13 -> x12, starting transfers between devices: 53.5 us -> 37.2 us  [pair_swap(): return lax.ppermute(x, axis, [(i, i ^ bit) for i in range(n)])]
    ppermute x13 -> x12, waiting for transfers between devices: 38.1 us -> 47.3 us  [pair_swap(): return lax.ppermute(x, axis, [(i, i ^ bit) for i in range(n)])]
    ppermute x8, waiting for transfers between devices: 33 us -> 26.2 us  [shifted(): return lax.ppermute(x, axis, [(i, (i + by) % n) for i in range(n)])]
    all_to_all x1, waiting for transfers between devices: 0.01 us -> 5.18 us  [shards(): group_spread = lax.all_to_all(spread, 'rep', 0, 0, tiled=True)]
    all_to_all x1, starting transfers between devices: 6.95 us -> 3.56 us  [shards(): lax.all_to_all(sums_2.reshape(rep_total, rows_here, half_in), 'rep', 0, 0...]
  transfers between devices with their start and end apart: 30 -> 29, of which waited for: 26 -> 26; matrix products, arithmetic and copies ran while one was open for 8% -> 7% of each run, Pallas kernels for 2% -> 3%
where the time goes in v5:
time: 323 us; the launch traced here: 321 us
  waiting for transfers between devices  142 us (44%)
  starting transfers between devices  120 us (37%)
  Pallas kernels  21.4 us (7%)
  other arithmetic  16.8 us (5%)
  local copies, waits for them, and re-layouts  14.6 us (5%)
  matrix products  5.48 us (2%)
    ppermute x12, waiting for transfers between devices, pair_swap(): return lax.ppermute(x, axis, [(i, i ^ bit) for i in range(n)])  47.3 us
    ppermute x12, starting transfers between devices, pair_swap(): return lax.ppermute(x, axis, [(i, i ^ bit) for i in range(n)])  37.2 us
    ppermute x8, starting transfers between devices, shifted(): return lax.ppermute(x, axis, [(i, (i + by) % n) for i in range(n)])  30.4 us
    ppermute x8, waiting for transfers between devices, shifted(): return lax.ppermute(x, axis, [(i, (i + by) % n) for i in range(n)])  26.2 us
    all_to_all x1, waiting for transfers between devices, shards(): lax.all_to_all(sums_2.reshape(rep_total, rows_here, half_in), 'rep', 0, 0...  20.2 us
    all_to_all x1, waiting for transfers between devices, shards(): lax.all_to_all(column_sums.reshape(z_total, rows_here, width_in), 'z', 0,...  18 us
    all_to_all x1, starting transfers between devices, shards(): lax.all_to_all(jnp.broadcast_to(node_feats[None, :, :half_in], (z_total,...  10.9 us
    convert_element_type x1, other arithmetic, edge_masks(): return (hashed < limits[:, None, None]).astype(jnp.bfloat16)  10.8 us
  transfers between devices with their start and end apart: 29, of which 26 were waited for; matrix products, arithmetic and copies ran while one was open for 7% of the time, Pallas kernels for 3%

profile of v5, /device:TPU:1, one launch (start us, length us, event | category | flops | bytes accessed | tf_op | source)
XLA Modules:
  0.0 321.2 jit_solution(16238630658784604228)
XLA Ops:
  2.7 10.9 %all-to-all-start = ((bf16[8,384,128]{2,1,0:T(8,128)(2,1)}), bf16[8,384,128]{2,1,0:T(8,128)(2,1)}, u32[]{:S(2)}, u32[]{:S(2)}) async-start(bf16[8,384,128]{2,1,0:T(8,128)(2,1)} %broadcast_in_dim.84), calls=%async_computation | async-start | bytes 1572864 | tf_op jit(solution)/shard_map/all_to_all | solution.py:258
  20.1 10.8 %fusion.10 = (bf16[64,128,128]{2,1,0:T(8,128)(2,1)}, bf16[64,128,128]{2,1,0:T(8,128)(2,1)S(1)}) fusion(s32[64,128]{1,0:T(8,128)S(1)} %get-tuple-element.61, s32[64,128]{1,0:T(8,128)S(1)} %get-tuple-element.60, s32[64,128]{1,0:T(8,128)S(1)} %add_select_fusion.5, s32[64]{0:T(128)S(1)} %get-tuple-element.66), kind=kLoop, calls=%fused_computation.22 | loop fusion | flops 46137344 | bytes 4292864 | tf_op jit(solution)/shard_map/convert_element_type | solution.py:26
  30.9 6.3 %all-to-all-done = bf16[8,384,128]{2,1,0:T(8,128)(2,1)} async-done(((bf16[8,384,128]{2,1,0:T(8,128)(2,1)}), bf16[8,384,128]{2,1,0:T(8,128)(2,1)}, u32[]{:S(2)}, u32[]{:S(2)}) %all-to-all-start) | async-done | bytes 786464 | tf_op jit(solution)/shard_map/all_to_all | solution.py:258
  37.2 3.8 %picked.2 = bf16[64,128,128]{2,1,0:T(8,128)(2,1)} custom-call(s32[64]{0:T(128)} %get-tuple-element.69.offset_ref, bf16[24,128,128]{2,1,0:T(8,128)(2,1)} %bitcast.1.refs_0_), custom_call_target="tpu_custom_call" | custom-call | bytes 2883584 | tf_op jit(solution)/shard_map/picked/pallas_call | solution.py:178
  41.0 4.8 %all-to-all-start.1 = ((bf16[64,128,128]{2,1,0:T(8,128)(2,1)}), bf16[64,128,128]{2,1,0:T(8,128)(2,1)}, u32[]{:S(2)}, u32[]{:S(2)}) async-start(bf16[64,128,128]{2,1,0:T(8,128)(2,1)} %picked.2), calls=%async_computation.1 | async-start | bytes 4194304 | tf_op jit(solution)/shard_map/all_to_all | solution.py:302
  47.7 6.4 %collective-permute-start.1 = (bf16[384,128]{1,0:T(8,128)(2,1)S(1)}, bf16[384,128]{1,0:T(8,128)(2,1)S(1)}, u32[]{:S(2)}, u32[]{:S(2)}) collective-permute-start(bf16[384,128]{1,0:T(8,128)(2,1)S(1)} %get-tuple-element.27), channel_id=1, source_target_pairs={{0,80},{16,96},{32,112},{48,0},{64,16},{80,32},{96,48},{112,64},{1... | collective-permute-start | bytes 294920 | tf_op jit(solution)/shard_map/ppermute | solution.py:198
  62.7 4.6 %collective-permute-start.3 = (bf16[2,384,128]{2,1,0:T(8,128)(2,1)S(1)}, bf16[2,384,128]{2,1,0:T(8,128)(2,1)S(1)}, u32[]{:S(2)}, u32[]{:S(2)}) collective-permute-start(bf16[2,384,128]{2,1,0:T(8,128)(2,1)S(1)} %pad_maximum_fusion.1), channel_id=1, source_target_pairs={{0,112},{16,0},{32,16},{48,32},{64,48},{80,64},{96,80},{112,96},{1... | collective-permute-start | bytes 589832 | tf_op jit(solution)/shard_map/ppermute | solution.py:198
  67.3 4.2 %collective-permute-done.3 = bf16[2,384,128]{2,1,0:T(8,128)(2,1)S(1)} collective-permute-done((bf16[2,384,128]{2,1,0:T(8,128)(2,1)S(1)}, bf16[2,384,128]{2,1,0:T(8,128)(2,1)S(1)}, u32[]{:S(2)}, u32[]{:S(2)}) %collective-permute-start.3) | collective-permute-done | bytes 196640 | tf_op jit(solution)/shard_map/ppermute | solution.py:198
  76.3 5.9 %all-to-all-start.2 = ((bf16[64,128,128]{2,1,0:T(8,128)(2,1)}), bf16[64,128,128]{2,1,0:T(8,128)(2,1)}, u32[]{:S(2)}, u32[]{:S(2)}) async-start(bf16[64,128,128]{2,1,0:T(8,128)(2,1)} %picked.3), calls=%async_computation.2 | async-start | bytes 4194304 | tf_op jit(solution)/shard_map/all_to_all | solution.py:306
  85.2 5.1 %collective-permute-start.4 = (bf16[3,384,128]{2,1,0:T(8,128)(2,1)S(1)}, bf16[3,384,128]{2,1,0:T(8,128)(2,1)S(1)}, u32[]{:S(2)}, u32[]{:S(2)}) collective-permute-start(bf16[3,384,128]{2,1,0:T(8,128)(2,1)S(1)} %bitcast.86), channel_id=1, source_target_pairs={{0,7},{1,0},{2,1},{3,2},{4,3},{5,4},{6,5},{7,6},{8,15},{9,8},{10,9... | collective-permute-start | bytes 884744 | tf_op jit(solution)/shard_map/ppermute | solution.py:198
  92.3 7.5 %collective-permute-done.5 = bf16[2,384,128]{2,1,0:T(8,128)(2,1)S(1)} collective-permute-done((bf16[2,384,128]{2,1,0:T(8,128)(2,1)S(1)}, bf16[2,384,128]{2,1,0:T(8,128)(2,1)S(1)}, u32[]{:S(2)}, u32[]{:S(2)}) %collective-permute-start.5) | collective-permute-done | bytes 196640 | tf_op jit(solution)/shard_map/ppermute | solution.py:198
  100.6 8.0 %all-to-all-done.2.feat_ref = bf16[64,128,128]{2,1,0:T(8,128)(2,1)} async-done(((bf16[64,128,128]{2,1,0:T(8,128)(2,1)}), bf16[64,128,128]{2,1,0:T(8,128)(2,1)}, u32[]{:S(2)}, u32[]{:S(2)}) %all-to-all-start.2) | async-done | bytes 2097184 | tf_op jit(solution)/shard_map/all_to_all | solution.py:306
  108.6 6.7 %collective-permute-start.6 = (bf16[384,128]{1,0:T(8,128)(2,1)}, bf16[384,128]{1,0:T(8,128)(2,1)S(1)}, u32[]{:S(2)}, u32[]{:S(2)}) collective-permute-start(bf16[384,128]{1,0:T(8,128)(2,1)} %get-tuple-element.32), channel_id=1, source_target_pairs={{0,5},{1,6},{2,7},{3,0},{4,1},{5,2},{6,3},{7,4},{8,13},{9,14},{10,... | collective-permute-start | bytes 294920 | tf_op jit(solution)/shard_map/ppermute | solution.py:198
  121.5 7.2 %collective-permute-done.7 = bf16[384,128]{1,0:T(8,128)(2,1)S(1)} collective-permute-done((bf16[384,128]{1,0:T(8,128)(2,1)}, bf16[384,128]{1,0:T(8,128)(2,1)S(1)}, u32[]{:S(2)}, u32[]{:S(2)}) %collective-permute-start.7) | collective-permute-done | bytes 98336 | tf_op jit(solution)/shard_map/ppermute | solution.py:198
  133.8 20.2 %all-to-all-done.3 = bf16[8,384,128]{2,1,0:T(8,128)(2,1)S(1)} async-done(((bf16[8,384,128]{2,1,0:T(8,128)(2,1)}), bf16[8,384,128]{2,1,0:T(8,128)(2,1)S(1)}, u32[]{:S(2)}, u32[]{:S(2)}) %all-to-all-start.3) | async-done | bytes 786464 | tf_op jit(solution)/shard_map/all_to_all | solution.py:313
  159.8 4.4 %collective-permute-start.8 = (f32[256,512]{1,0:T(8,128)}, f32[256,512]{1,0:T(8,128)}, u32[]{:S(2)}, u32[]{:S(2)}) collective-permute-start(f32[256,512]{1,0:T(8,128)} %get-tuple-element.67), channel_id=1, source_target_pairs={{0,8},{8,0},{1,9},{9,1},{2,10},{10,2},{3,11},{11,3},{4,12},{12,4},... | collective-permute-start | bytes 1572872 | tf_op jit(solution)/shard_map/ppermute | solution.py:349
  164.2 4.3 %all-to-all-start.4 = ((bf16[8,384,256]{2,1,0:T(8,128)(2,1)}), bf16[8,384,256]{2,1,0:T(8,128)(2,1)}, u32[]{:S(2)}, u32[]{:S(2)}) async-start(bf16[8,384,256]{2,1,0:T(8,128)(2,1)} %broadcast_in_dim.92), calls=%async_computation.4 | async-start | bytes 3145728 | tf_op jit(solution)/shard_map/all_to_all | solution.py:341
  172.9 7.8 %collective-permute-done.9 = f32[128,512]{1,0:T(8,128)S(1)} collective-permute-done((f32[128,512]{1,0:T(8,128)S(1)}, f32[128,512]{1,0:T(8,128)S(1)}, u32[]{:S(2)}, u32[]{:S(2)}) %collective-permute-start.9) | collective-permute-done | bytes 262176 | tf_op jit(solution)/shard_map/ppermute | solution.py:31
  184.5 5.3 %collective-permute-done.10 = f32[64,512]{1,0:T(8,128)S(1)} collective-permute-done((f32[64,512]{1,0:T(8,128)S(1)}, f32[64,512]{1,0:T(8,128)S(1)}, u32[]{:S(2)}, u32[]{:S(2)}) %collective-permute-start.10) | collective-permute-done | bytes 131104 | tf_op jit(solution)/shard_map/ppermute | solution.py:31
  195.3 4.8 %collective-permute-start.12 = (f32[16,512]{1,0:T(8,128)S(1)}, f32[16,512]{1,0:T(8,128)S(1)}, u32[]{:S(2)}, u32[]{:S(2)}) collective-permute-start(f32[16,512]{1,0:T(8,128)S(1)} %slice_select_fusion.3), channel_id=1, source_target_pairs={{0,32},{16,48},{32,0},{48,16},{64,96},{80,112},{96,64},{112,80},{1... | collective-permute-start | bytes 98312 | tf_op jit(solution)/shard_map/ppermute | solution.py:31
  201.8 5.2 %all-to-all-done.4 = bf16[8,384,256]{2,1,0:T(8,128)(2,1)} async-done(((bf16[8,384,256]{2,1,0:T(8,128)(2,1)}), bf16[8,384,256]{2,1,0:T(8,128)(2,1)}, u32[]{:S(2)}, u32[]{:S(2)}) %all-to-all-start.4) | async-done | bytes 1572896 | tf_op jit(solution)/shard_map/all_to_all | solution.py:341
  212.4 7.0 %all-to-all-start.5 = ((bf16[64,128,256]{2,1,0:T(8,128)(2,1)}), bf16[64,128,256]{2,1,0:T(8,128)(2,1)}, u32[]{:S(2)}, u32[]{:S(2)}) async-start(bf16[64,128,256]{2,1,0:T(8,128)(2,1)} %copy-done.1), calls=%async_computation.5 | async-start | bytes 8388608 | tf_op jit(solution)/shard_map/all_to_all | solution.py:357
  219.4 7.1 %collective-permute-start.13 = (f32[16,512]{1,0:T(8,128)S(1)}, f32[16,512]{1,0:T(8,128)S(1)}, u32[]{:S(2)}, u32[]{:S(2)}) collective-permute-start(f32[16,512]{1,0:T(8,128)S(1)} %select_add_fusion.4), channel_id=1, source_target_pairs={{0,64},{16,80},{32,96},{48,112},{64,0},{80,16},{96,32},{112,48},{1... | collective-permute-start | bytes 98312 | tf_op jit(solution)/shard_map/ppermute | solution.py:31
  240.8 6.7 %collective-permute-done.16 = f32[16,512]{1,0:T(8,128)S(1)} collective-permute-done((f32[16,512]{1,0:T(8,128)S(1)}, f32[16,512]{1,0:T(8,128)S(1)}, u32[]{:S(2)}, u32[]{:S(2)}) %collective-permute-start.16) | collective-permute-done | bytes 32800 | tf_op jit(solution)/shard_map/ppermute | solution.py:31
  253.5 3.9 %collective-permute-start.18 = (f32[32,512]{1,0:T(8,128)S(1)}, f32[32,512]{1,0:T(8,128)S(1)}, u32[]{:S(2)}, u32[]{:S(2)}) collective-permute-start(f32[32,512]{1,0:T(8,128)S(1)} %maximum_select_fusion.3), channel_id=1, source_target_pairs={{0,16},{16,0},{32,48},{48,32},{64,80},{80,64},{96,112},{112,96},{1... | collective-permute-start | bytes 196616 | tf_op jit(solution)/shard_map/ppermute | solution.py:31
  259.5 8.8 %all-to-all-done.5.part_ref = bf16[64,128,256]{2,1,0:T(8,128)(2,1)} async-done(((bf16[64,128,256]{2,1,0:T(8,128)(2,1)}), bf16[64,128,256]{2,1,0:T(8,128)(2,1)}, u32[]{:S(2)}, u32[]{:S(2)}) %all-to-all-start.5) | async-done | bytes 4194336 | tf_op jit(solution)/shard_map/all_to_all | solution.py:357
  268.3 4.5 %summed_into.1 = bf16[24,128,256]{2,1,0:T(8,128)(2,1)} custom-call(s32[64]{0:T(128)S(1)} %copy-done.4, bf16[64,128,256]{2,1,0:T(8,128)(2,1)} %all-to-all-done.5.part_ref), custom_call_target="tpu_custom_call" | custom-call | flops 2097152 | bytes 4194304 | tf_op jit(solution)/shard_map/summed_into/pallas_call | solution.py:129
  272.9 6.6 %all-to-all-start.6 = ((bf16[8,384,256]{2,1,0:T(8,128)(2,1)}), bf16[8,384,256]{2,1,0:T(8,128)(2,1)S(1)}, u32[]{:S(2)}, u32[]{:S(2)}) async-start(bf16[8,384,256]{2,1,0:T(8,128)(2,1)} %bitcast.28), calls=%async_computation.6 | async-start | bytes 3145728 | tf_op jit(solution)/shard_map/all_to_all | solution.py:365
  281.7 5.0 %collective-permute-done.19 = f32[64,512]{1,0:T(8,128)S(1)} collective-permute-done((f32[64,512]{1,0:T(8,128)S(1)}, f32[64,512]{1,0:T(8,128)S(1)}, u32[]{:S(2)}, u32[]{:S(2)}) %collective-permute-start.19) | collective-permute-done | bytes 131104 | tf_op jit(solution)/shard_map/ppermute | solution.py:31
  288.9 5.2 %collective-permute-done.20 = f32[128,512]{1,0:T(8,128)S(1)} collective-permute-done((f32[128,512]{1,0:T(8,128)S(1)}, f32[128,512]{1,0:T(8,128)S(1)}, u32[]{:S(2)}, u32[]{:S(2)}) %collective-permute-start.20) | collective-permute-done | bytes 262176 | tf_op jit(solution)/shard_map/ppermute | solution.py:31
  294.2 5.1 %collective-permute-start.21 = (f32[256,512]{1,0:T(8,128)S(1)}, f32[256,512]{1,0:T(8,128)S(1)}, u32[]{:S(2)}, u32[]{:S(2)}) collective-permute-start(f32[256,512]{1,0:T(8,128)S(1)} %maximum_select_fusion), channel_id=1, source_target_pairs={{0,8},{8,0},{1,9},{9,1},{2,10},{10,2},{3,11},{11,3},{4,12},{12,4},... | collective-permute-start | bytes 1572872 | tf_op jit(solution)/shard_map/ppermute | solution.py:370
  301.9 18.0 %all-to-all-done.6 = bf16[8,384,256]{2,1,0:T(8,128)(2,1)S(1)} async-done(((bf16[8,384,256]{2,1,0:T(8,128)(2,1)}), bf16[8,384,256]{2,1,0:T(8,128)(2,1)S(1)}, u32[]{:S(2)}, u32[]{:S(2)}) %all-to-all-start.6) | async-done | bytes 1572896 | tf_op jit(solution)/shard_map/all_to_all | solution.py:365
  (141 shorter events, 97.8 us)
Async XLA Ops:
  2.7 34.5 %all-to-all-start = ((bf16[8,384,128]{2,1,0:T(8,128)(2,1)}), bf16[8,384,128]{2,1,0:T(8,128)(2,1)}, u32[]{:S(2)}, u32[]{:S(2)}) async-start(bf16[8,384,128]{2,1,0:T(8,128)(2,1)} %broadcast_in_dim.84), calls=%async_computation | async-start | bytes 1572864 | tf_op jit(solution)/shard_map/all_to_all | solution.py:258
  41.0 35.3 %all-to-all-start.1 = ((bf16[64,128,128]{2,1,0:T(8,128)(2,1)}), bf16[64,128,128]{2,1,0:T(8,128)(2,1)}, u32[]{:S(2)}, u32[]{:S(2)}) async-start(bf16[64,128,128]{2,1,0:T(8,128)(2,1)} %picked.2), calls=%async_computation.1 | async-start | bytes 4194304 | tf_op jit(solution)/shard_map/all_to_all | solution.py:302
  45.8 11.2 %collective-permute-start = (bf16[384,128]{1,0:T(8,128)(2,1)S(1)}, bf16[384,128]{1,0:T(8,128)(2,1)S(1)}, u32[]{:S(2)}, u32[]{:S(2)}) collective-permute-start(bf16[384,128]{1,0:T(8,128)(2,1)S(1)} %get-tuple-element.27), channel_id=1, source_target_pairs={{0,48},{16,64},{32,80},{48,96},{64,112},{80,0},{96,16},{112,32},{1... | collective-permute-start | bytes 294920 | tf_op jit(solution)/shard_map/ppermute | solution.py:198
  47.7 12.9 %collective-permute-start.1 = (bf16[384,128]{1,0:T(8,128)(2,1)S(1)}, bf16[384,128]{1,0:T(8,128)(2,1)S(1)}, u32[]{:S(2)}, u32[]{:S(2)}) collective-permute-start(bf16[384,128]{1,0:T(8,128)(2,1)S(1)} %get-tuple-element.27), channel_id=1, source_target_pairs={{0,80},{16,96},{32,112},{48,0},{64,16},{80,32},{96,48},{112,64},{1... | collective-permute-start | bytes 294920 | tf_op jit(solution)/shard_map/ppermute | solution.py:198
  60.7 11.1 %collective-permute-start.2 = (bf16[3,384,128]{2,1,0:T(8,128)(2,1)S(1)}, bf16[3,384,128]{2,1,0:T(8,128)(2,1)S(1)}, u32[]{:S(2)}, u32[]{:S(2)}) collective-permute-start(bf16[3,384,128]{2,1,0:T(8,128)(2,1)S(1)} %pad_maximum_fusion), channel_id=1, source_target_pairs={{0,16},{16,32},{32,48},{48,64},{64,80},{80,96},{96,112},{112,0},{1... | collective-permute-start | bytes 884744 | tf_op jit(solution)/shard_map/ppermute | solution.py:198
  62.7 8.8 %collective-permute-start.3 = (bf16[2,384,128]{2,1,0:T(8,128)(2,1)S(1)}, bf16[2,384,128]{2,1,0:T(8,128)(2,1)S(1)}, u32[]{:S(2)}, u32[]{:S(2)}) collective-permute-start(bf16[2,384,128]{2,1,0:T(8,128)(2,1)S(1)} %pad_maximum_fusion.1), channel_id=1, source_target_pairs={{0,112},{16,0},{32,16},{48,32},{64,48},{80,64},{96,80},{112,96},{1... | collective-permute-start | bytes 589832 | tf_op jit(solution)/shard_map/ppermute | solution.py:198
  76.3 32.3 %all-to-all-start.2 = ((bf16[64,128,128]{2,1,0:T(8,128)(2,1)}), bf16[64,128,128]{2,1,0:T(8,128)(2,1)}, u32[]{:S(2)}, u32[]{:S(2)}) async-start(bf16[64,128,128]{2,1,0:T(8,128)(2,1)} %picked.3), calls=%async_computation.2 | async-start | bytes 4194304 | tf_op jit(solution)/shard_map/all_to_all | solution.py:306
  85.2 14.6 %collective-permute-start.4 = (bf16[3,384,128]{2,1,0:T(8,128)(2,1)S(1)}, bf16[3,384,128]{2,1,0:T(8,128)(2,1)S(1)}, u32[]{:S(2)}, u32[]{:S(2)}) collective-permute-start(bf16[3,384,128]{2,1,0:T(8,128)(2,1)S(1)} %bitcast.86), channel_id=1, source_target_pairs={{0,7},{1,0},{2,1},{3,2},{4,3},{5,4},{6,5},{7,6},{8,15},{9,8},{10,9... | collective-permute-start | bytes 884744 | tf_op jit(solution)/shard_map/ppermute | solution.py:198
  90.3 9.4 %collective-permute-start.5 = (bf16[2,384,128]{2,1,0:T(8,128)(2,1)S(1)}, bf16[2,384,128]{2,1,0:T(8,128)(2,1)S(1)}, u32[]{:S(2)}, u32[]{:S(2)}) collective-permute-start(bf16[2,384,128]{2,1,0:T(8,128)(2,1)S(1)} %bitcast.88), channel_id=1, source_target_pairs={{0,1},{1,2},{2,3},{3,4},{4,5},{5,6},{6,7},{7,0},{8,9},{9,10},{10,1... | collective-permute-start | bytes 589832 | tf_op jit(solution)/shard_map/ppermute | solution.py:198
  108.6 12.9 %collective-permute-start.6 = (bf16[384,128]{1,0:T(8,128)(2,1)}, bf16[384,128]{1,0:T(8,128)(2,1)S(1)}, u32[]{:S(2)}, u32[]{:S(2)}) collective-permute-start(bf16[384,128]{1,0:T(8,128)(2,1)} %get-tuple-element.32), channel_id=1, source_target_pairs={{0,5},{1,6},{2,7},{3,0},{4,1},{5,2},{6,3},{7,4},{8,13},{9,14},{10,... | collective-permute-start | bytes 294920 | tf_op jit(solution)/shard_map/ppermute | solution.py:198
  115.3 13.5 %collective-permute-start.7 = (bf16[384,128]{1,0:T(8,128)(2,1)}, bf16[384,128]{1,0:T(8,128)(2,1)S(1)}, u32[]{:S(2)}, u32[]{:S(2)}) collective-permute-start(bf16[384,128]{1,0:T(8,128)(2,1)} %get-tuple-element.33), channel_id=1, source_target_pairs={{0,3},{1,4},{2,5},{3,6},{4,7},{5,0},{6,1},{7,2},{8,11},{9,12},{10,... | collective-permute-start | bytes 294920 | tf_op jit(solution)/shard_map/ppermute | solution.py:198
  128.8 25.2 %all-to-all-start.3 = ((bf16[8,384,128]{2,1,0:T(8,128)(2,1)}), bf16[8,384,128]{2,1,0:T(8,128)(2,1)S(1)}, u32[]{:S(2)}, u32[]{:S(2)}) async-start(bf16[8,384,128]{2,1,0:T(8,128)(2,1)} %bitcast.79), calls=%async_computation.3 | async-start | bytes 1572864 | tf_op jit(solution)/shard_map/all_to_all | solution.py:313
  159.8 8.7 %collective-permute-start.8 = (f32[256,512]{1,0:T(8,128)}, f32[256,512]{1,0:T(8,128)}, u32[]{:S(2)}, u32[]{:S(2)}) collective-permute-start(f32[256,512]{1,0:T(8,128)} %get-tuple-element.67), channel_id=1, source_target_pairs={{0,8},{8,0},{1,9},{9,1},{2,10},{10,2},{3,11},{11,3},{4,12},{12,4},... | collective-permute-start | bytes 1572872 | tf_op jit(solution)/shard_map/ppermute | solution.py:349
  164.2 42.8 %all-to-all-start.4 = ((bf16[8,384,256]{2,1,0:T(8,128)(2,1)}), bf16[8,384,256]{2,1,0:T(8,128)(2,1)}, u32[]{:S(2)}, u32[]{:S(2)}) async-start(bf16[8,384,256]{2,1,0:T(8,128)(2,1)} %broadcast_in_dim.92), calls=%async_computation.4 | async-start | bytes 3145728 | tf_op jit(solution)/shard_map/all_to_all | solution.py:341
  170.7 10.0 %collective-permute-start.9 = (f32[128,512]{1,0:T(8,128)S(1)}, f32[128,512]{1,0:T(8,128)S(1)}, u32[]{:S(2)}, u32[]{:S(2)}) collective-permute-start(f32[128,512]{1,0:T(8,128)S(1)} %slice_select_fusion), channel_id=1, source_target_pairs={{0,128},{128,0},{256,384},{384,256},{1,129},{129,1},{257,385},{385... | collective-permute-start | bytes 786440 | tf_op jit(solution)/shard_map/ppermute | solution.py:31
  181.8 7.9 %collective-permute-start.10 = (f32[64,512]{1,0:T(8,128)S(1)}, f32[64,512]{1,0:T(8,128)S(1)}, u32[]{:S(2)}, u32[]{:S(2)}) collective-permute-start(f32[64,512]{1,0:T(8,128)S(1)} %slice_select_fusion.1), channel_id=1, source_target_pairs={{0,256},{128,384},{256,0},{384,128},{1,257},{129,385},{257,1},{385... | collective-permute-start | bytes 393224 | tf_op jit(solution)/shard_map/ppermute | solution.py:31
  189.8 5.4 %collective-permute-start.11 = (f32[32,512]{1,0:T(8,128)S(1)}, f32[32,512]{1,0:T(8,128)S(1)}, u32[]{:S(2)}, u32[]{:S(2)}) collective-permute-start(f32[32,512]{1,0:T(8,128)S(1)} %slice_select_fusion.2), channel_id=1, source_target_pairs={{0,16},{16,0},{32,48},{48,32},{64,80},{80,64},{96,112},{112,96},{1... | collective-permute-start | bytes 196616 | tf_op jit(solution)/shard_map/ppermute | solution.py:31
  195.3 6.5 %collective-permute-start.12 = (f32[16,512]{1,0:T(8,128)S(1)}, f32[16,512]{1,0:T(8,128)S(1)}, u32[]{:S(2)}, u32[]{:S(2)}) collective-permute-start(f32[16,512]{1,0:T(8,128)S(1)} %slice_select_fusion.3), channel_id=1, source_target_pairs={{0,32},{16,48},{32,0},{48,16},{64,96},{80,112},{96,64},{112,80},{1... | collective-permute-start | bytes 98312 | tf_op jit(solution)/shard_map/ppermute | solution.py:31
  212.4 55.9 %copy-start.4 = (s32[64]{0:T(128)S(1)}, s32[64]{0:T(128)}, u32[]{:S(2)}) copy-start(s32[64]{0:T(128)} %get-tuple-element.69.offset_ref) | copy-start | bytes 772
  212.4 55.9 %all-to-all-start.5 = ((bf16[64,128,256]{2,1,0:T(8,128)(2,1)}), bf16[64,128,256]{2,1,0:T(8,128)(2,1)}, u32[]{:S(2)}, u32[]{:S(2)}) async-start(bf16[64,128,256]{2,1,0:T(8,128)(2,1)} %copy-done.1), calls=%async_computation.5 | async-start | bytes 8388608 | tf_op jit(solution)/shard_map/all_to_all | solution.py:357
  219.4 8.6 %collective-permute-start.13 = (f32[16,512]{1,0:T(8,128)S(1)}, f32[16,512]{1,0:T(8,128)S(1)}, u32[]{:S(2)}, u32[]{:S(2)}) collective-permute-start(f32[16,512]{1,0:T(8,128)S(1)} %select_add_fusion.4), channel_id=1, source_target_pairs={{0,64},{16,80},{32,96},{48,112},{64,0},{80,16},{96,32},{112,48},{1... | collective-permute-start | bytes 98312 | tf_op jit(solution)/shard_map/ppermute | solution.py:31
  227.9 5.0 %collective-permute-start.14 = (f32[16,512]{1,0:T(8,128)S(1)}, f32[16,512]{1,0:T(8,128)S(1)}, u32[]{:S(2)}, u32[]{:S(2)}) collective-permute-start(f32[16,512]{1,0:T(8,128)S(1)} %add.369), channel_id=1, source_target_pairs={{0,1},{1,0},{2,3},{3,2},{4,5},{5,4},{6,7},{7,6},{8,9},{9,8},{10,11... | collective-permute-start | bytes 98312 | tf_op jit(solution)/shard_map/ppermute | solution.py:31
  233.0 5.9 %collective-permute-start.15 = (f32[16,512]{1,0:T(8,128)S(1)}, f32[16,512]{1,0:T(8,128)S(1)}, u32[]{:S(2)}, u32[]{:S(2)}) collective-permute-start(f32[16,512]{1,0:T(8,128)S(1)} %add.370), channel_id=1, source_target_pairs={{0,2},{1,3},{2,0},{3,1},{4,6},{5,7},{6,4},{7,5},{8,10},{9,11},{10,... | collective-permute-start | bytes 98312 | tf_op jit(solution)/shard_map/ppermute | solution.py:31
  238.9 8.7 %collective-permute-start.16 = (f32[16,512]{1,0:T(8,128)S(1)}, f32[16,512]{1,0:T(8,128)S(1)}, u32[]{:S(2)}, u32[]{:S(2)}) collective-permute-start(f32[16,512]{1,0:T(8,128)S(1)} %add.371), channel_id=1, source_target_pairs={{0,4},{1,5},{2,6},{3,7},{4,0},{5,1},{6,2},{7,3},{8,12},{9,13},{10,... | collective-permute-start | bytes 98312 | tf_op jit(solution)/shard_map/ppermute | solution.py:31
  247.6 6.0 %collective-permute-start.17 = (f32[16,512]{1,0:T(8,128)S(1)}, f32[16,512]{1,0:T(8,128)S(1)}, u32[]{:S(2)}, u32[]{:S(2)}) collective-permute-start(f32[16,512]{1,0:T(8,128)S(1)} %add_multiply_fusion), channel_id=1, source_target_pairs={{0,32},{16,48},{32,0},{48,16},{64,96},{80,112},{96,64},{112,80},{1... | collective-permute-start | bytes 98312 | tf_op jit(solution)/shard_map/ppermute | solution.py:31
  253.5 6.0 %collective-permute-start.18 = (f32[32,512]{1,0:T(8,128)S(1)}, f32[32,512]{1,0:T(8,128)S(1)}, u32[]{:S(2)}, u32[]{:S(2)}) collective-permute-start(f32[32,512]{1,0:T(8,128)S(1)} %maximum_select_fusion.3), channel_id=1, source_target_pairs={{0,16},{16,0},{32,48},{48,32},{64,80},{80,64},{96,112},{112,96},{1... | collective-permute-start | bytes 196616 | tf_op jit(solution)/shard_map/ppermute | solution.py:31
  272.9 47.3 %copy-start.7 = (bf16[384,512]{1,0:T(8,128)(2,1)S(1)}, bf16[384,512]{1,0:T(8,128)(2,1)}, u32[]{:S(2)}) copy-start(bf16[384,512]{1,0:T(8,128)(2,1)} %copy-done.6) | copy-start | bytes 1179652
  272.9 47.3 %copy-start.12 = (bf16[256,512]{1,0:T(8,128)(2,1)S(1)}, bf16[256,512]{1,0:T(8,128)(2,1)}, u32[]{:S(2)}) copy-start(bf16[256,512]{1,0:T(8,128)(2,1)} %param.13) | copy-start | bytes 786436
  272.9 47.1 %all-to-all-start.6 = ((bf16[8,384,256]{2,1,0:T(8,128)(2,1)}), bf16[8,384,256]{2,1,0:T(8,128)(2,1)S(1)}, u32[]{:S(2)}, u32[]{:S(2)}) async-start(bf16[8,384,256]{2,1,0:T(8,128)(2,1)} %bitcast.28), calls=%async_computation.6 | async-start | bytes 3145728 | tf_op jit(solution)/shard_map/all_to_all | solution.py:365
  279.5 7.2 %collective-permute-start.19 = (f32[64,512]{1,0:T(8,128)S(1)}, f32[64,512]{1,0:T(8,128)S(1)}, u32[]{:S(2)}, u32[]{:S(2)}) collective-permute-start(f32[64,512]{1,0:T(8,128)S(1)} %maximum_select_fusion.2), channel_id=1, source_target_pairs={{0,256},{128,384},{256,0},{384,128},{1,257},{129,385},{257,1},{385... | collective-permute-start | bytes 393224 | tf_op jit(solution)/shard_map/ppermute | solution.py:31
  286.7 7.4 %collective-permute-start.20 = (f32[128,512]{1,0:T(8,128)S(1)}, f32[128,512]{1,0:T(8,128)S(1)}, u32[]{:S(2)}, u32[]{:S(2)}) collective-permute-start(f32[128,512]{1,0:T(8,128)S(1)} %maximum_select_fusion.1), channel_id=1, source_target_pairs={{0,128},{128,0},{256,384},{384,256},{1,129},{129,1},{257,385},{385... | collective-permute-start | bytes 786440 | tf_op jit(solution)/shard_map/ppermute | solution.py:31
  294.2 6.6 %collective-permute-start.21 = (f32[256,512]{1,0:T(8,128)S(1)}, f32[256,512]{1,0:T(8,128)S(1)}, u32[]{:S(2)}, u32[]{:S(2)}) collective-permute-start(f32[256,512]{1,0:T(8,128)S(1)} %maximum_select_fusion), channel_id=1, source_target_pairs={{0,8},{8,0},{1,9},{9,1},{2,10},{10,2},{3,11},{11,3},{4,12},{12,4},... | collective-permute-start | bytes 1572872 | tf_op jit(solution)/shard_map/ppermute | solution.py:370
  (13 other events, 187.2 us)

commit v6 on v5

--- a/solution.py
+++ b/solution.py
@@ -12,7 +12,6 @@
 DOM = ("x", "z", "core")
 ALL = ("x", "z", "core", "rep")
 STEP = 32
-LIMIT = pltpu.CompilerParams(vmem_limit_bytes=40 << 20)
 
 
 def edge_masks(row_ids, col_ids, limits, swapped):
@@ -69,7 +68,7 @@
             bytes_accessed=slots * tile * (tile + width) * 2,
             transcendentals=0,
         ),
-        compiler_params=LIMIT,
+        compiler_params=pltpu.CompilerParams(vmem_limit_bytes=40 << 20),
         name="tile_sums",
     )(offsets, masks, feats)
 
@@ -84,9 +83,10 @@
         ).astype(out_ref.dtype)
 
 
-def tile_products(offsets, masks, blocks):
+def tile_products(offsets, masks, blocks, half):
     slots, tile, _ = masks.shape
     n, _, width = blocks.shape
+    width = width // 2
     return pl.pallas_call(
         products_kernel,
         grid_spec=pltpu.PrefetchScalarGridSpec(
@@ -94,7 +94,7 @@
             grid=(slots // STEP,),
             in_specs=[
                 pl.BlockSpec((STEP, tile, tile), lambda i, o: (i, 0, 0)),
-                pl.BlockSpec((n, tile, width), lambda i, o: (0, 0, 0)),
+                pl.BlockSpec((n, tile, width), lambda i, o: (0, 0, half)),
             ],
             out_specs=pl.BlockSpec((STEP, tile, width), lambda i, o: (i, 0, 0)),
         ),
@@ -104,7 +104,7 @@
             bytes_accessed=slots * tile * (tile + width) * 2,
             transcendentals=0,
         ),
-        compiler_params=LIMIT,
+        compiler_params=pltpu.CompilerParams(vmem_limit_bytes=60 << 20),
         name="tile_products",
     )(offsets, masks, blocks)
 
@@ -139,7 +139,7 @@
         cost_estimate=pl.CostEstimate(
             flops=slots * tile * width, bytes_accessed=slots * tile * width * 2, transcendentals=0
         ),
-        compiler_params=LIMIT,
+        compiler_params=pltpu.CompilerParams(vmem_limit_bytes=40 << 20),
         name="summed_into",
     )(offsets, parts)
 
@@ -217,13 +217,7 @@
     low = x[0].astype(jnp.float32) + above[0] + below[0]
     own = x[1].astype(jnp.float32) + above[1] + below[1]
     high = x[2].astype(jnp.float32) + above[2]
-    return own, low.astype(x.dtype), high.astype(x.dtype)
-
-
-def sum_of_eight_ended(own, low, high, axis):
-    low = shifted(low, axis, -3).astype(jnp.float32)
-    high = shifted(high, axis, 3).astype(jnp.float32)
-    return own + low + high
+    return own, shifted(low.astype(x.dtype), axis, -3), shifted(high.astype(x.dtype), axis, 3)
 
 
 def halved(x, axis, bit):
@@ -305,11 +299,10 @@
     arrived_1, leaving_2 = lax.optimization_barrier((arrived_1, leaving_2))
     arrived_2 = lax.all_to_all(leaving_2, ("x", "core"), 0, 0, tiled=True)
     sums_1 = tile_sums(held_near, masks, arrived_1, group_blocks)
-    begun_1 = sum_of_eight(sums_1.reshape(rep_total, rows_here, half_in), "rep")
-    arrived_2, begun_1 = lax.optimization_barrier((arrived_2, begun_1))
-    summed_1 = sum_of_eight_ended(*begun_1, "rep")
+    own_1, low_1, high_1 = sum_of_eight(sums_1.reshape(rep_total, rows_here, half_in), "rep")
+    arrived_2, low_1, high_1 = lax.optimization_barrier((arrived_2, low_1, high_1))
+    summed_1 = own_1 + low_1.astype(jnp.float32) + high_1.astype(jnp.float32)
     sums_2 = tile_sums(held_offset, masks, arrived_2, group_blocks)
-    sums_2, summed_1 = lax.optimization_barrier((sums_2, summed_1))
     pieces = lax.all_to_all(
         sums_2.reshape(rep_total, rows_here, half_in), "rep", 0, 0, tiled=True
     )
@@ -349,22 +342,28 @@
     share = jnp.where(first, self_term, neigh_term) + lax.ppermute(
         jnp.where(first, neigh_term, self_term), "core", [(0, 1), (1, 0)]
     )
-    for axis, bit in (("x", 1), ("x", 2), ("z", 1), ("z", 2)):
+    for axis, bit in (("x", 1), ("x", 2), ("z", 1)):
         share = halved(share, axis, bit)
-
-    returning = tile_products(held_offset, masks_swapped, group_spread)
-    returning, share = lax.optimization_barrier((returning, share))
-    returned = lax.all_to_all(returning, ("x", "core"), 0, 0, tiled=True)
+    share = share + pair_swap(share, "z", 2)
+
+    returning_1 = tile_products(held_offset, masks_swapped, group_spread, 0)
+    returning_1, group_spread, share = lax.optimization_barrier((returning_1, group_spread, share))
+    returned_1 = lax.all_to_all(returning_1, ("x", "core"), 0, 0, tiled=True)
+    returning_2 = tile_products(held_offset, masks_swapped, group_spread, 1)
     for axis, bit in (("z", 4), ("rep", 1), ("rep", 2), ("rep", 4)):
         share = share + pair_swap(share, axis, bit)
     share = share * (1.0 / math.sqrt(rows_here * dom_total * rep_total))
-    for bit in (2, 1):
-        share = doubled(share, "z", bit)
-    column_sums = summed_into(passed_offset, returned, z_total * blocks_here)
-    column_sums, share = lax.optimization_barrier((column_sums, share))
-    parts = lax.all_to_all(
-        column_sums.reshape(z_total, rows_here, width_in), "z", 0, 0, tiled=True
-    )
+    share = doubled(share, "z", 1)
+
+    returned_1, returning_2, share = lax.optimization_barrier((returned_1, returning_2, share))
+    returned_2 = lax.all_to_all(returning_2, ("x", "core"), 0, 0, tiled=True)
+    column_1 = summed_into(passed_near, returned_1, z_total * blocks_here)
+    own_1, low_1, high_1 = sum_of_eight(column_1.reshape(z_total, rows_here, half_in), "z")
+    returned_2, low_1, high_1 = lax.optimization_barrier((returned_2, low_1, high_1))
+    column_2 = summed_into(passed_offset, returned_2, z_total * blocks_here)
+
+    column_2, share = lax.optimization_barrier((column_2, share))
+    parts = lax.all_to_all(column_2.reshape(z_total, rows_here, half_in), "z", 0, 0, tiled=True)
     for bit in (2, 1):
         share = doubled(share, "x", bit)
     other = lax.ppermute(share, "core", [(0, 1), (1, 0)])
@@ -374,7 +373,13 @@
     self_back = lax.dot_general(
         pre_grad, self_weight, over_cols, preferred_element_type=jnp.float32
     )
-    transposed = parts.astype(jnp.float32).sum(axis=0)
+    transposed = jnp.concatenate(
+        [
+            own_1 + low_1.astype(jnp.float32) + high_1.astype(jnp.float32),
+            parts.astype(jnp.float32).sum(axis=0),
+        ],
+        axis=1,
+    )
     feat_grad = (self_back + transposed).astype(jnp.bfloat16)
     return (hidden_out, feat_grad, self_grad, neigh_grad)
 

time: 323 us -> 324 us (level)
  waiting for transfers between devices: 142 us -> 97.6 us
  starting transfers between devices: 120 us -> 155 us
  Pallas kernels: 21.4 us -> 26 us
    all_to_all x2 -> x3, waiting for transfers between devices: 26.8 us -> 8.23 us  [the longest x1 8.21 us: shards(): lax.all_to_all(column_2.reshape(z_total, rows_here, half_in), 'z', 0, 0,...]
    ppermute x12 -> x11, waiting for transfers between devices: 47.3 us -> 29.5 us  [pair_swap(): return lax.ppermute(x, axis, [(i, i ^ bit) for i in range(n)])]
    ppermute x8 -> x12, starting transfers between devices: 30.4 us -> 42.5 us  [shifted(): return lax.ppermute(x, axis, [(i, (i + by) % n) for i in range(n)])]
    all_to_all x2 -> x3, starting transfers between devices: 13.6 us -> 24.7 us  [the longest x1 8.98 us: shards(): lax.all_to_all(column_2.reshape(z_total, rows_here, half_in), 'z', 0, 0,...]
    ppermute x12 -> x11, starting transfers between devices: 37.2 us -> 46 us  [pair_swap(): return lax.ppermute(x, axis, [(i, i ^ bit) for i in range(n)])]
    ppermute x8 -> x12, waiting for transfers between devices: 26.2 us -> 34.2 us  [shifted(): return lax.ppermute(x, axis, [(i, (i + by) % n) for i in range(n)])]
    all_to_all x1, waiting for transfers between devices: 8 us -> 0.01 us  [shards(): arrived_2 = lax.all_to_all(leaving_2, ('x', 'core'), 0, 0, tiled=True)]
    all_to_all x1, waiting for transfers between devices: 5.18 us -> 0.01 us  [shards(): group_spread = lax.all_to_all(spread, 'rep', 0, 0, tiled=True)]
  transfers between devices with their start and end apart: 29 -> 33, of which waited for: 26 -> 22; matrix products, arithmetic and copies ran while one was open for 7% -> 9% of each run, Pallas kernels for 3% -> 4%
where the time goes in v6:
time: 324 us; the launch traced here: 322 us
  starting transfers between devices  155 us (48%)
  waiting for transfers between devices  97.6 us (30%)
  Pallas kernels  26 us (8%)
  other arithmetic  18.7 us (6%)
  local copies, waits for them, and re-layouts  15.8 us (5%)
  matrix products  7.58 us (2%)
    ppermute x11, starting transfers between devices, pair_swap(): return lax.ppermute(x, axis, [(i, i ^ bit) for i in range(n)])  46 us
    ppermute x12, starting transfers between devices, shifted(): return lax.ppermute(x, axis, [(i, (i + by) % n) for i in range(n)])  42.5 us
    ppermute x12, waiting for transfers between devices, shifted(): return lax.ppermute(x, axis, [(i, (i + by) % n) for i in range(n)])  34.2 us
    ppermute x11, waiting for transfers between devices, pair_swap(): return lax.ppermute(x, axis, [(i, i ^ bit) for i in range(n)])  29.5 us
    all_to_all x1, waiting for transfers between devices, shards(): lax.all_to_all(sums_2.reshape(rep_total, rows_here, half_in), 'rep', 0, 0...  17 us
    all_to_all x1, starting transfers between devices, shards(): lax.all_to_all(jnp.broadcast_to(node_feats[None, :, :half_in], (z_total,...  10.9 us
    convert_element_type x1, other arithmetic, edge_masks(): return (hashed < limits[:, None, None]).astype(jnp.bfloat16)  10.8 us
    all_to_all x1, starting transfers between devices, shards(): lax.all_to_all(column_2.reshape(z_total, rows_here, half_in), 'z', 0, 0,...  8.98 us
  transfers between devices with their start and end apart: 33, of which 22 were waited for; matrix products, arithmetic and copies ran while one was open for 9% of the time, Pallas kernels for 4%

profile of v6, /device:TPU:1, one launch (start us, length us, event | category | flops | bytes accessed | tf_op | source)
XLA Modules:
  0.0 321.8 jit_solution(5274547909327598801)
XLA Ops:
  2.7 10.9 %all-to-all-start = ((bf16[8,384,128]{2,1,0:T(8,128)(2,1)}), bf16[8,384,128]{2,1,0:T(8,128)(2,1)}, u32[]{:S(2)}, u32[]{:S(2)}) async-start(bf16[8,384,128]{2,1,0:T(8,128)(2,1)} %broadcast_in_dim.89), calls=%async_computation | async-start | bytes 1572864 | tf_op jit(solution)/shard_map/all_to_all | solution.py:252
  20.1 10.8 %fusion.10 = (bf16[64,128,128]{2,1,0:T(8,128)(2,1)}, bf16[64,128,128]{2,1,0:T(8,128)(2,1)S(1)}) fusion(s32[64,128]{1,0:T(8,128)S(1)} %get-tuple-element.73, s32[64,128]{1,0:T(8,128)S(1)} %get-tuple-element.72, s32[64,128]{1,0:T(8,128)S(1)} %add_select_fusion.5, s32[64]{0:T(128)S(1)} %get-tuple-element.78), kind=kLoop, calls=%fused_computation.22 | loop fusion | flops 46137344 | bytes 4292864 | tf_op jit(solution)/shard_map/convert_element_type | solution.py:25
  31.0 6.3 %all-to-all-done = bf16[8,384,128]{2,1,0:T(8,128)(2,1)} async-done(((bf16[8,384,128]{2,1,0:T(8,128)(2,1)}), bf16[8,384,128]{2,1,0:T(8,128)(2,1)}, u32[]{:S(2)}, u32[]{:S(2)}) %all-to-all-start) | async-done | bytes 786464 | tf_op jit(solution)/shard_map/all_to_all | solution.py:252
  41.0 4.8 %all-to-all-start.1 = ((bf16[64,128,128]{2,1,0:T(8,128)(2,1)}), bf16[64,128,128]{2,1,0:T(8,128)(2,1)}, u32[]{:S(2)}, u32[]{:S(2)}) async-start(bf16[64,128,128]{2,1,0:T(8,128)(2,1)} %picked.2), calls=%async_computation.1 | async-start | bytes 4194304 | tf_op jit(solution)/shard_map/all_to_all | solution.py:296
  47.9 5.0 %collective-permute-start = (bf16[384,128]{1,0:T(8,128)(2,1)S(1)}, bf16[384,128]{1,0:T(8,128)(2,1)S(1)}, u32[]{:S(2)}, u32[]{:S(2)}) collective-permute-start(bf16[384,128]{1,0:T(8,128)(2,1)S(1)} %get-tuple-element.31), channel_id=1, source_target_pairs={{0,48},{16,64},{32,80},{48,96},{64,112},{80,0},{96,16},{112,32},{1... | collective-permute-start | bytes 294920 | tf_op jit(solution)/shard_map/ppermute | solution.py:198
  55.2 5.6 %collective-permute-done = bf16[384,128]{1,0:T(8,128)(2,1)S(1)} collective-permute-done((bf16[384,128]{1,0:T(8,128)(2,1)S(1)}, bf16[384,128]{1,0:T(8,128)(2,1)S(1)}, u32[]{:S(2)}, u32[]{:S(2)}) %collective-permute-start) | collective-permute-done | bytes 98336 | tf_op jit(solution)/shard_map/ppermute | solution.py:198
  67.4 4.8 %collective-permute-done.3 = bf16[2,384,128]{2,1,0:T(8,128)(2,1)S(1)} collective-permute-done((bf16[2,384,128]{2,1,0:T(8,128)(2,1)S(1)}, bf16[2,384,128]{2,1,0:T(8,128)(2,1)S(1)}, u32[]{:S(2)}, u32[]{:S(2)}) %collective-permute-start.3) | collective-permute-done | bytes 196640 | tf_op jit(solution)/shard_map/ppermute | solution.py:198
  76.7 5.9 %all-to-all-start.2 = ((bf16[64,128,128]{2,1,0:T(8,128)(2,1)}), bf16[64,128,128]{2,1,0:T(8,128)(2,1)}, u32[]{:S(2)}, u32[]{:S(2)}) async-start(bf16[64,128,128]{2,1,0:T(8,128)(2,1)} %picked.3), calls=%async_computation.2 | async-start | bytes 4194304 | tf_op jit(solution)/shard_map/all_to_all | solution.py:300
  85.7 5.1 %collective-permute-start.4 = (bf16[3,384,128]{2,1,0:T(8,128)(2,1)S(1)}, bf16[3,384,128]{2,1,0:T(8,128)(2,1)S(1)}, u32[]{:S(2)}, u32[]{:S(2)}) collective-permute-start(bf16[3,384,128]{2,1,0:T(8,128)(2,1)S(1)} %bitcast.135), channel_id=1, source_target_pairs={{0,7},{1,0},{2,1},{3,2},{4,3},{5,4},{6,5},{7,6},{8,15},{9,8},{10,9... | collective-permute-start | bytes 884744 | tf_op jit(solution)/shard_map/ppermute | solution.py:198
  93.4 6.8 %collective-permute-done.5 = bf16[2,384,128]{2,1,0:T(8,128)(2,1)S(1)} collective-permute-done((bf16[2,384,128]{2,1,0:T(8,128)(2,1)S(1)}, bf16[2,384,128]{2,1,0:T(8,128)(2,1)S(1)}, u32[]{:S(2)}, u32[]{:S(2)}) %collective-permute-start.5) | collective-permute-done | bytes 196640 | tf_op jit(solution)/shard_map/ppermute | solution.py:198
  103.0 6.4 %collective-permute-start.6 = (bf16[384,128]{1,0:T(8,128)(2,1)S(1)}, bf16[384,128]{1,0:T(8,128)(2,1)}, u32[]{:S(2)}, u32[]{:S(2)}) collective-permute-start(bf16[384,128]{1,0:T(8,128)(2,1)S(1)} %get-tuple-element.67), channel_id=1, source_target_pairs={{0,5},{1,6},{2,7},{3,0},{4,1},{5,2},{6,3},{7,4},{8,13},{9,14},{10,... | collective-permute-start | bytes 294920 | tf_op jit(solution)/shard_map/ppermute | solution.py:198
  116.7 7.1 %all-to-all-start.3 = ((bf16[8,384,128]{2,1,0:T(8,128)(2,1)}), bf16[8,384,128]{2,1,0:T(8,128)(2,1)S(1)}, u32[]{:S(2)}, u32[]{:S(2)}) async-start(bf16[8,384,128]{2,1,0:T(8,128)(2,1)} %bitcast.126), calls=%async_computation.3 | async-start | bytes 1572864 | tf_op jit(solution)/shard_map/all_to_all | solution.py:306
  128.0 17.0 %all-to-all-done.3 = bf16[8,384,128]{2,1,0:T(8,128)(2,1)S(1)} async-done(((bf16[8,384,128]{2,1,0:T(8,128)(2,1)}), bf16[8,384,128]{2,1,0:T(8,128)(2,1)S(1)}, u32[]{:S(2)}, u32[]{:S(2)}) %all-to-all-start.3) | async-done | bytes 786464 | tf_op jit(solution)/shard_map/all_to_all | solution.py:306
  156.3 4.8 %collective-permute-start.8 = (f32[256,512]{1,0:T(8,128)}, f32[256,512]{1,0:T(8,128)S(1)}, u32[]{:S(2)}, u32[]{:S(2)}) collective-permute-start(f32[256,512]{1,0:T(8,128)} %get-tuple-element.79), channel_id=1, source_target_pairs={{0,8},{8,0},{1,9},{9,1},{2,10},{10,2},{3,11},{11,3},{4,12},{12,4},... | collective-permute-start | bytes 1572872 | tf_op jit(solution)/shard_map/ppermute | solution.py:342
  168.0 6.7 %collective-permute-done.9 = f32[128,512]{1,0:T(8,128)S(1)} collective-permute-done((f32[128,512]{1,0:T(8,128)S(1)}, f32[128,512]{1,0:T(8,128)S(1)}, u32[]{:S(2)}, u32[]{:S(2)}) %collective-permute-start.9) | collective-permute-done | bytes 262176 | tf_op jit(solution)/shard_map/ppermute | solution.py:30
  174.8 4.4 %collective-permute-start.10 = (f32[64,512]{1,0:T(8,128)S(1)}, f32[64,512]{1,0:T(8,128)S(1)}, u32[]{:S(2)}, u32[]{:S(2)}) collective-permute-start(f32[64,512]{1,0:T(8,128)S(1)} %slice_select_fusion.1), channel_id=1, source_target_pairs={{0,256},{128,384},{256,0},{384,128},{1,257},{129,385},{257,1},{385... | collective-permute-start | bytes 393224 | tf_op jit(solution)/shard_map/ppermute | solution.py:30
  187.5 4.9 %collective-permute-start.12 = (f32[32,512]{1,0:T(8,128)S(1)}, f32[32,512]{1,0:T(8,128)S(1)}, u32[]{:S(2)}, u32[]{:S(2)}) collective-permute-start(f32[32,512]{1,0:T(8,128)S(1)} %select_add_fusion.3), channel_id=1, source_target_pairs={{0,32},{16,48},{32,0},{48,16},{64,96},{80,112},{96,64},{112,80},{1... | collective-permute-start | bytes 196616 | tf_op jit(solution)/shard_map/ppermute | solution.py:30
  195.4 4.0 %tile_products.2 = bf16[64,128,128]{2,1,0:T(8,128)(2,1)} custom-call(s32[64]{0:T(128)} %copy-done.2, bf16[64,128,128]{2,1,0:T(8,128)(2,1)} %get-tuple-element.37.mask_ref, bf16[24,128,256]{2,1,0:T(8,128)(2,1)} %bitcast.127), custom_call_target="tpu_custom_call" | custom-call | flops 268435456 | bytes 4194304 | tf_op jit(solution)/shard_map/tile_products/pallas_call | solution.py:90
  199.4 7.4 %all-to-all-start.5 = ((bf16[64,128,128]{2,1,0:T(8,128)(2,1)}), bf16[64,128,128]{2,1,0:T(8,128)(2,1)S(1)}, u32[]{:S(2)}, u32[]{:S(2)}) async-start(bf16[64,128,128]{2,1,0:T(8,128)(2,1)} %tile_products.2), calls=%async_computation.5 | async-start | bytes 4194304 | tf_op jit(solution)/shard_map/all_to_all | solution.py:351
  206.8 6.0 %collective-permute-start.13 = (f32[32,512]{1,0:T(8,128)S(1)}, f32[32,512]{1,0:T(8,128)S(1)}, u32[]{:S(2)}, u32[]{:S(2)}) collective-permute-start(f32[32,512]{1,0:T(8,128)S(1)} %add.389), channel_id=1, source_target_pairs={{0,64},{16,80},{32,96},{48,112},{64,0},{80,16},{96,32},{112,48},{1... | collective-permute-start | bytes 196616 | tf_op jit(solution)/shard_map/ppermute | solution.py:30
  221.8 4.3 %collective-permute-start.15 = (f32[32,512]{1,0:T(8,128)S(1)}, f32[32,512]{1,0:T(8,128)S(1)}, u32[]{:S(2)}, u32[]{:S(2)}) collective-permute-start(f32[32,512]{1,0:T(8,128)S(1)} %add.391), channel_id=1, source_target_pairs={{0,2},{1,3},{2,0},{3,1},{4,6},{5,7},{6,4},{7,5},{8,10},{9,11},{10,... | collective-permute-start | bytes 196616 | tf_op jit(solution)/shard_map/ppermute | solution.py:30
  227.8 8.3 %collective-permute-start.16 = (f32[32,512]{1,0:T(8,128)S(1)}, f32[32,512]{1,0:T(8,128)S(1)}, u32[]{:S(2)}, u32[]{:S(2)}) collective-permute-start(f32[32,512]{1,0:T(8,128)S(1)} %add.392), channel_id=1, source_target_pairs={{0,4},{1,5},{2,6},{3,7},{4,0},{5,1},{6,2},{7,3},{8,12},{9,13},{10,... | collective-permute-start | bytes 196616 | tf_op jit(solution)/shard_map/ppermute | solution.py:30
  241.4 4.0 %tile_products.3 = bf16[64,128,128]{2,1,0:T(8,128)(2,1)} custom-call(s32[64]{0:T(128)} %copy-done.2, bf16[64,128,128]{2,1,0:T(8,128)(2,1)} %get-tuple-element.37.mask_ref, bf16[24,128,256]{2,1,0:T(8,128)(2,1)} %bitcast.128), custom_call_target="tpu_custom_call" | custom-call | flops 268435456 | bytes 4194304 | tf_op jit(solution)/shard_map/tile_products/pallas_call | solution.py:90
  245.4 8.3 %all-to-all-start.6 = ((bf16[64,128,128]{2,1,0:T(8,128)(2,1)}), bf16[64,128,128]{2,1,0:T(8,128)(2,1)}, u32[]{:S(2)}, u32[]{:S(2)}) async-start(bf16[64,128,128]{2,1,0:T(8,128)(2,1)} %tile_products.3), calls=%async_computation.6 | async-start | bytes 4194304 | tf_op jit(solution)/shard_map/all_to_all | solution.py:359
  260.5 6.3 %collective-permute-done.19 = bf16[2,384,128]{2,1,0:T(8,128)(2,1)S(1)} collective-permute-done((bf16[2,384,128]{2,1,0:T(8,128)(2,1)S(1)}, bf16[2,384,128]{2,1,0:T(8,128)(2,1)S(1)}, u32[]{:S(2)}, u32[]{:S(2)}) %collective-permute-start.19) | collective-permute-done | bytes 196640 | tf_op jit(solution)/shard_map/ppermute | solution.py:198
  267.0 5.6 %collective-permute-start.21 = (bf16[384,128]{1,0:T(8,128)(2,1)S(1)}, bf16[384,128]{1,0:T(8,128)(2,1)S(1)}, u32[]{:S(2)}, u32[]{:S(2)}) collective-permute-start(bf16[384,128]{1,0:T(8,128)(2,1)S(1)} %get-tuple-element.64), channel_id=1, source_target_pairs={{0,48},{16,64},{32,80},{48,96},{64,112},{80,0},{96,16},{112,32},{1... | collective-permute-start | bytes 294920 | tf_op jit(solution)/shard_map/ppermute | solution.py:198
  275.4 4.7 %collective-permute-done.20 = bf16[384,128]{1,0:T(8,128)(2,1)S(1)} collective-permute-done((bf16[384,128]{1,0:T(8,128)(2,1)S(1)}, bf16[384,128]{1,0:T(8,128)(2,1)S(1)}, u32[]{:S(2)}, u32[]{:S(2)}) %collective-permute-start.20) | collective-permute-done | bytes 98336 | tf_op jit(solution)/shard_map/ppermute | solution.py:198
  284.1 4.0 %collective-permute-start.22 = (f32[64,512]{1,0:T(8,128)S(1)}, f32[64,512]{1,0:T(8,128)S(1)}, u32[]{:S(2)}, u32[]{:S(2)}) collective-permute-start(f32[64,512]{1,0:T(8,128)S(1)} %maximum_select_fusion.2), channel_id=1, source_target_pairs={{0,256},{128,384},{256,0},{384,128},{1,257},{129,385},{257,1},{385... | collective-permute-start | bytes 393224 | tf_op jit(solution)/shard_map/ppermute | solution.py:30
  288.1 9.0 %all-to-all-start.7 = ((bf16[8,384,128]{2,1,0:T(8,128)(2,1)}), bf16[8,384,128]{2,1,0:T(8,128)(2,1)S(1)}, u32[]{:S(2)}, u32[]{:S(2)}) async-start(bf16[8,384,128]{2,1,0:T(8,128)(2,1)} %bitcast.38), calls=%async_computation.7 | async-start | bytes 1572864 | tf_op jit(solution)/shard_map/all_to_all | solution.py:366
  299.2 6.1 %collective-permute-done.23 = f32[128,512]{1,0:T(8,128)S(1)} collective-permute-done((f32[128,512]{1,0:T(8,128)S(1)}, f32[128,512]{1,0:T(8,128)S(1)}, u32[]{:S(2)}, u32[]{:S(2)}) %collective-permute-start.23) | collective-permute-done | bytes 262176 | tf_op jit(solution)/shard_map/ppermute | solution.py:30
  305.4 4.5 %collective-permute-start.24 = (f32[256,512]{1,0:T(8,128)S(1)}, f32[256,512]{1,0:T(8,128)S(1)}, u32[]{:S(2)}, u32[]{:S(2)}) collective-permute-start(f32[256,512]{1,0:T(8,128)S(1)} %maximum_select_fusion), channel_id=1, source_target_pairs={{0,8},{8,0},{1,9},{9,1},{2,10},{10,2},{3,11},{11,3},{4,12},{12,4},... | collective-permute-start | bytes 1572872 | tf_op jit(solution)/shard_map/ppermute | solution.py:369
  312.5 8.2 %all-to-all-done.7 = bf16[8,384,128]{2,1,0:T(8,128)(2,1)S(1)} async-done(((bf16[8,384,128]{2,1,0:T(8,128)(2,1)}), bf16[8,384,128]{2,1,0:T(8,128)(2,1)S(1)}, u32[]{:S(2)}, u32[]{:S(2)}) %all-to-all-start.7) | async-done | bytes 786464 | tf_op jit(solution)/shard_map/all_to_all | solution.py:366
  (166 shorter events, 112.4 us)
Async XLA Ops:
  2.7 34.5 %all-to-all-start = ((bf16[8,384,128]{2,1,0:T(8,128)(2,1)}), bf16[8,384,128]{2,1,0:T(8,128)(2,1)}, u32[]{:S(2)}, u32[]{:S(2)}) async-start(bf16[8,384,128]{2,1,0:T(8,128)(2,1)} %broadcast_in_dim.89), calls=%async_computation | async-start | bytes 1572864 | tf_op jit(solution)/shard_map/all_to_all | solution.py:252
  41.0 35.7 %all-to-all-start.1 = ((bf16[64,128,128]{2,1,0:T(8,128)(2,1)}), bf16[64,128,128]{2,1,0:T(8,128)(2,1)}, u32[]{:S(2)}, u32[]{:S(2)}) async-start(bf16[64,128,128]{2,1,0:T(8,128)(2,1)} %picked.2), calls=%async_computation.1 | async-start | bytes 4194304 | tf_op jit(solution)/shard_map/all_to_all | solution.py:296
  45.8 9.5 %collective-permute-start.1 = (bf16[384,128]{1,0:T(8,128)(2,1)S(1)}, bf16[384,128]{1,0:T(8,128)(2,1)S(1)}, u32[]{:S(2)}, u32[]{:S(2)}) collective-permute-start(bf16[384,128]{1,0:T(8,128)(2,1)S(1)} %get-tuple-element.31), channel_id=1, source_target_pairs={{0,80},{16,96},{32,112},{48,0},{64,16},{80,32},{96,48},{112,64},{1... | collective-permute-start | bytes 294920 | tf_op jit(solution)/shard_map/ppermute | solution.py:198
  47.9 12.9 %collective-permute-start = (bf16[384,128]{1,0:T(8,128)(2,1)S(1)}, bf16[384,128]{1,0:T(8,128)(2,1)S(1)}, u32[]{:S(2)}, u32[]{:S(2)}) collective-permute-start(bf16[384,128]{1,0:T(8,128)(2,1)S(1)} %get-tuple-element.31), channel_id=1, source_target_pairs={{0,48},{16,64},{32,80},{48,96},{64,112},{80,0},{96,16},{112,32},{1... | collective-permute-start | bytes 294920 | tf_op jit(solution)/shard_map/ppermute | solution.py:198
  60.9 11.3 %collective-permute-start.2 = (bf16[3,384,128]{2,1,0:T(8,128)(2,1)S(1)}, bf16[3,384,128]{2,1,0:T(8,128)(2,1)S(1)}, u32[]{:S(2)}, u32[]{:S(2)}) collective-permute-start(bf16[3,384,128]{2,1,0:T(8,128)(2,1)S(1)} %pad_maximum_fusion), channel_id=1, source_target_pairs={{0,16},{16,32},{32,48},{48,64},{64,80},{80,96},{96,112},{112,0},{1... | collective-permute-start | bytes 884744 | tf_op jit(solution)/shard_map/ppermute | solution.py:198
  64.5 7.7 %collective-permute-start.3 = (bf16[2,384,128]{2,1,0:T(8,128)(2,1)S(1)}, bf16[2,384,128]{2,1,0:T(8,128)(2,1)S(1)}, u32[]{:S(2)}, u32[]{:S(2)}) collective-permute-start(bf16[2,384,128]{2,1,0:T(8,128)(2,1)S(1)} %pad_maximum_fusion.1), channel_id=1, source_target_pairs={{0,112},{16,0},{32,16},{48,32},{64,48},{80,64},{96,80},{112,96},{1... | collective-permute-start | bytes 589832 | tf_op jit(solution)/shard_map/ppermute | solution.py:198
  76.7 36.1 %all-to-all-start.2 = ((bf16[64,128,128]{2,1,0:T(8,128)(2,1)}), bf16[64,128,128]{2,1,0:T(8,128)(2,1)}, u32[]{:S(2)}, u32[]{:S(2)}) async-start(bf16[64,128,128]{2,1,0:T(8,128)(2,1)} %picked.3), calls=%async_computation.2 | async-start | bytes 4194304 | tf_op jit(solution)/shard_map/all_to_all | solution.py:300
  85.7 14.6 %collective-permute-start.4 = (bf16[3,384,128]{2,1,0:T(8,128)(2,1)S(1)}, bf16[3,384,128]{2,1,0:T(8,128)(2,1)S(1)}, u32[]{:S(2)}, u32[]{:S(2)}) collective-permute-start(bf16[3,384,128]{2,1,0:T(8,128)(2,1)S(1)} %bitcast.135), channel_id=1, source_target_pairs={{0,7},{1,0},{2,1},{3,2},{4,3},{5,4},{6,5},{7,6},{8,15},{9,8},{10,9... | collective-permute-start | bytes 884744 | tf_op jit(solution)/shard_map/ppermute | solution.py:198
  90.8 9.4 %collective-permute-start.5 = (bf16[2,384,128]{2,1,0:T(8,128)(2,1)S(1)}, bf16[2,384,128]{2,1,0:T(8,128)(2,1)S(1)}, u32[]{:S(2)}, u32[]{:S(2)}) collective-permute-start(bf16[2,384,128]{2,1,0:T(8,128)(2,1)S(1)} %bitcast.138), channel_id=1, source_target_pairs={{0,1},{1,2},{2,3},{3,4},{4,5},{5,6},{6,7},{7,0},{8,9},{9,10},{10,1... | collective-permute-start | bytes 589832 | tf_op jit(solution)/shard_map/ppermute | solution.py:198
  101.1 11.8 %collective-permute-start.7 = (bf16[384,128]{1,0:T(8,128)(2,1)S(1)}, bf16[384,128]{1,0:T(8,128)(2,1)}, u32[]{:S(2)}, u32[]{:S(2)}) collective-permute-start(bf16[384,128]{1,0:T(8,128)(2,1)S(1)} %get-tuple-element.66), channel_id=1, source_target_pairs={{0,3},{1,4},{2,5},{3,6},{4,7},{5,0},{6,1},{7,2},{8,11},{9,12},{10,... | collective-permute-start | bytes 294920 | tf_op jit(solution)/shard_map/ppermute | solution.py:198
  103.0 9.8 %collective-permute-start.6 = (bf16[384,128]{1,0:T(8,128)(2,1)S(1)}, bf16[384,128]{1,0:T(8,128)(2,1)}, u32[]{:S(2)}, u32[]{:S(2)}) collective-permute-start(bf16[384,128]{1,0:T(8,128)(2,1)S(1)} %get-tuple-element.67), channel_id=1, source_target_pairs={{0,5},{1,6},{2,7},{3,0},{4,1},{5,2},{6,3},{7,4},{8,13},{9,14},{10,... | collective-permute-start | bytes 294920 | tf_op jit(solution)/shard_map/ppermute | solution.py:198
  116.7 28.3 %all-to-all-start.3 = ((bf16[8,384,128]{2,1,0:T(8,128)(2,1)}), bf16[8,384,128]{2,1,0:T(8,128)(2,1)S(1)}, u32[]{:S(2)}, u32[]{:S(2)}) async-start(bf16[8,384,128]{2,1,0:T(8,128)(2,1)} %bitcast.126), calls=%async_computation.3 | async-start | bytes 1572864 | tf_op jit(solution)/shard_map/all_to_all | solution.py:306
  150.2 44.0 %all-to-all-start.4 = ((bf16[8,384,256]{2,1,0:T(8,128)(2,1)}), bf16[8,384,256]{2,1,0:T(8,128)(2,1)S(1)}, u32[]{:S(2)}, u32[]{:S(2)}) async-start(bf16[8,384,256]{2,1,0:T(8,128)(2,1)} %broadcast_in_dim.95), calls=%async_computation.4 | async-start | bytes 3145728 | tf_op jit(solution)/shard_map/all_to_all | solution.py:334
  156.3 6.6 %collective-permute-start.8 = (f32[256,512]{1,0:T(8,128)}, f32[256,512]{1,0:T(8,128)S(1)}, u32[]{:S(2)}, u32[]{:S(2)}) collective-permute-start(f32[256,512]{1,0:T(8,128)} %get-tuple-element.79), channel_id=1, source_target_pairs={{0,8},{8,0},{1,9},{9,1},{2,10},{10,2},{3,11},{11,3},{4,12},{12,4},... | collective-permute-start | bytes 1572872 | tf_op jit(solution)/shard_map/ppermute | solution.py:342
  165.1 9.6 %collective-permute-start.9 = (f32[128,512]{1,0:T(8,128)S(1)}, f32[128,512]{1,0:T(8,128)S(1)}, u32[]{:S(2)}, u32[]{:S(2)}) collective-permute-start(f32[128,512]{1,0:T(8,128)S(1)} %slice_select_fusion), channel_id=1, source_target_pairs={{0,128},{128,0},{256,384},{384,256},{1,129},{129,1},{257,385},{385... | collective-permute-start | bytes 786440 | tf_op jit(solution)/shard_map/ppermute | solution.py:30
  174.8 7.4 %collective-permute-start.10 = (f32[64,512]{1,0:T(8,128)S(1)}, f32[64,512]{1,0:T(8,128)S(1)}, u32[]{:S(2)}, u32[]{:S(2)}) collective-permute-start(f32[64,512]{1,0:T(8,128)S(1)} %slice_select_fusion.1), channel_id=1, source_target_pairs={{0,256},{128,384},{256,0},{384,128},{1,257},{129,385},{257,1},{385... | collective-permute-start | bytes 393224 | tf_op jit(solution)/shard_map/ppermute | solution.py:30
  187.5 6.7 %collective-permute-start.12 = (f32[32,512]{1,0:T(8,128)S(1)}, f32[32,512]{1,0:T(8,128)S(1)}, u32[]{:S(2)}, u32[]{:S(2)}) collective-permute-start(f32[32,512]{1,0:T(8,128)S(1)} %select_add_fusion.3), channel_id=1, source_target_pairs={{0,32},{16,48},{32,0},{48,16},{64,96},{80,112},{96,64},{112,80},{1... | collective-permute-start | bytes 196616 | tf_op jit(solution)/shard_map/ppermute | solution.py:30
  199.4 46.0 %all-to-all-start.5 = ((bf16[64,128,128]{2,1,0:T(8,128)(2,1)}), bf16[64,128,128]{2,1,0:T(8,128)(2,1)S(1)}, u32[]{:S(2)}, u32[]{:S(2)}) async-start(bf16[64,128,128]{2,1,0:T(8,128)(2,1)} %tile_products.2), calls=%async_computation.5 | async-start | bytes 4194304 | tf_op jit(solution)/shard_map/all_to_all | solution.py:351
  206.8 9.5 %collective-permute-start.13 = (f32[32,512]{1,0:T(8,128)S(1)}, f32[32,512]{1,0:T(8,128)S(1)}, u32[]{:S(2)}, u32[]{:S(2)}) collective-permute-start(f32[32,512]{1,0:T(8,128)S(1)} %add.389), channel_id=1, source_target_pairs={{0,64},{16,80},{32,96},{48,112},{64,0},{80,16},{96,32},{112,48},{1... | collective-permute-start | bytes 196616 | tf_op jit(solution)/shard_map/ppermute | solution.py:30
  216.4 5.5 %collective-permute-start.14 = (f32[32,512]{1,0:T(8,128)S(1)}, f32[32,512]{1,0:T(8,128)S(1)}, u32[]{:S(2)}, u32[]{:S(2)}) collective-permute-start(f32[32,512]{1,0:T(8,128)S(1)} %add.390), channel_id=1, source_target_pairs={{0,1},{1,0},{2,3},{3,2},{4,5},{5,4},{6,7},{7,6},{8,9},{9,8},{10,11... | collective-permute-start | bytes 196616 | tf_op jit(solution)/shard_map/ppermute | solution.py:30
  221.8 5.9 %collective-permute-start.15 = (f32[32,512]{1,0:T(8,128)S(1)}, f32[32,512]{1,0:T(8,128)S(1)}, u32[]{:S(2)}, u32[]{:S(2)}) collective-permute-start(f32[32,512]{1,0:T(8,128)S(1)} %add.391), channel_id=1, source_target_pairs={{0,2},{1,3},{2,0},{3,1},{4,6},{5,7},{6,4},{7,5},{8,10},{9,11},{10,... | collective-permute-start | bytes 196616 | tf_op jit(solution)/shard_map/ppermute | solution.py:30
  227.8 10.0 %collective-permute-start.16 = (f32[32,512]{1,0:T(8,128)S(1)}, f32[32,512]{1,0:T(8,128)S(1)}, u32[]{:S(2)}, u32[]{:S(2)}) collective-permute-start(f32[32,512]{1,0:T(8,128)S(1)} %add.392), channel_id=1, source_target_pairs={{0,4},{1,5},{2,6},{3,7},{4,0},{5,1},{6,2},{7,3},{8,12},{9,13},{10,... | collective-permute-start | bytes 196616 | tf_op jit(solution)/shard_map/ppermute | solution.py:30
  237.8 7.6 %collective-permute-start.17 = (f32[32,512]{1,0:T(8,128)S(1)}, f32[32,512]{1,0:T(8,128)S(1)}, u32[]{:S(2)}, u32[]{:S(2)}) collective-permute-start(f32[32,512]{1,0:T(8,128)S(1)} %add_multiply_fusion), channel_id=1, source_target_pairs={{0,16},{16,0},{32,48},{48,32},{64,80},{80,64},{96,112},{112,96},{1... | collective-permute-start | bytes 196616 | tf_op jit(solution)/shard_map/ppermute | solution.py:30
  245.4 34.7 %all-to-all-start.6 = ((bf16[64,128,128]{2,1,0:T(8,128)(2,1)}), bf16[64,128,128]{2,1,0:T(8,128)(2,1)}, u32[]{:S(2)}, u32[]{:S(2)}) async-start(bf16[64,128,128]{2,1,0:T(8,128)(2,1)} %tile_products.3), calls=%async_computation.6 | async-start | bytes 4194304 | tf_op jit(solution)/shard_map/all_to_all | solution.py:359
  255.1 11.7 %collective-permute-start.18 = (bf16[3,384,128]{2,1,0:T(8,128)(2,1)S(1)}, bf16[3,384,128]{2,1,0:T(8,128)(2,1)S(1)}, u32[]{:S(2)}, u32[]{:S(2)}) collective-permute-start(bf16[3,384,128]{2,1,0:T(8,128)(2,1)S(1)} %bitcast.136), channel_id=1, source_target_pairs={{0,112},{16,0},{32,16},{48,32},{64,48},{80,64},{96,80},{112,96},{1... | collective-permute-start | bytes 884744 | tf_op jit(solution)/shard_map/ppermute | solution.py:198
  257.5 9.3 %collective-permute-start.19 = (bf16[2,384,128]{2,1,0:T(8,128)(2,1)S(1)}, bf16[2,384,128]{2,1,0:T(8,128)(2,1)S(1)}, u32[]{:S(2)}, u32[]{:S(2)}) collective-permute-start(bf16[2,384,128]{2,1,0:T(8,128)(2,1)S(1)} %bitcast.139), channel_id=1, source_target_pairs={{0,16},{16,32},{32,48},{48,64},{64,80},{80,96},{96,112},{112,0},{1... | collective-permute-start | bytes 589832 | tf_op jit(solution)/shard_map/ppermute | solution.py:198
  267.0 8.4 %collective-permute-start.21 = (bf16[384,128]{1,0:T(8,128)(2,1)S(1)}, bf16[384,128]{1,0:T(8,128)(2,1)S(1)}, u32[]{:S(2)}, u32[]{:S(2)}) collective-permute-start(bf16[384,128]{1,0:T(8,128)(2,1)S(1)} %get-tuple-element.64), channel_id=1, source_target_pairs={{0,48},{16,64},{32,80},{48,96},{64,112},{80,0},{96,16},{112,32},{1... | collective-permute-start | bytes 294920 | tf_op jit(solution)/shard_map/ppermute | solution.py:198
  272.6 7.6 %collective-permute-start.20 = (bf16[384,128]{1,0:T(8,128)(2,1)S(1)}, bf16[384,128]{1,0:T(8,128)(2,1)S(1)}, u32[]{:S(2)}, u32[]{:S(2)}) collective-permute-start(bf16[384,128]{1,0:T(8,128)(2,1)S(1)} %get-tuple-element.65), channel_id=1, source_target_pairs={{0,80},{16,96},{32,112},{48,0},{64,16},{80,32},{96,48},{112,64},{1... | collective-permute-start | bytes 294920 | tf_op jit(solution)/shard_map/ppermute | solution.py:198
  284.1 13.0 %collective-permute-start.22 = (f32[64,512]{1,0:T(8,128)S(1)}, f32[64,512]{1,0:T(8,128)S(1)}, u32[]{:S(2)}, u32[]{:S(2)}) collective-permute-start(f32[64,512]{1,0:T(8,128)S(1)} %maximum_select_fusion.2), channel_id=1, source_target_pairs={{0,256},{128,384},{256,0},{384,128},{1,257},{129,385},{257,1},{385... | collective-permute-start | bytes 393224 | tf_op jit(solution)/shard_map/ppermute | solution.py:30
  288.1 32.6 %all-to-all-start.7 = ((bf16[8,384,128]{2,1,0:T(8,128)(2,1)}), bf16[8,384,128]{2,1,0:T(8,128)(2,1)S(1)}, u32[]{:S(2)}, u32[]{:S(2)}) async-start(bf16[8,384,128]{2,1,0:T(8,128)(2,1)} %bitcast.38), calls=%async_computation.7 | async-start | bytes 1572864 | tf_op jit(solution)/shard_map/all_to_all | solution.py:366
  297.2 8.1 %collective-permute-start.23 = (f32[128,512]{1,0:T(8,128)S(1)}, f32[128,512]{1,0:T(8,128)S(1)}, u32[]{:S(2)}, u32[]{:S(2)}) collective-permute-start(f32[128,512]{1,0:T(8,128)S(1)} %maximum_select_fusion.1), channel_id=1, source_target_pairs={{0,128},{128,0},{256,384},{384,256},{1,129},{129,1},{257,385},{385... | collective-permute-start | bytes 786440 | tf_op jit(solution)/shard_map/ppermute | solution.py:30
  305.4 6.0 %collective-permute-start.24 = (f32[256,512]{1,0:T(8,128)S(1)}, f32[256,512]{1,0:T(8,128)S(1)}, u32[]{:S(2)}, u32[]{:S(2)}) collective-permute-start(f32[256,512]{1,0:T(8,128)S(1)} %maximum_select_fusion), channel_id=1, source_target_pairs={{0,8},{8,0},{1,9},{9,1},{2,10},{10,2},{3,11},{11,3},{4,12},{12,4},... | collective-permute-start | bytes 1572872 | tf_op jit(solution)/shard_map/ppermute | solution.py:369
  (22 other events, 236.4 us)

commit v7 on v5

--- a/solution.py
+++ b/solution.py
@@ -12,7 +12,6 @@
 DOM = ("x", "z", "core")
 ALL = ("x", "z", "core", "rep")
 STEP = 32
-LIMIT = pltpu.CompilerParams(vmem_limit_bytes=40 << 20)
 
 
 def edge_masks(row_ids, col_ids, limits, swapped):
@@ -69,7 +68,7 @@
             bytes_accessed=slots * tile * (tile + width) * 2,
             transcendentals=0,
         ),
-        compiler_params=LIMIT,
+        compiler_params=pltpu.CompilerParams(vmem_limit_bytes=40 << 20),
         name="tile_sums",
     )(offsets, masks, feats)
 
@@ -104,7 +103,7 @@
             bytes_accessed=slots * tile * (tile + width) * 2,
             transcendentals=0,
         ),
-        compiler_params=LIMIT,
+        compiler_params=pltpu.CompilerParams(vmem_limit_bytes=60 << 20),
         name="tile_products",
     )(offsets, masks, blocks)
 
@@ -139,7 +138,7 @@
         cost_estimate=pl.CostEstimate(
             flops=slots * tile * width, bytes_accessed=slots * tile * width * 2, transcendentals=0
         ),
-        compiler_params=LIMIT,
+        compiler_params=pltpu.CompilerParams(vmem_limit_bytes=40 << 20),
         name="summed_into",
     )(offsets, parts)
 
@@ -217,13 +216,7 @@
     low = x[0].astype(jnp.float32) + above[0] + below[0]
     own = x[1].astype(jnp.float32) + above[1] + below[1]
     high = x[2].astype(jnp.float32) + above[2]
-    return own, low.astype(x.dtype), high.astype(x.dtype)
-
-
-def sum_of_eight_ended(own, low, high, axis):
-    low = shifted(low, axis, -3).astype(jnp.float32)
-    high = shifted(high, axis, 3).astype(jnp.float32)
-    return own + low + high
+    return own, shifted(low.astype(x.dtype), axis, -3), shifted(high.astype(x.dtype), axis, 3)
 
 
 def halved(x, axis, bit):
@@ -305,11 +298,10 @@
     arrived_1, leaving_2 = lax.optimization_barrier((arrived_1, leaving_2))
     arrived_2 = lax.all_to_all(leaving_2, ("x", "core"), 0, 0, tiled=True)
     sums_1 = tile_sums(held_near, masks, arrived_1, group_blocks)
-    begun_1 = sum_of_eight(sums_1.reshape(rep_total, rows_here, half_in), "rep")
-    arrived_2, begun_1 = lax.optimization_barrier((arrived_2, begun_1))
-    summed_1 = sum_of_eight_ended(*begun_1, "rep")
+    own_1, low_1, high_1 = sum_of_eight(sums_1.reshape(rep_total, rows_here, half_in), "rep")
+    arrived_2, low_1, high_1 = lax.optimization_barrier((arrived_2, low_1, high_1))
+    summed_1 = own_1 + low_1.astype(jnp.float32) + high_1.astype(jnp.float32)
     sums_2 = tile_sums(held_offset, masks, arrived_2, group_blocks)
-    sums_2, summed_1 = lax.optimization_barrier((sums_2, summed_1))
     pieces = lax.all_to_all(
         sums_2.reshape(rep_total, rows_here, half_in), "rep", 0, 0, tiled=True
     )
@@ -349,17 +341,17 @@
     share = jnp.where(first, self_term, neigh_term) + lax.ppermute(
         jnp.where(first, neigh_term, self_term), "core", [(0, 1), (1, 0)]
     )
-    for axis, bit in (("x", 1), ("x", 2), ("z", 1), ("z", 2)):
+    for axis, bit in (("x", 1), ("x", 2), ("z", 1)):
         share = halved(share, axis, bit)
+    share = share + pair_swap(share, "z", 2)
 
     returning = tile_products(held_offset, masks_swapped, group_spread)
-    returning, share = lax.optimization_barrier((returning, share))
+    returning, group_spread, share = lax.optimization_barrier((returning, group_spread, share))
     returned = lax.all_to_all(returning, ("x", "core"), 0, 0, tiled=True)
     for axis, bit in (("z", 4), ("rep", 1), ("rep", 2), ("rep", 4)):
         share = share + pair_swap(share, axis, bit)
     share = share * (1.0 / math.sqrt(rows_here * dom_total * rep_total))
-    for bit in (2, 1):
-        share = doubled(share, "z", bit)
+    share = doubled(share, "z", 1)
     column_sums = summed_into(passed_offset, returned, z_total * blocks_here)
     column_sums, share = lax.optimization_barrier((column_sums, share))
     parts = lax.all_to_all(

time: 323 us -> 311 us (0.963)
  waiting for transfers between devices: 142 us -> 117 us
  starting transfers between devices: 120 us -> 128 us
    ppermute x12 -> x11, waiting for transfers between devices: 47.3 us -> 36.2 us  [pair_swap(): return lax.ppermute(x, axis, [(i, i ^ bit) for i in range(n)])]
    all_to_all x1, waiting for transfers between devices: 8 us -> 0.01 us  [shards(): arrived_2 = lax.all_to_all(leaving_2, ('x', 'core'), 0, 0, tiled=True)]
    ppermute x12 -> x11, starting transfers between devices: 37.2 us -> 44 us  [pair_swap(): return lax.ppermute(x, axis, [(i, i ^ bit) for i in range(n)])]
    all_to_all x1, waiting for transfers between devices: 5.18 us -> 0.01 us  [shards(): group_spread = lax.all_to_all(spread, 'rep', 0, 0, tiled=True)]
    all_to_all x1, starting transfers between devices: 3.56 us -> 6.98 us  [shards(): lax.all_to_all(sums_2.reshape(rep_total, rows_here, half_in), 'rep', 0, 0...]
    all_to_all x1, waiting for transfers between devices: 8.78 us -> 12.2 us  [shards(): returned = lax.all_to_all(returning, ('x', 'core'), 0, 0, tiled=True)]
  transfers between devices with their start and end apart: 29 -> 28, of which waited for: 26 -> 22; matrix products, arithmetic and copies ran while one was open for 7% -> 9% of each run, Pallas kernels for 3% -> 2%
where the time goes in v7:
time: 311 us; the launch traced here: 309 us
  starting transfers between devices  128 us (41%)
  waiting for transfers between devices  117 us (38%)
  Pallas kernels  23.1 us (7%)
  other arithmetic  16.2 us (5%)
  local copies, waits for them, and re-layouts  15.1 us (5%)
  matrix products  8.68 us (3%)
    ppermute x11, starting transfers between devices, pair_swap(): return lax.ppermute(x, axis, [(i, i ^ bit) for i in range(n)])  44 us
    ppermute x11, waiting for transfers between devices, pair_swap(): return lax.ppermute(x, axis, [(i, i ^ bit) for i in range(n)])  36.2 us
    ppermute x8, starting transfers between devices, shifted(): return lax.ppermute(x, axis, [(i, (i + by) % n) for i in range(n)])  28.9 us
    ppermute x8, waiting for transfers between devices, shifted(): return lax.ppermute(x, axis, [(i, (i + by) % n) for i in range(n)])  23.1 us
    all_to_all x1, waiting for transfers between devices, shards(): lax.all_to_all(column_sums.reshape(z_total, rows_here, width_in), 'z', 0,...  18 us
    all_to_all x1, waiting for transfers between devices, shards(): lax.all_to_all(sums_2.reshape(rep_total, rows_here, half_in), 'rep', 0, 0...  17.6 us
    all_to_all x1, waiting for transfers between devices, shards(): returned = lax.all_to_all(returning, ('x', 'core'), 0, 0, tiled=True)  12.2 us
    all_to_all x1, starting transfers between devices, shards(): lax.all_to_all(jnp.broadcast_to(node_feats[None, :, :half_in], (z_total,...  10.9 us
  transfers between devices with their start and end apart: 28, of which 22 were waited for; matrix products, arithmetic and copies ran while one was open for 9% of the time, Pallas kernels for 2%

profile of v7, /device:TPU:1, one launch (start us, length us, event | category | flops | bytes accessed | tf_op | source)
XLA Modules:
  0.0 309.3 jit_solution(7441169846450828799)
XLA Ops:
  2.7 10.9 %all-to-all-start = ((bf16[8,384,128]{2,1,0:T(8,128)(2,1)}), bf16[8,384,128]{2,1,0:T(8,128)(2,1)}, u32[]{:S(2)}, u32[]{:S(2)}) async-start(bf16[8,384,128]{2,1,0:T(8,128)(2,1)} %broadcast_in_dim.89), calls=%async_computation | async-start | bytes 1572864 | tf_op jit(solution)/shard_map/all_to_all | solution.py:251
  20.1 10.8 %fusion.10 = (bf16[64,128,128]{2,1,0:T(8,128)(2,1)}, bf16[64,128,128]{2,1,0:T(8,128)(2,1)S(1)}) fusion(s32[64,128]{1,0:T(8,128)S(1)} %get-tuple-element.54, s32[64,128]{1,0:T(8,128)S(1)} %get-tuple-element.53, s32[64,128]{1,0:T(8,128)S(1)} %add_select_fusion.5, s32[64]{0:T(128)S(1)} %get-tuple-element.59), kind=kLoop, calls=%fused_computation.22 | loop fusion | flops 46137344 | bytes 4292864 | tf_op jit(solution)/shard_map/convert_element_type | solution.py:25
  31.0 6.3 %all-to-all-done = bf16[8,384,128]{2,1,0:T(8,128)(2,1)} async-done(((bf16[8,384,128]{2,1,0:T(8,128)(2,1)}), bf16[8,384,128]{2,1,0:T(8,128)(2,1)}, u32[]{:S(2)}, u32[]{:S(2)}) %all-to-all-start) | async-done | bytes 786464 | tf_op jit(solution)/shard_map/all_to_all | solution.py:251
  37.2 3.7 %picked.2 = bf16[64,128,128]{2,1,0:T(8,128)(2,1)} custom-call(s32[64]{0:T(128)} %get-tuple-element.62.offset_ref, bf16[24,128,128]{2,1,0:T(8,128)(2,1)} %bitcast.1.refs_0_), custom_call_target="tpu_custom_call" | custom-call | bytes 2883584 | tf_op jit(solution)/shard_map/picked/pallas_call | solution.py:177
  40.9 4.8 %all-to-all-start.1 = ((bf16[64,128,128]{2,1,0:T(8,128)(2,1)}), bf16[64,128,128]{2,1,0:T(8,128)(2,1)}, u32[]{:S(2)}, u32[]{:S(2)}) async-start(bf16[64,128,128]{2,1,0:T(8,128)(2,1)} %picked.2), calls=%async_computation.1 | async-start | bytes 4194304 | tf_op jit(solution)/shard_map/all_to_all | solution.py:295
  47.9 5.0 %collective-permute-start = (bf16[384,128]{1,0:T(8,128)(2,1)S(1)}, bf16[384,128]{1,0:T(8,128)(2,1)S(1)}, u32[]{:S(2)}, u32[]{:S(2)}) collective-permute-start(bf16[384,128]{1,0:T(8,128)(2,1)S(1)} %get-tuple-element.24), channel_id=1, source_target_pairs={{0,48},{16,64},{32,80},{48,96},{64,112},{80,0},{96,16},{112,32},{1... | collective-permute-start | bytes 294920 | tf_op jit(solution)/shard_map/ppermute | solution.py:197
  55.1 5.7 %collective-permute-done = bf16[384,128]{1,0:T(8,128)(2,1)S(1)} collective-permute-done((bf16[384,128]{1,0:T(8,128)(2,1)S(1)}, bf16[384,128]{1,0:T(8,128)(2,1)S(1)}, u32[]{:S(2)}, u32[]{:S(2)}) %collective-permute-start) | collective-permute-done | bytes 98336 | tf_op jit(solution)/shard_map/ppermute | solution.py:197
  60.8 3.6 %collective-permute-start.2 = (bf16[3,384,128]{2,1,0:T(8,128)(2,1)S(1)}, bf16[3,384,128]{2,1,0:T(8,128)(2,1)S(1)}, u32[]{:S(2)}, u32[]{:S(2)}) collective-permute-start(bf16[3,384,128]{2,1,0:T(8,128)(2,1)S(1)} %pad_maximum_fusion), channel_id=1, source_target_pairs={{0,16},{16,32},{32,48},{48,64},{64,80},{80,96},{96,112},{112,0},{1... | collective-permute-start | bytes 884744 | tf_op jit(solution)/shard_map/ppermute | solution.py:197
  67.4 4.8 %collective-permute-done.3 = bf16[2,384,128]{2,1,0:T(8,128)(2,1)S(1)} collective-permute-done((bf16[2,384,128]{2,1,0:T(8,128)(2,1)S(1)}, bf16[2,384,128]{2,1,0:T(8,128)(2,1)S(1)}, u32[]{:S(2)}, u32[]{:S(2)}) %collective-permute-start.3) | collective-permute-done | bytes 196640 | tf_op jit(solution)/shard_map/ppermute | solution.py:197
  73.0 3.7 %picked.3 = bf16[64,128,128]{2,1,0:T(8,128)(2,1)} custom-call(s32[64]{0:T(128)} %get-tuple-element.63.offset_ref, bf16[9,128,128]{2,1,0:T(8,128)(2,1)} %bitcast.85, bf16[9,128,128]{2,1,0:T(8,128)(2,1)} %bitcast.90, bf16[6,128,128]{2,1,0:T(8,128)(2,1)} %bitcast.92), custom_call_target="tpu_custom_call" | custom-call | bytes 2883584 | tf_op jit(solution)/shard_map/picked/pallas_call | solution.py:177
  76.7 5.9 %all-to-all-start.2 = ((bf16[64,128,128]{2,1,0:T(8,128)(2,1)}), bf16[64,128,128]{2,1,0:T(8,128)(2,1)}, u32[]{:S(2)}, u32[]{:S(2)}) async-start(bf16[64,128,128]{2,1,0:T(8,128)(2,1)} %picked.3), calls=%async_computation.2 | async-start | bytes 4194304 | tf_op jit(solution)/shard_map/all_to_all | solution.py:299
  85.7 5.1 %collective-permute-start.4 = (bf16[3,384,128]{2,1,0:T(8,128)(2,1)S(1)}, bf16[3,384,128]{2,1,0:T(8,128)(2,1)S(1)}, u32[]{:S(2)}, u32[]{:S(2)}) collective-permute-start(bf16[3,384,128]{2,1,0:T(8,128)(2,1)S(1)} %bitcast.91), channel_id=1, source_target_pairs={{0,7},{1,0},{2,1},{3,2},{4,3},{5,4},{6,5},{7,6},{8,15},{9,8},{10,9... | collective-permute-start | bytes 884744 | tf_op jit(solution)/shard_map/ppermute | solution.py:197
  93.4 6.8 %collective-permute-done.5 = bf16[2,384,128]{2,1,0:T(8,128)(2,1)S(1)} collective-permute-done((bf16[2,384,128]{2,1,0:T(8,128)(2,1)S(1)}, bf16[2,384,128]{2,1,0:T(8,128)(2,1)S(1)}, u32[]{:S(2)}, u32[]{:S(2)}) %collective-permute-start.5) | collective-permute-done | bytes 196640 | tf_op jit(solution)/shard_map/ppermute | solution.py:197
  103.0 6.4 %collective-permute-start.6 = (bf16[384,128]{1,0:T(8,128)(2,1)S(1)}, bf16[384,128]{1,0:T(8,128)(2,1)}, u32[]{:S(2)}, u32[]{:S(2)}) collective-permute-start(bf16[384,128]{1,0:T(8,128)(2,1)S(1)} %get-tuple-element.48), channel_id=1, source_target_pairs={{0,5},{1,6},{2,7},{3,0},{4,1},{5,2},{6,3},{7,4},{8,13},{9,14},{10,... | collective-permute-start | bytes 294920 | tf_op jit(solution)/shard_map/ppermute | solution.py:197
  116.7 7.0 %all-to-all-start.3 = ((bf16[8,384,128]{2,1,0:T(8,128)(2,1)}), bf16[8,384,128]{2,1,0:T(8,128)(2,1)S(1)}, u32[]{:S(2)}, u32[]{:S(2)}) async-start(bf16[8,384,128]{2,1,0:T(8,128)(2,1)} %bitcast.83), calls=%async_computation.3 | async-start | bytes 1572864 | tf_op jit(solution)/shard_map/all_to_all | solution.py:305
  127.3 17.6 %all-to-all-done.3 = bf16[8,384,128]{2,1,0:T(8,128)(2,1)S(1)} async-done(((bf16[8,384,128]{2,1,0:T(8,128)(2,1)}), bf16[8,384,128]{2,1,0:T(8,128)(2,1)S(1)}, u32[]{:S(2)}, u32[]{:S(2)}) %all-to-all-start.3) | async-done | bytes 786464 | tf_op jit(solution)/shard_map/all_to_all | solution.py:305
  156.4 4.9 %collective-permute-start.8 = (f32[256,512]{1,0:T(8,128)}, f32[256,512]{1,0:T(8,128)S(1)}, u32[]{:S(2)}, u32[]{:S(2)}) collective-permute-start(f32[256,512]{1,0:T(8,128)} %get-tuple-element.60), channel_id=1, source_target_pairs={{0,8},{8,0},{1,9},{9,1},{2,10},{10,2},{3,11},{11,3},{4,12},{12,4},... | collective-permute-start | bytes 1572872 | tf_op jit(solution)/shard_map/ppermute | solution.py:341
  168.1 6.7 %collective-permute-done.9 = f32[128,512]{1,0:T(8,128)S(1)} collective-permute-done((f32[128,512]{1,0:T(8,128)S(1)}, f32[128,512]{1,0:T(8,128)S(1)}, u32[]{:S(2)}, u32[]{:S(2)}) %collective-permute-start.9) | collective-permute-done | bytes 262176 | tf_op jit(solution)/shard_map/ppermute | solution.py:30
  174.8 4.4 %collective-permute-start.10 = (f32[64,512]{1,0:T(8,128)S(1)}, f32[64,512]{1,0:T(8,128)S(1)}, u32[]{:S(2)}, u32[]{:S(2)}) collective-permute-start(f32[64,512]{1,0:T(8,128)S(1)} %slice_select_fusion.1), channel_id=1, source_target_pairs={{0,256},{128,384},{256,0},{384,128},{1,257},{129,385},{257,1},{385... | collective-permute-start | bytes 393224 | tf_op jit(solution)/shard_map/ppermute | solution.py:30
  187.6 4.9 %collective-permute-start.12 = (f32[32,512]{1,0:T(8,128)S(1)}, f32[32,512]{1,0:T(8,128)S(1)}, u32[]{:S(2)}, u32[]{:S(2)}) collective-permute-start(f32[32,512]{1,0:T(8,128)S(1)} %select_add_fusion.3), channel_id=1, source_target_pairs={{0,32},{16,48},{32,0},{48,16},{64,96},{80,112},{96,64},{112,80},{1... | collective-permute-start | bytes 196616 | tf_op jit(solution)/shard_map/ppermute | solution.py:30
  195.5 5.2 %tile_products.1 = bf16[64,128,256]{2,1,0:T(8,128)(2,1)} custom-call(s32[64]{0:T(128)} %copy-done.3, bf16[64,128,128]{2,1,0:T(8,128)(2,1)} %get-tuple-element.30.mask_ref, bf16[24,128,256]{2,1,0:T(8,128)(2,1)} %bitcast.84), custom_call_target="tpu_custom_call" | custom-call | flops 536870912 | bytes 6291456 | tf_op jit(solution)/shard_map/tile_products/pallas_call | solution.py:89
  200.6 7.9 %all-to-all-start.5 = ((bf16[64,128,256]{2,1,0:T(8,128)(2,1)}), bf16[64,128,256]{2,1,0:T(8,128)(2,1)}, u32[]{:S(2)}, u32[]{:S(2)}) async-start(bf16[64,128,256]{2,1,0:T(8,128)(2,1)} %tile_products.1), calls=%async_computation.5 | async-start | bytes 8388608 | tf_op jit(solution)/shard_map/all_to_all | solution.py:350
  208.5 5.9 %collective-permute-start.13 = (f32[32,512]{1,0:T(8,128)S(1)}, f32[32,512]{1,0:T(8,128)S(1)}, u32[]{:S(2)}, u32[]{:S(2)}) collective-permute-start(f32[32,512]{1,0:T(8,128)S(1)} %add.368), channel_id=1, source_target_pairs={{0,64},{16,80},{32,96},{48,112},{64,0},{80,16},{96,32},{112,48},{1... | collective-permute-start | bytes 196616 | tf_op jit(solution)/shard_map/ppermute | solution.py:30
  223.5 4.3 %collective-permute-start.15 = (f32[32,512]{1,0:T(8,128)S(1)}, f32[32,512]{1,0:T(8,128)S(1)}, u32[]{:S(2)}, u32[]{:S(2)}) collective-permute-start(f32[32,512]{1,0:T(8,128)S(1)} %add.370), channel_id=1, source_target_pairs={{0,2},{1,3},{2,0},{3,1},{4,6},{5,7},{6,4},{7,5},{8,10},{9,11},{10,... | collective-permute-start | bytes 196616 | tf_op jit(solution)/shard_map/ppermute | solution.py:30
  229.8 8.0 %collective-permute-start.16 = (f32[32,512]{1,0:T(8,128)S(1)}, f32[32,512]{1,0:T(8,128)S(1)}, u32[]{:S(2)}, u32[]{:S(2)}) collective-permute-start(f32[32,512]{1,0:T(8,128)S(1)} %add.371), channel_id=1, source_target_pairs={{0,4},{1,5},{2,6},{3,7},{4,0},{5,1},{6,2},{7,3},{8,12},{9,13},{10,... | collective-permute-start | bytes 196616 | tf_op jit(solution)/shard_map/ppermute | solution.py:30
  245.2 12.2 %all-to-all-done.5.part_ref = bf16[64,128,256]{2,1,0:T(8,128)(2,1)} async-done(((bf16[64,128,256]{2,1,0:T(8,128)(2,1)}), bf16[64,128,256]{2,1,0:T(8,128)(2,1)}, u32[]{:S(2)}, u32[]{:S(2)}) %all-to-all-start.5) | async-done | bytes 4194336 | tf_op jit(solution)/shard_map/all_to_all | solution.py:350
  257.4 4.6 %summed_into.1 = bf16[24,128,256]{2,1,0:T(8,128)(2,1)} custom-call(s32[64]{0:T(128)S(1)} %copy-done.2, bf16[64,128,256]{2,1,0:T(8,128)(2,1)} %all-to-all-done.5.part_ref), custom_call_target="tpu_custom_call" | custom-call | flops 2097152 | bytes 4194304 | tf_op jit(solution)/shard_map/summed_into/pallas_call | solution.py:128
  262.0 5.6 %all-to-all-start.6 = ((bf16[8,384,256]{2,1,0:T(8,128)(2,1)}), bf16[8,384,256]{2,1,0:T(8,128)(2,1)S(1)}, u32[]{:S(2)}, u32[]{:S(2)}) async-start(bf16[8,384,256]{2,1,0:T(8,128)(2,1)} %bitcast.28), calls=%async_computation.6 | async-start | bytes 3145728 | tf_op jit(solution)/shard_map/all_to_all | solution.py:357
  269.8 5.0 %collective-permute-done.18 = f32[64,512]{1,0:T(8,128)S(1)} collective-permute-done((f32[64,512]{1,0:T(8,128)S(1)}, f32[64,512]{1,0:T(8,128)S(1)}, u32[]{:S(2)}, u32[]{:S(2)}) %collective-permute-start.18) | collective-permute-done | bytes 131104 | tf_op jit(solution)/shard_map/ppermute | solution.py:30
  277.1 5.2 %collective-permute-done.19 = f32[128,512]{1,0:T(8,128)S(1)} collective-permute-done((f32[128,512]{1,0:T(8,128)S(1)}, f32[128,512]{1,0:T(8,128)S(1)}, u32[]{:S(2)}, u32[]{:S(2)}) %collective-permute-start.19) | collective-permute-done | bytes 262176 | tf_op jit(solution)/shard_map/ppermute | solution.py:30
  282.3 5.1 %collective-permute-start.20 = (f32[256,512]{1,0:T(8,128)S(1)}, f32[256,512]{1,0:T(8,128)S(1)}, u32[]{:S(2)}, u32[]{:S(2)}) collective-permute-start(f32[256,512]{1,0:T(8,128)S(1)} %maximum_select_fusion), channel_id=1, source_target_pairs={{0,8},{8,0},{1,9},{9,1},{2,10},{10,2},{3,11},{11,3},{4,12},{12,4},... | collective-permute-start | bytes 1572872 | tf_op jit(solution)/shard_map/ppermute | solution.py:362
  290.0 18.0 %all-to-all-done.6 = bf16[8,384,256]{2,1,0:T(8,128)(2,1)S(1)} async-done(((bf16[8,384,256]{2,1,0:T(8,128)(2,1)}), bf16[8,384,256]{2,1,0:T(8,128)(2,1)S(1)}, u32[]{:S(2)}, u32[]{:S(2)}) %all-to-all-start.6) | async-done | bytes 1572896 | tf_op jit(solution)/shard_map/all_to_all | solution.py:357
  (135 shorter events, 92.2 us)
Async XLA Ops:
  2.7 34.5 %all-to-all-start = ((bf16[8,384,128]{2,1,0:T(8,128)(2,1)}), bf16[8,384,128]{2,1,0:T(8,128)(2,1)}, u32[]{:S(2)}, u32[]{:S(2)}) async-start(bf16[8,384,128]{2,1,0:T(8,128)(2,1)} %broadcast_in_dim.89), calls=%async_computation | async-start | bytes 1572864 | tf_op jit(solution)/shard_map/all_to_all | solution.py:251
  20.1 92.7 %copy-start.3 = (s32[64]{0:T(128)}, s32[64]{0:T(128)S(1)}, u32[]{:S(2)}) copy-start(s32[64]{0:T(128)S(1)} %get-tuple-element.39.offset_ref) | copy-start | bytes 772
  40.9 35.8 %all-to-all-start.1 = ((bf16[64,128,128]{2,1,0:T(8,128)(2,1)}), bf16[64,128,128]{2,1,0:T(8,128)(2,1)}, u32[]{:S(2)}, u32[]{:S(2)}) async-start(bf16[64,128,128]{2,1,0:T(8,128)(2,1)} %picked.2), calls=%async_computation.1 | async-start | bytes 4194304 | tf_op jit(solution)/shard_map/all_to_all | solution.py:295
  45.7 9.4 %collective-permute-start.1 = (bf16[384,128]{1,0:T(8,128)(2,1)S(1)}, bf16[384,128]{1,0:T(8,128)(2,1)S(1)}, u32[]{:S(2)}, u32[]{:S(2)}) collective-permute-start(bf16[384,128]{1,0:T(8,128)(2,1)S(1)} %get-tuple-element.24), channel_id=1, source_target_pairs={{0,80},{16,96},{32,112},{48,0},{64,16},{80,32},{96,48},{112,64},{1... | collective-permute-start | bytes 294920 | tf_op jit(solution)/shard_map/ppermute | solution.py:197
  47.9 12.9 %collective-permute-start = (bf16[384,128]{1,0:T(8,128)(2,1)S(1)}, bf16[384,128]{1,0:T(8,128)(2,1)S(1)}, u32[]{:S(2)}, u32[]{:S(2)}) collective-permute-start(bf16[384,128]{1,0:T(8,128)(2,1)S(1)} %get-tuple-element.24), channel_id=1, source_target_pairs={{0,48},{16,64},{32,80},{48,96},{64,112},{80,0},{96,16},{112,32},{1... | collective-permute-start | bytes 294920 | tf_op jit(solution)/shard_map/ppermute | solution.py:197
  60.8 11.4 %collective-permute-start.2 = (bf16[3,384,128]{2,1,0:T(8,128)(2,1)S(1)}, bf16[3,384,128]{2,1,0:T(8,128)(2,1)S(1)}, u32[]{:S(2)}, u32[]{:S(2)}) collective-permute-start(bf16[3,384,128]{2,1,0:T(8,128)(2,1)S(1)} %pad_maximum_fusion), channel_id=1, source_target_pairs={{0,16},{16,32},{32,48},{48,64},{64,80},{80,96},{96,112},{112,0},{1... | collective-permute-start | bytes 884744 | tf_op jit(solution)/shard_map/ppermute | solution.py:197
  64.5 7.7 %collective-permute-start.3 = (bf16[2,384,128]{2,1,0:T(8,128)(2,1)S(1)}, bf16[2,384,128]{2,1,0:T(8,128)(2,1)S(1)}, u32[]{:S(2)}, u32[]{:S(2)}) collective-permute-start(bf16[2,384,128]{2,1,0:T(8,128)(2,1)S(1)} %pad_maximum_fusion.1), channel_id=1, source_target_pairs={{0,112},{16,0},{32,16},{48,32},{64,48},{80,64},{96,80},{112,96},{1... | collective-permute-start | bytes 589832 | tf_op jit(solution)/shard_map/ppermute | solution.py:197
  76.7 36.1 %all-to-all-start.2 = ((bf16[64,128,128]{2,1,0:T(8,128)(2,1)}), bf16[64,128,128]{2,1,0:T(8,128)(2,1)}, u32[]{:S(2)}, u32[]{:S(2)}) async-start(bf16[64,128,128]{2,1,0:T(8,128)(2,1)} %picked.3), calls=%async_computation.2 | async-start | bytes 4194304 | tf_op jit(solution)/shard_map/all_to_all | solution.py:299
  85.7 14.6 %collective-permute-start.4 = (bf16[3,384,128]{2,1,0:T(8,128)(2,1)S(1)}, bf16[3,384,128]{2,1,0:T(8,128)(2,1)S(1)}, u32[]{:S(2)}, u32[]{:S(2)}) collective-permute-start(bf16[3,384,128]{2,1,0:T(8,128)(2,1)S(1)} %bitcast.91), channel_id=1, source_target_pairs={{0,7},{1,0},{2,1},{3,2},{4,3},{5,4},{6,5},{7,6},{8,15},{9,8},{10,9... | collective-permute-start | bytes 884744 | tf_op jit(solution)/shard_map/ppermute | solution.py:197
  90.8 9.4 %collective-permute-start.5 = (bf16[2,384,128]{2,1,0:T(8,128)(2,1)S(1)}, bf16[2,384,128]{2,1,0:T(8,128)(2,1)S(1)}, u32[]{:S(2)}, u32[]{:S(2)}) collective-permute-start(bf16[2,384,128]{2,1,0:T(8,128)(2,1)S(1)} %bitcast.93), channel_id=1, source_target_pairs={{0,1},{1,2},{2,3},{3,4},{4,5},{5,6},{6,7},{7,0},{8,9},{9,10},{10,1... | collective-permute-start | bytes 589832 | tf_op jit(solution)/shard_map/ppermute | solution.py:197
  101.1 11.8 %collective-permute-start.7 = (bf16[384,128]{1,0:T(8,128)(2,1)S(1)}, bf16[384,128]{1,0:T(8,128)(2,1)}, u32[]{:S(2)}, u32[]{:S(2)}) collective-permute-start(bf16[384,128]{1,0:T(8,128)(2,1)S(1)} %get-tuple-element.47), channel_id=1, source_target_pairs={{0,3},{1,4},{2,5},{3,6},{4,7},{5,0},{6,1},{7,2},{8,11},{9,12},{10,... | collective-permute-start | bytes 294920 | tf_op jit(solution)/shard_map/ppermute | solution.py:197
  103.0 9.8 %collective-permute-start.6 = (bf16[384,128]{1,0:T(8,128)(2,1)S(1)}, bf16[384,128]{1,0:T(8,128)(2,1)}, u32[]{:S(2)}, u32[]{:S(2)}) collective-permute-start(bf16[384,128]{1,0:T(8,128)(2,1)S(1)} %get-tuple-element.48), channel_id=1, source_target_pairs={{0,5},{1,6},{2,7},{3,0},{4,1},{5,2},{6,3},{7,4},{8,13},{9,14},{10,... | collective-permute-start | bytes 294920 | tf_op jit(solution)/shard_map/ppermute | solution.py:197
  116.7 28.1 %all-to-all-start.3 = ((bf16[8,384,128]{2,1,0:T(8,128)(2,1)}), bf16[8,384,128]{2,1,0:T(8,128)(2,1)S(1)}, u32[]{:S(2)}, u32[]{:S(2)}) async-start(bf16[8,384,128]{2,1,0:T(8,128)(2,1)} %bitcast.83), calls=%async_computation.3 | async-start | bytes 1572864 | tf_op jit(solution)/shard_map/all_to_all | solution.py:305
  150.2 44.0 %all-to-all-start.4 = ((bf16[8,384,256]{2,1,0:T(8,128)(2,1)}), bf16[8,384,256]{2,1,0:T(8,128)(2,1)S(1)}, u32[]{:S(2)}, u32[]{:S(2)}) async-start(bf16[8,384,256]{2,1,0:T(8,128)(2,1)} %broadcast_in_dim.95), calls=%async_computation.4 | async-start | bytes 3145728 | tf_op jit(solution)/shard_map/all_to_all | solution.py:333
  156.4 6.6 %collective-permute-start.8 = (f32[256,512]{1,0:T(8,128)}, f32[256,512]{1,0:T(8,128)S(1)}, u32[]{:S(2)}, u32[]{:S(2)}) collective-permute-start(f32[256,512]{1,0:T(8,128)} %get-tuple-element.60), channel_id=1, source_target_pairs={{0,8},{8,0},{1,9},{9,1},{2,10},{10,2},{3,11},{11,3},{4,12},{12,4},... | collective-permute-start | bytes 1572872 | tf_op jit(solution)/shard_map/ppermute | solution.py:341
  165.2 9.6 %collective-permute-start.9 = (f32[128,512]{1,0:T(8,128)S(1)}, f32[128,512]{1,0:T(8,128)S(1)}, u32[]{:S(2)}, u32[]{:S(2)}) collective-permute-start(f32[128,512]{1,0:T(8,128)S(1)} %slice_select_fusion), channel_id=1, source_target_pairs={{0,128},{128,0},{256,384},{384,256},{1,129},{129,1},{257,385},{385... | collective-permute-start | bytes 786440 | tf_op jit(solution)/shard_map/ppermute | solution.py:30
  174.8 7.4 %collective-permute-start.10 = (f32[64,512]{1,0:T(8,128)S(1)}, f32[64,512]{1,0:T(8,128)S(1)}, u32[]{:S(2)}, u32[]{:S(2)}) collective-permute-start(f32[64,512]{1,0:T(8,128)S(1)} %slice_select_fusion.1), channel_id=1, source_target_pairs={{0,256},{128,384},{256,0},{384,128},{1,257},{129,385},{257,1},{385... | collective-permute-start | bytes 393224 | tf_op jit(solution)/shard_map/ppermute | solution.py:30
  182.3 5.3 %collective-permute-start.11 = (f32[32,512]{1,0:T(8,128)S(1)}, f32[32,512]{1,0:T(8,128)S(1)}, u32[]{:S(2)}, u32[]{:S(2)}) collective-permute-start(f32[32,512]{1,0:T(8,128)S(1)} %slice_select_fusion.2), channel_id=1, source_target_pairs={{0,16},{16,0},{32,48},{48,32},{64,80},{80,64},{96,112},{112,96},{1... | collective-permute-start | bytes 196616 | tf_op jit(solution)/shard_map/ppermute | solution.py:30
  187.6 6.7 %collective-permute-start.12 = (f32[32,512]{1,0:T(8,128)S(1)}, f32[32,512]{1,0:T(8,128)S(1)}, u32[]{:S(2)}, u32[]{:S(2)}) collective-permute-start(f32[32,512]{1,0:T(8,128)S(1)} %select_add_fusion.3), channel_id=1, source_target_pairs={{0,32},{16,48},{32,0},{48,16},{64,96},{80,112},{96,64},{112,80},{1... | collective-permute-start | bytes 196616 | tf_op jit(solution)/shard_map/ppermute | solution.py:30
  200.6 56.8 %copy-start.2 = (s32[64]{0:T(128)S(1)}, s32[64]{0:T(128)}, u32[]{:S(2)}) copy-start(s32[64]{0:T(128)} %get-tuple-element.62.offset_ref) | copy-start | bytes 772
  200.6 56.8 %all-to-all-start.5 = ((bf16[64,128,256]{2,1,0:T(8,128)(2,1)}), bf16[64,128,256]{2,1,0:T(8,128)(2,1)}, u32[]{:S(2)}, u32[]{:S(2)}) async-start(bf16[64,128,256]{2,1,0:T(8,128)(2,1)} %tile_products.1), calls=%async_computation.5 | async-start | bytes 8388608 | tf_op jit(solution)/shard_map/all_to_all | solution.py:350
  208.5 9.3 %collective-permute-start.13 = (f32[32,512]{1,0:T(8,128)S(1)}, f32[32,512]{1,0:T(8,128)S(1)}, u32[]{:S(2)}, u32[]{:S(2)}) collective-permute-start(f32[32,512]{1,0:T(8,128)S(1)} %add.368), channel_id=1, source_target_pairs={{0,64},{16,80},{32,96},{48,112},{64,0},{80,16},{96,32},{112,48},{1... | collective-permute-start | bytes 196616 | tf_op jit(solution)/shard_map/ppermute | solution.py:30
  217.8 5.6 %collective-permute-start.14 = (f32[32,512]{1,0:T(8,128)S(1)}, f32[32,512]{1,0:T(8,128)S(1)}, u32[]{:S(2)}, u32[]{:S(2)}) collective-permute-start(f32[32,512]{1,0:T(8,128)S(1)} %add.369), channel_id=1, source_target_pairs={{0,1},{1,0},{2,3},{3,2},{4,5},{5,4},{6,7},{7,6},{8,9},{9,8},{10,11... | collective-permute-start | bytes 196616 | tf_op jit(solution)/shard_map/ppermute | solution.py:30
  223.5 6.3 %collective-permute-start.15 = (f32[32,512]{1,0:T(8,128)S(1)}, f32[32,512]{1,0:T(8,128)S(1)}, u32[]{:S(2)}, u32[]{:S(2)}) collective-permute-start(f32[32,512]{1,0:T(8,128)S(1)} %add.370), channel_id=1, source_target_pairs={{0,2},{1,3},{2,0},{3,1},{4,6},{5,7},{6,4},{7,5},{8,10},{9,11},{10,... | collective-permute-start | bytes 196616 | tf_op jit(solution)/shard_map/ppermute | solution.py:30
  229.8 9.7 %collective-permute-start.16 = (f32[32,512]{1,0:T(8,128)S(1)}, f32[32,512]{1,0:T(8,128)S(1)}, u32[]{:S(2)}, u32[]{:S(2)}) collective-permute-start(f32[32,512]{1,0:T(8,128)S(1)} %add.371), channel_id=1, source_target_pairs={{0,4},{1,5},{2,6},{3,7},{4,0},{5,1},{6,2},{7,3},{8,12},{9,13},{10,... | collective-permute-start | bytes 196616 | tf_op jit(solution)/shard_map/ppermute | solution.py:30
  239.5 5.7 %collective-permute-start.17 = (f32[32,512]{1,0:T(8,128)S(1)}, f32[32,512]{1,0:T(8,128)S(1)}, u32[]{:S(2)}, u32[]{:S(2)}) collective-permute-start(f32[32,512]{1,0:T(8,128)S(1)} %add_multiply_fusion), channel_id=1, source_target_pairs={{0,16},{16,0},{32,48},{48,32},{64,80},{80,64},{96,112},{112,96},{1... | collective-permute-start | bytes 196616 | tf_op jit(solution)/shard_map/ppermute | solution.py:30
  262.0 46.3 %copy-start.6 = (bf16[384,512]{1,0:T(8,128)(2,1)S(1)}, bf16[384,512]{1,0:T(8,128)(2,1)}, u32[]{:S(2)}) copy-start(bf16[384,512]{1,0:T(8,128)(2,1)} %copy-done.5) | copy-start | bytes 1179652
  262.0 46.3 %copy-start.10 = (bf16[256,512]{1,0:T(8,128)(2,1)S(1)}, bf16[256,512]{1,0:T(8,128)(2,1)}, u32[]{:S(2)}) copy-start(bf16[256,512]{1,0:T(8,128)(2,1)} %param.13) | copy-start | bytes 786436
  262.0 46.1 %all-to-all-start.6 = ((bf16[8,384,256]{2,1,0:T(8,128)(2,1)}), bf16[8,384,256]{2,1,0:T(8,128)(2,1)S(1)}, u32[]{:S(2)}, u32[]{:S(2)}) async-start(bf16[8,384,256]{2,1,0:T(8,128)(2,1)} %bitcast.28), calls=%async_computation.6 | async-start | bytes 3145728 | tf_op jit(solution)/shard_map/all_to_all | solution.py:357
  267.6 7.2 %collective-permute-start.18 = (f32[64,512]{1,0:T(8,128)S(1)}, f32[64,512]{1,0:T(8,128)S(1)}, u32[]{:S(2)}, u32[]{:S(2)}) collective-permute-start(f32[64,512]{1,0:T(8,128)S(1)} %maximum_select_fusion.2), channel_id=1, source_target_pairs={{0,256},{128,384},{256,0},{384,128},{1,257},{129,385},{257,1},{385... | collective-permute-start | bytes 393224 | tf_op jit(solution)/shard_map/ppermute | solution.py:30
  274.9 7.4 %collective-permute-start.19 = (f32[128,512]{1,0:T(8,128)S(1)}, f32[128,512]{1,0:T(8,128)S(1)}, u32[]{:S(2)}, u32[]{:S(2)}) collective-permute-start(f32[128,512]{1,0:T(8,128)S(1)} %maximum_select_fusion.1), channel_id=1, source_target_pairs={{0,128},{128,0},{256,384},{384,256},{1,129},{129,1},{257,385},{385... | collective-permute-start | bytes 786440 | tf_op jit(solution)/shard_map/ppermute | solution.py:30
  282.3 6.6 %collective-permute-start.20 = (f32[256,512]{1,0:T(8,128)S(1)}, f32[256,512]{1,0:T(8,128)S(1)}, u32[]{:S(2)}, u32[]{:S(2)}) collective-permute-start(f32[256,512]{1,0:T(8,128)S(1)} %maximum_select_fusion), channel_id=1, source_target_pairs={{0,8},{8,0},{1,9},{9,1},{2,10},{10,2},{3,11},{11,3},{4,12},{12,4},... | collective-permute-start | bytes 1572872 | tf_op jit(solution)/shard_map/ppermute | solution.py:362
  (11 other events, 53.9 us)

commit v8 on v7

--- a/solution.py
+++ b/solution.py
@@ -73,29 +73,38 @@
     )(offsets, masks, feats)
 
 
-def products_kernel(offset_ref, mask_ref, block_ref, out_ref):
+def products_kernel(offset_ref, mask_ref, *refs):
+    *piece_refs, out_ref, held_ref = refs
     step = pl.program_id(0)
+
+    @pl.when(step == 0)
+    def _():
+        first = 0
+        for piece in piece_refs:
+            held_ref[first : first + piece.shape[0]] = piece[...]
+            first += piece.shape[0]
+
     for t in range(STEP):
         out_ref[t] = jnp.dot(
             mask_ref[t],
-            block_ref[offset_ref[step * STEP + t]],
+            held_ref[offset_ref[step * STEP + t]],
             preferred_element_type=jnp.float32,
         ).astype(out_ref.dtype)
 
 
-def tile_products(offsets, masks, blocks):
+def tile_products(offsets, masks, *pieces):
     slots, tile, _ = masks.shape
-    n, _, width = blocks.shape
+    n = sum(len(piece) for piece in pieces)
+    width = pieces[0].shape[2]
     return pl.pallas_call(
         products_kernel,
         grid_spec=pltpu.PrefetchScalarGridSpec(
             num_scalar_prefetch=1,
             grid=(slots // STEP,),
-            in_specs=[
-                pl.BlockSpec((STEP, tile, tile), lambda i, o: (i, 0, 0)),
-                pl.BlockSpec((n, tile, width), lambda i, o: (0, 0, 0)),
-            ],
+            in_specs=[pl.BlockSpec((STEP, tile, tile), lambda i, o: (i, 0, 0))]
+            + [pl.BlockSpec(piece.shape, lambda i, o: (0, 0, 0)) for piece in pieces],
             out_specs=pl.BlockSpec((STEP, tile, width), lambda i, o: (i, 0, 0)),
+            scratch_shapes=[pltpu.VMEM((n, tile, width), pieces[0].dtype)],
         ),
         out_shape=jax.ShapeDtypeStruct((slots, tile, width), jnp.bfloat16),
         cost_estimate=pl.CostEstimate(
@@ -105,10 +114,11 @@
         ),
         compiler_params=pltpu.CompilerParams(vmem_limit_bytes=60 << 20),
         name="tile_products",
-    )(offsets, masks, blocks)
-
-
-def gathered_kernel(offset_ref, part_ref, out_ref, total_ref):
+    )(offsets, masks, *pieces)
+
+
+def gathered_kernel(offset_ref, part_ref, *refs):
+    *beside_ref, out_ref, total_ref = refs
     step = pl.program_id(0)
 
     @pl.when(step == 0)
@@ -120,27 +130,32 @@
 
     @pl.when(step == pl.num_programs(0) - 1)
     def _():
-        out_ref[...] = total_ref[...].astype(out_ref.dtype)
-
-
-def summed_into(offsets, parts, blocks):
+        width = total_ref.shape[2]
+        if beside_ref:
+            out_ref[:, :, :width] = beside_ref[0][...]
+        out_ref[:, :, -width:] = total_ref[...].astype(out_ref.dtype)
+
+
+def summed_into(offsets, parts, blocks, *beside):
     slots, tile, width = parts.shape
+    out = (blocks, tile, width * (1 + len(beside)))
     return pl.pallas_call(
         gathered_kernel,
         grid_spec=pltpu.PrefetchScalarGridSpec(
             num_scalar_prefetch=1,
             grid=(slots // STEP,),
-            in_specs=[pl.BlockSpec((STEP, tile, width), lambda i, o: (i, 0, 0))],
-            out_specs=pl.BlockSpec((blocks, tile, width), lambda i, o: (0, 0, 0)),
+            in_specs=[pl.BlockSpec((STEP, tile, width), lambda i, o: (i, 0, 0))]
+            + [pl.BlockSpec(x.shape, lambda i, o: (0, 0, 0)) for x in beside],
+            out_specs=pl.BlockSpec(out, lambda i, o: (0, 0, 0)),
             scratch_shapes=[pltpu.VMEM((blocks, tile, width), jnp.float32)],
         ),
-        out_shape=jax.ShapeDtypeStruct((blocks, tile, width), jnp.bfloat16),
+        out_shape=jax.ShapeDtypeStruct(out, jnp.bfloat16),
         cost_estimate=pl.CostEstimate(
             flops=slots * tile * width, bytes_accessed=slots * tile * width * 2, transcendentals=0
         ),
         compiler_params=pltpu.CompilerParams(vmem_limit_bytes=40 << 20),
         name="summed_into",
-    )(offsets, parts)
+    )(offsets, parts, *beside)
 
 
 def pick_kernel(offset_ref, *refs):
@@ -299,12 +314,13 @@
     arrived_2 = lax.all_to_all(leaving_2, ("x", "core"), 0, 0, tiled=True)
     sums_1 = tile_sums(held_near, masks, arrived_1, group_blocks)
     own_1, low_1, high_1 = sum_of_eight(sums_1.reshape(rep_total, rows_here, half_in), "rep")
-    arrived_2, low_1, high_1 = lax.optimization_barrier((arrived_2, low_1, high_1))
-    summed_1 = own_1 + low_1.astype(jnp.float32) + high_1.astype(jnp.float32)
+    arrived_2, low_1 = lax.optimization_barrier((arrived_2, low_1))
     sums_2 = tile_sums(held_offset, masks, arrived_2, group_blocks)
+    sums_2, high_1 = lax.optimization_barrier((sums_2, high_1))
     pieces = lax.all_to_all(
         sums_2.reshape(rep_total, rows_here, half_in), "rep", 0, 0, tiled=True
     )
+    summed_1 = own_1 + low_1.astype(jnp.float32) + high_1.astype(jnp.float32)
     summed = jnp.concatenate([summed_1, pieces.astype(jnp.float32).sum(axis=0)], axis=1)
 
     own_first = group_first + rep_here * blocks_here
@@ -328,10 +344,12 @@
         pre_grad, neigh_weight, over_cols, preferred_element_type=jnp.float32
     )
     spread = (mean_grad / divisor).astype(jnp.bfloat16)
-    spread = jnp.broadcast_to(spread[None], (rep_total, rows_here, width_in))
-    spread, mean_feats, summing = lax.optimization_barrier((spread, mean_feats, pre_grad))
-    group_spread = lax.all_to_all(spread, "rep", 0, 0, tiled=True)
-    group_spread = group_spread.reshape(group_blocks, TILE, width_in)
+    spread_1 = jnp.broadcast_to(spread[None, :, :half_in], (rep_total, rows_here, half_in))
+    spread_1, spread_2, mean_feats, summing = lax.optimization_barrier(
+        (spread_1, spread[:, half_in:], mean_feats, pre_grad)
+    )
+    group_1 = lax.all_to_all(spread_1, "rep", 0, 0, tiled=True)
+    group_1 = group_1.reshape(group_blocks, TILE, half_in)
 
     self_term = lax.dot_general(node_feats, summing, over_rows, preferred_element_type=jnp.float32)
     neigh_term = lax.dot_general(
@@ -341,22 +359,31 @@
     share = jnp.where(first, self_term, neigh_term) + lax.ppermute(
         jnp.where(first, neigh_term, self_term), "core", [(0, 1), (1, 0)]
     )
-    for axis, bit in (("x", 1), ("x", 2), ("z", 1)):
-        share = halved(share, axis, bit)
-    share = share + pair_swap(share, "z", 2)
-
-    returning = tile_products(held_offset, masks_swapped, group_spread)
-    returning, group_spread, share = lax.optimization_barrier((returning, group_spread, share))
-    returned = lax.all_to_all(returning, ("x", "core"), 0, 0, tiled=True)
-    for axis, bit in (("z", 4), ("rep", 1), ("rep", 2), ("rep", 4)):
+    for bit in (1, 2):
+        share = halved(share, "x", bit)
+
+    returning_1 = tile_products(held_offset, masks_swapped, group_1)
+    returning_1, spread_2, share = lax.optimization_barrier((returning_1, spread_2, share))
+    returned_1 = lax.all_to_all(returning_1, ("x", "core"), 0, 0, tiled=True)
+    group_2 = [x.reshape(-1, TILE, half_in) for x in gather_of_eight(spread_2, "rep")]
+    share = halved(share, "z", 1)
+    returning_2 = tile_products(held_near, masks_swapped, *group_2)
+
+    returned_1, returning_2, share = lax.optimization_barrier((returned_1, returning_2, share))
+    returned_2 = lax.all_to_all(returning_2, ("x", "core"), 0, 0, tiled=True)
+    column_1 = summed_into(passed_offset, returned_1, z_total * blocks_here)
+    for axis, bit in (("z", 2), ("z", 4), ("rep", 1)):
         share = share + pair_swap(share, axis, bit)
-    share = share * (1.0 / math.sqrt(rows_here * dom_total * rep_total))
     share = doubled(share, "z", 1)
-    column_sums = summed_into(passed_offset, returned, z_total * blocks_here)
+    column_sums = summed_into(passed_offset, returned_2, z_total * blocks_here, column_1)
+
     column_sums, share = lax.optimization_barrier((column_sums, share))
     parts = lax.all_to_all(
         column_sums.reshape(z_total, rows_here, width_in), "z", 0, 0, tiled=True
     )
+    for bit in (2, 4):
+        share = share + pair_swap(share, "rep", bit)
+    share = share * (1.0 / math.sqrt(rows_here * dom_total * rep_total))
     for bit in (2, 1):
         share = doubled(share, "x", bit)
     other = lax.ppermute(share, "core", [(0, 1), (1, 0)])

time: 311 us -> 317 us (1.019)
  waiting for transfers between devices: 117 us -> 103 us
  starting transfers between devices: 128 us -> 141 us
  Pallas kernels: 23.1 us -> 26.7 us
    all_to_all x1, waiting for transfers between devices: 18 us -> 0.01 us  [shards(): lax.all_to_all(column_sums.reshape(z_total, rows_here, width_in), 'z', 0,...]
    ppermute x8 -> x12, starting transfers between devices: 28.9 us -> 41.2 us  [shifted(): return lax.ppermute(x, axis, [(i, (i + by) % n) for i in range(n)])]
    ppermute x8 -> x12, waiting for transfers between devices: 23.1 us -> 34.3 us  [shifted(): return lax.ppermute(x, axis, [(i, (i + by) % n) for i in range(n)])]
    all_to_all x2 -> x3, waiting for transfers between devices: 12.2 us -> 3.65 us  [the longest x1 3.64 us: shards(): group_1 = lax.all_to_all(spread_1, 'rep', 0, 0, tiled=True)]
    ppermute x1, starting transfers between devices: 5.11 us -> 8.68 us  [shards(): other = lax.ppermute(share, 'core', [(0, 1), (1, 0)])]
    pallas_call x1 -> x2, Pallas kernels: 5.16 us -> 8.09 us  [tile_products(): pl.pallas_call(products_kernel, grid_spec=pltpu.PrefetchScalarGridSpec(nu...]
    all_to_all x2 -> x3, starting transfers between devices: 11.5 us -> 14.2 us  [the longest x1 6.28 us: shards(): returned_2 = lax.all_to_all(returning_2, ('x', 'core'), 0, 0, tiled=True)]
    unnamed x30 -> x42, local copies, waits for them, and re-layouts: 4.34 us -> 6.8 us
  transfers between devices with their start and end apart: 28 -> 33, of which waited for: 22 -> 21; matrix products, arithmetic and copies ran while one was open for 9% -> 8% of each run, Pallas kernels for 2% -> 5%
where the time goes in v8:
time: 317 us; the launch traced here: 315 us
  starting transfers between devices  141 us (44%)
  waiting for transfers between devices  103 us (32%)
  Pallas kernels  26.7 us (8%)
  other arithmetic  18.4 us (6%)
  local copies, waits for them, and re-layouts  17.2 us (5%)
  matrix products  6.62 us (2%)
    ppermute x11, starting transfers between devices, pair_swap(): return lax.ppermute(x, axis, [(i, i ^ bit) for i in range(n)])  41.7 us
    ppermute x12, starting transfers between devices, shifted(): return lax.ppermute(x, axis, [(i, (i + by) % n) for i in range(n)])  41.2 us
    ppermute x11, waiting for transfers between devices, pair_swap(): return lax.ppermute(x, axis, [(i, i ^ bit) for i in range(n)])  38.3 us
    ppermute x12, waiting for transfers between devices, shifted(): return lax.ppermute(x, axis, [(i, (i + by) % n) for i in range(n)])  34.3 us
    all_to_all x1, waiting for transfers between devices, shards(): lax.all_to_all(sums_2.reshape(rep_total, rows_here, half_in), 'rep', 0, 0...  19.4 us
    convert_element_type x1, other arithmetic, edge_masks(): return (hashed < limits[:, None, None]).astype(jnp.bfloat16)  10.9 us
    all_to_all x1, starting transfers between devices, shards(): lax.all_to_all(jnp.broadcast_to(node_feats[None, :, :half_in], (z_total,...  10.9 us
    ppermute x1, starting transfers between devices, shards(): other = lax.ppermute(share, 'core', [(0, 1), (1, 0)])  8.68 us
  transfers between devices with their start and end apart: 33, of which 21 were waited for; matrix products, arithmetic and copies ran while one was open for 8% of the time, Pallas kernels for 5%

profile of v8, /device:TPU:1, one launch (start us, length us, event | category | flops | bytes accessed | tf_op | source)
XLA Modules:
  0.0 314.8 jit_solution(12838482903784457698)
XLA Ops:
  2.7 10.9 %all-to-all-start = ((bf16[8,384,128]{2,1,0:T(8,128)(2,1)}), bf16[8,384,128]{2,1,0:T(8,128)(2,1)}, u32[]{:S(2)}, u32[]{:S(2)}) async-start(bf16[8,384,128]{2,1,0:T(8,128)(2,1)} %broadcast_in_dim.89), calls=%async_computation | async-start | bytes 1572864 | tf_op jit(solution)/shard_map/all_to_all | solution.py:266
  20.1 10.9 %fusion.10 = (bf16[64,128,128]{2,1,0:T(8,128)(2,1)}, bf16[64,128,128]{2,1,0:T(8,128)(2,1)S(1)}) fusion(s32[64,128]{1,0:T(8,128)S(1)} %get-tuple-element.68, s32[64,128]{1,0:T(8,128)S(1)} %get-tuple-element.67, s32[64,128]{1,0:T(8,128)S(1)} %add_select_fusion.5, s32[64]{0:T(128)S(1)} %get-tuple-element.73), kind=kLoop, calls=%fused_computation.22 | loop fusion | flops 46137344 | bytes 4292864 | tf_op jit(solution)/shard_map/convert_element_type | solution.py:25
  31.0 6.2 %all-to-all-done = bf16[8,384,128]{2,1,0:T(8,128)(2,1)} async-done(((bf16[8,384,128]{2,1,0:T(8,128)(2,1)}), bf16[8,384,128]{2,1,0:T(8,128)(2,1)}, u32[]{:S(2)}, u32[]{:S(2)}) %all-to-all-start) | async-done | bytes 786464 | tf_op jit(solution)/shard_map/all_to_all | solution.py:266
  41.0 4.8 %all-to-all-start.1 = ((bf16[64,128,128]{2,1,0:T(8,128)(2,1)}), bf16[64,128,128]{2,1,0:T(8,128)(2,1)}, u32[]{:S(2)}, u32[]{:S(2)}) async-start(bf16[64,128,128]{2,1,0:T(8,128)(2,1)} %picked.2), calls=%async_computation.1 | async-start | bytes 4194304 | tf_op jit(solution)/shard_map/all_to_all | solution.py:310
  47.9 5.0 %collective-permute-start = (bf16[384,128]{1,0:T(8,128)(2,1)S(1)}, bf16[384,128]{1,0:T(8,128)(2,1)S(1)}, u32[]{:S(2)}, u32[]{:S(2)}) collective-permute-start(bf16[384,128]{1,0:T(8,128)(2,1)S(1)} %get-tuple-element.30), channel_id=1, source_target_pairs={{0,48},{16,64},{32,80},{48,96},{64,112},{80,0},{96,16},{112,32},{1... | collective-permute-start | bytes 294920 | tf_op jit(solution)/shard_map/ppermute | solution.py:212
  55.1 5.7 %collective-permute-done = bf16[384,128]{1,0:T(8,128)(2,1)S(1)} collective-permute-done((bf16[384,128]{1,0:T(8,128)(2,1)S(1)}, bf16[384,128]{1,0:T(8,128)(2,1)S(1)}, u32[]{:S(2)}, u32[]{:S(2)}) %collective-permute-start) | collective-permute-done | bytes 98336 | tf_op jit(solution)/shard_map/ppermute | solution.py:212
  67.4 4.8 %collective-permute-done.3 = bf16[2,384,128]{2,1,0:T(8,128)(2,1)S(1)} collective-permute-done((bf16[2,384,128]{2,1,0:T(8,128)(2,1)S(1)}, bf16[2,384,128]{2,1,0:T(8,128)(2,1)S(1)}, u32[]{:S(2)}, u32[]{:S(2)}) %collective-permute-start.3) | collective-permute-done | bytes 196640 | tf_op jit(solution)/shard_map/ppermute | solution.py:212
  76.7 5.9 %all-to-all-start.2 = ((bf16[64,128,128]{2,1,0:T(8,128)(2,1)}), bf16[64,128,128]{2,1,0:T(8,128)(2,1)}, u32[]{:S(2)}, u32[]{:S(2)}) async-start(bf16[64,128,128]{2,1,0:T(8,128)(2,1)} %picked.3), calls=%async_computation.2 | async-start | bytes 4194304 | tf_op jit(solution)/shard_map/all_to_all | solution.py:314
  85.7 5.1 %collective-permute-start.4 = (bf16[3,384,128]{2,1,0:T(8,128)(2,1)S(1)}, bf16[3,384,128]{2,1,0:T(8,128)(2,1)S(1)}, u32[]{:S(2)}, u32[]{:S(2)}) collective-permute-start(bf16[3,384,128]{2,1,0:T(8,128)(2,1)S(1)} %bitcast.103), channel_id=1, source_target_pairs={{0,7},{1,0},{2,1},{3,2},{4,3},{5,4},{6,5},{7,6},{8,15},{9,8},{10,9... | collective-permute-start | bytes 884744 | tf_op jit(solution)/shard_map/ppermute | solution.py:212
  93.4 6.8 %collective-permute-done.5 = bf16[2,384,128]{2,1,0:T(8,128)(2,1)S(1)} collective-permute-done((bf16[2,384,128]{2,1,0:T(8,128)(2,1)S(1)}, bf16[2,384,128]{2,1,0:T(8,128)(2,1)S(1)}, u32[]{:S(2)}, u32[]{:S(2)}) %collective-permute-start.5) | collective-permute-done | bytes 196640 | tf_op jit(solution)/shard_map/ppermute | solution.py:212
  105.0 3.7 %collective-permute-start.7 = (bf16[384,128]{1,0:T(8,128)(2,1)}, bf16[384,128]{1,0:T(8,128)(2,1)}, u32[]{:S(2)}, u32[]{:S(2)}) collective-permute-start(bf16[384,128]{1,0:T(8,128)(2,1)} %get-tuple-element.59), channel_id=1, source_target_pairs={{0,3},{1,4},{2,5},{3,6},{4,7},{5,0},{6,1},{7,2},{8,11},{9,12},{10,... | collective-permute-start | bytes 294920 | tf_op jit(solution)/shard_map/ppermute | solution.py:212
  115.8 6.1 %all-to-all-start.3 = ((bf16[8,384,128]{2,1,0:T(8,128)(2,1)}), bf16[8,384,128]{2,1,0:T(8,128)(2,1)S(1)}, u32[]{:S(2)}, u32[]{:S(2)}) async-start(bf16[8,384,128]{2,1,0:T(8,128)(2,1)} %bitcast.89), calls=%async_computation.3 | async-start | bytes 1572864 | tf_op jit(solution)/shard_map/all_to_all | solution.py:320
  126.0 19.4 %all-to-all-done.3 = bf16[8,384,128]{2,1,0:T(8,128)(2,1)S(1)} async-done(((bf16[8,384,128]{2,1,0:T(8,128)(2,1)}), bf16[8,384,128]{2,1,0:T(8,128)(2,1)S(1)}, u32[]{:S(2)}, u32[]{:S(2)}) %all-to-all-start.3) | async-done | bytes 786464 | tf_op jit(solution)/shard_map/all_to_all | solution.py:320
  162.9 7.1 %collective-permute-done.9 = f32[128,512]{1,0:T(8,128)S(1)} collective-permute-done((f32[128,512]{1,0:T(8,128)S(1)}, f32[128,512]{1,0:T(8,128)S(1)}, u32[]{:S(2)}, u32[]{:S(2)}) %collective-permute-start.9) | collective-permute-done | bytes 262176 | tf_op jit(solution)/shard_map/ppermute | solution.py:30
  170.1 4.3 %collective-permute-start.10 = (f32[64,512]{1,0:T(8,128)S(1)}, f32[64,512]{1,0:T(8,128)S(1)}, u32[]{:S(2)}, u32[]{:S(2)}) collective-permute-start(f32[64,512]{1,0:T(8,128)S(1)} %slice_select_fusion.1), channel_id=1, source_target_pairs={{0,256},{128,384},{256,0},{384,128},{1,257},{129,385},{257,1},{385... | collective-permute-start | bytes 393224 | tf_op jit(solution)/shard_map/ppermute | solution.py:30
  182.4 4.1 %tile_products.2 = bf16[64,128,128]{2,1,0:T(8,128)(2,1)} custom-call(s32[64]{0:T(128)} %copy-done.6, bf16[64,128,128]{2,1,0:T(8,128)(2,1)} %get-tuple-element.37.mask_ref, bf16[24,128,128]{2,1,0:T(8,128)(2,1)} %bitcast.90), custom_call_target="tpu_custom_call" | custom-call | flops 268435456 | bytes 4194304 | tf_op jit(solution)/shard_map/tile_products/pallas_call | solution.py:99
  186.5 4.4 %all-to-all-start.5 = ((bf16[64,128,128]{2,1,0:T(8,128)(2,1)}), bf16[64,128,128]{2,1,0:T(8,128)(2,1)S(1)}, u32[]{:S(2)}, u32[]{:S(2)}) async-start(bf16[64,128,128]{2,1,0:T(8,128)(2,1)} %tile_products.2), calls=%async_computation.5 | async-start | bytes 4194304 | tf_op jit(solution)/shard_map/all_to_all | solution.py:367
  200.0 7.5 %collective-permute-done.11 = bf16[384,128]{1,0:T(8,128)(2,1)S(1)} collective-permute-done((bf16[384,128]{1,0:T(8,128)(2,1)S(1)}, bf16[384,128]{1,0:T(8,128)(2,1)S(1)}, u32[]{:S(2)}, u32[]{:S(2)}) %collective-permute-start.11) | collective-permute-done | bytes 98336 | tf_op jit(solution)/shard_map/ppermute | solution.py:212
  209.5 4.6 %collective-permute-start.14 = (bf16[2,384,128]{2,1,0:T(8,128)(2,1)S(1)}, bf16[2,384,128]{2,1,0:T(8,128)(2,1)S(1)}, u32[]{:S(2)}, u32[]{:S(2)}) collective-permute-start(bf16[2,384,128]{2,1,0:T(8,128)(2,1)S(1)} %pad_maximum_fusion.3), channel_id=1, source_target_pairs={{0,7},{1,0},{2,1},{3,2},{4,3},{5,4},{6,5},{7,6},{8,15},{9,8},{10,9... | collective-permute-start | bytes 589832 | tf_op jit(solution)/shard_map/ppermute | solution.py:212
  218.9 4.0 %tile_products.3 = bf16[64,128,128]{2,1,0:T(8,128)(2,1)} custom-call(s32[64]{0:T(128)} %copy-done.5, bf16[64,128,128]{2,1,0:T(8,128)(2,1)} %get-tuple-element.37.mask_ref, bf16[9,128,128]{2,1,0:T(8,128)(2,1)} %bitcast.91, bf16[9,128,128]{2,1,0:T(8,128)(2,1)} %bitcast.101, bf16[6,128,128]{2,1,0:T(8,128)(2,1)} %bitcast.104), custom_call_target="tpu_custom_call" | custom-call | flops 268435456 | bytes 4194304 | tf_op jit(solution)/shard_map/tile_products/pallas_call | solution.py:99
  222.9 6.3 %all-to-all-start.6 = ((bf16[64,128,128]{2,1,0:T(8,128)(2,1)}), bf16[64,128,128]{2,1,0:T(8,128)(2,1)}, u32[]{:S(2)}, u32[]{:S(2)}) async-start(bf16[64,128,128]{2,1,0:T(8,128)(2,1)} %tile_products.3), calls=%async_computation.6 | async-start | bytes 4194304 | tf_op jit(solution)/shard_map/all_to_all | solution.py:373
  235.8 6.1 %collective-permute-start.17 = (f32[32,512]{1,0:T(8,128)S(1)}, f32[32,512]{1,0:T(8,128)S(1)}, u32[]{:S(2)}, u32[]{:S(2)}) collective-permute-start(f32[32,512]{1,0:T(8,128)S(1)} %add.368), channel_id=1, source_target_pairs={{0,64},{16,80},{32,96},{48,112},{64,0},{80,16},{96,32},{112,48},{1... | collective-permute-start | bytes 196616 | tf_op jit(solution)/shard_map/ppermute | solution.py:30
  249.9 4.5 %collective-permute-start.19 = (f32[32,512]{1,0:T(8,128)S(1)}, f32[32,512]{1,0:T(8,128)S(1)}, u32[]{:S(2)}, u32[]{:S(2)}) collective-permute-start(f32[32,512]{1,0:T(8,128)S(1)} %add.370), channel_id=1, source_target_pairs={{0,16},{16,0},{32,48},{48,32},{64,80},{80,64},{96,112},{112,96},{1... | collective-permute-start | bytes 196616 | tf_op jit(solution)/shard_map/ppermute | solution.py:30
  257.8 3.8 %summed_into.3 = bf16[24,128,256]{2,1,0:T(8,128)(2,1)} custom-call(s32[64]{0:T(128)S(1)} %copy-done.4, bf16[64,128,128]{2,1,0:T(8,128)(2,1)} %all-to-all-done.6.part_ref, bf16[24,128,128]{2,1,0:T(8,128)(2,1)S(1)} %copy-done.3), custom_call_target="tpu_custom_call" | custom-call | flops 1048576 | bytes 2097152 | tf_op jit(solution)/shard_map/summed_into/pallas_call | solution.py:142
  261.7 5.2 %all-to-all-start.7 = ((bf16[8,384,256]{2,1,0:T(8,128)(2,1)}), bf16[8,384,256]{2,1,0:T(8,128)(2,1)S(1)}, u32[]{:S(2)}, u32[]{:S(2)}) async-start(bf16[8,384,256]{2,1,0:T(8,128)(2,1)} %bitcast.34), calls=%async_computation.7 | async-start | bytes 3145728 | tf_op jit(solution)/shard_map/all_to_all | solution.py:381
  266.8 3.9 %collective-permute-start.20 = (f32[64,512]{1,0:T(8,128)S(1)}, f32[64,512]{1,0:T(8,128)S(1)}, u32[]{:S(2)}, u32[]{:S(2)}) collective-permute-start(f32[64,512]{1,0:T(8,128)S(1)} %maximum_select_fusion.2), channel_id=1, source_target_pairs={{0,2},{1,3},{2,0},{3,1},{4,6},{5,7},{6,4},{7,5},{8,10},{9,11},{10,... | collective-permute-start | bytes 393224 | tf_op jit(solution)/shard_map/ppermute | solution.py:30
  270.8 4.1 %collective-permute-done.20 = f32[64,512]{1,0:T(8,128)S(1)} collective-permute-done((f32[64,512]{1,0:T(8,128)S(1)}, f32[64,512]{1,0:T(8,128)S(1)}, u32[]{:S(2)}, u32[]{:S(2)}) %collective-permute-start.20) | collective-permute-done | bytes 131104 | tf_op jit(solution)/shard_map/ppermute | solution.py:30
  274.9 4.9 %collective-permute-start.21 = (f32[64,512]{1,0:T(8,128)S(1)}, f32[64,512]{1,0:T(8,128)S(1)}, u32[]{:S(2)}, u32[]{:S(2)}) collective-permute-start(f32[64,512]{1,0:T(8,128)S(1)} %add.372), channel_id=1, source_target_pairs={{0,4},{1,5},{2,6},{3,7},{4,0},{5,1},{6,2},{7,3},{8,12},{9,13},{10,... | collective-permute-start | bytes 393224 | tf_op jit(solution)/shard_map/ppermute | solution.py:30
  279.8 6.1 %collective-permute-done.21 = f32[64,512]{1,0:T(8,128)S(1)} collective-permute-done((f32[64,512]{1,0:T(8,128)S(1)}, f32[64,512]{1,0:T(8,128)S(1)}, u32[]{:S(2)}, u32[]{:S(2)}) %collective-permute-start.21) | collective-permute-done | bytes 131104 | tf_op jit(solution)/shard_map/ppermute | solution.py:30
  285.9 4.6 %collective-permute-start.22 = (f32[64,512]{1,0:T(8,128)S(1)}, f32[64,512]{1,0:T(8,128)S(1)}, u32[]{:S(2)}, u32[]{:S(2)}) collective-permute-start(f32[64,512]{1,0:T(8,128)S(1)} %add_multiply_fusion), channel_id=1, source_target_pairs={{0,256},{128,384},{256,0},{384,128},{1,257},{129,385},{257,1},{385... | collective-permute-start | bytes 393224 | tf_op jit(solution)/shard_map/ppermute | solution.py:30
  296.5 5.8 %collective-permute-done.23 = f32[128,512]{1,0:T(8,128)S(1)} collective-permute-done((f32[128,512]{1,0:T(8,128)S(1)}, f32[128,512]{1,0:T(8,128)S(1)}, u32[]{:S(2)}, u32[]{:S(2)}) %collective-permute-start.23) | collective-permute-done | bytes 262176 | tf_op jit(solution)/shard_map/ppermute | solution.py:30
  302.3 8.7 %collective-permute-start.24 = (f32[256,512]{1,0:T(8,128)S(1)}, f32[256,512]{1,0:T(8,128)S(1)}, u32[]{:S(2)}, u32[]{:S(2)}) collective-permute-start(f32[256,512]{1,0:T(8,128)S(1)} %maximum_select_fusion), channel_id=1, source_target_pairs={{0,8},{8,0},{1,9},{9,1},{2,10},{10,2},{3,11},{11,3},{4,12},{12,4},... | collective-permute-start | bytes 1572872 | tf_op jit(solution)/shard_map/ppermute | solution.py:389
  (162 shorter events, 118.2 us)
Async XLA Ops:
  2.7 34.5 %all-to-all-start = ((bf16[8,384,128]{2,1,0:T(8,128)(2,1)}), bf16[8,384,128]{2,1,0:T(8,128)(2,1)}, u32[]{:S(2)}, u32[]{:S(2)}) async-start(bf16[8,384,128]{2,1,0:T(8,128)(2,1)} %broadcast_in_dim.89), calls=%async_computation | async-start | bytes 1572864 | tf_op jit(solution)/shard_map/all_to_all | solution.py:266
  41.0 35.8 %all-to-all-start.1 = ((bf16[64,128,128]{2,1,0:T(8,128)(2,1)}), bf16[64,128,128]{2,1,0:T(8,128)(2,1)}, u32[]{:S(2)}, u32[]{:S(2)}) async-start(bf16[64,128,128]{2,1,0:T(8,128)(2,1)} %picked.2), calls=%async_computation.1 | async-start | bytes 4194304 | tf_op jit(solution)/shard_map/all_to_all | solution.py:310
  45.8 9.4 %collective-permute-start.1 = (bf16[384,128]{1,0:T(8,128)(2,1)S(1)}, bf16[384,128]{1,0:T(8,128)(2,1)S(1)}, u32[]{:S(2)}, u32[]{:S(2)}) collective-permute-start(bf16[384,128]{1,0:T(8,128)(2,1)S(1)} %get-tuple-element.30), channel_id=1, source_target_pairs={{0,80},{16,96},{32,112},{48,0},{64,16},{80,32},{96,48},{112,64},{1... | collective-permute-start | bytes 294920 | tf_op jit(solution)/shard_map/ppermute | solution.py:212
  47.9 12.9 %collective-permute-start = (bf16[384,128]{1,0:T(8,128)(2,1)S(1)}, bf16[384,128]{1,0:T(8,128)(2,1)S(1)}, u32[]{:S(2)}, u32[]{:S(2)}) collective-permute-start(bf16[384,128]{1,0:T(8,128)(2,1)S(1)} %get-tuple-element.30), channel_id=1, source_target_pairs={{0,48},{16,64},{32,80},{48,96},{64,112},{80,0},{96,16},{112,32},{1... | collective-permute-start | bytes 294920 | tf_op jit(solution)/shard_map/ppermute | solution.py:212
  60.8 11.4 %collective-permute-start.2 = (bf16[3,384,128]{2,1,0:T(8,128)(2,1)S(1)}, bf16[3,384,128]{2,1,0:T(8,128)(2,1)S(1)}, u32[]{:S(2)}, u32[]{:S(2)}) collective-permute-start(bf16[3,384,128]{2,1,0:T(8,128)(2,1)S(1)} %pad_maximum_fusion), channel_id=1, source_target_pairs={{0,16},{16,32},{32,48},{48,64},{64,80},{80,96},{96,112},{112,0},{1... | collective-permute-start | bytes 884744 | tf_op jit(solution)/shard_map/ppermute | solution.py:212
  64.5 7.7 %collective-permute-start.3 = (bf16[2,384,128]{2,1,0:T(8,128)(2,1)S(1)}, bf16[2,384,128]{2,1,0:T(8,128)(2,1)S(1)}, u32[]{:S(2)}, u32[]{:S(2)}) collective-permute-start(bf16[2,384,128]{2,1,0:T(8,128)(2,1)S(1)} %pad_maximum_fusion.2), channel_id=1, source_target_pairs={{0,112},{16,0},{32,16},{48,32},{64,48},{80,64},{96,80},{112,96},{1... | collective-permute-start | bytes 589832 | tf_op jit(solution)/shard_map/ppermute | solution.py:212
  76.7 35.2 %all-to-all-start.2 = ((bf16[64,128,128]{2,1,0:T(8,128)(2,1)}), bf16[64,128,128]{2,1,0:T(8,128)(2,1)}, u32[]{:S(2)}, u32[]{:S(2)}) async-start(bf16[64,128,128]{2,1,0:T(8,128)(2,1)} %picked.3), calls=%async_computation.2 | async-start | bytes 4194304 | tf_op jit(solution)/shard_map/all_to_all | solution.py:314
  85.7 14.6 %collective-permute-start.4 = (bf16[3,384,128]{2,1,0:T(8,128)(2,1)S(1)}, bf16[3,384,128]{2,1,0:T(8,128)(2,1)S(1)}, u32[]{:S(2)}, u32[]{:S(2)}) collective-permute-start(bf16[3,384,128]{2,1,0:T(8,128)(2,1)S(1)} %bitcast.103), channel_id=1, source_target_pairs={{0,7},{1,0},{2,1},{3,2},{4,3},{5,4},{6,5},{7,6},{8,15},{9,8},{10,9... | collective-permute-start | bytes 884744 | tf_op jit(solution)/shard_map/ppermute | solution.py:212
  90.8 9.4 %collective-permute-start.5 = (bf16[2,384,128]{2,1,0:T(8,128)(2,1)S(1)}, bf16[2,384,128]{2,1,0:T(8,128)(2,1)S(1)}, u32[]{:S(2)}, u32[]{:S(2)}) collective-permute-start(bf16[2,384,128]{2,1,0:T(8,128)(2,1)S(1)} %bitcast.106), channel_id=1, source_target_pairs={{0,1},{1,2},{2,3},{3,4},{4,5},{5,6},{6,7},{7,0},{8,9},{9,10},{10,1... | collective-permute-start | bytes 589832 | tf_op jit(solution)/shard_map/ppermute | solution.py:212
  101.7 10.2 %collective-permute-start.6 = (bf16[384,128]{1,0:T(8,128)(2,1)S(1)}, bf16[384,128]{1,0:T(8,128)(2,1)}, u32[]{:S(2)}, u32[]{:S(2)}) collective-permute-start(bf16[384,128]{1,0:T(8,128)(2,1)S(1)} %get-tuple-element.60), channel_id=1, source_target_pairs={{0,5},{1,6},{2,7},{3,0},{4,1},{5,2},{6,3},{7,4},{8,13},{9,14},{10,... | collective-permute-start | bytes 294920 | tf_op jit(solution)/shard_map/ppermute | solution.py:212
  105.0 10.8 %collective-permute-start.7 = (bf16[384,128]{1,0:T(8,128)(2,1)}, bf16[384,128]{1,0:T(8,128)(2,1)}, u32[]{:S(2)}, u32[]{:S(2)}) collective-permute-start(bf16[384,128]{1,0:T(8,128)(2,1)} %get-tuple-element.59), channel_id=1, source_target_pairs={{0,3},{1,4},{2,5},{3,6},{4,7},{5,0},{6,1},{7,2},{8,11},{9,12},{10,... | collective-permute-start | bytes 294920 | tf_op jit(solution)/shard_map/ppermute | solution.py:212
  115.8 29.6 %all-to-all-start.3 = ((bf16[8,384,128]{2,1,0:T(8,128)(2,1)}), bf16[8,384,128]{2,1,0:T(8,128)(2,1)S(1)}, u32[]{:S(2)}, u32[]{:S(2)}) async-start(bf16[8,384,128]{2,1,0:T(8,128)(2,1)} %bitcast.89), calls=%async_computation.3 | async-start | bytes 1572864 | tf_op jit(solution)/shard_map/all_to_all | solution.py:320
  152.0 6.0 %collective-permute-start.8 = (f32[256,512]{1,0:T(8,128)}, f32[256,512]{1,0:T(8,128)S(1)}, u32[]{:S(2)}, u32[]{:S(2)}) collective-permute-start(f32[256,512]{1,0:T(8,128)} %get-tuple-element.74), channel_id=1, source_target_pairs={{0,8},{8,0},{1,9},{9,1},{2,10},{10,2},{3,11},{11,3},{4,12},{12,4},... | collective-permute-start | bytes 1572872 | tf_op jit(solution)/shard_map/ppermute | solution.py:359
  154.4 27.1 %all-to-all-start.4 = ((bf16[8,384,128]{2,1,0:T(8,128)(2,1)}), bf16[8,384,128]{2,1,0:T(8,128)(2,1)S(1)}, u32[]{:S(2)}, u32[]{:S(2)}) async-start(bf16[8,384,128]{2,1,0:T(8,128)(2,1)} %broadcast_in_dim.95), calls=%async_computation.4 | async-start | bytes 1572864 | tf_op jit(solution)/shard_map/all_to_all | solution.py:351
  160.1 9.9 %collective-permute-start.9 = (f32[128,512]{1,0:T(8,128)S(1)}, f32[128,512]{1,0:T(8,128)S(1)}, u32[]{:S(2)}, u32[]{:S(2)}) collective-permute-start(f32[128,512]{1,0:T(8,128)S(1)} %slice_select_fusion), channel_id=1, source_target_pairs={{0,128},{128,0},{256,384},{384,256},{1,129},{129,1},{257,385},{385... | collective-permute-start | bytes 786440 | tf_op jit(solution)/shard_map/ppermute | solution.py:30
  170.1 7.7 %collective-permute-start.10 = (f32[64,512]{1,0:T(8,128)S(1)}, f32[64,512]{1,0:T(8,128)S(1)}, u32[]{:S(2)}, u32[]{:S(2)}) collective-permute-start(f32[64,512]{1,0:T(8,128)S(1)} %slice_select_fusion.1), channel_id=1, source_target_pairs={{0,256},{128,384},{256,0},{384,128},{1,257},{129,385},{257,1},{385... | collective-permute-start | bytes 393224 | tf_op jit(solution)/shard_map/ppermute | solution.py:30
  186.5 36.4 %all-to-all-start.5 = ((bf16[64,128,128]{2,1,0:T(8,128)(2,1)}), bf16[64,128,128]{2,1,0:T(8,128)(2,1)S(1)}, u32[]{:S(2)}, u32[]{:S(2)}) async-start(bf16[64,128,128]{2,1,0:T(8,128)(2,1)} %tile_products.2), calls=%async_computation.5 | async-start | bytes 4194304 | tf_op jit(solution)/shard_map/all_to_all | solution.py:367
  190.9 9.1 %collective-permute-start.12 = (bf16[384,128]{1,0:T(8,128)(2,1)S(1)}, bf16[384,128]{1,0:T(8,128)(2,1)S(1)}, u32[]{:S(2)}, u32[]{:S(2)}) collective-permute-start(bf16[384,128]{1,0:T(8,128)(2,1)S(1)} %get-tuple-element.43), channel_id=1, source_target_pairs={{0,5},{1,6},{2,7},{3,0},{4,1},{5,2},{6,3},{7,4},{8,13},{9,14},{10,... | collective-permute-start | bytes 294920 | tf_op jit(solution)/shard_map/ppermute | solution.py:212
  194.4 13.1 %collective-permute-start.11 = (bf16[384,128]{1,0:T(8,128)(2,1)S(1)}, bf16[384,128]{1,0:T(8,128)(2,1)S(1)}, u32[]{:S(2)}, u32[]{:S(2)}) collective-permute-start(bf16[384,128]{1,0:T(8,128)(2,1)S(1)} %get-tuple-element.43), channel_id=1, source_target_pairs={{0,3},{1,4},{2,5},{3,6},{4,7},{5,0},{6,1},{7,2},{8,11},{9,12},{10,... | collective-permute-start | bytes 294920 | tf_op jit(solution)/shard_map/ppermute | solution.py:212
  198.0 16.1 %collective-permute-start.15 = (f32[32,512]{1,0:T(8,128)S(1)}, f32[32,512]{1,0:T(8,128)S(1)}, u32[]{:S(2)}, u32[]{:S(2)}) collective-permute-start(f32[32,512]{1,0:T(8,128)S(1)} %slice_select_fusion.2), channel_id=1, source_target_pairs={{0,16},{16,0},{32,48},{48,32},{64,80},{80,64},{96,112},{112,96},{1... | collective-permute-start | bytes 196616 | tf_op jit(solution)/shard_map/ppermute | solution.py:30
  207.6 10.6 %collective-permute-start.13 = (bf16[3,384,128]{2,1,0:T(8,128)(2,1)S(1)}, bf16[3,384,128]{2,1,0:T(8,128)(2,1)S(1)}, u32[]{:S(2)}, u32[]{:S(2)}) collective-permute-start(bf16[3,384,128]{2,1,0:T(8,128)(2,1)S(1)} %pad_maximum_fusion.1), channel_id=1, source_target_pairs={{0,1},{1,2},{2,3},{3,4},{4,5},{5,6},{6,7},{7,0},{8,9},{9,10},{10,1... | collective-permute-start | bytes 884744 | tf_op jit(solution)/shard_map/ppermute | solution.py:212
  209.5 7.5 %collective-permute-start.14 = (bf16[2,384,128]{2,1,0:T(8,128)(2,1)S(1)}, bf16[2,384,128]{2,1,0:T(8,128)(2,1)S(1)}, u32[]{:S(2)}, u32[]{:S(2)}) collective-permute-start(bf16[2,384,128]{2,1,0:T(8,128)(2,1)S(1)} %pad_maximum_fusion.3), channel_id=1, source_target_pairs={{0,7},{1,0},{2,1},{3,2},{4,3},{5,4},{6,5},{7,6},{8,15},{9,8},{10,9... | collective-permute-start | bytes 589832 | tf_op jit(solution)/shard_map/ppermute | solution.py:212
  222.9 33.8 %all-to-all-start.6 = ((bf16[64,128,128]{2,1,0:T(8,128)(2,1)}), bf16[64,128,128]{2,1,0:T(8,128)(2,1)}, u32[]{:S(2)}, u32[]{:S(2)}) async-start(bf16[64,128,128]{2,1,0:T(8,128)(2,1)} %tile_products.3), calls=%async_computation.6 | async-start | bytes 4194304 | tf_op jit(solution)/shard_map/all_to_all | solution.py:373
  229.2 6.6 %collective-permute-start.16 = (f32[32,512]{1,0:T(8,128)S(1)}, f32[32,512]{1,0:T(8,128)S(1)}, u32[]{:S(2)}, u32[]{:S(2)}) collective-permute-start(f32[32,512]{1,0:T(8,128)S(1)} %select_add_fusion.3), channel_id=1, source_target_pairs={{0,32},{16,48},{32,0},{48,16},{64,96},{80,112},{96,64},{112,80},{1... | collective-permute-start | bytes 196616 | tf_op jit(solution)/shard_map/ppermute | solution.py:30
  235.8 9.0 %collective-permute-start.17 = (f32[32,512]{1,0:T(8,128)S(1)}, f32[32,512]{1,0:T(8,128)S(1)}, u32[]{:S(2)}, u32[]{:S(2)}) collective-permute-start(f32[32,512]{1,0:T(8,128)S(1)} %add.368), channel_id=1, source_target_pairs={{0,64},{16,80},{32,96},{48,112},{64,0},{80,16},{96,32},{112,48},{1... | collective-permute-start | bytes 196616 | tf_op jit(solution)/shard_map/ppermute | solution.py:30
  249.9 6.8 %collective-permute-start.19 = (f32[32,512]{1,0:T(8,128)S(1)}, f32[32,512]{1,0:T(8,128)S(1)}, u32[]{:S(2)}, u32[]{:S(2)}) collective-permute-start(f32[32,512]{1,0:T(8,128)S(1)} %add.370), channel_id=1, source_target_pairs={{0,16},{16,0},{32,48},{48,32},{64,80},{80,64},{96,112},{112,96},{1... | collective-permute-start | bytes 196616 | tf_op jit(solution)/shard_map/ppermute | solution.py:30
  261.7 51.9 %all-to-all-start.7 = ((bf16[8,384,256]{2,1,0:T(8,128)(2,1)}), bf16[8,384,256]{2,1,0:T(8,128)(2,1)S(1)}, u32[]{:S(2)}, u32[]{:S(2)}) async-start(bf16[8,384,256]{2,1,0:T(8,128)(2,1)} %bitcast.34), calls=%async_computation.7 | async-start | bytes 3145728 | tf_op jit(solution)/shard_map/all_to_all | solution.py:381
  266.8 8.0 %collective-permute-start.20 = (f32[64,512]{1,0:T(8,128)S(1)}, f32[64,512]{1,0:T(8,128)S(1)}, u32[]{:S(2)}, u32[]{:S(2)}) collective-permute-start(f32[64,512]{1,0:T(8,128)S(1)} %maximum_select_fusion.2), channel_id=1, source_target_pairs={{0,2},{1,3},{2,0},{3,1},{4,6},{5,7},{6,4},{7,5},{8,10},{9,11},{10,... | collective-permute-start | bytes 393224 | tf_op jit(solution)/shard_map/ppermute | solution.py:30
  274.9 11.0 %collective-permute-start.21 = (f32[64,512]{1,0:T(8,128)S(1)}, f32[64,512]{1,0:T(8,128)S(1)}, u32[]{:S(2)}, u32[]{:S(2)}) collective-permute-start(f32[64,512]{1,0:T(8,128)S(1)} %add.372), channel_id=1, source_target_pairs={{0,4},{1,5},{2,6},{3,7},{4,0},{5,1},{6,2},{7,3},{8,12},{9,13},{10,... | collective-permute-start | bytes 393224 | tf_op jit(solution)/shard_map/ppermute | solution.py:30
  285.9 7.5 %collective-permute-start.22 = (f32[64,512]{1,0:T(8,128)S(1)}, f32[64,512]{1,0:T(8,128)S(1)}, u32[]{:S(2)}, u32[]{:S(2)}) collective-permute-start(f32[64,512]{1,0:T(8,128)S(1)} %add_multiply_fusion), channel_id=1, source_target_pairs={{0,256},{128,384},{256,0},{384,128},{1,257},{129,385},{257,1},{385... | collective-permute-start | bytes 393224 | tf_op jit(solution)/shard_map/ppermute | solution.py:30
  293.4 8.8 %collective-permute-start.23 = (f32[128,512]{1,0:T(8,128)S(1)}, f32[128,512]{1,0:T(8,128)S(1)}, u32[]{:S(2)}, u32[]{:S(2)}) collective-permute-start(f32[128,512]{1,0:T(8,128)S(1)} %maximum_select_fusion.1), channel_id=1, source_target_pairs={{0,128},{128,0},{256,384},{384,256},{1,129},{129,1},{257,385},{385... | collective-permute-start | bytes 786440 | tf_op jit(solution)/shard_map/ppermute | solution.py:30
  302.3 10.2 %collective-permute-start.24 = (f32[256,512]{1,0:T(8,128)S(1)}, f32[256,512]{1,0:T(8,128)S(1)}, u32[]{:S(2)}, u32[]{:S(2)}) collective-permute-start(f32[256,512]{1,0:T(8,128)S(1)} %maximum_select_fusion), channel_id=1, source_target_pairs={{0,8},{8,0},{1,9},{9,1},{2,10},{10,2},{3,11},{11,3},{4,12},{12,4},... | collective-permute-start | bytes 1572872 | tf_op jit(solution)/shard_map/ppermute | solution.py:389
  (22 other events, 272.5 us)

commit v9 on v7

--- a/solution.py
+++ b/solution.py
@@ -74,28 +74,28 @@
 
 
 def products_kernel(offset_ref, mask_ref, block_ref, out_ref):
-    step = pl.program_id(0)
-    for t in range(STEP):
+    first = pl.program_id(0) * len(mask_ref)
+    for t in range(len(mask_ref)):
         out_ref[t] = jnp.dot(
             mask_ref[t],
-            block_ref[offset_ref[step * STEP + t]],
+            block_ref[offset_ref[first + t]],
             preferred_element_type=jnp.float32,
         ).astype(out_ref.dtype)
 
 
-def tile_products(offsets, masks, blocks):
+def tile_products(offsets, masks, blocks, step):
     slots, tile, _ = masks.shape
     n, _, width = blocks.shape
     return pl.pallas_call(
         products_kernel,
         grid_spec=pltpu.PrefetchScalarGridSpec(
             num_scalar_prefetch=1,
-            grid=(slots // STEP,),
+            grid=(slots // step,),
             in_specs=[
-                pl.BlockSpec((STEP, tile, tile), lambda i, o: (i, 0, 0)),
+                pl.BlockSpec((step, tile, tile), lambda i, o: (i, 0, 0)),
                 pl.BlockSpec((n, tile, width), lambda i, o: (0, 0, 0)),
             ],
-            out_specs=pl.BlockSpec((STEP, tile, width), lambda i, o: (i, 0, 0)),
+            out_specs=pl.BlockSpec((step, tile, width), lambda i, o: (i, 0, 0)),
         ),
         out_shape=jax.ShapeDtypeStruct((slots, tile, width), jnp.bfloat16),
         cost_estimate=pl.CostEstimate(
@@ -115,26 +115,26 @@
     def _():
         total_ref[...] = jnp.zeros_like(total_ref)
 
-    for t in range(STEP):
-        total_ref[offset_ref[step * STEP + t]] += part_ref[t].astype(jnp.float32)
+    for t in range(len(part_ref)):
+        total_ref[offset_ref[step * len(part_ref) + t]] += part_ref[t].astype(jnp.float32)
 
     @pl.when(step == pl.num_programs(0) - 1)
     def _():
         out_ref[...] = total_ref[...].astype(out_ref.dtype)
 
 
-def summed_into(offsets, parts, blocks):
+def summed_into(offsets, parts, blocks, step, dtype):
     slots, tile, width = parts.shape
     return pl.pallas_call(
         gathered_kernel,
         grid_spec=pltpu.PrefetchScalarGridSpec(
             num_scalar_prefetch=1,
-            grid=(slots // STEP,),
-            in_specs=[pl.BlockSpec((STEP, tile, width), lambda i, o: (i, 0, 0))],
+            grid=(slots // step,),
+            in_specs=[pl.BlockSpec((step, tile, width), lambda i, o: (i, 0, 0))],
             out_specs=pl.BlockSpec((blocks, tile, width), lambda i, o: (0, 0, 0)),
             scratch_shapes=[pltpu.VMEM((blocks, tile, width), jnp.float32)],
         ),
-        out_shape=jax.ShapeDtypeStruct((blocks, tile, width), jnp.bfloat16),
+        out_shape=jax.ShapeDtypeStruct((blocks, tile, width), dtype),
         cost_estimate=pl.CostEstimate(
             flops=slots * tile * width, bytes_accessed=slots * tile * width * 2, transcendentals=0
         ),
@@ -256,40 +256,58 @@
         tiled=True,
     ).reshape(z_total * blocks_here, TILE, half_in)
 
-    def passed_tiles(table):
-        table = table.reshape(x_total, z_total, core_total, rep_total, dom_total)
-        table = lax.dynamic_slice(
-            table, (0, z_here, 0, rep_here, 0), (x_total, 1, core_total, 1, dom_total)
-        ).reshape(x_total * core_total, x_total, z_total, core_total)
-        table = lax.dynamic_slice_in_dim(table, x_here, 1, 1)
-        return lax.dynamic_slice_in_dim(table, core, 1, 3).reshape(-1)
-
-    passed_cols = passed_tiles(tile_col)
-    place = jnp.tile(jnp.arange(z_total), x_total * core_total)
+    groups = x_total * core_total
+
+    def by_distance(table):
+        table = lax.dynamic_slice_in_dim(jnp.concatenate([table, table], axis=1), z_here, z_total, 1)
+        table = jnp.stack([table[:, d % z_total] for d in DISTANCES], axis=2)
+        return table.reshape(groups, z_total)
+
+    table = tile_col.reshape(x_total, z_total, core_total, rep_total, dom_total)
+    table = lax.dynamic_slice(
+        table, (0, z_here, 0, rep_here, 0), (x_total, 1, core_total, 1, dom_total)
+    ).reshape(groups, x_total, z_total, core_total)
+    table = lax.dynamic_slice_in_dim(table, x_here, 1, 1)
+    table = lax.dynamic_slice_in_dim(table, core, 1, 3).reshape(groups, z_total)
+    table = lax.dynamic_slice_in_dim(jnp.concatenate([table, table], axis=1), z_here, z_total, 1)
+    passed_cols = jnp.stack([table[:, d % z_total] for d in DISTANCES], axis=1)
+    place = (z_here + jnp.array(DISTANCES)[None, :]) % z_total
     passed_first = ((x_here * z_total + place) * core_total + core) * group_blocks
     passed_first = passed_first + rep_here * blocks_here
     passed_block = jnp.where(passed_cols >= 0, passed_cols - passed_first, 0)
-    passed_offset = place * blocks_here + passed_block
-    passed_near = place_of(place, z_here) * blocks_here + passed_block
+    passed_offset = (place * blocks_here + passed_block).reshape(-1)
+    near = jnp.arange(z_total)[None, :] * blocks_here
+    passed_near = (near + passed_block).reshape(-1)
 
     def held_tiles(table):
         row = lax.dynamic_slice(table, (dom_here, rep_here, 0), (1, 1, dom_total))
-        return row.reshape(x_total, z_total, core_total).swapaxes(1, 2).reshape(-1)
+        return by_distance(row.reshape(x_total, z_total, core_total))
 
     held_rows = held_tiles(tile_row)
     held_there = held_rows >= 0
     held_block = jnp.where(held_there, held_rows, 0)
     held_cols = jnp.where(held_there, held_tiles(tile_col), 0)
     held_limits = jnp.where(held_there, held_tiles(tile_count), 0)
-    held_offset = jnp.where(held_there, held_block - group_first, 0)
-    row_ids, col_ids = id_blocks[held_block], id_blocks[held_cols]
-    masks = edge_masks(row_ids, col_ids, held_limits, False)
-    masks_swapped = edge_masks(row_ids, col_ids, held_limits, True)
-
+    held_place = jnp.where(held_there, held_block - group_first, 0)
+    row_ids, col_ids = id_blocks[held_block.reshape(-1)], id_blocks[held_cols.reshape(-1)]
+    masks = edge_masks(row_ids, col_ids, held_limits.reshape(-1), False)
+    held_offset = held_place.reshape(-1)
+
+    def masks_of(part):
+        ids = [x.reshape(groups, z_total, TILE)[:, part].reshape(-1, TILE) for x in (row_ids, col_ids)]
+        return edge_masks(*ids, held_limits[:, part].reshape(-1), True)
+
+    one, three = slice(3, None), slice(0, 3)
+    masks_one, masks_three = masks_of(one), masks_of(three)
+    place_one, place_three = (held_place[:, part].reshape(-1) for part in (one, three))
+    back_one = (near[:, three.stop :] - three.stop * blocks_here + passed_block[:, one]).reshape(-1)
+    back_three = (near[:, three] + passed_block[:, three]).reshape(-1)
     held_owner = held_offset // blocks_here
     held_near = place_of(held_owner, rep_here) * blocks_here + held_offset % blocks_here
 
-    column_1, masks, masks_swapped = lax.optimization_barrier((column_1, masks, masks_swapped))
+    column_1, masks, masks_one, masks_three = lax.optimization_barrier(
+        (column_1, masks, masks_one, masks_three)
+    )
     leaving_1 = picked(passed_offset, column_1)
     leaving_1, second = lax.optimization_barrier((leaving_1, node_feats[:, half_in:]))
     arrived_1 = lax.all_to_all(leaving_1, ("x", "core"), 0, 0, tiled=True)
@@ -299,12 +317,13 @@
     arrived_2 = lax.all_to_all(leaving_2, ("x", "core"), 0, 0, tiled=True)
     sums_1 = tile_sums(held_near, masks, arrived_1, group_blocks)
     own_1, low_1, high_1 = sum_of_eight(sums_1.reshape(rep_total, rows_here, half_in), "rep")
-    arrived_2, low_1, high_1 = lax.optimization_barrier((arrived_2, low_1, high_1))
-    summed_1 = own_1 + low_1.astype(jnp.float32) + high_1.astype(jnp.float32)
+    arrived_2, low_1 = lax.optimization_barrier((arrived_2, low_1))
     sums_2 = tile_sums(held_offset, masks, arrived_2, group_blocks)
+    sums_2, high_1 = lax.optimization_barrier((sums_2, high_1))
     pieces = lax.all_to_all(
         sums_2.reshape(rep_total, rows_here, half_in), "rep", 0, 0, tiled=True
     )
+    summed_1 = own_1 + low_1.astype(jnp.float32) + high_1.astype(jnp.float32)
     summed = jnp.concatenate([summed_1, pieces.astype(jnp.float32).sum(axis=0)], axis=1)
 
     own_first = group_first + rep_here * blocks_here
@@ -345,20 +364,33 @@
         share = halved(share, axis, bit)
     share = share + pair_swap(share, "z", 2)
 
-    returning = tile_products(held_offset, masks_swapped, group_spread)
-    returning, group_spread, share = lax.optimization_barrier((returning, group_spread, share))
-    returned = lax.all_to_all(returning, ("x", "core"), 0, 0, tiled=True)
+    returning_1 = tile_products(place_one, masks_one, group_spread, 20)
+    returning_1, group_spread, share = lax.optimization_barrier((returning_1, group_spread, share))
+    returned_1 = lax.all_to_all(returning_1, ("x", "core"), 0, 0, tiled=True)
+    returning_2 = tile_products(place_three, masks_three, group_spread, 24)
     for axis, bit in (("z", 4), ("rep", 1), ("rep", 2), ("rep", 4)):
         share = share + pair_swap(share, axis, bit)
     share = share * (1.0 / math.sqrt(rows_here * dom_total * rep_total))
     share = doubled(share, "z", 1)
-    column_sums = summed_into(passed_offset, returned, z_total * blocks_here)
-    column_sums, share = lax.optimization_barrier((column_sums, share))
-    parts = lax.all_to_all(
-        column_sums.reshape(z_total, rows_here, width_in), "z", 0, 0, tiled=True
-    )
+
+    returned_1, returning_2, share = lax.optimization_barrier((returned_1, returning_2, share))
+    returned_2 = lax.all_to_all(returning_2, ("x", "core"), 0, 0, tiled=True)
+    column = summed_into(back_one, returned_1, 5 * blocks_here, 20, jnp.bfloat16)
+    column = column.reshape(5, rows_here, width_in)
+    above, below = shifted(column[:3], "z", -1), shifted(column[3:], "z", 1)
+    returned_2, above, below, share = lax.optimization_barrier((returned_2, above, below, share))
+    column = summed_into(back_three, returned_2, 3 * blocks_here, 24, jnp.float32)
+    column = column.reshape(3, rows_here, width_in)
+
+    low = column[0] + above[0].astype(jnp.float32) + below[0].astype(jnp.float32)
+    high = column[2] + above[2].astype(jnp.float32)
+    low, high, share = lax.optimization_barrier(
+        (low.astype(jnp.bfloat16), high.astype(jnp.bfloat16), share)
+    )
+    low, high = shifted(low, "z", -3), shifted(high, "z", 3)
     for bit in (2, 1):
         share = doubled(share, "x", bit)
+    share, low, high = lax.optimization_barrier((share, low, high))
     other = lax.ppermute(share, "core", [(0, 1), (1, 0)])
     self_grad = jnp.where(first, share, other)
     neigh_grad = jnp.where(first, other, share)
@@ -366,7 +398,8 @@
     self_back = lax.dot_general(
         pre_grad, self_weight, over_cols, preferred_element_type=jnp.float32
     )
-    transposed = parts.astype(jnp.float32).sum(axis=0)
+    transposed = column[1] + above[1].astype(jnp.float32) + below[1].astype(jnp.float32)
+    transposed = transposed + low.astype(jnp.float32) + high.astype(jnp.float32)
     feat_grad = (self_back + transposed).astype(jnp.bfloat16)
     return (hidden_out, feat_grad, self_grad, neigh_grad)
 

time: 311 us -> 324 us (1.042)
  waiting for transfers between devices: 117 us -> 102 us
  starting transfers between devices: 128 us -> 138 us
  local copies, waits for them, and re-layouts: 15.1 us -> 23.1 us
  other arithmetic: 16.2 us -> 23.9 us
    all_to_all x2, waiting for transfers between devices: 30.2 us -> 0.01 us  [the longest x1 0.01 us: shards(): returned_2 = lax.all_to_all(returning_2, ('x', 'core'), 0, 0, tiled=True)]
    ppermute x8 -> x12, waiting for transfers between devices: 23.1 us -> 50.3 us  [shifted(): return lax.ppermute(x, axis, [(i, (i + by) % n) for i in range(n)])]
    ppermute x8 -> x12, starting transfers between devices: 28.9 us -> 44 us  [shifted(): return lax.ppermute(x, axis, [(i, (i + by) % n) for i in range(n)])]
    all_to_all x1, waiting for transfers between devices: 6.25 us -> 0.01 us  [shards(): lax.all_to_all(jnp.broadcast_to(node_feats[None, :, :half_in], (z_total,...]
    ppermute x11, waiting for transfers between devices: 36.2 us -> 30 us  [pair_swap(): return lax.ppermute(x, axis, [(i, i ^ bit) for i in range(n)])]
    slice x0 -> x40, local copies, waits for them, and re-layouts: none -> 3.37 us  [the longest x27 2.87 us: by_distance(): table = jnp.stack([table[:, d % z_total] for d in DISTANCES], axis=2)]
    pallas_call x1 -> x2, Pallas kernels: 5.16 us -> 8.44 us  [tile_products(): pl.pallas_call(products_kernel, grid_spec=pltpu.PrefetchScalarGridSpec(nu...]
    convert_element_type x1 -> x3, other arithmetic: 10.8 us -> 13.9 us  [edge_masks(): return (hashed < limits[:, None, None]).astype(jnp.bfloat16)]
  transfers between devices with their start and end apart: 28 -> 32, of which waited for: 22 -> 22; matrix products, arithmetic and copies ran while one was open for 9% -> 13% of each run, Pallas kernels for 2% -> 5%
where the time goes in v9:
time: 324 us; the launch traced here: 321 us
  starting transfers between devices  138 us (43%)
  waiting for transfers between devices  102 us (31%)
  Pallas kernels  25.6 us (8%)
  other arithmetic  23.9 us (7%)
  local copies, waits for them, and re-layouts  23.1 us (7%)
  matrix products  6.88 us (2%)
    ppermute x12, waiting for transfers between devices, shifted(): return lax.ppermute(x, axis, [(i, (i + by) % n) for i in range(n)])  50.3 us
    ppermute x12, starting transfers between devices, shifted(): return lax.ppermute(x, axis, [(i, (i + by) % n) for i in range(n)])  44 us
    ppermute x11, starting transfers between devices, pair_swap(): return lax.ppermute(x, axis, [(i, i ^ bit) for i in range(n)])  41.3 us
    ppermute x11, waiting for transfers between devices, pair_swap(): return lax.ppermute(x, axis, [(i, i ^ bit) for i in range(n)])  30 us
    all_to_all x1, waiting for transfers between devices, shards(): lax.all_to_all(sums_2.reshape(rep_total, rows_here, half_in), 'rep', 0, 0...  19.4 us
    convert_element_type x3, other arithmetic, edge_masks(): return (hashed < limits[:, None, None]).astype(jnp.bfloat16)  13.9 us
    all_to_all x1, starting transfers between devices, shards(): lax.all_to_all(jnp.broadcast_to(node_feats[None, :, :half_in], (z_total,...  10.9 us
    pallas_call x2, Pallas kernels, tile_products(): pl.pallas_call(products_kernel, grid_spec=pltpu.PrefetchScalarGridSpec(nu...  8.44 us
  transfers between devices with their start and end apart: 32, of which 22 were waited for; matrix products, arithmetic and copies ran while one was open for 13% of the time, Pallas kernels for 5%

profile of v9, /device:TPU:1, one launch (start us, length us, event | category | flops | bytes accessed | tf_op | source)
XLA Modules:
  0.0 321.1 jit_solution(17663735595960756582)
XLA Ops:
  2.7 10.9 %all-to-all-start = ((bf16[8,384,128]{2,1,0:T(8,128)(2,1)}), bf16[8,384,128]{2,1,0:T(8,128)(2,1)}, u32[]{:S(2)}, u32[]{:S(2)}) async-start(bf16[8,384,128]{2,1,0:T(8,128)(2,1)} %broadcast_in_dim.73), calls=%async_computation | async-start | bytes 1572864 | tf_op jit(solution)/shard_map/all_to_all | solution.py:251
  29.6 5.5 %fusion.11.mask_ref = bf16[40,128,128]{2,1,0:T(8,128)(2,1)} fusion(s32[40]{0:T(128)S(1)} %lt.167, s32[40,128]{1,0:T(8,128)S(1)} %get-tuple-element.91, s32[40,128]{1,0:T(8,128)S(1)} %get-tuple-element.90, s32[40,128]{1,0:T(8,128)S(1)} %add_select_fusion.9), kind=kLoop, calls=%fused_computation.23 | loop fusion | flops 14417920 | bytes 1372320 | tf_op jit(solution)/shard_map/convert_element_type | solution.py:25
  35.0 5.0 %fusion.5.mask_ref = bf16[64,128,128]{2,1,0:T(8,128)(2,1)S(1)} fusion(s32[64]{0:T(128)S(1)} %get-tuple-element.128, s32[64,128]{1,0:T(8,128)S(1)} %get-tuple-element.89, s32[64,128]{1,0:T(8,128)S(1)} %get-tuple-element.88, s32[64,128]{1,0:T(8,128)S(1)} %add_select_fusion.7), kind=kLoop, calls=%fused_computation.12 | loop fusion | flops 23068672 | bytes 2195712 | tf_op jit(solution)/shard_map/convert_element_type | solution.py:25
  40.1 3.7 %picked.2 = bf16[64,128,128]{2,1,0:T(8,128)(2,1)} custom-call(s32[64]{0:T(128)} %add.459.offset_ref, bf16[24,128,128]{2,1,0:T(8,128)(2,1)} %bitcast.refs_0_), custom_call_target="tpu_custom_call" | custom-call | bytes 2883584 | tf_op jit(solution)/shard_map/picked/pallas_call | solution.py:177
  43.8 5.3 %all-to-all-start.1 = ((bf16[64,128,128]{2,1,0:T(8,128)(2,1)}), bf16[64,128,128]{2,1,0:T(8,128)(2,1)}, u32[]{:S(2)}, u32[]{:S(2)}) async-start(bf16[64,128,128]{2,1,0:T(8,128)(2,1)} %picked.2), calls=%async_computation.1 | async-start | bytes 4194304 | tf_op jit(solution)/shard_map/all_to_all | solution.py:313
  49.1 6.6 %collective-permute-start.1 = (bf16[384,128]{1,0:T(8,128)(2,1)S(1)}, bf16[384,128]{1,0:T(8,128)(2,1)S(1)}, u32[]{:S(2)}, u32[]{:S(2)}) collective-permute-start(bf16[384,128]{1,0:T(8,128)(2,1)S(1)} %get-tuple-element.38), channel_id=1, source_target_pairs={{0,80},{16,96},{32,112},{48,0},{64,16},{80,32},{96,48},{112,64},{1... | collective-permute-start | bytes 294920 | tf_op jit(solution)/shard_map/ppermute | solution.py:197
  57.7 4.4 %collective-permute-done.1 = bf16[384,128]{1,0:T(8,128)(2,1)S(1)} collective-permute-done((bf16[384,128]{1,0:T(8,128)(2,1)S(1)}, bf16[384,128]{1,0:T(8,128)(2,1)S(1)}, u32[]{:S(2)}, u32[]{:S(2)}) %collective-permute-start.1) | collective-permute-done | bytes 98336 | tf_op jit(solution)/shard_map/ppermute | solution.py:197
  62.0 7.0 %collective-permute-done = bf16[384,128]{1,0:T(8,128)(2,1)S(1)} collective-permute-done((bf16[384,128]{1,0:T(8,128)(2,1)S(1)}, bf16[384,128]{1,0:T(8,128)(2,1)S(1)}, u32[]{:S(2)}, u32[]{:S(2)}) %collective-permute-start) | collective-permute-done | bytes 98336 | tf_op jit(solution)/shard_map/ppermute | solution.py:197
  71.7 4.6 %collective-permute-start.3 = (bf16[2,384,128]{2,1,0:T(8,128)(2,1)}, bf16[2,384,128]{2,1,0:T(8,128)(2,1)S(1)}, u32[]{:S(2)}, u32[]{:S(2)}) collective-permute-start(bf16[2,384,128]{2,1,0:T(8,128)(2,1)} %pad_maximum_fusion.1), channel_id=1, source_target_pairs={{0,112},{16,0},{32,16},{48,32},{64,48},{80,64},{96,80},{112,96},{1... | collective-permute-start | bytes 589832 | tf_op jit(solution)/shard_map/ppermute | solution.py:197
  80.8 3.7 %picked.3 = bf16[64,128,128]{2,1,0:T(8,128)(2,1)} custom-call(s32[64]{0:T(128)} %add.462.offset_ref, bf16[9,128,128]{2,1,0:T(8,128)(2,1)} %bitcast.160, bf16[9,128,128]{2,1,0:T(8,128)(2,1)} %bitcast.11.refs_1_, bf16[6,128,128]{2,1,0:T(8,128)(2,1)} %bitcast.172), custom_call_target="tpu_custom_call" | custom-call | bytes 2883584 | tf_op jit(solution)/shard_map/picked/pallas_call | solution.py:177
  84.5 6.0 %all-to-all-start.2 = ((bf16[64,128,128]{2,1,0:T(8,128)(2,1)}), bf16[64,128,128]{2,1,0:T(8,128)(2,1)}, u32[]{:S(2)}, u32[]{:S(2)}) async-start(bf16[64,128,128]{2,1,0:T(8,128)(2,1)} %picked.3), calls=%async_computation.2 | async-start | bytes 4194304 | tf_op jit(solution)/shard_map/all_to_all | solution.py:317
  93.5 5.1 %collective-permute-start.4 = (bf16[3,384,128]{2,1,0:T(8,128)(2,1)S(1)}, bf16[3,384,128]{2,1,0:T(8,128)(2,1)S(1)}, u32[]{:S(2)}, u32[]{:S(2)}) collective-permute-start(bf16[3,384,128]{2,1,0:T(8,128)(2,1)S(1)} %bitcast.171), channel_id=1, source_target_pairs={{0,7},{1,0},{2,1},{3,2},{4,3},{5,4},{6,5},{7,6},{8,15},{9,8},{10,9... | collective-permute-start | bytes 884744 | tf_op jit(solution)/shard_map/ppermute | solution.py:197
  101.2 6.8 %collective-permute-done.5 = bf16[2,384,128]{2,1,0:T(8,128)(2,1)S(1)} collective-permute-done((bf16[2,384,128]{2,1,0:T(8,128)(2,1)S(1)}, bf16[2,384,128]{2,1,0:T(8,128)(2,1)S(1)}, u32[]{:S(2)}, u32[]{:S(2)}) %collective-permute-start.5) | collective-permute-done | bytes 196640 | tf_op jit(solution)/shard_map/ppermute | solution.py:197
  112.9 3.7 %collective-permute-start.7 = (bf16[384,128]{1,0:T(8,128)(2,1)}, bf16[384,128]{1,0:T(8,128)(2,1)}, u32[]{:S(2)}, u32[]{:S(2)}) collective-permute-start(bf16[384,128]{1,0:T(8,128)(2,1)} %get-tuple-element.84), channel_id=1, source_target_pairs={{0,3},{1,4},{2,5},{3,6},{4,7},{5,0},{6,1},{7,2},{8,11},{9,12},{10,... | collective-permute-start | bytes 294920 | tf_op jit(solution)/shard_map/ppermute | solution.py:197
  123.7 6.1 %all-to-all-start.3 = ((bf16[8,384,128]{2,1,0:T(8,128)(2,1)}), bf16[8,384,128]{2,1,0:T(8,128)(2,1)S(1)}, u32[]{:S(2)}, u32[]{:S(2)}) async-start(bf16[8,384,128]{2,1,0:T(8,128)(2,1)} %bitcast.157), calls=%async_computation.3 | async-start | bytes 1572864 | tf_op jit(solution)/shard_map/all_to_all | solution.py:323
  133.9 19.4 %all-to-all-done.3 = bf16[8,384,128]{2,1,0:T(8,128)(2,1)S(1)} async-done(((bf16[8,384,128]{2,1,0:T(8,128)(2,1)}), bf16[8,384,128]{2,1,0:T(8,128)(2,1)S(1)}, u32[]{:S(2)}, u32[]{:S(2)}) %all-to-all-start.3) | async-done | bytes 786464 | tf_op jit(solution)/shard_map/all_to_all | solution.py:323
  158.6 3.6 %all-to-all-start.4 = ((bf16[8,384,256]{2,1,0:T(8,128)(2,1)}), bf16[8,384,256]{2,1,0:T(8,128)(2,1)S(1)}, u32[]{:S(2)}, u32[]{:S(2)}) async-start(bf16[8,384,256]{2,1,0:T(8,128)(2,1)} %broadcast_in_dim.78), calls=%async_computation.4 | async-start | bytes 3145728 | tf_op jit(solution)/shard_map/all_to_all | solution.py:352
  173.9 6.8 %collective-permute-done.9 = f32[128,512]{1,0:T(8,128)S(1)} collective-permute-done((f32[128,512]{1,0:T(8,128)S(1)}, f32[128,512]{1,0:T(8,128)S(1)}, u32[]{:S(2)}, u32[]{:S(2)}) %collective-permute-start.9) | collective-permute-done | bytes 262176 | tf_op jit(solution)/shard_map/ppermute | solution.py:30
  180.7 4.3 %collective-permute-start.10 = (f32[64,512]{1,0:T(8,128)S(1)}, f32[64,512]{1,0:T(8,128)S(1)}, u32[]{:S(2)}, u32[]{:S(2)}) collective-permute-start(f32[64,512]{1,0:T(8,128)S(1)} %slice_select_fusion.1), channel_id=1, source_target_pairs={{0,256},{128,384},{256,0},{384,128},{1,257},{129,385},{257,1},{385... | collective-permute-start | bytes 393224 | tf_op jit(solution)/shard_map/ppermute | solution.py:30
  201.5 4.4 %tile_products.2 = bf16[40,128,256]{2,1,0:T(8,128)(2,1)} custom-call(s32[40]{0:T(128)} %reshape.369.offset_ref, bf16[40,128,128]{2,1,0:T(8,128)(2,1)} %fusion.11.mask_ref, bf16[24,128,256]{2,1,0:T(8,128)(2,1)} %bitcast.158), custom_call_target="tpu_custom_call" | custom-call | flops 335544320 | bytes 3932160 | tf_op jit(solution)/shard_map/tile_products/pallas_call | solution.py:89
  205.8 7.5 %all-to-all-start.5 = ((bf16[40,128,256]{2,1,0:T(8,128)(2,1)}), bf16[40,128,256]{2,1,0:T(8,128)(2,1)S(1)}, u32[]{:S(2)}, u32[]{:S(2)}) async-start(bf16[40,128,256]{2,1,0:T(8,128)(2,1)} %tile_products.2), calls=%async_computation.5 | async-start | bytes 5242880 | tf_op jit(solution)/shard_map/all_to_all | solution.py:369
  213.4 3.6 %collective-permute-start.13 = (f32[32,512]{1,0:T(8,128)S(1)}, f32[32,512]{1,0:T(8,128)S(1)}, u32[]{:S(2)}, u32[]{:S(2)}) collective-permute-start(f32[32,512]{1,0:T(8,128)S(1)} %add.483), channel_id=1, source_target_pairs={{0,64},{16,80},{32,96},{48,112},{64,0},{80,16},{96,32},{112,48},{1... | collective-permute-start | bytes 196616 | tf_op jit(solution)/shard_map/ppermute | solution.py:30
  217.0 5.9 %collective-permute-done.13 = f32[32,512]{1,0:T(8,128)S(1)} collective-permute-done((f32[32,512]{1,0:T(8,128)S(1)}, f32[32,512]{1,0:T(8,128)S(1)}, u32[]{:S(2)}, u32[]{:S(2)}) %collective-permute-start.13) | collective-permute-done | bytes 65568 | tf_op jit(solution)/shard_map/ppermute | solution.py:30
  228.4 4.3 %collective-permute-start.15 = (f32[32,512]{1,0:T(8,128)S(1)}, f32[32,512]{1,0:T(8,128)S(1)}, u32[]{:S(2)}, u32[]{:S(2)}) collective-permute-start(f32[32,512]{1,0:T(8,128)S(1)} %add.485), channel_id=1, source_target_pairs={{0,2},{1,3},{2,0},{3,1},{4,6},{5,7},{6,4},{7,5},{8,10},{9,11},{10,... | collective-permute-start | bytes 196616 | tf_op jit(solution)/shard_map/ppermute | solution.py:30
  234.6 8.0 %collective-permute-start.16 = (f32[32,512]{1,0:T(8,128)S(1)}, f32[32,512]{1,0:T(8,128)S(1)}, u32[]{:S(2)}, u32[]{:S(2)}) collective-permute-start(f32[32,512]{1,0:T(8,128)S(1)} %add.486), channel_id=1, source_target_pairs={{0,4},{1,5},{2,6},{3,7},{4,0},{5,1},{6,2},{7,3},{8,12},{9,13},{10,... | collective-permute-start | bytes 196616 | tf_op jit(solution)/shard_map/ppermute | solution.py:30
  247.0 4.1 %tile_products.3 = bf16[24,128,256]{2,1,0:T(8,128)(2,1)} custom-call(s32[24]{0:T(128)} %reshape.371.offset_ref, bf16[24,128,128]{2,1,0:T(8,128)(2,1)} %fusion.17.mask_ref, bf16[24,128,256]{2,1,0:T(8,128)(2,1)} %bitcast.159), custom_call_target="tpu_custom_call" | custom-call | flops 201326592 | bytes 2359296 | tf_op jit(solution)/shard_map/tile_products/pallas_call | solution.py:89
  252.1 8.1 %all-to-all-start.6 = ((bf16[24,128,256]{2,1,0:T(8,128)(2,1)}), bf16[24,128,256]{2,1,0:T(8,128)(2,1)}, u32[]{:S(2)}, u32[]{:S(2)}) async-start(bf16[24,128,256]{2,1,0:T(8,128)(2,1)} %tile_products.3), calls=%async_computation.6 | async-start | bytes 3145728 | tf_op jit(solution)/shard_map/all_to_all | solution.py:377
  261.8 5.8 %collective-permute-start.18 = (bf16[3,384,256]{2,1,0:T(8,128)(2,1)S(1)}, bf16[3,384,256]{2,1,0:T(8,128)(2,1)S(1)}, u32[]{:S(2)}, u32[]{:S(2)}) collective-permute-start(bf16[3,384,256]{2,1,0:T(8,128)(2,1)S(1)} %bitcast.163), channel_id=1, source_target_pairs={{0,112},{16,0},{32,16},{48,32},{64,48},{80,64},{96,80},{112,96},{1... | collective-permute-start | bytes 1769480 | tf_op jit(solution)/shard_map/ppermute | solution.py:197
  269.9 11.3 %collective-permute-done.19 = bf16[2,384,256]{2,1,0:T(8,128)(2,1)S(1)} collective-permute-done((bf16[2,384,256]{2,1,0:T(8,128)(2,1)S(1)}, bf16[2,384,256]{2,1,0:T(8,128)(2,1)S(1)}, u32[]{:S(2)}, u32[]{:S(2)}) %collective-permute-start.19) | collective-permute-done | bytes 393248 | tf_op jit(solution)/shard_map/ppermute | solution.py:197
  283.8 4.5 %collective-permute-start.20 = (f32[64,512]{1,0:T(8,128)S(1)}, f32[64,512]{1,0:T(8,128)S(1)}, u32[]{:S(2)}, u32[]{:S(2)}) collective-permute-start(f32[64,512]{1,0:T(8,128)S(1)} %maximum_select_fusion.2), channel_id=1, source_target_pairs={{0,256},{128,384},{256,0},{384,128},{1,257},{129,385},{257,1},{385... | collective-permute-start | bytes 393224 | tf_op jit(solution)/shard_map/ppermute | solution.py:30
  294.0 4.4 %collective-permute-start.22 = (bf16[384,256]{1,0:T(8,128)(2,1)S(1)}, bf16[384,256]{1,0:T(8,128)(2,1)S(1)}, u32[]{:S(2)}, u32[]{:S(2)}) collective-permute-start(bf16[384,256]{1,0:T(8,128)(2,1)S(1)} %get-tuple-element.61), channel_id=1, source_target_pairs={{0,80},{16,96},{32,112},{48,0},{64,16},{80,32},{96,48},{112,64},{1... | collective-permute-start | bytes 589832 | tf_op jit(solution)/shard_map/ppermute | solution.py:197
  304.4 10.9 %collective-permute-done.23 = bf16[384,256]{1,0:T(8,128)(2,1)S(1)} collective-permute-done((bf16[384,256]{1,0:T(8,128)(2,1)S(1)}, bf16[384,256]{1,0:T(8,128)(2,1)S(1)}, u32[]{:S(2)}, u32[]{:S(2)}) %collective-permute-start.23) | collective-permute-done | bytes 196640 | tf_op jit(solution)/shard_map/ppermute | solution.py:197
  (255 shorter events, 118.3 us)
Async XLA Ops:
  2.7 37.4 %all-to-all-start = ((bf16[8,384,128]{2,1,0:T(8,128)(2,1)}), bf16[8,384,128]{2,1,0:T(8,128)(2,1)}, u32[]{:S(2)}, u32[]{:S(2)}) async-start(bf16[8,384,128]{2,1,0:T(8,128)(2,1)} %broadcast_in_dim.73), calls=%async_computation | async-start | bytes 1572864 | tf_op jit(solution)/shard_map/all_to_all | solution.py:251
  43.8 40.7 %all-to-all-start.1 = ((bf16[64,128,128]{2,1,0:T(8,128)(2,1)}), bf16[64,128,128]{2,1,0:T(8,128)(2,1)}, u32[]{:S(2)}, u32[]{:S(2)}) async-start(bf16[64,128,128]{2,1,0:T(8,128)(2,1)} %picked.2), calls=%async_computation.1 | async-start | bytes 4194304 | tf_op jit(solution)/shard_map/all_to_all | solution.py:313
  49.1 12.9 %collective-permute-start.1 = (bf16[384,128]{1,0:T(8,128)(2,1)S(1)}, bf16[384,128]{1,0:T(8,128)(2,1)S(1)}, u32[]{:S(2)}, u32[]{:S(2)}) collective-permute-start(bf16[384,128]{1,0:T(8,128)(2,1)S(1)} %get-tuple-element.38), channel_id=1, source_target_pairs={{0,80},{16,96},{32,112},{48,0},{64,16},{80,32},{96,48},{112,64},{1... | collective-permute-start | bytes 294920 | tf_op jit(solution)/shard_map/ppermute | solution.py:197
  55.7 13.3 %collective-permute-start = (bf16[384,128]{1,0:T(8,128)(2,1)S(1)}, bf16[384,128]{1,0:T(8,128)(2,1)S(1)}, u32[]{:S(2)}, u32[]{:S(2)}) collective-permute-start(bf16[384,128]{1,0:T(8,128)(2,1)S(1)} %get-tuple-element.38), channel_id=1, source_target_pairs={{0,48},{16,64},{32,80},{48,96},{64,112},{80,0},{96,16},{112,32},{1... | collective-permute-start | bytes 294920 | tf_op jit(solution)/shard_map/ppermute | solution.py:197
  69.1 11.3 %collective-permute-start.2 = (bf16[3,384,128]{2,1,0:T(8,128)(2,1)S(1)}, bf16[3,384,128]{2,1,0:T(8,128)(2,1)}, u32[]{:S(2)}, u32[]{:S(2)}) collective-permute-start(bf16[3,384,128]{2,1,0:T(8,128)(2,1)S(1)} %pad_maximum_fusion), channel_id=1, source_target_pairs={{0,16},{16,32},{32,48},{48,64},{64,80},{80,96},{96,112},{112,0},{1... | collective-permute-start | bytes 884744 | tf_op jit(solution)/shard_map/ppermute | solution.py:197
  71.7 8.3 %collective-permute-start.3 = (bf16[2,384,128]{2,1,0:T(8,128)(2,1)}, bf16[2,384,128]{2,1,0:T(8,128)(2,1)S(1)}, u32[]{:S(2)}, u32[]{:S(2)}) collective-permute-start(bf16[2,384,128]{2,1,0:T(8,128)(2,1)} %pad_maximum_fusion.1), channel_id=1, source_target_pairs={{0,112},{16,0},{32,16},{48,32},{64,48},{80,64},{96,80},{112,96},{1... | collective-permute-start | bytes 589832 | tf_op jit(solution)/shard_map/ppermute | solution.py:197
  84.5 35.3 %all-to-all-start.2 = ((bf16[64,128,128]{2,1,0:T(8,128)(2,1)}), bf16[64,128,128]{2,1,0:T(8,128)(2,1)}, u32[]{:S(2)}, u32[]{:S(2)}) async-start(bf16[64,128,128]{2,1,0:T(8,128)(2,1)} %picked.3), calls=%async_computation.2 | async-start | bytes 4194304 | tf_op jit(solution)/shard_map/all_to_all | solution.py:317
  93.5 14.6 %collective-permute-start.4 = (bf16[3,384,128]{2,1,0:T(8,128)(2,1)S(1)}, bf16[3,384,128]{2,1,0:T(8,128)(2,1)S(1)}, u32[]{:S(2)}, u32[]{:S(2)}) collective-permute-start(bf16[3,384,128]{2,1,0:T(8,128)(2,1)S(1)} %bitcast.171), channel_id=1, source_target_pairs={{0,7},{1,0},{2,1},{3,2},{4,3},{5,4},{6,5},{7,6},{8,15},{9,8},{10,9... | collective-permute-start | bytes 884744 | tf_op jit(solution)/shard_map/ppermute | solution.py:197
  98.7 9.4 %collective-permute-start.5 = (bf16[2,384,128]{2,1,0:T(8,128)(2,1)S(1)}, bf16[2,384,128]{2,1,0:T(8,128)(2,1)S(1)}, u32[]{:S(2)}, u32[]{:S(2)}) collective-permute-start(bf16[2,384,128]{2,1,0:T(8,128)(2,1)S(1)} %bitcast.173), channel_id=1, source_target_pairs={{0,1},{1,2},{2,3},{3,4},{4,5},{5,6},{6,7},{7,0},{8,9},{9,10},{10,1... | collective-permute-start | bytes 589832 | tf_op jit(solution)/shard_map/ppermute | solution.py:197
  109.6 10.2 %collective-permute-start.6 = (bf16[384,128]{1,0:T(8,128)(2,1)S(1)}, bf16[384,128]{1,0:T(8,128)(2,1)}, u32[]{:S(2)}, u32[]{:S(2)}) collective-permute-start(bf16[384,128]{1,0:T(8,128)(2,1)S(1)} %get-tuple-element.85), channel_id=1, source_target_pairs={{0,5},{1,6},{2,7},{3,0},{4,1},{5,2},{6,3},{7,4},{8,13},{9,14},{10,... | collective-permute-start | bytes 294920 | tf_op jit(solution)/shard_map/ppermute | solution.py:197
  112.9 10.8 %collective-permute-start.7 = (bf16[384,128]{1,0:T(8,128)(2,1)}, bf16[384,128]{1,0:T(8,128)(2,1)}, u32[]{:S(2)}, u32[]{:S(2)}) collective-permute-start(bf16[384,128]{1,0:T(8,128)(2,1)} %get-tuple-element.84), channel_id=1, source_target_pairs={{0,3},{1,4},{2,5},{3,6},{4,7},{5,0},{6,1},{7,2},{8,11},{9,12},{10,... | collective-permute-start | bytes 294920 | tf_op jit(solution)/shard_map/ppermute | solution.py:197
  123.7 29.7 %all-to-all-start.3 = ((bf16[8,384,128]{2,1,0:T(8,128)(2,1)}), bf16[8,384,128]{2,1,0:T(8,128)(2,1)S(1)}, u32[]{:S(2)}, u32[]{:S(2)}) async-start(bf16[8,384,128]{2,1,0:T(8,128)(2,1)} %bitcast.157), calls=%async_computation.3 | async-start | bytes 1572864 | tf_op jit(solution)/shard_map/all_to_all | solution.py:323
  158.6 41.7 %all-to-all-start.4 = ((bf16[8,384,256]{2,1,0:T(8,128)(2,1)}), bf16[8,384,256]{2,1,0:T(8,128)(2,1)S(1)}, u32[]{:S(2)}, u32[]{:S(2)}) async-start(bf16[8,384,256]{2,1,0:T(8,128)(2,1)} %broadcast_in_dim.78), calls=%async_computation.4 | async-start | bytes 3145728 | tf_op jit(solution)/shard_map/all_to_all | solution.py:352
  164.7 4.1 %collective-permute-start.8 = (f32[256,512]{1,0:T(8,128)}, f32[256,512]{1,0:T(8,128)S(1)}, u32[]{:S(2)}, u32[]{:S(2)}) collective-permute-start(f32[256,512]{1,0:T(8,128)} %get-tuple-element.129), channel_id=1, source_target_pairs={{0,8},{8,0},{1,9},{9,1},{2,10},{10,2},{3,11},{11,3},{4,12},{12,4},... | collective-permute-start | bytes 1572872 | tf_op jit(solution)/shard_map/ppermute | solution.py:360
  171.0 9.6 %collective-permute-start.9 = (f32[128,512]{1,0:T(8,128)S(1)}, f32[128,512]{1,0:T(8,128)S(1)}, u32[]{:S(2)}, u32[]{:S(2)}) collective-permute-start(f32[128,512]{1,0:T(8,128)S(1)} %slice_select_fusion), channel_id=1, source_target_pairs={{0,128},{128,0},{256,384},{384,256},{1,129},{129,1},{257,385},{385... | collective-permute-start | bytes 786440 | tf_op jit(solution)/shard_map/ppermute | solution.py:30
  180.7 7.5 %collective-permute-start.10 = (f32[64,512]{1,0:T(8,128)S(1)}, f32[64,512]{1,0:T(8,128)S(1)}, u32[]{:S(2)}, u32[]{:S(2)}) collective-permute-start(f32[64,512]{1,0:T(8,128)S(1)} %slice_select_fusion.1), channel_id=1, source_target_pairs={{0,256},{128,384},{256,0},{384,128},{1,257},{129,385},{257,1},{385... | collective-permute-start | bytes 393224 | tf_op jit(solution)/shard_map/ppermute | solution.py:30
  188.3 5.0 %collective-permute-start.11 = (f32[32,512]{1,0:T(8,128)S(1)}, f32[32,512]{1,0:T(8,128)S(1)}, u32[]{:S(2)}, u32[]{:S(2)}) collective-permute-start(f32[32,512]{1,0:T(8,128)S(1)} %slice_select_fusion.2), channel_id=1, source_target_pairs={{0,16},{16,0},{32,48},{48,32},{64,80},{80,64},{96,112},{112,96},{1... | collective-permute-start | bytes 196616 | tf_op jit(solution)/shard_map/ppermute | solution.py:30
  193.3 6.9 %collective-permute-start.12 = (f32[32,512]{1,0:T(8,128)S(1)}, f32[32,512]{1,0:T(8,128)S(1)}, u32[]{:S(2)}, u32[]{:S(2)}) collective-permute-start(f32[32,512]{1,0:T(8,128)S(1)} %select_add_fusion.3), channel_id=1, source_target_pairs={{0,32},{16,48},{32,0},{48,16},{64,96},{80,112},{96,64},{112,80},{1... | collective-permute-start | bytes 196616 | tf_op jit(solution)/shard_map/ppermute | solution.py:30
  205.8 46.2 %all-to-all-start.5 = ((bf16[40,128,256]{2,1,0:T(8,128)(2,1)}), bf16[40,128,256]{2,1,0:T(8,128)(2,1)S(1)}, u32[]{:S(2)}, u32[]{:S(2)}) async-start(bf16[40,128,256]{2,1,0:T(8,128)(2,1)} %tile_products.2), calls=%async_computation.5 | async-start | bytes 5242880 | tf_op jit(solution)/shard_map/all_to_all | solution.py:369
  213.4 9.5 %collective-permute-start.13 = (f32[32,512]{1,0:T(8,128)S(1)}, f32[32,512]{1,0:T(8,128)S(1)}, u32[]{:S(2)}, u32[]{:S(2)}) collective-permute-start(f32[32,512]{1,0:T(8,128)S(1)} %add.483), channel_id=1, source_target_pairs={{0,64},{16,80},{32,96},{48,112},{64,0},{80,16},{96,32},{112,48},{1... | collective-permute-start | bytes 196616 | tf_op jit(solution)/shard_map/ppermute | solution.py:30
  222.9 5.5 %collective-permute-start.14 = (f32[32,512]{1,0:T(8,128)S(1)}, f32[32,512]{1,0:T(8,128)S(1)}, u32[]{:S(2)}, u32[]{:S(2)}) collective-permute-start(f32[32,512]{1,0:T(8,128)S(1)} %add.484), channel_id=1, source_target_pairs={{0,1},{1,0},{2,3},{3,2},{4,5},{5,4},{6,7},{7,6},{8,9},{9,8},{10,11... | collective-permute-start | bytes 196616 | tf_op jit(solution)/shard_map/ppermute | solution.py:30
  228.4 6.2 %collective-permute-start.15 = (f32[32,512]{1,0:T(8,128)S(1)}, f32[32,512]{1,0:T(8,128)S(1)}, u32[]{:S(2)}, u32[]{:S(2)}) collective-permute-start(f32[32,512]{1,0:T(8,128)S(1)} %add.485), channel_id=1, source_target_pairs={{0,2},{1,3},{2,0},{3,1},{4,6},{5,7},{6,4},{7,5},{8,10},{9,11},{10,... | collective-permute-start | bytes 196616 | tf_op jit(solution)/shard_map/ppermute | solution.py:30
  234.6 9.7 %collective-permute-start.16 = (f32[32,512]{1,0:T(8,128)S(1)}, f32[32,512]{1,0:T(8,128)S(1)}, u32[]{:S(2)}, u32[]{:S(2)}) collective-permute-start(f32[32,512]{1,0:T(8,128)S(1)} %add.486), channel_id=1, source_target_pairs={{0,4},{1,5},{2,6},{3,7},{4,0},{5,1},{6,2},{7,3},{8,12},{9,13},{10,... | collective-permute-start | bytes 196616 | tf_op jit(solution)/shard_map/ppermute | solution.py:30
  244.4 6.7 %collective-permute-start.17 = (f32[32,512]{1,0:T(8,128)S(1)}, f32[32,512]{1,0:T(8,128)}, u32[]{:S(2)}, u32[]{:S(2)}) collective-permute-start(f32[32,512]{1,0:T(8,128)S(1)} %add_multiply_fusion), channel_id=1, source_target_pairs={{0,16},{16,0},{32,48},{48,32},{64,80},{80,64},{96,112},{112,96},{1... | collective-permute-start | bytes 196616 | tf_op jit(solution)/shard_map/ppermute | solution.py:30
  252.1 29.1 %all-to-all-start.6 = ((bf16[24,128,256]{2,1,0:T(8,128)(2,1)}), bf16[24,128,256]{2,1,0:T(8,128)(2,1)}, u32[]{:S(2)}, u32[]{:S(2)}) async-start(bf16[24,128,256]{2,1,0:T(8,128)(2,1)} %tile_products.3), calls=%async_computation.6 | async-start | bytes 3145728 | tf_op jit(solution)/shard_map/all_to_all | solution.py:377
  261.8 19.4 %collective-permute-start.18 = (bf16[3,384,256]{2,1,0:T(8,128)(2,1)S(1)}, bf16[3,384,256]{2,1,0:T(8,128)(2,1)S(1)}, u32[]{:S(2)}, u32[]{:S(2)}) collective-permute-start(bf16[3,384,256]{2,1,0:T(8,128)(2,1)S(1)} %bitcast.163), channel_id=1, source_target_pairs={{0,112},{16,0},{32,16},{48,32},{64,48},{80,64},{96,80},{112,96},{1... | collective-permute-start | bytes 1769480 | tf_op jit(solution)/shard_map/ppermute | solution.py:197
  267.7 13.5 %collective-permute-start.19 = (bf16[2,384,256]{2,1,0:T(8,128)(2,1)S(1)}, bf16[2,384,256]{2,1,0:T(8,128)(2,1)S(1)}, u32[]{:S(2)}, u32[]{:S(2)}) collective-permute-start(bf16[2,384,256]{2,1,0:T(8,128)(2,1)S(1)} %bitcast.168), channel_id=1, source_target_pairs={{0,16},{16,32},{32,48},{48,64},{64,80},{80,96},{96,112},{112,0},{1... | collective-permute-start | bytes 1179656 | tf_op jit(solution)/shard_map/ppermute | solution.py:197
  283.8 7.2 %collective-permute-start.20 = (f32[64,512]{1,0:T(8,128)S(1)}, f32[64,512]{1,0:T(8,128)S(1)}, u32[]{:S(2)}, u32[]{:S(2)}) collective-permute-start(f32[64,512]{1,0:T(8,128)S(1)} %maximum_select_fusion.2), channel_id=1, source_target_pairs={{0,256},{128,384},{256,0},{384,128},{1,257},{129,385},{257,1},{385... | collective-permute-start | bytes 393224 | tf_op jit(solution)/shard_map/ppermute | solution.py:30
  291.1 10.1 %collective-permute-start.21 = (f32[128,512]{1,0:T(8,128)S(1)}, f32[128,512]{1,0:T(8,128)S(1)}, u32[]{:S(2)}, u32[]{:S(2)}) collective-permute-start(f32[128,512]{1,0:T(8,128)S(1)} %maximum_select_fusion.1), channel_id=1, source_target_pairs={{0,128},{128,0},{256,384},{384,256},{1,129},{129,1},{257,385},{385... | collective-permute-start | bytes 786440 | tf_op jit(solution)/shard_map/ppermute | solution.py:30
  294.0 10.4 %collective-permute-start.22 = (bf16[384,256]{1,0:T(8,128)(2,1)S(1)}, bf16[384,256]{1,0:T(8,128)(2,1)S(1)}, u32[]{:S(2)}, u32[]{:S(2)}) collective-permute-start(bf16[384,256]{1,0:T(8,128)(2,1)S(1)} %get-tuple-element.61), channel_id=1, source_target_pairs={{0,80},{16,96},{32,112},{48,0},{64,16},{80,32},{96,48},{112,64},{1... | collective-permute-start | bytes 589832 | tf_op jit(solution)/shard_map/ppermute | solution.py:197
  298.4 16.9 %collective-permute-start.23 = (bf16[384,256]{1,0:T(8,128)(2,1)S(1)}, bf16[384,256]{1,0:T(8,128)(2,1)S(1)}, u32[]{:S(2)}, u32[]{:S(2)}) collective-permute-start(bf16[384,256]{1,0:T(8,128)(2,1)S(1)} %get-tuple-element.62), channel_id=1, source_target_pairs={{0,48},{16,64},{32,80},{48,96},{64,112},{80,0},{96,16},{112,32},{1... | collective-permute-start | bytes 589832 | tf_op jit(solution)/shard_map/ppermute | solution.py:197
  315.4 4.7 %collective-permute-start.24 = (f32[256,512]{1,0:T(8,128)S(1)}, f32[256,512]{1,0:T(8,128)S(1)}, u32[]{:S(2)}, u32[]{:S(2)}) collective-permute-start(f32[256,512]{1,0:T(8,128)S(1)} %maximum_select_fusion), channel_id=1, source_target_pairs={{0,8},{8,0},{1,9},{9,1},{2,10},{10,2},{3,11},{11,3},{4,12},{12,4},... | collective-permute-start | bytes 1572872 | tf_op jit(solution)/shard_map/ppermute | solution.py:394
  (17 other events, 165.4 us)

commit v10 on v7

--- a/solution.py
+++ b/solution.py
@@ -144,29 +144,18 @@
 
 
 def pick_kernel(offset_ref, *refs):
-    *piece_refs, out_ref, held_ref, in_sems, out_sems = refs
-    first = 0
-    copies = []
-    for piece in piece_refs:
-        count = piece.shape[0]
-        copies.append(
-            pltpu.make_async_copy(
-                piece, held_ref.at[pl.ds(first, count)], in_sems.at[len(copies)]
-            )
-        )
-        first += count
-    for copy in copies:
-        copy.start()
-    for copy in copies:
-        copy.wait()
-    copies = [
-        pltpu.make_async_copy(held_ref.at[offset_ref[t]], out_ref.at[t], out_sems.at[t])
-        for t in range(out_ref.shape[0])
-    ]
-    for copy in copies:
-        copy.start()
-    for copy in copies:
-        copy.wait()
+    *piece_refs, out_ref, held_ref = refs
+    step = pl.program_id(0)
+
+    @pl.when(step == 0)
+    def _():
+        first = 0
+        for piece in piece_refs:
+            held_ref[first : first + len(piece)] = piece[...]
+            first += len(piece)
+
+    for t in range(STEP):
+        out_ref[t] = held_ref[offset_ref[step * STEP + t]]
 
 
 def picked(offsets, *pieces):
@@ -176,18 +165,18 @@
     dtype = pieces[0].dtype
     return pl.pallas_call(
         pick_kernel,
-        in_specs=[pl.BlockSpec(memory_space=pltpu.SMEM)]
-        + [pl.BlockSpec(memory_space=pl.ANY)] * len(pieces),
-        out_specs=pl.BlockSpec(memory_space=pl.ANY),
-        scratch_shapes=[
-            pltpu.VMEM((n, tile, width), dtype),
-            pltpu.SemaphoreType.DMA((len(pieces),)),
-            pltpu.SemaphoreType.DMA((slots,)),
-        ],
+        grid_spec=pltpu.PrefetchScalarGridSpec(
+            num_scalar_prefetch=1,
+            grid=(slots // STEP,),
+            in_specs=[pl.BlockSpec(piece.shape, lambda i, o: (0, 0, 0)) for piece in pieces],
+            out_specs=pl.BlockSpec((STEP, tile, width), lambda i, o: (i, 0, 0)),
+            scratch_shapes=[pltpu.VMEM((n, tile, width), dtype)],
+        ),
         out_shape=jax.ShapeDtypeStruct((slots, tile, width), dtype),
         cost_estimate=pl.CostEstimate(
             flops=0, bytes_accessed=(n + slots) * tile * width * 2, transcendentals=0
         ),
+        compiler_params=pltpu.CompilerParams(vmem_limit_bytes=60 << 20),
         name="picked",
     )(offsets, *pieces)
 
@@ -299,12 +288,13 @@
     arrived_2 = lax.all_to_all(leaving_2, ("x", "core"), 0, 0, tiled=True)
     sums_1 = tile_sums(held_near, masks, arrived_1, group_blocks)
     own_1, low_1, high_1 = sum_of_eight(sums_1.reshape(rep_total, rows_here, half_in), "rep")
-    arrived_2, low_1, high_1 = lax.optimization_barrier((arrived_2, low_1, high_1))
-    summed_1 = own_1 + low_1.astype(jnp.float32) + high_1.astype(jnp.float32)
+    arrived_2, low_1 = lax.optimization_barrier((arrived_2, low_1))
     sums_2 = tile_sums(held_offset, masks, arrived_2, group_blocks)
+    sums_2, high_1 = lax.optimization_barrier((sums_2, high_1))
     pieces = lax.all_to_all(
         sums_2.reshape(rep_total, rows_here, half_in), "rep", 0, 0, tiled=True
     )
+    summed_1 = own_1 + low_1.astype(jnp.float32) + high_1.astype(jnp.float32)
     summed = jnp.concatenate([summed_1, pieces.astype(jnp.float32).sum(axis=0)], axis=1)
 
     own_first = group_first + rep_here * blocks_here

time: 311 us -> 308 us (level)
  starting transfers between devices: 128 us -> 124 us
  transfers between devices with their start and end apart: 28 -> 28, of which waited for: 22 -> 22; matrix products, arithmetic and copies ran while one was open for 9% -> 9% of each run, Pallas kernels for 2% -> 3%
where the time goes in v10:
time: 308 us; the launch traced here: 306 us
  starting transfers between devices  124 us (40%)
  waiting for transfers between devices  119 us (39%)
  Pallas kernels  22.2 us (7%)
  other arithmetic  16.9 us (5%)
  local copies, waits for them, and re-layouts  15.1 us (5%)
  matrix products  8.68 us (3%)
    ppermute x11, starting transfers between devices, pair_swap(): return lax.ppermute(x, axis, [(i, i ^ bit) for i in range(n)])  44 us
    ppermute x11, waiting for transfers between devices, pair_swap(): return lax.ppermute(x, axis, [(i, i ^ bit) for i in range(n)])  36.4 us
    ppermute x8, starting transfers between devices, shifted(): return lax.ppermute(x, axis, [(i, (i + by) % n) for i in range(n)])  27.7 us
    ppermute x8, waiting for transfers between devices, shifted(): return lax.ppermute(x, axis, [(i, (i + by) % n) for i in range(n)])  22.7 us
    all_to_all x1, waiting for transfers between devices, shards(): lax.all_to_all(sums_2.reshape(rep_total, rows_here, half_in), 'rep', 0, 0...  20 us
    all_to_all x1, waiting for transfers between devices, shards(): lax.all_to_all(column_sums.reshape(z_total, rows_here, width_in), 'z', 0,...  18 us
    all_to_all x1, waiting for transfers between devices, shards(): returned = lax.all_to_all(returning, ('x', 'core'), 0, 0, tiled=True)  12.2 us
    all_to_all x1, starting transfers between devices, shards(): lax.all_to_all(jnp.broadcast_to(node_feats[None, :, :half_in], (z_total,...  10.9 us
  transfers between devices with their start and end apart: 28, of which 22 were waited for; matrix products, arithmetic and copies ran while one was open for 9% of the time, Pallas kernels for 3%

profile of v10, /device:TPU:1, one launch (start us, length us, event | category | flops | bytes accessed | tf_op | source)
XLA Modules:
  0.0 306.4 jit_solution(4664009993068750990)
XLA Ops:
  2.7 10.9 %all-to-all-start = ((bf16[8,384,128]{2,1,0:T(8,128)(2,1)}), bf16[8,384,128]{2,1,0:T(8,128)(2,1)}, u32[]{:S(2)}, u32[]{:S(2)}) async-start(bf16[8,384,128]{2,1,0:T(8,128)(2,1)} %broadcast_in_dim.89), calls=%async_computation | async-start | bytes 1572864 | tf_op jit(solution)/shard_map/all_to_all | solution.py:240
  20.1 10.8 %fusion.10 = (bf16[64,128,128]{2,1,0:T(8,128)(2,1)}, bf16[64,128,128]{2,1,0:T(8,128)(2,1)S(1)}) fusion(s32[64,128]{1,0:T(8,128)S(1)} %get-tuple-element.56, s32[64,128]{1,0:T(8,128)S(1)} %get-tuple-element.55, s32[64,128]{1,0:T(8,128)S(1)} %add_select_fusion.5, s32[64]{0:T(128)S(1)} %get-tuple-element.61), kind=kLoop, calls=%fused_computation.22 | loop fusion | flops 46137344 | bytes 4292864 | tf_op jit(solution)/shard_map/convert_element_type | solution.py:25
  31.0 6.3 %all-to-all-done = bf16[8,384,128]{2,1,0:T(8,128)(2,1)} async-done(((bf16[8,384,128]{2,1,0:T(8,128)(2,1)}), bf16[8,384,128]{2,1,0:T(8,128)(2,1)}, u32[]{:S(2)}, u32[]{:S(2)}) %all-to-all-start) | async-done | bytes 786464 | tf_op jit(solution)/shard_map/all_to_all | solution.py:240
  40.5 4.8 %all-to-all-start.1 = ((bf16[64,128,128]{2,1,0:T(8,128)(2,1)}), bf16[64,128,128]{2,1,0:T(8,128)(2,1)}, u32[]{:S(2)}, u32[]{:S(2)}) async-start(bf16[64,128,128]{2,1,0:T(8,128)(2,1)} %picked.2), calls=%async_computation.1 | async-start | bytes 4194304 | tf_op jit(solution)/shard_map/all_to_all | solution.py:284
  47.4 5.0 %collective-permute-start = (bf16[384,128]{1,0:T(8,128)(2,1)S(1)}, bf16[384,128]{1,0:T(8,128)(2,1)S(1)}, u32[]{:S(2)}, u32[]{:S(2)}) collective-permute-start(bf16[384,128]{1,0:T(8,128)(2,1)S(1)} %get-tuple-element.25), channel_id=1, source_target_pairs={{0,48},{16,64},{32,80},{48,96},{64,112},{80,0},{96,16},{112,32},{1... | collective-permute-start | bytes 294920 | tf_op jit(solution)/shard_map/ppermute | solution.py:186
  54.7 5.7 %collective-permute-done = bf16[384,128]{1,0:T(8,128)(2,1)S(1)} collective-permute-done((bf16[384,128]{1,0:T(8,128)(2,1)S(1)}, bf16[384,128]{1,0:T(8,128)(2,1)S(1)}, u32[]{:S(2)}, u32[]{:S(2)}) %collective-permute-start) | collective-permute-done | bytes 98336 | tf_op jit(solution)/shard_map/ppermute | solution.py:186
  60.4 3.6 %collective-permute-start.2 = (bf16[3,384,128]{2,1,0:T(8,128)(2,1)S(1)}, bf16[3,384,128]{2,1,0:T(8,128)(2,1)S(1)}, u32[]{:S(2)}, u32[]{:S(2)}) collective-permute-start(bf16[3,384,128]{2,1,0:T(8,128)(2,1)S(1)} %pad_maximum_fusion), channel_id=1, source_target_pairs={{0,16},{16,32},{32,48},{48,64},{64,80},{80,96},{96,112},{112,0},{1... | collective-permute-start | bytes 884744 | tf_op jit(solution)/shard_map/ppermute | solution.py:186
  66.9 4.8 %collective-permute-done.3 = bf16[2,384,128]{2,1,0:T(8,128)(2,1)S(1)} collective-permute-done((bf16[2,384,128]{2,1,0:T(8,128)(2,1)S(1)}, bf16[2,384,128]{2,1,0:T(8,128)(2,1)S(1)}, u32[]{:S(2)}, u32[]{:S(2)}) %collective-permute-start.3) | collective-permute-done | bytes 196640 | tf_op jit(solution)/shard_map/ppermute | solution.py:186
  75.8 5.9 %all-to-all-start.2 = ((bf16[64,128,128]{2,1,0:T(8,128)(2,1)}), bf16[64,128,128]{2,1,0:T(8,128)(2,1)}, u32[]{:S(2)}, u32[]{:S(2)}) async-start(bf16[64,128,128]{2,1,0:T(8,128)(2,1)} %picked.3), calls=%async_computation.2 | async-start | bytes 4194304 | tf_op jit(solution)/shard_map/all_to_all | solution.py:288
  84.7 5.1 %collective-permute-start.4 = (bf16[3,384,128]{2,1,0:T(8,128)(2,1)S(1)}, bf16[3,384,128]{2,1,0:T(8,128)(2,1)S(1)}, u32[]{:S(2)}, u32[]{:S(2)}) collective-permute-start(bf16[3,384,128]{2,1,0:T(8,128)(2,1)S(1)} %bitcast.91), channel_id=1, source_target_pairs={{0,7},{1,0},{2,1},{3,2},{4,3},{5,4},{6,5},{7,6},{8,15},{9,8},{10,9... | collective-permute-start | bytes 884744 | tf_op jit(solution)/shard_map/ppermute | solution.py:186
  92.5 6.8 %collective-permute-done.5 = bf16[2,384,128]{2,1,0:T(8,128)(2,1)S(1)} collective-permute-done((bf16[2,384,128]{2,1,0:T(8,128)(2,1)S(1)}, bf16[2,384,128]{2,1,0:T(8,128)(2,1)S(1)}, u32[]{:S(2)}, u32[]{:S(2)}) %collective-permute-start.5) | collective-permute-done | bytes 196640 | tf_op jit(solution)/shard_map/ppermute | solution.py:186
  104.1 3.8 %collective-permute-start.7 = (bf16[384,128]{1,0:T(8,128)(2,1)}, bf16[384,128]{1,0:T(8,128)(2,1)}, u32[]{:S(2)}, u32[]{:S(2)}) collective-permute-start(bf16[384,128]{1,0:T(8,128)(2,1)} %get-tuple-element.49), channel_id=1, source_target_pairs={{0,3},{1,4},{2,5},{3,6},{4,7},{5,0},{6,1},{7,2},{8,11},{9,12},{10,... | collective-permute-start | bytes 294920 | tf_op jit(solution)/shard_map/ppermute | solution.py:186
  114.9 6.0 %all-to-all-start.3 = ((bf16[8,384,128]{2,1,0:T(8,128)(2,1)}), bf16[8,384,128]{2,1,0:T(8,128)(2,1)S(1)}, u32[]{:S(2)}, u32[]{:S(2)}) async-start(bf16[8,384,128]{2,1,0:T(8,128)(2,1)} %bitcast.83), calls=%async_computation.3 | async-start | bytes 1572864 | tf_op jit(solution)/shard_map/all_to_all | solution.py:294
  124.4 20.0 %all-to-all-done.3 = bf16[8,384,128]{2,1,0:T(8,128)(2,1)S(1)} async-done(((bf16[8,384,128]{2,1,0:T(8,128)(2,1)}), bf16[8,384,128]{2,1,0:T(8,128)(2,1)S(1)}, u32[]{:S(2)}, u32[]{:S(2)}) %all-to-all-start.3) | async-done | bytes 786464 | tf_op jit(solution)/shard_map/all_to_all | solution.py:294
  149.8 3.6 %all-to-all-start.4 = ((bf16[8,384,256]{2,1,0:T(8,128)(2,1)}), bf16[8,384,256]{2,1,0:T(8,128)(2,1)S(1)}, u32[]{:S(2)}, u32[]{:S(2)}) async-start(bf16[8,384,256]{2,1,0:T(8,128)(2,1)} %broadcast_in_dim.95), calls=%async_computation.4 | async-start | bytes 3145728 | tf_op jit(solution)/shard_map/all_to_all | solution.py:323
  165.0 6.8 %collective-permute-done.9 = f32[128,512]{1,0:T(8,128)S(1)} collective-permute-done((f32[128,512]{1,0:T(8,128)S(1)}, f32[128,512]{1,0:T(8,128)S(1)}, u32[]{:S(2)}, u32[]{:S(2)}) %collective-permute-start.9) | collective-permute-done | bytes 262176 | tf_op jit(solution)/shard_map/ppermute | solution.py:30
  171.9 4.3 %collective-permute-start.10 = (f32[64,512]{1,0:T(8,128)S(1)}, f32[64,512]{1,0:T(8,128)S(1)}, u32[]{:S(2)}, u32[]{:S(2)}) collective-permute-start(f32[64,512]{1,0:T(8,128)S(1)} %slice_select_fusion.1), channel_id=1, source_target_pairs={{0,256},{128,384},{256,0},{384,128},{1,257},{129,385},{257,1},{385... | collective-permute-start | bytes 393224 | tf_op jit(solution)/shard_map/ppermute | solution.py:30
  184.5 5.2 %collective-permute-start.12 = (f32[32,512]{1,0:T(8,128)S(1)}, f32[32,512]{1,0:T(8,128)S(1)}, u32[]{:S(2)}, u32[]{:S(2)}) collective-permute-start(f32[32,512]{1,0:T(8,128)S(1)} %select_add_fusion.3), channel_id=1, source_target_pairs={{0,32},{16,48},{32,0},{48,16},{64,96},{80,112},{96,64},{112,80},{1... | collective-permute-start | bytes 196616 | tf_op jit(solution)/shard_map/ppermute | solution.py:30
  192.8 5.2 %tile_products.1 = bf16[64,128,256]{2,1,0:T(8,128)(2,1)} custom-call(s32[64]{0:T(128)} %copy-done.3, bf16[64,128,128]{2,1,0:T(8,128)(2,1)} %get-tuple-element.32.mask_ref, bf16[24,128,256]{2,1,0:T(8,128)(2,1)} %bitcast.84), custom_call_target="tpu_custom_call" | custom-call | flops 536870912 | bytes 6291456 | tf_op jit(solution)/shard_map/tile_products/pallas_call | solution.py:89
  198.0 7.6 %all-to-all-start.5 = ((bf16[64,128,256]{2,1,0:T(8,128)(2,1)}), bf16[64,128,256]{2,1,0:T(8,128)(2,1)}, u32[]{:S(2)}, u32[]{:S(2)}) async-start(bf16[64,128,256]{2,1,0:T(8,128)(2,1)} %tile_products.1), calls=%async_computation.5 | async-start | bytes 8388608 | tf_op jit(solution)/shard_map/all_to_all | solution.py:340
  205.6 5.9 %collective-permute-start.13 = (f32[32,512]{1,0:T(8,128)S(1)}, f32[32,512]{1,0:T(8,128)S(1)}, u32[]{:S(2)}, u32[]{:S(2)}) collective-permute-start(f32[32,512]{1,0:T(8,128)S(1)} %add.368), channel_id=1, source_target_pairs={{0,64},{16,80},{32,96},{48,112},{64,0},{80,16},{96,32},{112,48},{1... | collective-permute-start | bytes 196616 | tf_op jit(solution)/shard_map/ppermute | solution.py:30
  214.9 3.5 %collective-permute-start.14 = (f32[32,512]{1,0:T(8,128)S(1)}, f32[32,512]{1,0:T(8,128)S(1)}, u32[]{:S(2)}, u32[]{:S(2)}) collective-permute-start(f32[32,512]{1,0:T(8,128)S(1)} %add.369), channel_id=1, source_target_pairs={{0,1},{1,0},{2,3},{3,2},{4,5},{5,4},{6,7},{7,6},{8,9},{9,8},{10,11... | collective-permute-start | bytes 196616 | tf_op jit(solution)/shard_map/ppermute | solution.py:30
  220.5 4.3 %collective-permute-start.15 = (f32[32,512]{1,0:T(8,128)S(1)}, f32[32,512]{1,0:T(8,128)S(1)}, u32[]{:S(2)}, u32[]{:S(2)}) collective-permute-start(f32[32,512]{1,0:T(8,128)S(1)} %add.370), channel_id=1, source_target_pairs={{0,2},{1,3},{2,0},{3,1},{4,6},{5,7},{6,4},{7,5},{8,10},{9,11},{10,... | collective-permute-start | bytes 196616 | tf_op jit(solution)/shard_map/ppermute | solution.py:30
  226.8 8.0 %collective-permute-start.16 = (f32[32,512]{1,0:T(8,128)S(1)}, f32[32,512]{1,0:T(8,128)S(1)}, u32[]{:S(2)}, u32[]{:S(2)}) collective-permute-start(f32[32,512]{1,0:T(8,128)S(1)} %add.371), channel_id=1, source_target_pairs={{0,4},{1,5},{2,6},{3,7},{4,0},{5,1},{6,2},{7,3},{8,12},{9,13},{10,... | collective-permute-start | bytes 196616 | tf_op jit(solution)/shard_map/ppermute | solution.py:30
  236.6 3.6 %collective-permute-start.17 = (f32[32,512]{1,0:T(8,128)S(1)}, f32[32,512]{1,0:T(8,128)S(1)}, u32[]{:S(2)}, u32[]{:S(2)}) collective-permute-start(f32[32,512]{1,0:T(8,128)S(1)} %add_multiply_fusion), channel_id=1, source_target_pairs={{0,16},{16,0},{32,48},{48,32},{64,80},{80,64},{96,112},{112,96},{1... | collective-permute-start | bytes 196616 | tf_op jit(solution)/shard_map/ppermute | solution.py:30
  242.3 12.2 %all-to-all-done.5.part_ref = bf16[64,128,256]{2,1,0:T(8,128)(2,1)} async-done(((bf16[64,128,256]{2,1,0:T(8,128)(2,1)}), bf16[64,128,256]{2,1,0:T(8,128)(2,1)}, u32[]{:S(2)}, u32[]{:S(2)}) %all-to-all-start.5) | async-done | bytes 4194336 | tf_op jit(solution)/shard_map/all_to_all | solution.py:340
  254.5 4.6 %summed_into.1 = bf16[24,128,256]{2,1,0:T(8,128)(2,1)} custom-call(s32[64]{0:T(128)S(1)} %copy-done.2, bf16[64,128,256]{2,1,0:T(8,128)(2,1)} %all-to-all-done.5.part_ref), custom_call_target="tpu_custom_call" | custom-call | flops 2097152 | bytes 4194304 | tf_op jit(solution)/shard_map/summed_into/pallas_call | solution.py:128
  259.1 5.6 %all-to-all-start.6 = ((bf16[8,384,256]{2,1,0:T(8,128)(2,1)}), bf16[8,384,256]{2,1,0:T(8,128)(2,1)S(1)}, u32[]{:S(2)}, u32[]{:S(2)}) async-start(bf16[8,384,256]{2,1,0:T(8,128)(2,1)} %bitcast.28), calls=%async_computation.6 | async-start | bytes 3145728 | tf_op jit(solution)/shard_map/all_to_all | solution.py:347
  266.9 5.0 %collective-permute-done.18 = f32[64,512]{1,0:T(8,128)S(1)} collective-permute-done((f32[64,512]{1,0:T(8,128)S(1)}, f32[64,512]{1,0:T(8,128)S(1)}, u32[]{:S(2)}, u32[]{:S(2)}) %collective-permute-start.18) | collective-permute-done | bytes 131104 | tf_op jit(solution)/shard_map/ppermute | solution.py:30
  274.1 5.2 %collective-permute-done.19 = f32[128,512]{1,0:T(8,128)S(1)} collective-permute-done((f32[128,512]{1,0:T(8,128)S(1)}, f32[128,512]{1,0:T(8,128)S(1)}, u32[]{:S(2)}, u32[]{:S(2)}) %collective-permute-start.19) | collective-permute-done | bytes 262176 | tf_op jit(solution)/shard_map/ppermute | solution.py:30
  279.4 5.1 %collective-permute-start.20 = (f32[256,512]{1,0:T(8,128)S(1)}, f32[256,512]{1,0:T(8,128)S(1)}, u32[]{:S(2)}, u32[]{:S(2)}) collective-permute-start(f32[256,512]{1,0:T(8,128)S(1)} %maximum_select_fusion), channel_id=1, source_target_pairs={{0,8},{8,0},{1,9},{9,1},{2,10},{10,2},{3,11},{11,3},{4,12},{12,4},... | collective-permute-start | bytes 1572872 | tf_op jit(solution)/shard_map/ppermute | solution.py:352
  287.1 18.0 %all-to-all-done.6 = bf16[8,384,256]{2,1,0:T(8,128)(2,1)S(1)} async-done(((bf16[8,384,256]{2,1,0:T(8,128)(2,1)}), bf16[8,384,256]{2,1,0:T(8,128)(2,1)S(1)}, u32[]{:S(2)}, u32[]{:S(2)}) %all-to-all-start.6) | async-done | bytes 1572896 | tf_op jit(solution)/shard_map/all_to_all | solution.py:347
  (135 shorter events, 92.0 us)
Async XLA Ops:
  2.7 34.5 %all-to-all-start = ((bf16[8,384,128]{2,1,0:T(8,128)(2,1)}), bf16[8,384,128]{2,1,0:T(8,128)(2,1)}, u32[]{:S(2)}, u32[]{:S(2)}) async-start(bf16[8,384,128]{2,1,0:T(8,128)(2,1)} %broadcast_in_dim.89), calls=%async_computation | async-start | bytes 1572864 | tf_op jit(solution)/shard_map/all_to_all | solution.py:240
  20.1 90.9 %copy-start.3 = (s32[64]{0:T(128)}, s32[64]{0:T(128)S(1)}, u32[]{:S(2)}) copy-start(s32[64]{0:T(128)S(1)} %get-tuple-element.41.offset_ref) | copy-start | bytes 772
  40.5 35.3 %all-to-all-start.1 = ((bf16[64,128,128]{2,1,0:T(8,128)(2,1)}), bf16[64,128,128]{2,1,0:T(8,128)(2,1)}, u32[]{:S(2)}, u32[]{:S(2)}) async-start(bf16[64,128,128]{2,1,0:T(8,128)(2,1)} %picked.2), calls=%async_computation.1 | async-start | bytes 4194304 | tf_op jit(solution)/shard_map/all_to_all | solution.py:284
  45.3 9.4 %collective-permute-start.1 = (bf16[384,128]{1,0:T(8,128)(2,1)S(1)}, bf16[384,128]{1,0:T(8,128)(2,1)S(1)}, u32[]{:S(2)}, u32[]{:S(2)}) collective-permute-start(bf16[384,128]{1,0:T(8,128)(2,1)S(1)} %get-tuple-element.25), channel_id=1, source_target_pairs={{0,80},{16,96},{32,112},{48,0},{64,16},{80,32},{96,48},{112,64},{1... | collective-permute-start | bytes 294920 | tf_op jit(solution)/shard_map/ppermute | solution.py:186
  47.4 12.9 %collective-permute-start = (bf16[384,128]{1,0:T(8,128)(2,1)S(1)}, bf16[384,128]{1,0:T(8,128)(2,1)S(1)}, u32[]{:S(2)}, u32[]{:S(2)}) collective-permute-start(bf16[384,128]{1,0:T(8,128)(2,1)S(1)} %get-tuple-element.25), channel_id=1, source_target_pairs={{0,48},{16,64},{32,80},{48,96},{64,112},{80,0},{96,16},{112,32},{1... | collective-permute-start | bytes 294920 | tf_op jit(solution)/shard_map/ppermute | solution.py:186
  60.4 11.4 %collective-permute-start.2 = (bf16[3,384,128]{2,1,0:T(8,128)(2,1)S(1)}, bf16[3,384,128]{2,1,0:T(8,128)(2,1)S(1)}, u32[]{:S(2)}, u32[]{:S(2)}) collective-permute-start(bf16[3,384,128]{2,1,0:T(8,128)(2,1)S(1)} %pad_maximum_fusion), channel_id=1, source_target_pairs={{0,16},{16,32},{32,48},{48,64},{64,80},{80,96},{96,112},{112,0},{1... | collective-permute-start | bytes 884744 | tf_op jit(solution)/shard_map/ppermute | solution.py:186
  64.1 7.7 %collective-permute-start.3 = (bf16[2,384,128]{2,1,0:T(8,128)(2,1)S(1)}, bf16[2,384,128]{2,1,0:T(8,128)(2,1)S(1)}, u32[]{:S(2)}, u32[]{:S(2)}) collective-permute-start(bf16[2,384,128]{2,1,0:T(8,128)(2,1)S(1)} %pad_maximum_fusion.1), channel_id=1, source_target_pairs={{0,112},{16,0},{32,16},{48,32},{64,48},{80,64},{96,80},{112,96},{1... | collective-permute-start | bytes 589832 | tf_op jit(solution)/shard_map/ppermute | solution.py:186
  75.8 35.2 %all-to-all-start.2 = ((bf16[64,128,128]{2,1,0:T(8,128)(2,1)}), bf16[64,128,128]{2,1,0:T(8,128)(2,1)}, u32[]{:S(2)}, u32[]{:S(2)}) async-start(bf16[64,128,128]{2,1,0:T(8,128)(2,1)} %picked.3), calls=%async_computation.2 | async-start | bytes 4194304 | tf_op jit(solution)/shard_map/all_to_all | solution.py:288
  84.7 14.6 %collective-permute-start.4 = (bf16[3,384,128]{2,1,0:T(8,128)(2,1)S(1)}, bf16[3,384,128]{2,1,0:T(8,128)(2,1)S(1)}, u32[]{:S(2)}, u32[]{:S(2)}) collective-permute-start(bf16[3,384,128]{2,1,0:T(8,128)(2,1)S(1)} %bitcast.91), channel_id=1, source_target_pairs={{0,7},{1,0},{2,1},{3,2},{4,3},{5,4},{6,5},{7,6},{8,15},{9,8},{10,9... | collective-permute-start | bytes 884744 | tf_op jit(solution)/shard_map/ppermute | solution.py:186
  89.9 9.4 %collective-permute-start.5 = (bf16[2,384,128]{2,1,0:T(8,128)(2,1)S(1)}, bf16[2,384,128]{2,1,0:T(8,128)(2,1)S(1)}, u32[]{:S(2)}, u32[]{:S(2)}) collective-permute-start(bf16[2,384,128]{2,1,0:T(8,128)(2,1)S(1)} %bitcast.93), channel_id=1, source_target_pairs={{0,1},{1,2},{2,3},{3,4},{4,5},{5,6},{6,7},{7,0},{8,9},{9,10},{10,1... | collective-permute-start | bytes 589832 | tf_op jit(solution)/shard_map/ppermute | solution.py:186
  100.8 10.2 %collective-permute-start.6 = (bf16[384,128]{1,0:T(8,128)(2,1)S(1)}, bf16[384,128]{1,0:T(8,128)(2,1)}, u32[]{:S(2)}, u32[]{:S(2)}) collective-permute-start(bf16[384,128]{1,0:T(8,128)(2,1)S(1)} %get-tuple-element.50), channel_id=1, source_target_pairs={{0,5},{1,6},{2,7},{3,0},{4,1},{5,2},{6,3},{7,4},{8,13},{9,14},{10,... | collective-permute-start | bytes 294920 | tf_op jit(solution)/shard_map/ppermute | solution.py:186
  104.1 10.7 %collective-permute-start.7 = (bf16[384,128]{1,0:T(8,128)(2,1)}, bf16[384,128]{1,0:T(8,128)(2,1)}, u32[]{:S(2)}, u32[]{:S(2)}) collective-permute-start(bf16[384,128]{1,0:T(8,128)(2,1)} %get-tuple-element.49), channel_id=1, source_target_pairs={{0,3},{1,4},{2,5},{3,6},{4,7},{5,0},{6,1},{7,2},{8,11},{9,12},{10,... | collective-permute-start | bytes 294920 | tf_op jit(solution)/shard_map/ppermute | solution.py:186
  114.9 29.5 %all-to-all-start.3 = ((bf16[8,384,128]{2,1,0:T(8,128)(2,1)}), bf16[8,384,128]{2,1,0:T(8,128)(2,1)S(1)}, u32[]{:S(2)}, u32[]{:S(2)}) async-start(bf16[8,384,128]{2,1,0:T(8,128)(2,1)} %bitcast.83), calls=%async_computation.3 | async-start | bytes 1572864 | tf_op jit(solution)/shard_map/all_to_all | solution.py:294
  149.8 41.9 %all-to-all-start.4 = ((bf16[8,384,256]{2,1,0:T(8,128)(2,1)}), bf16[8,384,256]{2,1,0:T(8,128)(2,1)S(1)}, u32[]{:S(2)}, u32[]{:S(2)}) async-start(bf16[8,384,256]{2,1,0:T(8,128)(2,1)} %broadcast_in_dim.95), calls=%async_computation.4 | async-start | bytes 3145728 | tf_op jit(solution)/shard_map/all_to_all | solution.py:323
  155.9 4.1 %collective-permute-start.8 = (f32[256,512]{1,0:T(8,128)}, f32[256,512]{1,0:T(8,128)S(1)}, u32[]{:S(2)}, u32[]{:S(2)}) collective-permute-start(f32[256,512]{1,0:T(8,128)} %get-tuple-element.62), channel_id=1, source_target_pairs={{0,8},{8,0},{1,9},{9,1},{2,10},{10,2},{3,11},{11,3},{4,12},{12,4},... | collective-permute-start | bytes 1572872 | tf_op jit(solution)/shard_map/ppermute | solution.py:331
  162.2 9.6 %collective-permute-start.9 = (f32[128,512]{1,0:T(8,128)S(1)}, f32[128,512]{1,0:T(8,128)S(1)}, u32[]{:S(2)}, u32[]{:S(2)}) collective-permute-start(f32[128,512]{1,0:T(8,128)S(1)} %slice_select_fusion), channel_id=1, source_target_pairs={{0,128},{128,0},{256,384},{384,256},{1,129},{129,1},{257,385},{385... | collective-permute-start | bytes 786440 | tf_op jit(solution)/shard_map/ppermute | solution.py:30
  171.9 7.5 %collective-permute-start.10 = (f32[64,512]{1,0:T(8,128)S(1)}, f32[64,512]{1,0:T(8,128)S(1)}, u32[]{:S(2)}, u32[]{:S(2)}) collective-permute-start(f32[64,512]{1,0:T(8,128)S(1)} %slice_select_fusion.1), channel_id=1, source_target_pairs={{0,256},{128,384},{256,0},{384,128},{1,257},{129,385},{257,1},{385... | collective-permute-start | bytes 393224 | tf_op jit(solution)/shard_map/ppermute | solution.py:30
  179.5 5.0 %collective-permute-start.11 = (f32[32,512]{1,0:T(8,128)S(1)}, f32[32,512]{1,0:T(8,128)S(1)}, u32[]{:S(2)}, u32[]{:S(2)}) collective-permute-start(f32[32,512]{1,0:T(8,128)S(1)} %slice_select_fusion.2), channel_id=1, source_target_pairs={{0,16},{16,0},{32,48},{48,32},{64,80},{80,64},{96,112},{112,96},{1... | collective-permute-start | bytes 196616 | tf_op jit(solution)/shard_map/ppermute | solution.py:30
  184.5 7.1 %collective-permute-start.12 = (f32[32,512]{1,0:T(8,128)S(1)}, f32[32,512]{1,0:T(8,128)S(1)}, u32[]{:S(2)}, u32[]{:S(2)}) collective-permute-start(f32[32,512]{1,0:T(8,128)S(1)} %select_add_fusion.3), channel_id=1, source_target_pairs={{0,32},{16,48},{32,0},{48,16},{64,96},{80,112},{96,64},{112,80},{1... | collective-permute-start | bytes 196616 | tf_op jit(solution)/shard_map/ppermute | solution.py:30
  198.0 56.5 %copy-start.2 = (s32[64]{0:T(128)S(1)}, s32[64]{0:T(128)}, u32[]{:S(2)}) copy-start(s32[64]{0:T(128)} %get-tuple-element.64.offset_ref) | copy-start | bytes 772
  198.0 56.5 %all-to-all-start.5 = ((bf16[64,128,256]{2,1,0:T(8,128)(2,1)}), bf16[64,128,256]{2,1,0:T(8,128)(2,1)}, u32[]{:S(2)}, u32[]{:S(2)}) async-start(bf16[64,128,256]{2,1,0:T(8,128)(2,1)} %tile_products.1), calls=%async_computation.5 | async-start | bytes 8388608 | tf_op jit(solution)/shard_map/all_to_all | solution.py:340
  205.6 9.3 %collective-permute-start.13 = (f32[32,512]{1,0:T(8,128)S(1)}, f32[32,512]{1,0:T(8,128)S(1)}, u32[]{:S(2)}, u32[]{:S(2)}) collective-permute-start(f32[32,512]{1,0:T(8,128)S(1)} %add.368), channel_id=1, source_target_pairs={{0,64},{16,80},{32,96},{48,112},{64,0},{80,16},{96,32},{112,48},{1... | collective-permute-start | bytes 196616 | tf_op jit(solution)/shard_map/ppermute | solution.py:30
  214.9 5.6 %collective-permute-start.14 = (f32[32,512]{1,0:T(8,128)S(1)}, f32[32,512]{1,0:T(8,128)S(1)}, u32[]{:S(2)}, u32[]{:S(2)}) collective-permute-start(f32[32,512]{1,0:T(8,128)S(1)} %add.369), channel_id=1, source_target_pairs={{0,1},{1,0},{2,3},{3,2},{4,5},{5,4},{6,7},{7,6},{8,9},{9,8},{10,11... | collective-permute-start | bytes 196616 | tf_op jit(solution)/shard_map/ppermute | solution.py:30
  220.5 6.3 %collective-permute-start.15 = (f32[32,512]{1,0:T(8,128)S(1)}, f32[32,512]{1,0:T(8,128)S(1)}, u32[]{:S(2)}, u32[]{:S(2)}) collective-permute-start(f32[32,512]{1,0:T(8,128)S(1)} %add.370), channel_id=1, source_target_pairs={{0,2},{1,3},{2,0},{3,1},{4,6},{5,7},{6,4},{7,5},{8,10},{9,11},{10,... | collective-permute-start | bytes 196616 | tf_op jit(solution)/shard_map/ppermute | solution.py:30
  226.8 9.7 %collective-permute-start.16 = (f32[32,512]{1,0:T(8,128)S(1)}, f32[32,512]{1,0:T(8,128)S(1)}, u32[]{:S(2)}, u32[]{:S(2)}) collective-permute-start(f32[32,512]{1,0:T(8,128)S(1)} %add.371), channel_id=1, source_target_pairs={{0,4},{1,5},{2,6},{3,7},{4,0},{5,1},{6,2},{7,3},{8,12},{9,13},{10,... | collective-permute-start | bytes 196616 | tf_op jit(solution)/shard_map/ppermute | solution.py:30
  236.6 5.7 %collective-permute-start.17 = (f32[32,512]{1,0:T(8,128)S(1)}, f32[32,512]{1,0:T(8,128)S(1)}, u32[]{:S(2)}, u32[]{:S(2)}) collective-permute-start(f32[32,512]{1,0:T(8,128)S(1)} %add_multiply_fusion), channel_id=1, source_target_pairs={{0,16},{16,0},{32,48},{48,32},{64,80},{80,64},{96,112},{112,96},{1... | collective-permute-start | bytes 196616 | tf_op jit(solution)/shard_map/ppermute | solution.py:30
  259.1 46.3 %copy-start.6 = (bf16[384,512]{1,0:T(8,128)(2,1)S(1)}, bf16[384,512]{1,0:T(8,128)(2,1)}, u32[]{:S(2)}) copy-start(bf16[384,512]{1,0:T(8,128)(2,1)} %copy-done.5) | copy-start | bytes 1179652
  259.1 46.3 %copy-start.10 = (bf16[256,512]{1,0:T(8,128)(2,1)S(1)}, bf16[256,512]{1,0:T(8,128)(2,1)}, u32[]{:S(2)}) copy-start(bf16[256,512]{1,0:T(8,128)(2,1)} %param.13) | copy-start | bytes 786436
  259.1 46.1 %all-to-all-start.6 = ((bf16[8,384,256]{2,1,0:T(8,128)(2,1)}), bf16[8,384,256]{2,1,0:T(8,128)(2,1)S(1)}, u32[]{:S(2)}, u32[]{:S(2)}) async-start(bf16[8,384,256]{2,1,0:T(8,128)(2,1)} %bitcast.28), calls=%async_computation.6 | async-start | bytes 3145728 | tf_op jit(solution)/shard_map/all_to_all | solution.py:347
  264.7 7.2 %collective-permute-start.18 = (f32[64,512]{1,0:T(8,128)S(1)}, f32[64,512]{1,0:T(8,128)S(1)}, u32[]{:S(2)}, u32[]{:S(2)}) collective-permute-start(f32[64,512]{1,0:T(8,128)S(1)} %maximum_select_fusion.2), channel_id=1, source_target_pairs={{0,256},{128,384},{256,0},{384,128},{1,257},{129,385},{257,1},{385... | collective-permute-start | bytes 393224 | tf_op jit(solution)/shard_map/ppermute | solution.py:30
  271.9 7.4 %collective-permute-start.19 = (f32[128,512]{1,0:T(8,128)S(1)}, f32[128,512]{1,0:T(8,128)S(1)}, u32[]{:S(2)}, u32[]{:S(2)}) collective-permute-start(f32[128,512]{1,0:T(8,128)S(1)} %maximum_select_fusion.1), channel_id=1, source_target_pairs={{0,128},{128,0},{256,384},{384,256},{1,129},{129,1},{257,385},{385... | collective-permute-start | bytes 786440 | tf_op jit(solution)/shard_map/ppermute | solution.py:30
  279.4 6.6 %collective-permute-start.20 = (f32[256,512]{1,0:T(8,128)S(1)}, f32[256,512]{1,0:T(8,128)S(1)}, u32[]{:S(2)}, u32[]{:S(2)}) collective-permute-start(f32[256,512]{1,0:T(8,128)S(1)} %maximum_select_fusion), channel_id=1, source_target_pairs={{0,8},{8,0},{1,9},{9,1},{2,10},{10,2},{3,11},{11,3},{4,12},{12,4},... | collective-permute-start | bytes 1572872 | tf_op jit(solution)/shard_map/ppermute | solution.py:352
  (11 other events, 53.1 us)

commit v11 on v10

--- a/solution.py
+++ b/solution.py
@@ -48,7 +48,7 @@
         out_ref[...] = total_ref[...].astype(out_ref.dtype)
 
 
-def tile_sums(offsets, masks, feats, blocks):
+def tile_sums(offsets, masks, feats, blocks, limit):
     slots, tile, width = feats.shape
     return pl.pallas_call(
         forward_kernel,
@@ -68,7 +68,7 @@
             bytes_accessed=slots * tile * (tile + width) * 2,
             transcendentals=0,
         ),
-        compiler_params=pltpu.CompilerParams(vmem_limit_bytes=40 << 20),
+        compiler_params=pltpu.CompilerParams(vmem_limit_bytes=limit << 20),
         name="tile_sums",
     )(offsets, masks, feats)
 
@@ -200,11 +200,14 @@
 
 
 def sum_of_eight(x, axis):
-    above = shifted(x[3:6], axis, -1).astype(jnp.float32)
-    below = shifted(x[6:8], axis, 1).astype(jnp.float32)
-    low = x[0].astype(jnp.float32) + above[0] + below[0]
-    own = x[1].astype(jnp.float32) + above[1] + below[1]
-    high = x[2].astype(jnp.float32) + above[2]
+    above, below = shifted(x[3:6], axis, -1), shifted(x[6:8], axis, 1)
+
+    def added(*parts):
+        return sum(part.astype(jnp.float32) for part in parts)
+
+    low = added(x[0], above[0], below[0])
+    own = added(x[1], above[1], below[1])
+    high = added(x[2], above[2])
     return own, shifted(low.astype(x.dtype), axis, -3), shifted(high.astype(x.dtype), axis, 3)
 
 
@@ -286,10 +289,10 @@
     leaving_2 = picked(passed_near, *column_2)
     arrived_1, leaving_2 = lax.optimization_barrier((arrived_1, leaving_2))
     arrived_2 = lax.all_to_all(leaving_2, ("x", "core"), 0, 0, tiled=True)
-    sums_1 = tile_sums(held_near, masks, arrived_1, group_blocks)
+    sums_1 = tile_sums(held_near, masks, arrived_1, group_blocks, 40)
     own_1, low_1, high_1 = sum_of_eight(sums_1.reshape(rep_total, rows_here, half_in), "rep")
     arrived_2, low_1 = lax.optimization_barrier((arrived_2, low_1))
-    sums_2 = tile_sums(held_offset, masks, arrived_2, group_blocks)
+    sums_2 = tile_sums(held_offset, masks, arrived_2, group_blocks, 60)
     sums_2, high_1 = lax.optimization_barrier((sums_2, high_1))
     pieces = lax.all_to_all(
         sums_2.reshape(rep_total, rows_here, half_in), "rep", 0, 0, tiled=True

time: 308 us -> 307 us (level)
  waiting for transfers between devices: 119 us -> 123 us
  transfers between devices with their start and end apart: 28 -> 28, of which waited for: 22 -> 22; matrix products, arithmetic and copies ran while one was open for 9% -> 8% of each run, Pallas kernels for 3% -> 3%
where the time goes in v11:
time: 307 us; the launch traced here: 306 us
  waiting for transfers between devices  123 us (40%)
  starting transfers between devices  122 us (40%)
  Pallas kernels  23.5 us (8%)
  other arithmetic  16 us (5%)
  local copies, waits for them, and re-layouts  12.9 us (4%)
  matrix products  7.61 us (2%)
    ppermute x11, starting transfers between devices, pair_swap(): return lax.ppermute(x, axis, [(i, i ^ bit) for i in range(n)])  43.8 us
    ppermute x11, waiting for transfers between devices, pair_swap(): return lax.ppermute(x, axis, [(i, i ^ bit) for i in range(n)])  36.6 us
    ppermute x8, starting transfers between devices, shifted(): return lax.ppermute(x, axis, [(i, (i + by) % n) for i in range(n)])  27.8 us
    ppermute x8, waiting for transfers between devices, shifted(): return lax.ppermute(x, axis, [(i, (i + by) % n) for i in range(n)])  25.1 us
    all_to_all x1, waiting for transfers between devices, shards(): lax.all_to_all(sums_2.reshape(rep_total, rows_here, half_in), 'rep', 0, 0...  21.2 us
    all_to_all x1, waiting for transfers between devices, shards(): lax.all_to_all(column_sums.reshape(z_total, rows_here, width_in), 'z', 0,...  18 us
    all_to_all x1, waiting for transfers between devices, shards(): returned = lax.all_to_all(returning, ('x', 'core'), 0, 0, tiled=True)  12.2 us
    all_to_all x1, starting transfers between devices, shards(): lax.all_to_all(jnp.broadcast_to(node_feats[None, :, :half_in], (z_total,...  10.9 us
  transfers between devices with their start and end apart: 28, of which 22 were waited for; matrix products, arithmetic and copies ran while one was open for 8% of the time, Pallas kernels for 3%

profile of v11, /device:TPU:1, one launch (start us, length us, event | category | flops | bytes accessed | tf_op | source)
XLA Modules:
  0.0 305.7 jit_solution(14466395489998175488)
XLA Ops:
  2.7 10.9 %all-to-all-start = ((bf16[8,384,128]{2,1,0:T(8,128)(2,1)}), bf16[8,384,128]{2,1,0:T(8,128)(2,1)}, u32[]{:S(2)}, u32[]{:S(2)}) async-start(bf16[8,384,128]{2,1,0:T(8,128)(2,1)} %broadcast_in_dim.89), calls=%async_computation | async-start | bytes 1572864 | tf_op jit(solution)/shard_map/all_to_all | solution.py:243
  20.1 10.9 %fusion.10 = (bf16[64,128,128]{2,1,0:T(8,128)(2,1)}, bf16[64,128,128]{2,1,0:T(8,128)(2,1)S(1)}) fusion(s32[64,128]{1,0:T(8,128)S(1)} %get-tuple-element.56, s32[64,128]{1,0:T(8,128)S(1)} %get-tuple-element.55, s32[64,128]{1,0:T(8,128)S(1)} %add_select_fusion.5, s32[64]{0:T(128)S(1)} %get-tuple-element.61), kind=kLoop, calls=%fused_computation.22 | loop fusion | flops 46137344 | bytes 4292864 | tf_op jit(solution)/shard_map/convert_element_type | solution.py:25
  30.9 6.3 %all-to-all-done = bf16[8,384,128]{2,1,0:T(8,128)(2,1)} async-done(((bf16[8,384,128]{2,1,0:T(8,128)(2,1)}), bf16[8,384,128]{2,1,0:T(8,128)(2,1)}, u32[]{:S(2)}, u32[]{:S(2)}) %all-to-all-start) | async-done | bytes 786464 | tf_op jit(solution)/shard_map/all_to_all | solution.py:243
  40.5 4.8 %all-to-all-start.1 = ((bf16[64,128,128]{2,1,0:T(8,128)(2,1)}), bf16[64,128,128]{2,1,0:T(8,128)(2,1)}, u32[]{:S(2)}, u32[]{:S(2)}) async-start(bf16[64,128,128]{2,1,0:T(8,128)(2,1)} %picked.2), calls=%async_computation.1 | async-start | bytes 4194304 | tf_op jit(solution)/shard_map/all_to_all | solution.py:287
  47.4 5.0 %collective-permute-start = (bf16[384,128]{1,0:T(8,128)(2,1)S(1)}, bf16[384,128]{1,0:T(8,128)(2,1)S(1)}, u32[]{:S(2)}, u32[]{:S(2)}) collective-permute-start(bf16[384,128]{1,0:T(8,128)(2,1)S(1)} %get-tuple-element.25), channel_id=1, source_target_pairs={{0,48},{16,64},{32,80},{48,96},{64,112},{80,0},{96,16},{112,32},{1... | collective-permute-start | bytes 294920 | tf_op jit(solution)/shard_map/ppermute | solution.py:186
  54.6 5.7 %collective-permute-done = bf16[384,128]{1,0:T(8,128)(2,1)S(1)} collective-permute-done((bf16[384,128]{1,0:T(8,128)(2,1)S(1)}, bf16[384,128]{1,0:T(8,128)(2,1)S(1)}, u32[]{:S(2)}, u32[]{:S(2)}) %collective-permute-start) | collective-permute-done | bytes 98336 | tf_op jit(solution)/shard_map/ppermute | solution.py:186
  60.4 3.6 %collective-permute-start.2 = (bf16[3,384,128]{2,1,0:T(8,128)(2,1)S(1)}, bf16[3,384,128]{2,1,0:T(8,128)(2,1)S(1)}, u32[]{:S(2)}, u32[]{:S(2)}) collective-permute-start(bf16[3,384,128]{2,1,0:T(8,128)(2,1)S(1)} %pad_maximum_fusion), channel_id=1, source_target_pairs={{0,16},{16,32},{32,48},{48,64},{64,80},{80,96},{96,112},{112,0},{1... | collective-permute-start | bytes 884744 | tf_op jit(solution)/shard_map/ppermute | solution.py:186
  66.9 4.8 %collective-permute-done.3 = bf16[2,384,128]{2,1,0:T(8,128)(2,1)S(1)} collective-permute-done((bf16[2,384,128]{2,1,0:T(8,128)(2,1)S(1)}, bf16[2,384,128]{2,1,0:T(8,128)(2,1)S(1)}, u32[]{:S(2)}, u32[]{:S(2)}) %collective-permute-start.3) | collective-permute-done | bytes 196640 | tf_op jit(solution)/shard_map/ppermute | solution.py:186
  75.8 6.0 %all-to-all-start.2 = ((bf16[64,128,128]{2,1,0:T(8,128)(2,1)}), bf16[64,128,128]{2,1,0:T(8,128)(2,1)}, u32[]{:S(2)}, u32[]{:S(2)}) async-start(bf16[64,128,128]{2,1,0:T(8,128)(2,1)} %picked.3), calls=%async_computation.2 | async-start | bytes 4194304 | tf_op jit(solution)/shard_map/all_to_all | solution.py:291
  84.8 5.2 %collective-permute-start.4 = (bf16[3,384,128]{2,1,0:T(8,128)(2,1)S(1)}, bf16[3,384,128]{2,1,0:T(8,128)(2,1)S(1)}, u32[]{:S(2)}, u32[]{:S(2)}) collective-permute-start(bf16[3,384,128]{2,1,0:T(8,128)(2,1)S(1)} %bitcast.84), channel_id=1, source_target_pairs={{0,7},{1,0},{2,1},{3,2},{4,3},{5,4},{6,5},{7,6},{8,15},{9,8},{10,9... | collective-permute-start | bytes 884744 | tf_op jit(solution)/shard_map/ppermute | solution.py:186
  92.0 7.5 %collective-permute-done.5 = bf16[2,384,128]{2,1,0:T(8,128)(2,1)S(1)} collective-permute-done((bf16[2,384,128]{2,1,0:T(8,128)(2,1)S(1)}, bf16[2,384,128]{2,1,0:T(8,128)(2,1)S(1)}, u32[]{:S(2)}, u32[]{:S(2)}) %collective-permute-start.5) | collective-permute-done | bytes 196640 | tf_op jit(solution)/shard_map/ppermute | solution.py:186
  102.9 3.7 %collective-permute-start.7 = (bf16[384,128]{1,0:T(8,128)(2,1)S(1)}, bf16[384,128]{1,0:T(8,128)(2,1)S(1)}, u32[]{:S(2)}, u32[]{:S(2)}) collective-permute-start(bf16[384,128]{1,0:T(8,128)(2,1)S(1)} %get-tuple-element.49), channel_id=1, source_target_pairs={{0,3},{1,4},{2,5},{3,6},{4,7},{5,0},{6,1},{7,2},{8,11},{9,12},{10,... | collective-permute-start | bytes 294920 | tf_op jit(solution)/shard_map/ppermute | solution.py:186
  106.6 4.8 %collective-permute-done.6 = bf16[384,128]{1,0:T(8,128)(2,1)S(1)} collective-permute-done((bf16[384,128]{1,0:T(8,128)(2,1)S(1)}, bf16[384,128]{1,0:T(8,128)(2,1)S(1)}, u32[]{:S(2)}, u32[]{:S(2)}) %collective-permute-start.6) | collective-permute-done | bytes 98336 | tf_op jit(solution)/shard_map/ppermute | solution.py:186
  111.5 4.3 %tile_sums.3 = bf16[24,128,128]{2,1,0:T(8,128)(2,1)} custom-call(s32[64]{0:T(128)} %get-tuple-element.41.offset_ref, bf16[64,128,128]{2,1,0:T(8,128)(2,1)} %copy-done.1, bf16[64,128,128]{2,1,0:T(8,128)(2,1)} %all-to-all-done.2.feat_ref), custom_call_target="tpu_custom_call" | custom-call | flops 268435456 | bytes 4194304 | tf_op jit(solution)/shard_map/tile_sums/pallas_call | solution.py:53
  115.7 4.5 %all-to-all-start.3 = ((bf16[8,384,128]{2,1,0:T(8,128)(2,1)}), bf16[8,384,128]{2,1,0:T(8,128)(2,1)S(1)}, u32[]{:S(2)}, u32[]{:S(2)}) async-start(bf16[8,384,128]{2,1,0:T(8,128)(2,1)} %bitcast.77), calls=%async_computation.3 | async-start | bytes 1572864 | tf_op jit(solution)/shard_map/all_to_all | solution.py:297
  122.6 21.2 %all-to-all-done.3 = bf16[8,384,128]{2,1,0:T(8,128)(2,1)S(1)} async-done(((bf16[8,384,128]{2,1,0:T(8,128)(2,1)}), bf16[8,384,128]{2,1,0:T(8,128)(2,1)S(1)}, u32[]{:S(2)}, u32[]{:S(2)}) %all-to-all-start.3) | async-done | bytes 786464 | tf_op jit(solution)/shard_map/all_to_all | solution.py:297
  164.3 6.9 %collective-permute-done.9 = f32[128,512]{1,0:T(8,128)S(1)} collective-permute-done((f32[128,512]{1,0:T(8,128)S(1)}, f32[128,512]{1,0:T(8,128)S(1)}, u32[]{:S(2)}, u32[]{:S(2)}) %collective-permute-start.9) | collective-permute-done | bytes 262176 | tf_op jit(solution)/shard_map/ppermute | solution.py:30
  171.3 4.2 %collective-permute-start.10 = (f32[64,512]{1,0:T(8,128)S(1)}, f32[64,512]{1,0:T(8,128)S(1)}, u32[]{:S(2)}, u32[]{:S(2)}) collective-permute-start(f32[64,512]{1,0:T(8,128)S(1)} %slice_select_fusion.1), channel_id=1, source_target_pairs={{0,256},{128,384},{256,0},{384,128},{1,257},{129,385},{257,1},{385... | collective-permute-start | bytes 393224 | tf_op jit(solution)/shard_map/ppermute | solution.py:30
  183.9 5.2 %collective-permute-start.12 = (f32[32,512]{1,0:T(8,128)S(1)}, f32[32,512]{1,0:T(8,128)S(1)}, u32[]{:S(2)}, u32[]{:S(2)}) collective-permute-start(f32[32,512]{1,0:T(8,128)S(1)} %select_add_fusion.3), channel_id=1, source_target_pairs={{0,32},{16,48},{32,0},{48,16},{64,96},{80,112},{96,64},{112,80},{1... | collective-permute-start | bytes 196616 | tf_op jit(solution)/shard_map/ppermute | solution.py:30
  192.2 5.2 %tile_products.1 = bf16[64,128,256]{2,1,0:T(8,128)(2,1)} custom-call(s32[64]{0:T(128)} %get-tuple-element.41.offset_ref, bf16[64,128,128]{2,1,0:T(8,128)(2,1)} %get-tuple-element.32.mask_ref, bf16[24,128,256]{2,1,0:T(8,128)(2,1)} %bitcast.76), custom_call_target="tpu_custom_call" | custom-call | flops 536870912 | bytes 6291456 | tf_op jit(solution)/shard_map/tile_products/pallas_call | solution.py:89
  197.4 7.6 %all-to-all-start.5 = ((bf16[64,128,256]{2,1,0:T(8,128)(2,1)}), bf16[64,128,256]{2,1,0:T(8,128)(2,1)}, u32[]{:S(2)}, u32[]{:S(2)}) async-start(bf16[64,128,256]{2,1,0:T(8,128)(2,1)} %tile_products.1), calls=%async_computation.5 | async-start | bytes 8388608 | tf_op jit(solution)/shard_map/all_to_all | solution.py:343
  204.9 5.9 %collective-permute-start.13 = (f32[32,512]{1,0:T(8,128)S(1)}, f32[32,512]{1,0:T(8,128)S(1)}, u32[]{:S(2)}, u32[]{:S(2)}) collective-permute-start(f32[32,512]{1,0:T(8,128)S(1)} %add.368), channel_id=1, source_target_pairs={{0,64},{16,80},{32,96},{48,112},{64,0},{80,16},{96,32},{112,48},{1... | collective-permute-start | bytes 196616 | tf_op jit(solution)/shard_map/ppermute | solution.py:30
  219.9 4.3 %collective-permute-start.15 = (f32[32,512]{1,0:T(8,128)S(1)}, f32[32,512]{1,0:T(8,128)S(1)}, u32[]{:S(2)}, u32[]{:S(2)}) collective-permute-start(f32[32,512]{1,0:T(8,128)S(1)} %add.370), channel_id=1, source_target_pairs={{0,2},{1,3},{2,0},{3,1},{4,6},{5,7},{6,4},{7,5},{8,10},{9,11},{10,... | collective-permute-start | bytes 196616 | tf_op jit(solution)/shard_map/ppermute | solution.py:30
  226.2 8.0 %collective-permute-start.16 = (f32[32,512]{1,0:T(8,128)S(1)}, f32[32,512]{1,0:T(8,128)S(1)}, u32[]{:S(2)}, u32[]{:S(2)}) collective-permute-start(f32[32,512]{1,0:T(8,128)S(1)} %add.371), channel_id=1, source_target_pairs={{0,4},{1,5},{2,6},{3,7},{4,0},{5,1},{6,2},{7,3},{8,12},{9,13},{10,... | collective-permute-start | bytes 196616 | tf_op jit(solution)/shard_map/ppermute | solution.py:30
  236.0 3.6 %collective-permute-start.17 = (f32[32,512]{1,0:T(8,128)S(1)}, f32[32,512]{1,0:T(8,128)S(1)}, u32[]{:S(2)}, u32[]{:S(2)}) collective-permute-start(f32[32,512]{1,0:T(8,128)S(1)} %add_multiply_fusion), channel_id=1, source_target_pairs={{0,16},{16,0},{32,48},{48,32},{64,80},{80,64},{96,112},{112,96},{1... | collective-permute-start | bytes 196616 | tf_op jit(solution)/shard_map/ppermute | solution.py:30
  241.7 12.2 %all-to-all-done.5.part_ref = bf16[64,128,256]{2,1,0:T(8,128)(2,1)} async-done(((bf16[64,128,256]{2,1,0:T(8,128)(2,1)}), bf16[64,128,256]{2,1,0:T(8,128)(2,1)}, u32[]{:S(2)}, u32[]{:S(2)}) %all-to-all-start.5) | async-done | bytes 4194336 | tf_op jit(solution)/shard_map/all_to_all | solution.py:343
  253.9 4.6 %summed_into.1 = bf16[24,128,256]{2,1,0:T(8,128)(2,1)} custom-call(s32[64]{0:T(128)S(1)} %copy-done.2, bf16[64,128,256]{2,1,0:T(8,128)(2,1)} %all-to-all-done.5.part_ref), custom_call_target="tpu_custom_call" | custom-call | flops 2097152 | bytes 4194304 | tf_op jit(solution)/shard_map/summed_into/pallas_call | solution.py:128
  258.4 5.6 %all-to-all-start.6 = ((bf16[8,384,256]{2,1,0:T(8,128)(2,1)}), bf16[8,384,256]{2,1,0:T(8,128)(2,1)S(1)}, u32[]{:S(2)}, u32[]{:S(2)}) async-start(bf16[8,384,256]{2,1,0:T(8,128)(2,1)} %bitcast.28), calls=%async_computation.6 | async-start | bytes 3145728 | tf_op jit(solution)/shard_map/all_to_all | solution.py:350
  266.3 5.0 %collective-permute-done.18 = f32[64,512]{1,0:T(8,128)S(1)} collective-permute-done((f32[64,512]{1,0:T(8,128)S(1)}, f32[64,512]{1,0:T(8,128)S(1)}, u32[]{:S(2)}, u32[]{:S(2)}) %collective-permute-start.18) | collective-permute-done | bytes 131104 | tf_op jit(solution)/shard_map/ppermute | solution.py:30
  273.5 5.2 %collective-permute-done.19 = f32[128,512]{1,0:T(8,128)S(1)} collective-permute-done((f32[128,512]{1,0:T(8,128)S(1)}, f32[128,512]{1,0:T(8,128)S(1)}, u32[]{:S(2)}, u32[]{:S(2)}) %collective-permute-start.19) | collective-permute-done | bytes 262176 | tf_op jit(solution)/shard_map/ppermute | solution.py:30
  278.8 5.1 %collective-permute-start.20 = (f32[256,512]{1,0:T(8,128)S(1)}, f32[256,512]{1,0:T(8,128)S(1)}, u32[]{:S(2)}, u32[]{:S(2)}) collective-permute-start(f32[256,512]{1,0:T(8,128)S(1)} %maximum_select_fusion), channel_id=1, source_target_pairs={{0,8},{8,0},{1,9},{9,1},{2,10},{10,2},{3,11},{11,3},{4,12},{12,4},... | collective-permute-start | bytes 1572872 | tf_op jit(solution)/shard_map/ppermute | solution.py:355
  286.5 18.0 %all-to-all-done.6 = bf16[8,384,256]{2,1,0:T(8,128)(2,1)S(1)} async-done(((bf16[8,384,256]{2,1,0:T(8,128)(2,1)}), bf16[8,384,256]{2,1,0:T(8,128)(2,1)S(1)}, u32[]{:S(2)}, u32[]{:S(2)}) %all-to-all-start.6) | async-done | bytes 1572896 | tf_op jit(solution)/shard_map/all_to_all | solution.py:350
  (135 shorter events, 88.9 us)
Async XLA Ops:
  2.7 34.5 %all-to-all-start = ((bf16[8,384,128]{2,1,0:T(8,128)(2,1)}), bf16[8,384,128]{2,1,0:T(8,128)(2,1)}, u32[]{:S(2)}, u32[]{:S(2)}) async-start(bf16[8,384,128]{2,1,0:T(8,128)(2,1)} %broadcast_in_dim.89), calls=%async_computation | async-start | bytes 1572864 | tf_op jit(solution)/shard_map/all_to_all | solution.py:243
  30.9 50.8 %copy-start.1 = (bf16[64,128,128]{2,1,0:T(8,128)(2,1)}, bf16[64,128,128]{2,1,0:T(8,128)(2,1)S(1)}, u32[]{:S(2)}) copy-start(bf16[64,128,128]{2,1,0:T(8,128)(2,1)S(1)} %get-tuple-element.22.mask_ref) | copy-start | bytes 6291460
  40.5 35.3 %all-to-all-start.1 = ((bf16[64,128,128]{2,1,0:T(8,128)(2,1)}), bf16[64,128,128]{2,1,0:T(8,128)(2,1)}, u32[]{:S(2)}, u32[]{:S(2)}) async-start(bf16[64,128,128]{2,1,0:T(8,128)(2,1)} %picked.2), calls=%async_computation.1 | async-start | bytes 4194304 | tf_op jit(solution)/shard_map/all_to_all | solution.py:287
  45.3 9.4 %collective-permute-start.1 = (bf16[384,128]{1,0:T(8,128)(2,1)S(1)}, bf16[384,128]{1,0:T(8,128)(2,1)S(1)}, u32[]{:S(2)}, u32[]{:S(2)}) collective-permute-start(bf16[384,128]{1,0:T(8,128)(2,1)S(1)} %get-tuple-element.25), channel_id=1, source_target_pairs={{0,80},{16,96},{32,112},{48,0},{64,16},{80,32},{96,48},{112,64},{1... | collective-permute-start | bytes 294920 | tf_op jit(solution)/shard_map/ppermute | solution.py:186
  47.4 12.9 %collective-permute-start = (bf16[384,128]{1,0:T(8,128)(2,1)S(1)}, bf16[384,128]{1,0:T(8,128)(2,1)S(1)}, u32[]{:S(2)}, u32[]{:S(2)}) collective-permute-start(bf16[384,128]{1,0:T(8,128)(2,1)S(1)} %get-tuple-element.25), channel_id=1, source_target_pairs={{0,48},{16,64},{32,80},{48,96},{64,112},{80,0},{96,16},{112,32},{1... | collective-permute-start | bytes 294920 | tf_op jit(solution)/shard_map/ppermute | solution.py:186
  60.4 11.4 %collective-permute-start.2 = (bf16[3,384,128]{2,1,0:T(8,128)(2,1)S(1)}, bf16[3,384,128]{2,1,0:T(8,128)(2,1)S(1)}, u32[]{:S(2)}, u32[]{:S(2)}) collective-permute-start(bf16[3,384,128]{2,1,0:T(8,128)(2,1)S(1)} %pad_maximum_fusion), channel_id=1, source_target_pairs={{0,16},{16,32},{32,48},{48,64},{64,80},{80,96},{96,112},{112,0},{1... | collective-permute-start | bytes 884744 | tf_op jit(solution)/shard_map/ppermute | solution.py:186
  64.0 7.7 %collective-permute-start.3 = (bf16[2,384,128]{2,1,0:T(8,128)(2,1)S(1)}, bf16[2,384,128]{2,1,0:T(8,128)(2,1)S(1)}, u32[]{:S(2)}, u32[]{:S(2)}) collective-permute-start(bf16[2,384,128]{2,1,0:T(8,128)(2,1)S(1)} %pad_maximum_fusion.1), channel_id=1, source_target_pairs={{0,112},{16,0},{32,16},{48,32},{64,48},{80,64},{96,80},{112,96},{1... | collective-permute-start | bytes 589832 | tf_op jit(solution)/shard_map/ppermute | solution.py:186
  75.8 35.7 %all-to-all-start.2 = ((bf16[64,128,128]{2,1,0:T(8,128)(2,1)}), bf16[64,128,128]{2,1,0:T(8,128)(2,1)}, u32[]{:S(2)}, u32[]{:S(2)}) async-start(bf16[64,128,128]{2,1,0:T(8,128)(2,1)} %picked.3), calls=%async_computation.2 | async-start | bytes 4194304 | tf_op jit(solution)/shard_map/all_to_all | solution.py:291
  84.8 14.7 %collective-permute-start.4 = (bf16[3,384,128]{2,1,0:T(8,128)(2,1)S(1)}, bf16[3,384,128]{2,1,0:T(8,128)(2,1)S(1)}, u32[]{:S(2)}, u32[]{:S(2)}) collective-permute-start(bf16[3,384,128]{2,1,0:T(8,128)(2,1)S(1)} %bitcast.84), channel_id=1, source_target_pairs={{0,7},{1,0},{2,1},{3,2},{4,3},{5,4},{6,5},{7,6},{8,15},{9,8},{10,9... | collective-permute-start | bytes 884744 | tf_op jit(solution)/shard_map/ppermute | solution.py:186
  90.0 9.4 %collective-permute-start.5 = (bf16[2,384,128]{2,1,0:T(8,128)(2,1)S(1)}, bf16[2,384,128]{2,1,0:T(8,128)(2,1)S(1)}, u32[]{:S(2)}, u32[]{:S(2)}) collective-permute-start(bf16[2,384,128]{2,1,0:T(8,128)(2,1)S(1)} %bitcast.86), channel_id=1, source_target_pairs={{0,1},{1,2},{2,3},{3,4},{4,5},{5,6},{6,7},{7,0},{8,9},{9,10},{10,1... | collective-permute-start | bytes 589832 | tf_op jit(solution)/shard_map/ppermute | solution.py:186
  99.5 11.9 %collective-permute-start.6 = (bf16[384,128]{1,0:T(8,128)(2,1)S(1)}, bf16[384,128]{1,0:T(8,128)(2,1)S(1)}, u32[]{:S(2)}, u32[]{:S(2)}) collective-permute-start(bf16[384,128]{1,0:T(8,128)(2,1)S(1)} %get-tuple-element.50), channel_id=1, source_target_pairs={{0,5},{1,6},{2,7},{3,0},{4,1},{5,2},{6,3},{7,4},{8,13},{9,14},{10,... | collective-permute-start | bytes 294920 | tf_op jit(solution)/shard_map/ppermute | solution.py:186
  102.9 12.9 %collective-permute-start.7 = (bf16[384,128]{1,0:T(8,128)(2,1)S(1)}, bf16[384,128]{1,0:T(8,128)(2,1)S(1)}, u32[]{:S(2)}, u32[]{:S(2)}) collective-permute-start(bf16[384,128]{1,0:T(8,128)(2,1)S(1)} %get-tuple-element.49), channel_id=1, source_target_pairs={{0,3},{1,4},{2,5},{3,6},{4,7},{5,0},{6,1},{7,2},{8,11},{9,12},{10,... | collective-permute-start | bytes 294920 | tf_op jit(solution)/shard_map/ppermute | solution.py:186
  115.7 28.1 %all-to-all-start.3 = ((bf16[8,384,128]{2,1,0:T(8,128)(2,1)}), bf16[8,384,128]{2,1,0:T(8,128)(2,1)S(1)}, u32[]{:S(2)}, u32[]{:S(2)}) async-start(bf16[8,384,128]{2,1,0:T(8,128)(2,1)} %bitcast.77), calls=%async_computation.3 | async-start | bytes 1572864 | tf_op jit(solution)/shard_map/all_to_all | solution.py:297
  149.2 41.9 %all-to-all-start.4 = ((bf16[8,384,256]{2,1,0:T(8,128)(2,1)}), bf16[8,384,256]{2,1,0:T(8,128)(2,1)S(1)}, u32[]{:S(2)}, u32[]{:S(2)}) async-start(bf16[8,384,256]{2,1,0:T(8,128)(2,1)} %broadcast_in_dim.95), calls=%async_computation.4 | async-start | bytes 3145728 | tf_op jit(solution)/shard_map/all_to_all | solution.py:326
  155.3 4.1 %collective-permute-start.8 = (f32[256,512]{1,0:T(8,128)}, f32[256,512]{1,0:T(8,128)S(1)}, u32[]{:S(2)}, u32[]{:S(2)}) collective-permute-start(f32[256,512]{1,0:T(8,128)} %get-tuple-element.62), channel_id=1, source_target_pairs={{0,8},{8,0},{1,9},{9,1},{2,10},{10,2},{3,11},{11,3},{4,12},{12,4},... | collective-permute-start | bytes 1572872 | tf_op jit(solution)/shard_map/ppermute | solution.py:334
  161.6 9.6 %collective-permute-start.9 = (f32[128,512]{1,0:T(8,128)S(1)}, f32[128,512]{1,0:T(8,128)S(1)}, u32[]{:S(2)}, u32[]{:S(2)}) collective-permute-start(f32[128,512]{1,0:T(8,128)S(1)} %slice_select_fusion), channel_id=1, source_target_pairs={{0,128},{128,0},{256,384},{384,256},{1,129},{129,1},{257,385},{385... | collective-permute-start | bytes 786440 | tf_op jit(solution)/shard_map/ppermute | solution.py:30
  171.3 7.5 %collective-permute-start.10 = (f32[64,512]{1,0:T(8,128)S(1)}, f32[64,512]{1,0:T(8,128)S(1)}, u32[]{:S(2)}, u32[]{:S(2)}) collective-permute-start(f32[64,512]{1,0:T(8,128)S(1)} %slice_select_fusion.1), channel_id=1, source_target_pairs={{0,256},{128,384},{256,0},{384,128},{1,257},{129,385},{257,1},{385... | collective-permute-start | bytes 393224 | tf_op jit(solution)/shard_map/ppermute | solution.py:30
  178.9 5.0 %collective-permute-start.11 = (f32[32,512]{1,0:T(8,128)S(1)}, f32[32,512]{1,0:T(8,128)S(1)}, u32[]{:S(2)}, u32[]{:S(2)}) collective-permute-start(f32[32,512]{1,0:T(8,128)S(1)} %slice_select_fusion.2), channel_id=1, source_target_pairs={{0,16},{16,0},{32,48},{48,32},{64,80},{80,64},{96,112},{112,96},{1... | collective-permute-start | bytes 196616 | tf_op jit(solution)/shard_map/ppermute | solution.py:30
  183.9 7.1 %collective-permute-start.12 = (f32[32,512]{1,0:T(8,128)S(1)}, f32[32,512]{1,0:T(8,128)S(1)}, u32[]{:S(2)}, u32[]{:S(2)}) collective-permute-start(f32[32,512]{1,0:T(8,128)S(1)} %select_add_fusion.3), channel_id=1, source_target_pairs={{0,32},{16,48},{32,0},{48,16},{64,96},{80,112},{96,64},{112,80},{1... | collective-permute-start | bytes 196616 | tf_op jit(solution)/shard_map/ppermute | solution.py:30
  197.4 56.5 %copy-start.2 = (s32[64]{0:T(128)S(1)}, s32[64]{0:T(128)}, u32[]{:S(2)}) copy-start(s32[64]{0:T(128)} %get-tuple-element.64.offset_ref) | copy-start | bytes 772
  197.4 56.5 %all-to-all-start.5 = ((bf16[64,128,256]{2,1,0:T(8,128)(2,1)}), bf16[64,128,256]{2,1,0:T(8,128)(2,1)}, u32[]{:S(2)}, u32[]{:S(2)}) async-start(bf16[64,128,256]{2,1,0:T(8,128)(2,1)} %tile_products.1), calls=%async_computation.5 | async-start | bytes 8388608 | tf_op jit(solution)/shard_map/all_to_all | solution.py:343
  204.9 9.3 %collective-permute-start.13 = (f32[32,512]{1,0:T(8,128)S(1)}, f32[32,512]{1,0:T(8,128)S(1)}, u32[]{:S(2)}, u32[]{:S(2)}) collective-permute-start(f32[32,512]{1,0:T(8,128)S(1)} %add.368), channel_id=1, source_target_pairs={{0,64},{16,80},{32,96},{48,112},{64,0},{80,16},{96,32},{112,48},{1... | collective-permute-start | bytes 196616 | tf_op jit(solution)/shard_map/ppermute | solution.py:30
  214.3 5.6 %collective-permute-start.14 = (f32[32,512]{1,0:T(8,128)S(1)}, f32[32,512]{1,0:T(8,128)S(1)}, u32[]{:S(2)}, u32[]{:S(2)}) collective-permute-start(f32[32,512]{1,0:T(8,128)S(1)} %add.369), channel_id=1, source_target_pairs={{0,1},{1,0},{2,3},{3,2},{4,5},{5,4},{6,7},{7,6},{8,9},{9,8},{10,11... | collective-permute-start | bytes 196616 | tf_op jit(solution)/shard_map/ppermute | solution.py:30
  219.9 6.3 %collective-permute-start.15 = (f32[32,512]{1,0:T(8,128)S(1)}, f32[32,512]{1,0:T(8,128)S(1)}, u32[]{:S(2)}, u32[]{:S(2)}) collective-permute-start(f32[32,512]{1,0:T(8,128)S(1)} %add.370), channel_id=1, source_target_pairs={{0,2},{1,3},{2,0},{3,1},{4,6},{5,7},{6,4},{7,5},{8,10},{9,11},{10,... | collective-permute-start | bytes 196616 | tf_op jit(solution)/shard_map/ppermute | solution.py:30
  226.2 9.7 %collective-permute-start.16 = (f32[32,512]{1,0:T(8,128)S(1)}, f32[32,512]{1,0:T(8,128)S(1)}, u32[]{:S(2)}, u32[]{:S(2)}) collective-permute-start(f32[32,512]{1,0:T(8,128)S(1)} %add.371), channel_id=1, source_target_pairs={{0,4},{1,5},{2,6},{3,7},{4,0},{5,1},{6,2},{7,3},{8,12},{9,13},{10,... | collective-permute-start | bytes 196616 | tf_op jit(solution)/shard_map/ppermute | solution.py:30
  236.0 5.7 %collective-permute-start.17 = (f32[32,512]{1,0:T(8,128)S(1)}, f32[32,512]{1,0:T(8,128)S(1)}, u32[]{:S(2)}, u32[]{:S(2)}) collective-permute-start(f32[32,512]{1,0:T(8,128)S(1)} %add_multiply_fusion), channel_id=1, source_target_pairs={{0,16},{16,0},{32,48},{48,32},{64,80},{80,64},{96,112},{112,96},{1... | collective-permute-start | bytes 196616 | tf_op jit(solution)/shard_map/ppermute | solution.py:30
  258.4 46.3 %copy-start.5 = (bf16[384,512]{1,0:T(8,128)(2,1)S(1)}, bf16[384,512]{1,0:T(8,128)(2,1)}, u32[]{:S(2)}) copy-start(bf16[384,512]{1,0:T(8,128)(2,1)} %copy-done.4) | copy-start | bytes 1179652
  258.4 46.3 %copy-start.9 = (bf16[256,512]{1,0:T(8,128)(2,1)S(1)}, bf16[256,512]{1,0:T(8,128)(2,1)}, u32[]{:S(2)}) copy-start(bf16[256,512]{1,0:T(8,128)(2,1)} %param.13) | copy-start | bytes 786436
  258.4 46.1 %all-to-all-start.6 = ((bf16[8,384,256]{2,1,0:T(8,128)(2,1)}), bf16[8,384,256]{2,1,0:T(8,128)(2,1)S(1)}, u32[]{:S(2)}, u32[]{:S(2)}) async-start(bf16[8,384,256]{2,1,0:T(8,128)(2,1)} %bitcast.28), calls=%async_computation.6 | async-start | bytes 3145728 | tf_op jit(solution)/shard_map/all_to_all | solution.py:350
  264.1 7.2 %collective-permute-start.18 = (f32[64,512]{1,0:T(8,128)S(1)}, f32[64,512]{1,0:T(8,128)S(1)}, u32[]{:S(2)}, u32[]{:S(2)}) collective-permute-start(f32[64,512]{1,0:T(8,128)S(1)} %maximum_select_fusion.2), channel_id=1, source_target_pairs={{0,256},{128,384},{256,0},{384,128},{1,257},{129,385},{257,1},{385... | collective-permute-start | bytes 393224 | tf_op jit(solution)/shard_map/ppermute | solution.py:30
  271.3 7.4 %collective-permute-start.19 = (f32[128,512]{1,0:T(8,128)S(1)}, f32[128,512]{1,0:T(8,128)S(1)}, u32[]{:S(2)}, u32[]{:S(2)}) collective-permute-start(f32[128,512]{1,0:T(8,128)S(1)} %maximum_select_fusion.1), channel_id=1, source_target_pairs={{0,128},{128,0},{256,384},{384,256},{1,129},{129,1},{257,385},{385... | collective-permute-start | bytes 786440 | tf_op jit(solution)/shard_map/ppermute | solution.py:30
  278.8 6.6 %collective-permute-start.20 = (f32[256,512]{1,0:T(8,128)S(1)}, f32[256,512]{1,0:T(8,128)S(1)}, u32[]{:S(2)}, u32[]{:S(2)}) collective-permute-start(f32[256,512]{1,0:T(8,128)S(1)} %maximum_select_fusion), channel_id=1, source_target_pairs={{0,8},{8,0},{1,9},{9,1},{2,10},{10,2},{3,11},{11,3},{4,12},{12,4},... | collective-permute-start | bytes 1572872 | tf_op jit(solution)/shard_map/ppermute | solution.py:355
  (12 other events, 162.1 us)

commit v12 on v11

--- a/solution.py
+++ b/solution.py
@@ -283,7 +283,8 @@
 
     column_1, masks, masks_swapped = lax.optimization_barrier((column_1, masks, masks_swapped))
     leaving_1 = picked(passed_offset, column_1)
-    leaving_1, second = lax.optimization_barrier((leaving_1, node_feats[:, half_in:]))
+    leaving_1, second = lax.optimization_barrier((leaving_1, node_feats))
+    second = second[:, half_in:]
     arrived_1 = lax.all_to_all(leaving_1, ("x", "core"), 0, 0, tiled=True)
     column_2 = [x.reshape(-1, TILE, half_in) for x in gather_of_eight(second, "z")]
     leaving_2 = picked(passed_near, *column_2)

time: 307 us -> 307 us (level)
  no operation moved by 1% of the time
where the time goes in v12:
time: 307 us; the launch traced here: 306 us
  waiting for transfers between devices  123 us (40%)
  starting transfers between devices  122 us (40%)
  Pallas kernels  23.5 us (8%)
  other arithmetic  16 us (5%)
  local copies, waits for them, and re-layouts  12.8 us (4%)
  matrix products  7.61 us (2%)
    ppermute x11, starting transfers between devices, pair_swap(): return lax.ppermute(x, axis, [(i, i ^ bit) for i in range(n)])  43.8 us
    ppermute x11, waiting for transfers between devices, pair_swap(): return lax.ppermute(x, axis, [(i, i ^ bit) for i in range(n)])  36.6 us
    ppermute x8, starting transfers between devices, shifted(): return lax.ppermute(x, axis, [(i, (i + by) % n) for i in range(n)])  27.8 us
    ppermute x8, waiting for transfers between devices, shifted(): return lax.ppermute(x, axis, [(i, (i + by) % n) for i in range(n)])  25.1 us
    all_to_all x1, waiting for transfers between devices, shards(): lax.all_to_all(sums_2.reshape(rep_total, rows_here, half_in), 'rep', 0, 0...  21.2 us
    all_to_all x1, waiting for transfers between devices, shards(): lax.all_to_all(column_sums.reshape(z_total, rows_here, width_in), 'z', 0,...  18 us
    all_to_all x1, waiting for transfers between devices, shards(): returned = lax.all_to_all(returning, ('x', 'core'), 0, 0, tiled=True)  12.2 us
    all_to_all x1, starting transfers between devices, shards(): lax.all_to_all(jnp.broadcast_to(node_feats[None, :, :half_in], (z_total,...  10.9 us
  transfers between devices with their start and end apart: 28, of which 22 were waited for; matrix products, arithmetic and copies ran while one was open for 8% of the time, Pallas kernels for 3%

profile of v12, /device:TPU:1, one launch (start us, length us, event | category | flops | bytes accessed | tf_op | source)
XLA Modules:
  0.0 305.7 jit_solution(9139685177512276966)
XLA Ops:
  2.6 10.9 %all-to-all-start = ((bf16[8,384,128]{2,1,0:T(8,128)(2,1)}), bf16[8,384,128]{2,1,0:T(8,128)(2,1)}, u32[]{:S(2)}, u32[]{:S(2)}) async-start(bf16[8,384,128]{2,1,0:T(8,128)(2,1)} %broadcast_in_dim.89), calls=%async_computation | async-start | bytes 1572864 | tf_op jit(solution)/shard_map/all_to_all | solution.py:243
  20.0 10.9 %fusion.10 = (bf16[64,128,128]{2,1,0:T(8,128)(2,1)}, bf16[64,128,128]{2,1,0:T(8,128)(2,1)S(1)}) fusion(s32[64,128]{1,0:T(8,128)S(1)} %get-tuple-element.56, s32[64,128]{1,0:T(8,128)S(1)} %get-tuple-element.55, s32[64,128]{1,0:T(8,128)S(1)} %add_select_fusion.5, s32[64]{0:T(128)S(1)} %get-tuple-element.61), kind=kLoop, calls=%fused_computation.22 | loop fusion | flops 46137344 | bytes 4292864 | tf_op jit(solution)/shard_map/convert_element_type | solution.py:25
  30.9 6.3 %all-to-all-done = bf16[8,384,128]{2,1,0:T(8,128)(2,1)} async-done(((bf16[8,384,128]{2,1,0:T(8,128)(2,1)}), bf16[8,384,128]{2,1,0:T(8,128)(2,1)}, u32[]{:S(2)}, u32[]{:S(2)}) %all-to-all-start) | async-done | bytes 786464 | tf_op jit(solution)/shard_map/all_to_all | solution.py:243
  40.4 4.8 %all-to-all-start.1 = ((bf16[64,128,128]{2,1,0:T(8,128)(2,1)}), bf16[64,128,128]{2,1,0:T(8,128)(2,1)}, u32[]{:S(2)}, u32[]{:S(2)}) async-start(bf16[64,128,128]{2,1,0:T(8,128)(2,1)} %picked.2), calls=%async_computation.1 | async-start | bytes 4194304 | tf_op jit(solution)/shard_map/all_to_all | solution.py:288
  47.3 5.0 %collective-permute-start = (bf16[384,128]{1,0:T(8,128)(2,1)S(1)}, bf16[384,128]{1,0:T(8,128)(2,1)S(1)}, u32[]{:S(2)}, u32[]{:S(2)}) collective-permute-start(bf16[384,128]{1,0:T(8,128)(2,1)S(1)} %get-tuple-element.52), channel_id=1, source_target_pairs={{0,48},{16,64},{32,80},{48,96},{64,112},{80,0},{96,16},{112,32},{1... | collective-permute-start | bytes 294920 | tf_op jit(solution)/shard_map/ppermute | solution.py:186
  54.6 5.7 %collective-permute-done = bf16[384,128]{1,0:T(8,128)(2,1)S(1)} collective-permute-done((bf16[384,128]{1,0:T(8,128)(2,1)S(1)}, bf16[384,128]{1,0:T(8,128)(2,1)S(1)}, u32[]{:S(2)}, u32[]{:S(2)}) %collective-permute-start) | collective-permute-done | bytes 98336 | tf_op jit(solution)/shard_map/ppermute | solution.py:186
  60.3 3.6 %collective-permute-start.2 = (bf16[3,384,128]{2,1,0:T(8,128)(2,1)S(1)}, bf16[3,384,128]{2,1,0:T(8,128)(2,1)S(1)}, u32[]{:S(2)}, u32[]{:S(2)}) collective-permute-start(bf16[3,384,128]{2,1,0:T(8,128)(2,1)S(1)} %pad_maximum_fusion), channel_id=1, source_target_pairs={{0,16},{16,32},{32,48},{48,64},{64,80},{80,96},{96,112},{112,0},{1... | collective-permute-start | bytes 884744 | tf_op jit(solution)/shard_map/ppermute | solution.py:186
  66.9 4.8 %collective-permute-done.3 = bf16[2,384,128]{2,1,0:T(8,128)(2,1)S(1)} collective-permute-done((bf16[2,384,128]{2,1,0:T(8,128)(2,1)S(1)}, bf16[2,384,128]{2,1,0:T(8,128)(2,1)S(1)}, u32[]{:S(2)}, u32[]{:S(2)}) %collective-permute-start.3) | collective-permute-done | bytes 196640 | tf_op jit(solution)/shard_map/ppermute | solution.py:186
  75.7 5.9 %all-to-all-start.2 = ((bf16[64,128,128]{2,1,0:T(8,128)(2,1)}), bf16[64,128,128]{2,1,0:T(8,128)(2,1)}, u32[]{:S(2)}, u32[]{:S(2)}) async-start(bf16[64,128,128]{2,1,0:T(8,128)(2,1)} %picked.3), calls=%async_computation.2 | async-start | bytes 4194304 | tf_op jit(solution)/shard_map/all_to_all | solution.py:292
  84.7 5.2 %collective-permute-start.4 = (bf16[3,384,128]{2,1,0:T(8,128)(2,1)S(1)}, bf16[3,384,128]{2,1,0:T(8,128)(2,1)S(1)}, u32[]{:S(2)}, u32[]{:S(2)}) collective-permute-start(bf16[3,384,128]{2,1,0:T(8,128)(2,1)S(1)} %bitcast.83), channel_id=1, source_target_pairs={{0,7},{1,0},{2,1},{3,2},{4,3},{5,4},{6,5},{7,6},{8,15},{9,8},{10,9... | collective-permute-start | bytes 884744 | tf_op jit(solution)/shard_map/ppermute | solution.py:186
  91.9 7.5 %collective-permute-done.5 = bf16[2,384,128]{2,1,0:T(8,128)(2,1)S(1)} collective-permute-done((bf16[2,384,128]{2,1,0:T(8,128)(2,1)S(1)}, bf16[2,384,128]{2,1,0:T(8,128)(2,1)S(1)}, u32[]{:S(2)}, u32[]{:S(2)}) %collective-permute-start.5) | collective-permute-done | bytes 196640 | tf_op jit(solution)/shard_map/ppermute | solution.py:186
  102.8 3.7 %collective-permute-start.7 = (bf16[384,128]{1,0:T(8,128)(2,1)S(1)}, bf16[384,128]{1,0:T(8,128)(2,1)S(1)}, u32[]{:S(2)}, u32[]{:S(2)}) collective-permute-start(bf16[384,128]{1,0:T(8,128)(2,1)S(1)} %get-tuple-element.49), channel_id=1, source_target_pairs={{0,3},{1,4},{2,5},{3,6},{4,7},{5,0},{6,1},{7,2},{8,11},{9,12},{10,... | collective-permute-start | bytes 294920 | tf_op jit(solution)/shard_map/ppermute | solution.py:186
  106.6 4.8 %collective-permute-done.6 = bf16[384,128]{1,0:T(8,128)(2,1)S(1)} collective-permute-done((bf16[384,128]{1,0:T(8,128)(2,1)S(1)}, bf16[384,128]{1,0:T(8,128)(2,1)S(1)}, u32[]{:S(2)}, u32[]{:S(2)}) %collective-permute-start.6) | collective-permute-done | bytes 98336 | tf_op jit(solution)/shard_map/ppermute | solution.py:186
  111.4 4.3 %tile_sums.3 = bf16[24,128,128]{2,1,0:T(8,128)(2,1)} custom-call(s32[64]{0:T(128)} %get-tuple-element.41.offset_ref, bf16[64,128,128]{2,1,0:T(8,128)(2,1)} %copy-done.1, bf16[64,128,128]{2,1,0:T(8,128)(2,1)} %all-to-all-done.2.feat_ref), custom_call_target="tpu_custom_call" | custom-call | flops 268435456 | bytes 4194304 | tf_op jit(solution)/shard_map/tile_sums/pallas_call | solution.py:53
  115.7 4.5 %all-to-all-start.3 = ((bf16[8,384,128]{2,1,0:T(8,128)(2,1)}), bf16[8,384,128]{2,1,0:T(8,128)(2,1)S(1)}, u32[]{:S(2)}, u32[]{:S(2)}) async-start(bf16[8,384,128]{2,1,0:T(8,128)(2,1)} %bitcast.78), calls=%async_computation.3 | async-start | bytes 1572864 | tf_op jit(solution)/shard_map/all_to_all | solution.py:298
  122.6 21.2 %all-to-all-done.3 = bf16[8,384,128]{2,1,0:T(8,128)(2,1)S(1)} async-done(((bf16[8,384,128]{2,1,0:T(8,128)(2,1)}), bf16[8,384,128]{2,1,0:T(8,128)(2,1)S(1)}, u32[]{:S(2)}, u32[]{:S(2)}) %all-to-all-start.3) | async-done | bytes 786464 | tf_op jit(solution)/shard_map/all_to_all | solution.py:298
  164.3 6.9 %collective-permute-done.9 = f32[128,512]{1,0:T(8,128)S(1)} collective-permute-done((f32[128,512]{1,0:T(8,128)S(1)}, f32[128,512]{1,0:T(8,128)S(1)}, u32[]{:S(2)}, u32[]{:S(2)}) %collective-permute-start.9) | collective-permute-done | bytes 262176 | tf_op jit(solution)/shard_map/ppermute | solution.py:30
  171.3 4.2 %collective-permute-start.10 = (f32[64,512]{1,0:T(8,128)S(1)}, f32[64,512]{1,0:T(8,128)S(1)}, u32[]{:S(2)}, u32[]{:S(2)}) collective-permute-start(f32[64,512]{1,0:T(8,128)S(1)} %slice_select_fusion.1), channel_id=1, source_target_pairs={{0,256},{128,384},{256,0},{384,128},{1,257},{129,385},{257,1},{385... | collective-permute-start | bytes 393224 | tf_op jit(solution)/shard_map/ppermute | solution.py:30
  183.8 5.2 %collective-permute-start.12 = (f32[32,512]{1,0:T(8,128)S(1)}, f32[32,512]{1,0:T(8,128)S(1)}, u32[]{:S(2)}, u32[]{:S(2)}) collective-permute-start(f32[32,512]{1,0:T(8,128)S(1)} %select_add_fusion.3), channel_id=1, source_target_pairs={{0,32},{16,48},{32,0},{48,16},{64,96},{80,112},{96,64},{112,80},{1... | collective-permute-start | bytes 196616 | tf_op jit(solution)/shard_map/ppermute | solution.py:30
  192.2 5.2 %tile_products.1 = bf16[64,128,256]{2,1,0:T(8,128)(2,1)} custom-call(s32[64]{0:T(128)} %get-tuple-element.41.offset_ref, bf16[64,128,128]{2,1,0:T(8,128)(2,1)} %get-tuple-element.32.mask_ref, bf16[24,128,256]{2,1,0:T(8,128)(2,1)} %bitcast.77), custom_call_target="tpu_custom_call" | custom-call | flops 536870912 | bytes 6291456 | tf_op jit(solution)/shard_map/tile_products/pallas_call | solution.py:89
  197.3 7.6 %all-to-all-start.5 = ((bf16[64,128,256]{2,1,0:T(8,128)(2,1)}), bf16[64,128,256]{2,1,0:T(8,128)(2,1)}, u32[]{:S(2)}, u32[]{:S(2)}) async-start(bf16[64,128,256]{2,1,0:T(8,128)(2,1)} %tile_products.1), calls=%async_computation.5 | async-start | bytes 8388608 | tf_op jit(solution)/shard_map/all_to_all | solution.py:344
  204.9 6.0 %collective-permute-start.13 = (f32[32,512]{1,0:T(8,128)S(1)}, f32[32,512]{1,0:T(8,128)S(1)}, u32[]{:S(2)}, u32[]{:S(2)}) collective-permute-start(f32[32,512]{1,0:T(8,128)S(1)} %add.368), channel_id=1, source_target_pairs={{0,64},{16,80},{32,96},{48,112},{64,0},{80,16},{96,32},{112,48},{1... | collective-permute-start | bytes 196616 | tf_op jit(solution)/shard_map/ppermute | solution.py:30
  219.9 4.3 %collective-permute-start.15 = (f32[32,512]{1,0:T(8,128)S(1)}, f32[32,512]{1,0:T(8,128)S(1)}, u32[]{:S(2)}, u32[]{:S(2)}) collective-permute-start(f32[32,512]{1,0:T(8,128)S(1)} %add.370), channel_id=1, source_target_pairs={{0,2},{1,3},{2,0},{3,1},{4,6},{5,7},{6,4},{7,5},{8,10},{9,11},{10,... | collective-permute-start | bytes 196616 | tf_op jit(solution)/shard_map/ppermute | solution.py:30
  226.2 8.0 %collective-permute-start.16 = (f32[32,512]{1,0:T(8,128)S(1)}, f32[32,512]{1,0:T(8,128)S(1)}, u32[]{:S(2)}, u32[]{:S(2)}) collective-permute-start(f32[32,512]{1,0:T(8,128)S(1)} %add.371), channel_id=1, source_target_pairs={{0,4},{1,5},{2,6},{3,7},{4,0},{5,1},{6,2},{7,3},{8,12},{9,13},{10,... | collective-permute-start | bytes 196616 | tf_op jit(solution)/shard_map/ppermute | solution.py:30
  235.9 3.6 %collective-permute-start.17 = (f32[32,512]{1,0:T(8,128)S(1)}, f32[32,512]{1,0:T(8,128)S(1)}, u32[]{:S(2)}, u32[]{:S(2)}) collective-permute-start(f32[32,512]{1,0:T(8,128)S(1)} %add_multiply_fusion), channel_id=1, source_target_pairs={{0,16},{16,0},{32,48},{48,32},{64,80},{80,64},{96,112},{112,96},{1... | collective-permute-start | bytes 196616 | tf_op jit(solution)/shard_map/ppermute | solution.py:30
  241.6 12.2 %all-to-all-done.5.part_ref = bf16[64,128,256]{2,1,0:T(8,128)(2,1)} async-done(((bf16[64,128,256]{2,1,0:T(8,128)(2,1)}), bf16[64,128,256]{2,1,0:T(8,128)(2,1)}, u32[]{:S(2)}, u32[]{:S(2)}) %all-to-all-start.5) | async-done | bytes 4194336 | tf_op jit(solution)/shard_map/all_to_all | solution.py:344
  253.8 4.6 %summed_into.1 = bf16[24,128,256]{2,1,0:T(8,128)(2,1)} custom-call(s32[64]{0:T(128)S(1)} %copy-done.2, bf16[64,128,256]{2,1,0:T(8,128)(2,1)} %all-to-all-done.5.part_ref), custom_call_target="tpu_custom_call" | custom-call | flops 2097152 | bytes 4194304 | tf_op jit(solution)/shard_map/summed_into/pallas_call | solution.py:128
  258.4 5.6 %all-to-all-start.6 = ((bf16[8,384,256]{2,1,0:T(8,128)(2,1)}), bf16[8,384,256]{2,1,0:T(8,128)(2,1)S(1)}, u32[]{:S(2)}, u32[]{:S(2)}) async-start(bf16[8,384,256]{2,1,0:T(8,128)(2,1)} %bitcast.28), calls=%async_computation.6 | async-start | bytes 3145728 | tf_op jit(solution)/shard_map/all_to_all | solution.py:351
  266.2 5.0 %collective-permute-done.18 = f32[64,512]{1,0:T(8,128)S(1)} collective-permute-done((f32[64,512]{1,0:T(8,128)S(1)}, f32[64,512]{1,0:T(8,128)S(1)}, u32[]{:S(2)}, u32[]{:S(2)}) %collective-permute-start.18) | collective-permute-done | bytes 131104 | tf_op jit(solution)/shard_map/ppermute | solution.py:30
  273.5 5.2 %collective-permute-done.19 = f32[128,512]{1,0:T(8,128)S(1)} collective-permute-done((f32[128,512]{1,0:T(8,128)S(1)}, f32[128,512]{1,0:T(8,128)S(1)}, u32[]{:S(2)}, u32[]{:S(2)}) %collective-permute-start.19) | collective-permute-done | bytes 262176 | tf_op jit(solution)/shard_map/ppermute | solution.py:30
  278.7 5.1 %collective-permute-start.20 = (f32[256,512]{1,0:T(8,128)S(1)}, f32[256,512]{1,0:T(8,128)S(1)}, u32[]{:S(2)}, u32[]{:S(2)}) collective-permute-start(f32[256,512]{1,0:T(8,128)S(1)} %maximum_select_fusion), channel_id=1, source_target_pairs={{0,8},{8,0},{1,9},{9,1},{2,10},{10,2},{3,11},{11,3},{4,12},{12,4},... | collective-permute-start | bytes 1572872 | tf_op jit(solution)/shard_map/ppermute | solution.py:356
  286.4 18.0 %all-to-all-done.6 = bf16[8,384,256]{2,1,0:T(8,128)(2,1)S(1)} async-done(((bf16[8,384,256]{2,1,0:T(8,128)(2,1)}), bf16[8,384,256]{2,1,0:T(8,128)(2,1)S(1)}, u32[]{:S(2)}, u32[]{:S(2)}) %all-to-all-start.6) | async-done | bytes 1572896 | tf_op jit(solution)/shard_map/all_to_all | solution.py:351
  (136 shorter events, 88.9 us)
Async XLA Ops:
  2.6 34.5 %all-to-all-start = ((bf16[8,384,128]{2,1,0:T(8,128)(2,1)}), bf16[8,384,128]{2,1,0:T(8,128)(2,1)}, u32[]{:S(2)}, u32[]{:S(2)}) async-start(bf16[8,384,128]{2,1,0:T(8,128)(2,1)} %broadcast_in_dim.89), calls=%async_computation | async-start | bytes 1572864 | tf_op jit(solution)/shard_map/all_to_all | solution.py:243
  30.9 50.8 %copy-start.1 = (bf16[64,128,128]{2,1,0:T(8,128)(2,1)}, bf16[64,128,128]{2,1,0:T(8,128)(2,1)S(1)}, u32[]{:S(2)}) copy-start(bf16[64,128,128]{2,1,0:T(8,128)(2,1)S(1)} %get-tuple-element.22.mask_ref) | copy-start | bytes 6291460
  40.4 35.3 %all-to-all-start.1 = ((bf16[64,128,128]{2,1,0:T(8,128)(2,1)}), bf16[64,128,128]{2,1,0:T(8,128)(2,1)}, u32[]{:S(2)}, u32[]{:S(2)}) async-start(bf16[64,128,128]{2,1,0:T(8,128)(2,1)} %picked.2), calls=%async_computation.1 | async-start | bytes 4194304 | tf_op jit(solution)/shard_map/all_to_all | solution.py:288
  45.2 9.4 %collective-permute-start.1 = (bf16[384,128]{1,0:T(8,128)(2,1)S(1)}, bf16[384,128]{1,0:T(8,128)(2,1)S(1)}, u32[]{:S(2)}, u32[]{:S(2)}) collective-permute-start(bf16[384,128]{1,0:T(8,128)(2,1)S(1)} %get-tuple-element.52), channel_id=1, source_target_pairs={{0,80},{16,96},{32,112},{48,0},{64,16},{80,32},{96,48},{112,64},{1... | collective-permute-start | bytes 294920 | tf_op jit(solution)/shard_map/ppermute | solution.py:186
  47.3 12.9 %collective-permute-start = (bf16[384,128]{1,0:T(8,128)(2,1)S(1)}, bf16[384,128]{1,0:T(8,128)(2,1)S(1)}, u32[]{:S(2)}, u32[]{:S(2)}) collective-permute-start(bf16[384,128]{1,0:T(8,128)(2,1)S(1)} %get-tuple-element.52), channel_id=1, source_target_pairs={{0,48},{16,64},{32,80},{48,96},{64,112},{80,0},{96,16},{112,32},{1... | collective-permute-start | bytes 294920 | tf_op jit(solution)/shard_map/ppermute | solution.py:186
  60.3 11.4 %collective-permute-start.2 = (bf16[3,384,128]{2,1,0:T(8,128)(2,1)S(1)}, bf16[3,384,128]{2,1,0:T(8,128)(2,1)S(1)}, u32[]{:S(2)}, u32[]{:S(2)}) collective-permute-start(bf16[3,384,128]{2,1,0:T(8,128)(2,1)S(1)} %pad_maximum_fusion), channel_id=1, source_target_pairs={{0,16},{16,32},{32,48},{48,64},{64,80},{80,96},{96,112},{112,0},{1... | collective-permute-start | bytes 884744 | tf_op jit(solution)/shard_map/ppermute | solution.py:186
  64.0 7.7 %collective-permute-start.3 = (bf16[2,384,128]{2,1,0:T(8,128)(2,1)S(1)}, bf16[2,384,128]{2,1,0:T(8,128)(2,1)S(1)}, u32[]{:S(2)}, u32[]{:S(2)}) collective-permute-start(bf16[2,384,128]{2,1,0:T(8,128)(2,1)S(1)} %pad_maximum_fusion.1), channel_id=1, source_target_pairs={{0,112},{16,0},{32,16},{48,32},{64,48},{80,64},{96,80},{112,96},{1... | collective-permute-start | bytes 589832 | tf_op jit(solution)/shard_map/ppermute | solution.py:186
  75.7 35.7 %all-to-all-start.2 = ((bf16[64,128,128]{2,1,0:T(8,128)(2,1)}), bf16[64,128,128]{2,1,0:T(8,128)(2,1)}, u32[]{:S(2)}, u32[]{:S(2)}) async-start(bf16[64,128,128]{2,1,0:T(8,128)(2,1)} %picked.3), calls=%async_computation.2 | async-start | bytes 4194304 | tf_op jit(solution)/shard_map/all_to_all | solution.py:292
  84.7 14.7 %collective-permute-start.4 = (bf16[3,384,128]{2,1,0:T(8,128)(2,1)S(1)}, bf16[3,384,128]{2,1,0:T(8,128)(2,1)S(1)}, u32[]{:S(2)}, u32[]{:S(2)}) collective-permute-start(bf16[3,384,128]{2,1,0:T(8,128)(2,1)S(1)} %bitcast.83), channel_id=1, source_target_pairs={{0,7},{1,0},{2,1},{3,2},{4,3},{5,4},{6,5},{7,6},{8,15},{9,8},{10,9... | collective-permute-start | bytes 884744 | tf_op jit(solution)/shard_map/ppermute | solution.py:186
  90.0 9.4 %collective-permute-start.5 = (bf16[2,384,128]{2,1,0:T(8,128)(2,1)S(1)}, bf16[2,384,128]{2,1,0:T(8,128)(2,1)S(1)}, u32[]{:S(2)}, u32[]{:S(2)}) collective-permute-start(bf16[2,384,128]{2,1,0:T(8,128)(2,1)S(1)} %bitcast.85), channel_id=1, source_target_pairs={{0,1},{1,2},{2,3},{3,4},{4,5},{5,6},{6,7},{7,0},{8,9},{9,10},{10,1... | collective-permute-start | bytes 589832 | tf_op jit(solution)/shard_map/ppermute | solution.py:186
  99.5 11.9 %collective-permute-start.6 = (bf16[384,128]{1,0:T(8,128)(2,1)S(1)}, bf16[384,128]{1,0:T(8,128)(2,1)S(1)}, u32[]{:S(2)}, u32[]{:S(2)}) collective-permute-start(bf16[384,128]{1,0:T(8,128)(2,1)S(1)} %get-tuple-element.50), channel_id=1, source_target_pairs={{0,5},{1,6},{2,7},{3,0},{4,1},{5,2},{6,3},{7,4},{8,13},{9,14},{10,... | collective-permute-start | bytes 294920 | tf_op jit(solution)/shard_map/ppermute | solution.py:186
  102.8 12.9 %collective-permute-start.7 = (bf16[384,128]{1,0:T(8,128)(2,1)S(1)}, bf16[384,128]{1,0:T(8,128)(2,1)S(1)}, u32[]{:S(2)}, u32[]{:S(2)}) collective-permute-start(bf16[384,128]{1,0:T(8,128)(2,1)S(1)} %get-tuple-element.49), channel_id=1, source_target_pairs={{0,3},{1,4},{2,5},{3,6},{4,7},{5,0},{6,1},{7,2},{8,11},{9,12},{10,... | collective-permute-start | bytes 294920 | tf_op jit(solution)/shard_map/ppermute | solution.py:186
  115.7 28.1 %all-to-all-start.3 = ((bf16[8,384,128]{2,1,0:T(8,128)(2,1)}), bf16[8,384,128]{2,1,0:T(8,128)(2,1)S(1)}, u32[]{:S(2)}, u32[]{:S(2)}) async-start(bf16[8,384,128]{2,1,0:T(8,128)(2,1)} %bitcast.78), calls=%async_computation.3 | async-start | bytes 1572864 | tf_op jit(solution)/shard_map/all_to_all | solution.py:298
  149.1 41.9 %all-to-all-start.4 = ((bf16[8,384,256]{2,1,0:T(8,128)(2,1)}), bf16[8,384,256]{2,1,0:T(8,128)(2,1)S(1)}, u32[]{:S(2)}, u32[]{:S(2)}) async-start(bf16[8,384,256]{2,1,0:T(8,128)(2,1)} %broadcast_in_dim.95), calls=%async_computation.4 | async-start | bytes 3145728 | tf_op jit(solution)/shard_map/all_to_all | solution.py:327
  155.3 4.1 %collective-permute-start.8 = (f32[256,512]{1,0:T(8,128)}, f32[256,512]{1,0:T(8,128)S(1)}, u32[]{:S(2)}, u32[]{:S(2)}) collective-permute-start(f32[256,512]{1,0:T(8,128)} %get-tuple-element.62), channel_id=1, source_target_pairs={{0,8},{8,0},{1,9},{9,1},{2,10},{10,2},{3,11},{11,3},{4,12},{12,4},... | collective-permute-start | bytes 1572872 | tf_op jit(solution)/shard_map/ppermute | solution.py:335
  161.6 9.6 %collective-permute-start.9 = (f32[128,512]{1,0:T(8,128)S(1)}, f32[128,512]{1,0:T(8,128)S(1)}, u32[]{:S(2)}, u32[]{:S(2)}) collective-permute-start(f32[128,512]{1,0:T(8,128)S(1)} %slice_select_fusion), channel_id=1, source_target_pairs={{0,128},{128,0},{256,384},{384,256},{1,129},{129,1},{257,385},{385... | collective-permute-start | bytes 786440 | tf_op jit(solution)/shard_map/ppermute | solution.py:30
  171.3 7.5 %collective-permute-start.10 = (f32[64,512]{1,0:T(8,128)S(1)}, f32[64,512]{1,0:T(8,128)S(1)}, u32[]{:S(2)}, u32[]{:S(2)}) collective-permute-start(f32[64,512]{1,0:T(8,128)S(1)} %slice_select_fusion.1), channel_id=1, source_target_pairs={{0,256},{128,384},{256,0},{384,128},{1,257},{129,385},{257,1},{385... | collective-permute-start | bytes 393224 | tf_op jit(solution)/shard_map/ppermute | solution.py:30
  178.8 5.0 %collective-permute-start.11 = (f32[32,512]{1,0:T(8,128)S(1)}, f32[32,512]{1,0:T(8,128)S(1)}, u32[]{:S(2)}, u32[]{:S(2)}) collective-permute-start(f32[32,512]{1,0:T(8,128)S(1)} %slice_select_fusion.2), channel_id=1, source_target_pairs={{0,16},{16,0},{32,48},{48,32},{64,80},{80,64},{96,112},{112,96},{1... | collective-permute-start | bytes 196616 | tf_op jit(solution)/shard_map/ppermute | solution.py:30
  183.8 7.1 %collective-permute-start.12 = (f32[32,512]{1,0:T(8,128)S(1)}, f32[32,512]{1,0:T(8,128)S(1)}, u32[]{:S(2)}, u32[]{:S(2)}) collective-permute-start(f32[32,512]{1,0:T(8,128)S(1)} %select_add_fusion.3), channel_id=1, source_target_pairs={{0,32},{16,48},{32,0},{48,16},{64,96},{80,112},{96,64},{112,80},{1... | collective-permute-start | bytes 196616 | tf_op jit(solution)/shard_map/ppermute | solution.py:30
  197.3 56.5 %copy-start.2 = (s32[64]{0:T(128)S(1)}, s32[64]{0:T(128)}, u32[]{:S(2)}) copy-start(s32[64]{0:T(128)} %get-tuple-element.64.offset_ref) | copy-start | bytes 772
  197.3 56.5 %all-to-all-start.5 = ((bf16[64,128,256]{2,1,0:T(8,128)(2,1)}), bf16[64,128,256]{2,1,0:T(8,128)(2,1)}, u32[]{:S(2)}, u32[]{:S(2)}) async-start(bf16[64,128,256]{2,1,0:T(8,128)(2,1)} %tile_products.1), calls=%async_computation.5 | async-start | bytes 8388608 | tf_op jit(solution)/shard_map/all_to_all | solution.py:344
  204.9 9.3 %collective-permute-start.13 = (f32[32,512]{1,0:T(8,128)S(1)}, f32[32,512]{1,0:T(8,128)S(1)}, u32[]{:S(2)}, u32[]{:S(2)}) collective-permute-start(f32[32,512]{1,0:T(8,128)S(1)} %add.368), channel_id=1, source_target_pairs={{0,64},{16,80},{32,96},{48,112},{64,0},{80,16},{96,32},{112,48},{1... | collective-permute-start | bytes 196616 | tf_op jit(solution)/shard_map/ppermute | solution.py:30
  214.2 5.6 %collective-permute-start.14 = (f32[32,512]{1,0:T(8,128)S(1)}, f32[32,512]{1,0:T(8,128)S(1)}, u32[]{:S(2)}, u32[]{:S(2)}) collective-permute-start(f32[32,512]{1,0:T(8,128)S(1)} %add.369), channel_id=1, source_target_pairs={{0,1},{1,0},{2,3},{3,2},{4,5},{5,4},{6,7},{7,6},{8,9},{9,8},{10,11... | collective-permute-start | bytes 196616 | tf_op jit(solution)/shard_map/ppermute | solution.py:30
  219.9 6.3 %collective-permute-start.15 = (f32[32,512]{1,0:T(8,128)S(1)}, f32[32,512]{1,0:T(8,128)S(1)}, u32[]{:S(2)}, u32[]{:S(2)}) collective-permute-start(f32[32,512]{1,0:T(8,128)S(1)} %add.370), channel_id=1, source_target_pairs={{0,2},{1,3},{2,0},{3,1},{4,6},{5,7},{6,4},{7,5},{8,10},{9,11},{10,... | collective-permute-start | bytes 196616 | tf_op jit(solution)/shard_map/ppermute | solution.py:30
  226.2 9.7 %collective-permute-start.16 = (f32[32,512]{1,0:T(8,128)S(1)}, f32[32,512]{1,0:T(8,128)S(1)}, u32[]{:S(2)}, u32[]{:S(2)}) collective-permute-start(f32[32,512]{1,0:T(8,128)S(1)} %add.371), channel_id=1, source_target_pairs={{0,4},{1,5},{2,6},{3,7},{4,0},{5,1},{6,2},{7,3},{8,12},{9,13},{10,... | collective-permute-start | bytes 196616 | tf_op jit(solution)/shard_map/ppermute | solution.py:30
  235.9 5.7 %collective-permute-start.17 = (f32[32,512]{1,0:T(8,128)S(1)}, f32[32,512]{1,0:T(8,128)S(1)}, u32[]{:S(2)}, u32[]{:S(2)}) collective-permute-start(f32[32,512]{1,0:T(8,128)S(1)} %add_multiply_fusion), channel_id=1, source_target_pairs={{0,16},{16,0},{32,48},{48,32},{64,80},{80,64},{96,112},{112,96},{1... | collective-permute-start | bytes 196616 | tf_op jit(solution)/shard_map/ppermute | solution.py:30
  258.4 46.3 %copy-start.5 = (bf16[384,512]{1,0:T(8,128)(2,1)S(1)}, bf16[384,512]{1,0:T(8,128)(2,1)}, u32[]{:S(2)}) copy-start(bf16[384,512]{1,0:T(8,128)(2,1)} %copy-done.4) | copy-start | bytes 1179652
  258.4 46.3 %copy-start.9 = (bf16[256,512]{1,0:T(8,128)(2,1)S(1)}, bf16[256,512]{1,0:T(8,128)(2,1)}, u32[]{:S(2)}) copy-start(bf16[256,512]{1,0:T(8,128)(2,1)} %param.13) | copy-start | bytes 786436
  258.4 46.1 %all-to-all-start.6 = ((bf16[8,384,256]{2,1,0:T(8,128)(2,1)}), bf16[8,384,256]{2,1,0:T(8,128)(2,1)S(1)}, u32[]{:S(2)}, u32[]{:S(2)}) async-start(bf16[8,384,256]{2,1,0:T(8,128)(2,1)} %bitcast.28), calls=%async_computation.6 | async-start | bytes 3145728 | tf_op jit(solution)/shard_map/all_to_all | solution.py:351
  264.0 7.2 %collective-permute-start.18 = (f32[64,512]{1,0:T(8,128)S(1)}, f32[64,512]{1,0:T(8,128)S(1)}, u32[]{:S(2)}, u32[]{:S(2)}) collective-permute-start(f32[64,512]{1,0:T(8,128)S(1)} %maximum_select_fusion.2), channel_id=1, source_target_pairs={{0,256},{128,384},{256,0},{384,128},{1,257},{129,385},{257,1},{385... | collective-permute-start | bytes 393224 | tf_op jit(solution)/shard_map/ppermute | solution.py:30
  271.3 7.4 %collective-permute-start.19 = (f32[128,512]{1,0:T(8,128)S(1)}, f32[128,512]{1,0:T(8,128)S(1)}, u32[]{:S(2)}, u32[]{:S(2)}) collective-permute-start(f32[128,512]{1,0:T(8,128)S(1)} %maximum_select_fusion.1), channel_id=1, source_target_pairs={{0,128},{128,0},{256,384},{384,256},{1,129},{129,1},{257,385},{385... | collective-permute-start | bytes 786440 | tf_op jit(solution)/shard_map/ppermute | solution.py:30
  278.7 6.6 %collective-permute-start.20 = (f32[256,512]{1,0:T(8,128)S(1)}, f32[256,512]{1,0:T(8,128)S(1)}, u32[]{:S(2)}, u32[]{:S(2)}) collective-permute-start(f32[256,512]{1,0:T(8,128)S(1)} %maximum_select_fusion), channel_id=1, source_target_pairs={{0,8},{8,0},{1,9},{9,1},{2,10},{10,2},{3,11},{11,3},{4,12},{12,4},... | collective-permute-start | bytes 1572872 | tf_op jit(solution)/shard_map/ppermute | solution.py:356
  (12 other events, 139.7 us)
